TPU v7x, 32 devices: a whole 2x2x4 slice. The times are simulated.
32 devices in a mesh: dp: 2 (over x), expert: 8 (over z, y), tensor: 2 (over core).
Axes of the slice: x: 2, y: 2, z: 4, core: 2. Of those that a mesh axis runs over, the one named last changes fastest.
Arguments:
- tokens: bfloat16 [2048, 2048], P(('dp', 'expert'), 'tensor'), may hold values from -6 to 6
- routes: int32 [2048, 4], P(('dp', 'expert')), may hold values from 0 to 7, all different within a row; in each aligned block of 128 rows (0 to 127, 128 to 255, ...) at most 80 rows name the same one
- gates: float32 [2048, 4], P(('dp', 'expert')), may hold values from 0.05 to 1
- w_in: bfloat16 [8, 768, 2048], P('expert', 'tensor'), may hold values from -0.125 to 0.125
- w_out: bfloat16 [8, 768, 2048], P('expert', 'tensor'), may hold values from -0.21875 to 0.21875
- cotangent: bfloat16 [2048, 2048], P(('dp', 'expert'), 'tensor'), may hold values from -1.796875 to 1.796875
Outputs:
- mixed: bfloat16 [2048, 2048], P(('dp', 'expert'), 'tensor')
- grad_tokens: bfloat16 [2048, 2048], P(('dp', 'expert'), 'tensor')
- grad_gates: float32 [2048, 4], P(('dp', 'expert'))
- grad_in: float32 [8, 768, 2048], P('expert', 'tensor', 'dp')
- grad_out: float32 [8, 768, 2048], P('expert', 'tensor', 'dp')
Inputs may be any that keep to these rules, and one draw needn't show every extreme that they name: `routes`: each row names 4 different experts. The rows of one device (aligned blocks of 128 rows) name no expert more than 80 times, and in every draw some block names some expert exactly 80 times.
All inputs are finite; a program needn't handle non-finite values.
Results may differ from a plain program's by a relative error of at most 0.018.
Values may be sent and summed in bfloat16 or wider, within the bound.
No kernel may reach another device: no remote copies, remote signals or barrier semaphores. Data moves between devices by JAX's collectives and lax.ppermute only.
A program may use at most 64 MiB of HBM per device.

v0:
```python
import jax
import jax.numpy as jnp
from jax import lax
from jax.sharding import PartitionSpec as P


def silu_slope(pre_value):
    logistic = jax.nn.sigmoid(pre_value)
    return logistic * (1.0 + pre_value * (1.0 - logistic))


def to_owner(slot_rows):
    return lax.all_to_all(slot_rows, "expert", split_axis=0, concat_axis=0, tiled=True)


def to_source(owner_rows):
    return lax.all_to_all(owner_rows, "expert", split_axis=0, concat_axis=0, tiled=True)


def core_halves(local_part):
    return lax.all_gather(local_part, "tensor", axis=3, tiled=True)


def per_device(tokens, routes, gates, w_in, w_out, cotangent):
    tok_count, top_count = routes.shape
    exp_local, hid_local, model_width = w_in.shape
    owners = lax.axis_size("expert")
    experts = exp_local * owners
    capacity = min(
        tok_count, ((tok_count * top_count * 5 + 4 * experts - 1) // (4 * experts) + 7) // 8 * 8
    )
    pair_count = tok_count * top_count
    half_width = tokens.shape[1]
    flat_routes = routes.reshape(pair_count)
    one_hot = (flat_routes[:, None] == jnp.arange(experts, dtype=jnp.int32)[None, :]).astype(
        jnp.int32
    )
    rank_before = jnp.cumsum(one_hot, axis=0) - one_hot
    slot_index = jnp.sum(rank_before * one_hot, axis=1)
    destination = flat_routes * capacity + slot_index
    source = (
        jnp.full((experts * capacity,), pair_count, jnp.int32)
        .at[destination]
        .set(jnp.arange(pair_count, dtype=jnp.int32))
    )
    source_row = source // top_count
    zero_row = jnp.zeros((1, half_width), tokens.dtype)
    tokens_pad = jnp.concatenate([tokens, zero_row], axis=0)
    cotangent_pad = jnp.concatenate([cotangent, zero_row], axis=0)
    gate_pad = jnp.concatenate([gates.reshape(pair_count), jnp.zeros((1,), jnp.float32)])
    w_in_cols, w_out_cols = (
        lax.all_to_all(w_in, "tensor", split_axis=2, concat_axis=1, tiled=True),
        lax.all_to_all(w_out, "tensor", split_axis=2, concat_axis=1, tiled=True),
    )
    rows_send = tokens_pad[source_row].reshape(experts, capacity, half_width)
    scaled = (gate_pad[source][:, None] * cotangent_pad[source_row].astype(jnp.float32)).astype(
        jnp.bfloat16
    )
    scaled_send = scaled.reshape(experts, capacity, half_width)
    received = to_owner(rows_send)
    grad_received = to_owner(scaled_send)
    received = received.reshape(owners, exp_local, capacity, half_width)
    grad_received = grad_received.reshape(owners, exp_local, capacity, half_width)
    rows_full = core_halves(received)
    pre_value = jnp.einsum("necd,efd->necf", rows_full, w_in, preferred_element_type=jnp.float32)
    hidden = jax.nn.silu(pre_value).astype(jnp.bfloat16)
    hidden_full = core_halves(hidden)
    expert_out = jnp.einsum(
        "necf,efd->necd", hidden_full, w_out_cols, preferred_element_type=jnp.float32
    ).astype(jnp.bfloat16)
    grad_full = core_halves(grad_received)
    grad_hidden = jnp.einsum("necd,efd->necf", grad_full, w_out, preferred_element_type=jnp.float32)
    grad_pre = (grad_hidden * silu_slope(pre_value)).astype(jnp.bfloat16)
    grad_pre_full = core_halves(grad_pre)
    grad_rows = jnp.einsum(
        "necf,efd->necd", grad_pre_full, w_in_cols, preferred_element_type=jnp.float32
    ).astype(jnp.bfloat16)
    out_send = expert_out.reshape(experts, capacity, half_width)
    back_send = grad_rows.reshape(experts, capacity, half_width)
    returned = to_source(out_send)
    grad_returned = to_source(back_send)
    returned = returned.reshape(experts * capacity, half_width)
    grad_returned = grad_returned.reshape(experts * capacity, half_width)
    picked = returned[destination].reshape(tok_count, top_count, half_width).astype(jnp.float32)
    mixed = jnp.sum(gates[:, :, None] * picked, axis=1).astype(jnp.bfloat16)
    cotangent_wide = cotangent.astype(jnp.float32)
    gate_part = jnp.sum(cotangent_wide[:, None, :] * picked, axis=2)
    grad_gates = lax.psum(gate_part, "tensor")
    gathered_back = (
        grad_returned[destination].reshape(tok_count, top_count, half_width).astype(jnp.float32)
    )
    grad_tokens = jnp.sum(gathered_back, axis=1).astype(jnp.bfloat16)
    block_part = rows_full
    grad_in_rows = lax.psum_scatter(
        jnp.einsum(
            "necd,necf->def", block_part, grad_pre, preferred_element_type=jnp.float32
        ).astype(jnp.bfloat16),
        "dp",
        scatter_dimension=0,
        tiled=True,
    ).astype(jnp.float32)
    block_part = grad_full
    grad_out_rows = lax.psum_scatter(
        jnp.einsum("necd,necf->def", block_part, hidden, preferred_element_type=jnp.float32).astype(
            jnp.bfloat16
        ),
        "dp",
        scatter_dimension=0,
        tiled=True,
    ).astype(jnp.float32)
    grad_in = jnp.transpose(grad_in_rows, (1, 2, 0))
    grad_out = jnp.transpose(grad_out_rows, (1, 2, 0))
    return (mixed, grad_tokens, grad_gates, grad_in, grad_out)


def solution(mesh):
    placed = (
        P(("dp", "expert"), "tensor"),
        P(("dp", "expert"), None),
        P(("dp", "expert"), None),
        P("expert", "tensor", None),
        P("expert", "tensor", None),
        P(("dp", "expert"), "tensor"),
    )
    return jax.shard_map(
        per_device,
        mesh=mesh,
        in_specs=placed,
        out_specs=(
            P(("dp", "expert"), "tensor"),
            P(("dp", "expert"), "tensor"),
            P(("dp", "expert"), None),
            P("expert", "tensor", "dp"),
            P("expert", "tensor", "dp"),
        ),
        check_vma=False,
    )
```

profile of v0, /device:TPU:0, one launch (start us, length us, event | category | flops | bytes accessed | tf_op | source)
XLA Modules:
  0.0 325.5 jit_solution(5582570963458357018)
XLA Ops:
  14.1 3.5 %gather_fusion = bf16[640,1024]{1,0:T(8,128)(2,1)} fusion(bf16[129,1024]{1,0:T(8,128)(2,1)S(1)} %concatenate.9, s32[1024]{0:T(1024)S(1)} %get-tuple-element.22), kind=kCustom, calls=%fused_computation | custom fusion | bytes 2624000 | tf_op jit(solution)/shard_map/gather | solution.py:55
  17.5 7.4 %all-to-all-start = ((bf16[8,80,1024]{2,1,0:T(8,128)(2,1)}), bf16[8,80,1024]{2,1,0:T(8,128)(2,1)S(1)}, u32[]{:S(2)}, u32[]{:S(2)}) async-start(bf16[8,80,1024]{2,1,0:T(8,128)(2,1)} %bitcast.4), calls=%async_computation | async-start | bytes 2621440 | tf_op jit(solution)/shard_map/all_to_all | solution.py:13
  25.2 31.1 %all-to-all-done = bf16[8,80,1024]{2,1,0:T(8,128)(2,1)S(1)} async-done(((bf16[8,80,1024]{2,1,0:T(8,128)(2,1)}), bf16[8,80,1024]{2,1,0:T(8,128)(2,1)S(1)}, u32[]{:S(2)}, u32[]{:S(2)}) %all-to-all-start) | async-done | bytes 1310752 | tf_op jit(solution)/shard_map/all_to_all | solution.py:13
  57.5 2.8 gather_fusion.3
  60.4 2.8 gather_fusion.2
  63.5 35.2 %all_to_all.50 = bf16[8,80,1024]{2,1,0:T(8,128)(2,1)} all-to-all(bf16[8,80,1024]{2,1,0:T(8,128)(2,1)S(1)} %fusion), channel_id=1, replica_groups=mesh['dp'=2,'expert'=8,'tensor'=2] {'expert'}, dimensions={0} | all-to-all | bytes 2621440 | tf_op jit(solution)/shard_map/all_to_all | solution.py:13
  99.0 4.5 %multiply_convert_fusion = (bf16[8,1,80,384]{3,2,0,1:T(8,128)(2,1)}, f32[8,1,80,384]{3,2,0,1:T(8,128)}) fusion(bf16[8,80,2048]{2,1,0:T(8,128)(2,1)} %all-gather.5.cloned.1.call-done, bf16[1,384,2048]{2,1,0:T(8,128)(2,1)S(1)} %copy-done.8), kind=kOutput, calls=%fused_computation.28 | convolution fusion | flops 1007861760 | bytes 5668864 | tf_op jit(solution)/shard_map/necd,efd->necf/dot_general | solution.py:65
  103.6 5.7 %all-gather.7.cloned.1.call-done = bf16[8,80,2048]{2,1,0:T(8,128)(2,1)} async-done(((bf16[8,80,1024]{2,1,0:T(8,128)(2,1)}), bf16[8,80,2048]{2,1,0:T(8,128)(2,1)}) %all-gather.7.cloned.1.call-update) | async-done | bytes 2621456 | tf_op jit(solution)/shard_map/all_gather | solution.py:21
  109.3 3.8 %fusion.16 = bf16[8,1,80,384]{3,2,0,1:T(8,128)(2,1)S(1)} fusion(bf16[8,80,2048]{2,1,0:T(8,128)(2,1)} %all-gather.7.cloned.1.call-done, bf16[1,384,2048]{2,1,0:T(8,128)(2,1)S(1)} %copy-done.7, f32[8,1,80,384]{3,2,0,1:T(8,128)} %get-tuple-element.20), kind=kOutput, calls=%fused_computation.25 | convolution fusion | flops 1008844800 | bytes 5668864 | tf_op jit(solution)/shard_map/necd,efd->necf/dot_general | solution.py:72
  113.9 2.6 fusion.1
  116.5 8.0 %copy.35 = bf16[1,384,2048]{1,0,2:T(2,128)(2,1)S(1)} copy(bf16[1,384,2048]{2,1,0:T(8,128)(2,1)} %param.10) | data formatting | bytes 3145728 | tf_op args[4]
  125.0 34.4 %reduce.7 = bf16[2048,384]{1,0:T(8,128)(2,1)} reduce(bf16[2048,1,384]{2,1,0:T(2,128)(2,1)S(1)} %bitcast.105, bf16[]{:T(256)} %broadcast.97), dimensions={1}, to_apply=%bitcast.91.reduce_sub_computation | reduce | bytes 3145730
  159.5 2.5 reshape.232
  162.0 4.8 %all-to-all-start.1 = ((bf16[2,2,196608]{2,1,0:T(2,128)(2,1)}), bf16[2,2,196608]{2,1,0:T(2,128)(2,1)}, u32[]{:S(2)}, u32[]{:S(2)}) async-start(bf16[2,2,196608]{2,1,0:T(2,128)(2,1)} %reshape.232), calls=%async_computation.1 | async-start | bytes 3145728 | tf_op jit(solution)/shard_map/all_to_all | solution.py:53
  166.8 7.9 %copy.38 = bf16[1,384,2048]{1,0,2:T(2,128)(2,1)S(1)} copy(bf16[1,384,2048]{2,1,0:T(8,128)(2,1)} %param.9) | data formatting | bytes 3145728 | tf_op args[3]
  174.8 34.4 %reduce.8 = bf16[2048,384]{1,0:T(8,128)(2,1)} reduce(bf16[2048,1,384]{2,1,0:T(2,128)(2,1)S(1)} %bitcast.106, bf16[]{:T(256)} %broadcast.97), dimensions={1}, to_apply=%bitcast.93.reduce_sub_computation | reduce | bytes 3145730
  209.2 2.5 reshape.234
  211.7 4.6 %all-to-all-start.4 = ((bf16[2,2,196608]{2,1,0:T(2,128)(2,1)}), bf16[2,2,196608]{2,1,0:T(2,128)(2,1)}, u32[]{:S(2)}, u32[]{:S(2)}) async-start(bf16[2,2,196608]{2,1,0:T(2,128)(2,1)} %reshape.234), calls=%async_computation.4 | async-start | bytes 3145728 | tf_op jit(solution)/shard_map/all_to_all | solution.py:52
  216.3 2.5 reshape.233
  222.0 2.6 all_gather.13
  226.8 5.8 %all-to-all-start.2 = ((bf16[8,80,1024]{2,1,0:T(8,128)(2,1)}), bf16[8,80,1024]{2,1,0:T(8,128)(2,1)S(1)}, u32[]{:S(2)}, u32[]{:S(2)}) async-start(bf16[8,80,1024]{2,1,0:T(8,128)(2,1)} %convolution_convert_fusion.1), calls=%async_computation.2 | async-start | bytes 2621440 | tf_op jit(solution)/shard_map/all_to_all | solution.py:17
  232.7 3.6 %reshape.235 = bf16[2048,1,384]{2,1,0:T(2,128)(2,1)} reshape(bf16[2,2,196608]{2,1,0:T(2,128)(2,1)} %all-to-all-done.4) | data formatting | bytes 3145728
  240.1 4.4 %fusion.2 = bf16[2048,1,384]{0,2,1:T(8,128)(2,1)} fusion(bf16[8,80,2048]{2,1,0:T(8,128)(2,1)} %all-gather.7.cloned.1.call-done, bf16[8,1,80,384]{3,2,0,1:T(8,128)(2,1)S(1)} %copy-done.5), kind=kOutput, calls=%fused_computation.11 | convolution fusion | flops 1007419392 | bytes 4685824 | tf_op jit(solution)/shard_map/necd,necf->def/dot_general | solution.py:104
  245.5 2.8 all_gather.15
  250.5 14.0 %all-to-all-done.2 = bf16[8,80,1024]{2,1,0:T(8,128)(2,1)S(1)} async-done(((bf16[8,80,1024]{2,1,0:T(8,128)(2,1)}), bf16[8,80,1024]{2,1,0:T(8,128)(2,1)S(1)}, u32[]{:S(2)}, u32[]{:S(2)}) %all-to-all-start.2) | async-done | bytes 1310752 | tf_op jit(solution)/shard_map/all_to_all | solution.py:17
  264.5 3.6 %all-to-all-start.5 = ((bf16[8,80,1024]{2,1,0:T(8,128)(2,1)}), bf16[8,80,1024]{2,1,0:T(8,128)(2,1)S(1)}, u32[]{:S(2)}, u32[]{:S(2)}) async-start(bf16[8,80,1024]{2,1,0:T(8,128)(2,1)} %convolution_convert_fusion), calls=%async_computation.5 | async-start | bytes 2621440 | tf_op jit(solution)/shard_map/all_to_all | solution.py:17
  269.1 2.8 gather_fusion.1
  271.8 2.8 reshape.166
  274.6 25.2 %all-to-all-done.5 = bf16[8,80,1024]{2,1,0:T(8,128)(2,1)S(1)} async-done(((bf16[8,80,1024]{2,1,0:T(8,128)(2,1)}), bf16[8,80,1024]{2,1,0:T(8,128)(2,1)S(1)}, u32[]{:S(2)}, u32[]{:S(2)}) %all-to-all-start.5) | async-done | bytes 1310752 | tf_op jit(solution)/shard_map/all_to_all | solution.py:17
  299.8 2.8 gather_fusion.4
  306.2 3.6 %multiply_reduce_fusion = (f32[128,4]{1,0:T(8,128)S(1)}, bf16[128,1024]{1,0:T(8,128)(2,1)}) fusion(f32[128,4,1024]{2,1,0:T(4,128)S(1)} %copy-done, f32[128,1024]{1,0:T(8,128)} %convert_element_type.86, f32[128,4]{1,0:T(8,128)S(1)} %copy.31), kind=kLoop, calls=%fused_computation.12 | loop fusion | flops 1965568 | bytes 2887680 | tf_op jit(solution)/shard_map/reduce_sum | solution.py:87
  309.9 3.6 %psum.7 = f32[128,4]{1,0:T(8,128)S(1)} all-reduce(f32[128,4]{1,0:T(8,128)S(1)} %get-tuple-element.15), channel_id=1, replica_groups=mesh['dp'=2,'expert'=8,'tensor'=2] {'tensor'}, use_global_device_ids=true, to_apply=%region_7.8 | all-reduce | flops 512 | bytes 4096 | tf_op jit(solution)/shard_map/psum | solution.py:88
  (75 shorter events, 32.8 us)
Async XLA Ops:
  17.5 7.5 %copy-start.11 = (f32[128,4]{0,1:T(4,128)S(1)}, f32[128,4]{0,1:T(4,128)}, u32[]{:S(2)}) copy-start(f32[128,4]{0,1:T(4,128)} %param.8) | copy-start | bytes 6148
  17.5 39.9 %copy-start.9 = (bf16[128,1024]{1,0:T(8,128)(2,1)S(1)}, bf16[128,1024]{1,0:T(8,128)(2,1)}, u32[]{:S(2)}) copy-start(bf16[128,1024]{1,0:T(8,128)(2,1)} %param.11) | copy-start | bytes 786436
  17.5 38.8 %all-to-all-start = ((bf16[8,80,1024]{2,1,0:T(8,128)(2,1)}), bf16[8,80,1024]{2,1,0:T(8,128)(2,1)S(1)}, u32[]{:S(2)}, u32[]{:S(2)}) async-start(bf16[8,80,1024]{2,1,0:T(8,128)(2,1)} %bitcast.4), calls=%async_computation | async-start | bytes 2621440 | tf_op jit(solution)/shard_map/all_to_all | solution.py:13
  25.0 74.1 %all-gather.5.cloned.1.call-start = ((), (), s32[]{:S(2)}) async-start(), calls=%async_computation.10 | async-start | bytes 3932160 | tf_op jit(solution)/shard_map/all_gather | solution.py:21
  56.3 1.1 copy-start.1
  57.4 51.9 %all-gather.7.cloned.1.call-start = ((), (), s32[]{:S(2)}) async-start(), calls=%async_computation.11 | async-start | bytes 3932160 | tf_op jit(solution)/shard_map/all_gather | solution.py:21
  63.5 35.5 %copy-start.8 = (bf16[1,384,2048]{2,1,0:T(8,128)(2,1)S(1)}, bf16[1,384,2048]{2,1,0:T(8,128)(2,1)}, u32[]{:S(2)}) copy-start(bf16[1,384,2048]{2,1,0:T(8,128)(2,1)} %param.9) | copy-start | bytes 4718596
  98.8 10.6 %copy-start.7 = (bf16[1,384,2048]{2,1,0:T(8,128)(2,1)S(1)}, bf16[1,384,2048]{2,1,0:T(8,128)(2,1)}, u32[]{:S(2)}) copy-start(bf16[1,384,2048]{2,1,0:T(8,128)(2,1)} %param.10) | copy-start | bytes 4718596
  98.8 215.3 %reduce-scatter.3.cloned.1.call-start = ((), (), s32[]{:S(2)}) async-start(), calls=%async_computation.8 | async-start | bytes 2359296 | tf_op jit(solution)/shard_map/reduce_scatter | solution.py:94
  109.3 4.6 %copy-start.2 = (bf16[8,80,2048]{2,1,0:T(8,128)(2,1)S(1)}, bf16[8,80,2048]{2,1,0:T(8,128)(2,1)}, u32[]{:S(2)}) copy-start(bf16[8,80,2048]{2,1,0:T(8,128)(2,1)} %all-gather.5.cloned.1.call-done) | copy-start | bytes 7864324
  113.1 0.8 copy-start.3
  162.0 49.7 %all-to-all-start.1 = ((bf16[2,2,196608]{2,1,0:T(2,128)(2,1)}), bf16[2,2,196608]{2,1,0:T(2,128)(2,1)}, u32[]{:S(2)}, u32[]{:S(2)}) async-start(bf16[2,2,196608]{2,1,0:T(2,128)(2,1)} %reshape.232), calls=%async_computation.1 | async-start | bytes 3145728 | tf_op jit(solution)/shard_map/all_to_all | solution.py:53
  211.7 15.2 %all-to-all-start.4 = ((bf16[2,2,196608]{2,1,0:T(2,128)(2,1)}), bf16[2,2,196608]{2,1,0:T(2,128)(2,1)}, u32[]{:S(2)}, u32[]{:S(2)}) async-start(bf16[2,2,196608]{2,1,0:T(2,128)(2,1)} %reshape.234), calls=%async_computation.4 | async-start | bytes 3145728 | tf_op jit(solution)/shard_map/all_to_all | solution.py:52
  220.2 1.8 copy-start.5
  226.8 37.7 %all-to-all-start.2 = ((bf16[8,80,1024]{2,1,0:T(8,128)(2,1)}), bf16[8,80,1024]{2,1,0:T(8,128)(2,1)S(1)}, u32[]{:S(2)}, u32[]{:S(2)}) async-start(bf16[8,80,1024]{2,1,0:T(8,128)(2,1)} %convolution_convert_fusion.1), calls=%async_computation.2 | async-start | bytes 2621440 | tf_op jit(solution)/shard_map/all_to_all | solution.py:17
  232.6 83.9 %reduce-scatter.5.cloned.1.call-start = ((), (), s32[]{:S(2)}) async-start(), calls=%async_computation.9 | async-start | bytes 2359296 | tf_op jit(solution)/shard_map/reduce_scatter | solution.py:103
  244.5 1.0 copy-start.4
  244.5 3.8 %copy-start.6 = (bf16[1,2,384,1024]{3,2,1,0:T(8,128)(2,1)S(1)}, bf16[1,2,384,1024]{3,2,1,0:T(8,128)(2,1)}, u32[]{:S(2)}) copy-start(bf16[1,2,384,1024]{3,2,1,0:T(8,128)(2,1)} %copy.39) | copy-start | bytes 4718596
  250.5 17.7 %copy-start.10 = (bf16[128,1024]{1,0:T(8,128)(2,1)S(1)}, bf16[128,1024]{1,0:T(8,128)(2,1)}, u32[]{:S(2)}) copy-start(bf16[128,1024]{1,0:T(8,128)(2,1)} %param.11) | copy-start | bytes 786436
  264.5 35.2 %all-to-all-start.5 = ((bf16[8,80,1024]{2,1,0:T(8,128)(2,1)}), bf16[8,80,1024]{2,1,0:T(8,128)(2,1)S(1)}, u32[]{:S(2)}, u32[]{:S(2)}) async-start(bf16[8,80,1024]{2,1,0:T(8,128)(2,1)} %convolution_convert_fusion), calls=%async_computation.5 | async-start | bytes 2621440 | tf_op jit(solution)/shard_map/all_to_all | solution.py:17
  302.5 3.7 %copy-start = (f32[128,4,1024]{2,1,0:T(4,128)S(1)}, f32[128,4,1024]{2,1,0:T(4,128)}, u32[]{:S(2)}) copy-start(f32[128,4,1024]{2,1,0:T(4,128)} %reshape.166) | copy-start | bytes 6291460
Sparse Core Ops, SparseCore 0:
  57.5 10.3 all-gather.4
  98.9 10.3 all-gather.6
  116.7 27.2 reduce-scatter.2
  244.6 27.4 reduce-scatter.4
where the time goes:
time: 327 us; the launch traced here: 326 us
  other arithmetic  82.6 us (25%)
  waiting for transfers between devices  76.1 us (23%)
  local copies, waits for them, and re-layouts  62.2 us (19%)
  blocking collectives  44.1 us (13%)
  starting transfers between devices  26.6 us (8%)
  matrix products  19.8 us (6%)
  between operations  14 us (4%)
    unnamed x2, other arithmetic  68.8 us
    all_to_all x2, waiting for transfers between devices, to_source(): lax.all_to_all(owner_rows, 'expert', split_axis=0, concat_axis=0, tiled=T...  39.2 us
    unnamed x36, local copies, waits for them, and re-layouts  35.5 us
    all_to_all x1, blocking collectives, to_owner(): lax.all_to_all(slot_rows, 'expert', split_axis=0, concat_axis=0, tiled=True)  35.2 us
    all_to_all x1, waiting for transfers between devices, to_owner(): lax.all_to_all(slot_rows, 'expert', split_axis=0, concat_axis=0, tiled=True)  31.1 us
    all_to_all x2, starting transfers between devices, to_source(): lax.all_to_all(owner_rows, 'expert', split_axis=0, concat_axis=0, tiled=T...  9.42 us
    all_to_all x1, starting transfers between devices, to_owner(): lax.all_to_all(slot_rows, 'expert', split_axis=0, concat_axis=0, tiled=True)  7.41 us
  transfers between devices with their start and end apart: 9, of which 4 were waited for; matrix products, arithmetic and copies ran while one was open for 44% of the time, Pallas kernels for 0%

commit v1 on v0

v1 whole, which is shorter than its diff:
```python
import jax
import jax.numpy as jnp
from jax import lax
from jax.sharding import PartitionSpec as P

BF16 = jnp.bfloat16
F32 = jnp.float32


def ring_order(count):
    if count % 2:
        return list(range(count))
    return list(range(0, count, 2)) + list(range(count - 1, 0, -2))


def swap_cores(value):
    return lax.ppermute(value, "tensor", [(0, 1), (1, 0)])


def rows_by_units(rows, weights):
    return lax.dot_general(rows, weights, (((1,), (1,)), ((), ())), preferred_element_type=F32)


def rows_by_width(rows, weights):
    return lax.dot_general(rows, weights, (((1,), (0,)), ((), ())), preferred_element_type=F32)


def over_rows(left, right):
    return lax.dot_general(left, right, (((0,), (0,)), ((), ())), preferred_element_type=F32)


def silu_slope(pre_value):
    logistic = jax.nn.sigmoid(pre_value)
    return logistic * (1.0 + pre_value * (1.0 - logistic))


def ring_gather(own, onward, back, size):
    groups = [own]
    ahead = behind = own
    for _ in range(1, size // 2):
        ahead = lax.ppermute(ahead, "expert", onward)
        behind = lax.ppermute(behind, "expert", back)
        groups.append(jnp.concatenate([ahead, behind], axis=0))
    half = own.shape[0] // 2
    low = lax.ppermute(ahead[:half], "expert", onward)
    high = lax.ppermute(behind[half:], "expert", back)
    groups.append(jnp.concatenate([low, high], axis=0))
    return groups


def ring_reduce(parts, onward, back, size):
    rows = parts[0].shape[0]
    half = rows // 2
    steps = size // 2
    far = parts[steps]
    to_ahead = lax.ppermute(far[half:].astype(BF16), "expert", onward)
    to_behind = lax.ppermute(far[:half].astype(BF16), "expert", back)
    for step in range(steps - 1, 0, -1):
        own_behind, own_ahead = parts[step][:rows], parts[step][rows:]
        if step == steps - 1:
            send_ahead = jnp.concatenate(
                [own_ahead[:half], own_ahead[half:] + to_ahead.astype(F32)], axis=0
            )
            send_behind = jnp.concatenate(
                [own_behind[:half] + to_behind.astype(F32), own_behind[half:]], axis=0
            )
        else:
            send_ahead = own_ahead + to_ahead.astype(F32)
            send_behind = own_behind + to_behind.astype(F32)
        to_ahead = lax.ppermute(send_ahead.astype(BF16), "expert", onward)
        to_behind = lax.ppermute(send_behind.astype(BF16), "expert", back)
    return (parts[0] + to_ahead.astype(F32) + to_behind.astype(F32)).astype(BF16)


def per_device(tokens, routes, gates, w_in, w_out, cotangent):
    size = lax.axis_size("expert")
    n_dp = lax.axis_size("dp")
    rows, half_width = tokens.shape
    experts = size * w_in.shape[0]
    core = lax.axis_index("tensor")
    place = lax.axis_index("expert")
    order = ring_order(size)
    onward = [(order[i], order[(i + 1) % size]) for i in range(size)]
    back = [(b, a) for a, b in onward]
    steps = size // 2

    gate_table = jnp.sum(
        jnp.where(
            routes.T[None, :, :] == jnp.arange(experts, dtype=jnp.int32)[:, None, None],
            gates.T[None, :, :],
            0.0,
        ),
        axis=1,
    )
    gate_recv = lax.all_to_all(gate_table, "expert", split_axis=0, concat_axis=0, tiled=True)
    position = jnp.where(place % 2 == 0, place // 2, size - 1 - place // 2)
    ring_table = jnp.array(order, dtype=jnp.int32)
    offsets = [0]
    for step in range(1, steps):
        offsets += [-step, step]
    offsets.append(steps)
    sources = ring_table[(position + jnp.array(offsets, dtype=jnp.int32)) % size]
    gate_rel = gate_recv[sources].reshape(size * rows, 1)

    def columns(weights, which):
        return lax.dynamic_slice_in_dim(weights, which * half_width, half_width, axis=1)

    in_mine, in_other = columns(w_in[0], core), columns(w_in[0], 1 - core)
    out_mine, out_other = columns(w_out[0], core), columns(w_out[0], 1 - core)
    in_cols = swap_cores(in_other)
    out_cols = swap_cores(out_other)

    tok_groups = ring_gather(tokens, onward, back, size)
    cot_groups = ring_gather(cotangent, onward, back, size)

    mixed_parts, back_parts, dots, pre_grads, gated, tok_other, cot_other = [], [], [], [], [], [], []
    start = 0
    for tok, cot in zip(tok_groups, cot_groups):
        count = tok.shape[0]
        gate = gate_rel[start : start + count]
        start += count
        tok_o, cot_o = swap_cores(tok), swap_cores(cot)
        pre_value = rows_by_units(tok, in_mine) + rows_by_units(tok_o, in_other)
        hidden = jax.nn.silu(pre_value).astype(BF16).astype(F32)
        gated_hidden = (gate * hidden).astype(BF16)
        mixed_parts.append(
            rows_by_width(gated_hidden, out_mine) + rows_by_width(swap_cores(gated_hidden), out_cols)
        )
        cot_units = rows_by_units(cot, out_mine) + rows_by_units(cot_o, out_other)
        grad_pre = (gate * cot_units * silu_slope(pre_value)).astype(BF16)
        dots.append(jnp.sum(hidden * cot_units, axis=1))
        back_parts.append(
            rows_by_width(grad_pre, in_mine) + rows_by_width(swap_cores(grad_pre), in_cols)
        )
        pre_grads.append(grad_pre)
        gated.append(gated_hidden)
        tok_other.append(tok_o)
        cot_other.append(cot_o)

    def weight_grad(left, mine, other):
        left, mine, other = (jnp.concatenate(v, axis=0) for v in (left, mine, other))
        part_mine, part_other = over_rows(left, mine), over_rows(left, other)
        part = jnp.concatenate(
            [
                jnp.where(core == 0, part_mine, part_other),
                jnp.where(core == 0, part_other, part_mine),
            ],
            axis=1,
        )
        width = part.shape[1] // n_dp
        group = lax.axis_index("dp")

        def piece(which):
            return lax.dynamic_slice_in_dim(part, which * width, width, axis=1)

        total = piece(group)
        for shift in range(1, n_dp):
            sent = piece((group + shift) % n_dp).astype(BF16)
            total = total + lax.ppermute(
                sent, "dp", [(i, (i + shift) % n_dp) for i in range(n_dp)]
            ).astype(F32)
        return total[None]

    grad_out = weight_grad(gated, cot_groups, cot_other)
    grad_in = weight_grad(pre_grads, tok_groups, tok_other)
    mixed = ring_reduce(mixed_parts, onward, back, size)
    grad_tokens = ring_reduce(back_parts, onward, back, size)

    dot_rel = jnp.concatenate(dots, axis=0)
    dot_rel = (dot_rel + swap_cores(dot_rel)).reshape(size, rows)
    dot_send = jnp.zeros((size, rows), F32).at[sources].set(dot_rel)
    dot_recv = lax.all_to_all(dot_send, "expert", split_axis=0, concat_axis=0, tiled=True)
    grad_gates = jnp.sum(
        jnp.where(
            routes[:, :, None] == jnp.arange(experts, dtype=jnp.int32)[None, None, :],
            dot_recv.T[:, None, :],
            0.0,
        ),
        axis=2,
    )
    return (mixed, grad_tokens, grad_gates, grad_in, grad_out)


def solution(mesh):
    placed = (
        P(("dp", "expert"), "tensor"),
        P(("dp", "expert"), None),
        P(("dp", "expert"), None),
        P("expert", "tensor", None),
        P("expert", "tensor", None),
        P(("dp", "expert"), "tensor"),
    )
    return jax.shard_map(
        per_device,
        mesh=mesh,
        in_specs=placed,
        out_specs=(
            P(("dp", "expert"), "tensor"),
            P(("dp", "expert"), "tensor"),
            P(("dp", "expert"), None),
            P("expert", "tensor", "dp"),
            P("expert", "tensor", "dp"),
        ),
        check_vma=False,
    )
```

time: 327 us -> 189 us (0.58)
  other arithmetic: 82.6 us -> 10.1 us
  local copies, waits for them, and re-layouts: 62.2 us -> 12.2 us
  blocking collectives: 44.1 us -> 0 us
  starting transfers between devices: 26.6 us -> 56 us
  matrix products: 19.8 us -> 48.2 us
  waiting for transfers between devices: 76.1 us -> 60.5 us
  between operations: 14 us -> 1.61 us
    unnamed x2 -> x1, other arithmetic: 68.8 us -> 0.01 us
    all_to_all x5 -> x2, waiting for transfers between devices: 70.3 us -> 5.2 us  [the longest x1 5.2 us: per_device(): lax.all_to_all(dot_send, 'expert', split_axis=0, concat_axis=0, tiled=True)]
    ppermute x0 -> x57, waiting for transfers between devices: none -> 55.3 us  [the longest x6 17.9 us: ring_reduce(): to_ahead = lax.ppermute(send_ahead.astype(BF16), 'expert', onward)]
    ppermute x0 -> x57, starting transfers between devices: none -> 45.6 us  [the longest x6 9.28 us: ring_gather(): behind = lax.ppermute(behind, 'expert', back)]
    all_to_all x1 -> x0, blocking collectives: 35.2 us -> none  [to_owner(): lax.all_to_all(slot_rows, 'expert', split_axis=0, concat_axis=0, tiled=True)]
    dot_general x6 -> x44, matrix products: 19.8 us -> 48.2 us  [the longest x20 26 us: rows_by_width(): lax.dot_general(rows, weights, (((1,), (0,)), ((), ())), preferred_elemen...]
    unnamed x36 -> x92, local copies, waits for them, and re-layouts: 35.5 us -> 8.61 us
    all_to_all x5 -> x2, starting transfers between devices: 26.3 us -> 10.4 us  [the longest x1 5.57 us: per_device(): lax.all_to_all(dot_send, 'expert', split_axis=0, concat_axis=0, tiled=True)]
  transfers between devices with their start and end apart: 9 -> 59, of which waited for: 4 -> 26; matrix products, arithmetic and copies ran while one was open for 44% -> 37% of each run, Pallas kernels for 0% -> 0%
where the time goes in v1:
time: 189 us
  waiting for transfers between devices  60.5 us (32%)
  starting transfers between devices  56 us (30%)
  matrix products  48.2 us (26%)
  local copies, waits for them, and re-layouts  12.2 us (6%)
  other arithmetic  10.1 us (5%)
    dot_general x20, matrix products, rows_by_width(): lax.dot_general(rows, weights, (((1,), (0,)), ((), ())), preferred_elemen...  26 us
    ppermute x6, waiting for transfers between devices, ring_reduce(): to_ahead = lax.ppermute(send_ahead.astype(BF16), 'expert', onward)  17.9 us
    dot_general x20, matrix products, rows_by_units(): lax.dot_general(rows, weights, (((1,), (1,)), ((), ())), preferred_elemen...  17.1 us
    ppermute x6, waiting for transfers between devices, ring_gather(): ahead = lax.ppermute(ahead, 'expert', onward)  10.2 us
    ppermute x6, starting transfers between devices, ring_gather(): behind = lax.ppermute(behind, 'expert', back)  9.28 us
    ppermute x6, waiting for transfers between devices, ring_reduce(): to_behind = lax.ppermute(send_behind.astype(BF16), 'expert', back)  8.62 us
    unnamed x92, local copies, waits for them, and re-layouts  8.61 us
    ppermute x6, starting transfers between devices, ring_gather(): ahead = lax.ppermute(ahead, 'expert', onward)  8.02 us
  transfers between devices with their start and end apart: 59, of which 26 were waited for; matrix products, arithmetic and copies ran while one was open for 37% of the time, Pallas kernels for 0%

profile of v1, /device:TPU:0, one launch (start us, length us, event | category | flops | bytes accessed | tf_op | source)
XLA Modules:
  0.0 188.6 jit_solution(7794238535620628585)
XLA Ops:
  1.2 2.6 %collective-permute-start.30 = (bf16[128,1024]{1,0:T(8,128)(2,1)}, bf16[128,1024]{1,0:T(8,128)(2,1)S(1)}, u32[]{:S(2)}, u32[]{:S(2)}) collective-permute-start(bf16[128,1024]{1,0:T(8,128)(2,1)} %param.13), channel_id=1, source_target_pairs={{0,4},{4,8},{8,12},{12,14},{14,10},{10,6},{6,2},{2,0},{1,5},{5,9},... | collective-permute-start | bytes 786440 | tf_op jit(solution)/shard_map/ppermute | solution.py:41
  7.1 4.8 %all-to-all-start = ((f32[8,1,128]{2,1,0:T(1,128)}), f32[8,1,128]{2,1,0:T(1,128)S(1)}, u32[]{:S(2)}, u32[]{:S(2)}) async-start(f32[8,1,128]{2,1,0:T(1,128)} %bitcast.3), calls=%async_computation | async-start | bytes 8192 | tf_op jit(solution)/shard_map/all_to_all | solution.py:95
  12.0 2.2 %fusion.24 = f32[384,128]{0,1:T(8,128)} fusion(bf16[128,1024]{1,0:T(8,128)(2,1)} %param.13, bf16[1,384,2048]{2,1,0:T(8,128)(2,1)} %param.12, s32[]{:T(128)S(6)} %select_n.92), kind=kOutput, calls=%fused_computation.55 | convolution fusion | flops 100663296 | bytes 1245188 | tf_op jit(solution)/shard_map/dot_general | solution.py:21
  15.5 2.0 %fusion.50 = f32[384,128]{0,1:T(8,128)} fusion(bf16[128,1024]{1,0:T(8,128)(2,1)} %param.8, bf16[1,384,2048]{2,1,0:T(8,128)(2,1)S(1)} %copy-done, s32[]{:T(128)S(6)} %select_n.92), kind=kOutput, calls=%fused_computation.81 | convolution fusion | flops 100663296 | bytes 1245188 | tf_op jit(solution)/shard_map/dot_general | solution.py:21
  22.2 2.1 %collective-permute-start.4 = (bf16[128,1024]{1,0:T(8,128)(2,1)}, bf16[128,1024]{1,0:T(8,128)(2,1)S(1)}, u32[]{:S(2)}, u32[]{:S(2)}) collective-permute-start(bf16[128,1024]{1,0:T(8,128)(2,1)} %param.8), channel_id=1, source_target_pairs={{4,0},{8,4},{12,8},{14,12},{10,14},{6,10},{2,6},{0,2},{5,1},{9,5},... | collective-permute-start | bytes 786440 | tf_op jit(solution)/shard_map/ppermute | solution.py:42
  28.8 2.4 %constant_dynamic-update-slice_fusion.21 = (bf16[1024,384]{1,0:T(8,128)(2,1)S(1)}, bf16[128,384]{1,0:T(8,128)(2,1)}, bf16[1024,384]{1,0:T(8,128)(2,1)S(1)}, bf16[128,384]{1,0:T(8,128)(2,1)S(1)}, bf16[128,384]{1,0:T(8,128)(2,1)S(1)}) fusion(f32[128,384]{1,0:T(8,128)S(1)} %fusion.18, f32[128]{0:T(128)S(1)} %get-tuple-element.102, ...), kind=kOutput, calls=%fused_computation.173 | convolution fusion | flops 101449728 | bytes 1933824 | tf_op jit(solution)/shard_map/dot_general | solution.py:21
  31.2 2.1 %fusion.44 = f32[128,1024]{1,0:T(8,128)} fusion(bf16[128,384]{1,0:T(8,128)(2,1)} %get-tuple-element.29, bf16[1,384,2048]{2,1,0:T(8,128)(2,1)S(1)} %copy-done, s32[]{:T(128)S(6)} %select_n.92), kind=kOutput, calls=%fused_computation.75 | convolution fusion | flops 100663296 | bytes 1409028 | tf_op jit(solution)/shard_map/dot_general | solution.py:25
  33.3 2.0 %collective-permute-start.35 = (bf16[128,1024]{1,0:T(8,128)(2,1)}, bf16[128,1024]{1,0:T(8,128)(2,1)S(1)}, u32[]{:S(2)}, u32[]{:S(2)}) collective-permute-start(bf16[128,1024]{1,0:T(8,128)(2,1)} %collective-permute-done.31), channel_id=1, source_target_pairs={{4,0},{8,4},{12,8},{14,12},{10,14},{6,10},{2,6},{0,2},{5,1},{9,5},... | collective-permute-start | bytes 786440 | tf_op jit(solution)/shard_map/ppermute | solution.py:42
  39.7 1.9 collective-permute-start.8
  41.6 3.8 %collective-permute-done.7 = bf16[128,1024]{1,0:T(8,128)(2,1)S(1)} collective-permute-done((bf16[128,1024]{1,0:T(8,128)(2,1)}, bf16[128,1024]{1,0:T(8,128)(2,1)S(1)}, u32[]{:S(2)}, u32[]{:S(2)}) %collective-permute-start.7) | collective-permute-done | bytes 262176 | tf_op jit(solution)/shard_map/ppermute | solution.py:41
  53.8 2.9 %collective-permute-done.38 = bf16[128,1024]{1,0:T(8,128)(2,1)S(1)} collective-permute-done((bf16[128,1024]{1,0:T(8,128)(2,1)S(1)}, bf16[128,1024]{1,0:T(8,128)(2,1)S(1)}, u32[]{:S(2)}, u32[]{:S(2)}) %collective-permute-start.38) | collective-permute-done | bytes 262176 | tf_op jit(solution)/shard_map/ppermute | solution.py:41
  58.4 3.5 %collective-permute-done.11 = bf16[128,1024]{1,0:T(8,128)(2,1)S(1)} collective-permute-done((bf16[128,1024]{1,0:T(8,128)(2,1)S(1)}, bf16[128,1024]{1,0:T(8,128)(2,1)S(1)}, u32[]{:S(2)}, u32[]{:S(2)}) %collective-permute-start.11) | collective-permute-done | bytes 262176 | tf_op jit(solution)/shard_map/ppermute | solution.py:41
  65.9 3.9 %collective-permute-done.12 = bf16[128,1024]{1,0:T(8,128)(2,1)S(1)} collective-permute-done((bf16[128,1024]{1,0:T(8,128)(2,1)S(1)}, bf16[128,1024]{1,0:T(8,128)(2,1)S(1)}, u32[]{:S(2)}, u32[]{:S(2)}) %collective-permute-start.12) | collective-permute-done | bytes 262176 | tf_op jit(solution)/shard_map/ppermute | solution.py:42
  72.0 2.8 %collective-permute-done.15 = bf16[64,1024]{1,0:T(8,128)(2,1)S(1)} collective-permute-done((bf16[64,1024]{1,0:T(8,128)(2,1)S(1)}, bf16[64,1024]{1,0:T(8,128)(2,1)S(1)}, u32[]{:S(2)}, u32[]{:S(2)}) %collective-permute-start.15) | collective-permute-done | bytes 131104 | tf_op jit(solution)/shard_map/ppermute | solution.py:45
  96.7 2.0 %fusion.36 = f32[128,1024]{1,0:T(8,128)} fusion(bf16[128,384]{1,0:T(8,128)(2,1)} %get-tuple-element.21, bf16[1,384,2048]{2,1,0:T(8,128)(2,1)S(1)} %copy-done, s32[]{:T(128)S(6)} %select_n.92), kind=kOutput, calls=%fused_computation.67 | convolution fusion | flops 100663296 | bytes 1409028 | tf_op jit(solution)/shard_map/dot_general | solution.py:25
  99.1 2.4 %fusion.38 = f32[256,1024]{1,0:T(8,128)} fusion(bf16[256,384]{1,0:T(8,128)(2,1)} %get-tuple-element.23, bf16[1,384,2048]{2,1,0:T(8,128)(2,1)S(1)} %copy-done, s32[]{:T(128)S(6)} %select_n.92), kind=kOutput, calls=%fused_computation.69 | convolution fusion | flops 201326592 | bytes 2031620 | tf_op jit(solution)/shard_map/dot_general | solution.py:25
  101.6 2.0 %fusion.26 = f32[128,1024]{1,0:T(8,128)} fusion(bf16[128,384]{1,0:T(8,128)(2,1)} %get-tuple-element.88, bf16[1,384,2048]{2,1,0:T(8,128)(2,1)S(1)} %copy-done.3, s32[]{:T(128)S(6)} %select_n.92), kind=kOutput, calls=%fused_computation.57 | convolution fusion | flops 100663296 | bytes 1409028 | tf_op jit(solution)/shard_map/dot_general | solution.py:25
  104.5 2.4 %fusion.28 = f32[256,1024]{1,0:T(8,128)} fusion(bf16[256,384]{1,0:T(8,128)(2,1)} %get-tuple-element.51, bf16[1,384,2048]{2,1,0:T(8,128)(2,1)S(1)} %copy-done.3, s32[]{:T(128)S(6)} %select_n.92), kind=kOutput, calls=%fused_computation.59 | convolution fusion | flops 201326592 | bytes 2031620 | tf_op jit(solution)/shard_map/dot_general | solution.py:25
  110.1 2.1 %broadcast_select_fusion.2 = (f32[384,1024]{1,0:T(8,128)S(1)}, f32[384,1024]{1,0:T(8,128)}) fusion(f32[384,1024]{1,0:T(8,128)S(1)} %fusion.99, pred[]{:T(512)S(6)} %eq.48, bf16[1024,384]{1,0:T(8,128)(2,1)S(1)} %get-tuple-element.20, bf16[1024,1024]{1,0:T(8,128)(2,1)S(1)} %constant_dynamic-update-slice_fusion.31), kind=kOutput, calls=%fused_computation.87 | convolution fusion | flops 806092800 | bytes 7602177 | tf_op jit(solution)/shard_map/dot_general | solution.py:29
  115.1 5.6 %all-to-all-start.1 = ((f32[8,1,128]{2,1,0:T(1,128)}), f32[8,1,128]{2,1,0:T(1,128)S(1)}, u32[]{:S(2)}, u32[]{:S(2)}) async-start(f32[8,1,128]{2,1,0:T(1,128)} %bitcast.20), calls=%async_computation.1 | async-start | bytes 8192 | tf_op jit(solution)/shard_map/all_to_all | solution.py:172
  121.9 5.2 %all-to-all-done.1 = f32[8,1,128]{2,1,0:T(1,128)S(1)} async-done(((f32[8,1,128]{2,1,0:T(1,128)}), f32[8,1,128]{2,1,0:T(1,128)S(1)}, u32[]{:S(2)}, u32[]{:S(2)}) %all-to-all-start.1) | async-done | bytes 4128 | tf_op jit(solution)/shard_map/all_to_all | solution.py:172
  135.6 1.9 %collective-permute-done.46 = bf16[64,1024]{1,0:T(8,128)(2,1)S(1)} collective-permute-done((bf16[64,1024]{1,0:T(8,128)(2,1)S(1)}, bf16[64,1024]{1,0:T(8,128)(2,1)S(1)}, u32[]{:S(2)}, u32[]{:S(2)}) %collective-permute-start.46) | collective-permute-done | bytes 131104 | tf_op jit(solution)/shard_map/ppermute | solution.py:56
  140.5 2.0 %collective-permute-done.19 = bf16[64,1024]{1,0:T(8,128)(2,1)S(1)} collective-permute-done((bf16[64,1024]{1,0:T(8,128)(2,1)S(1)}, bf16[64,1024]{1,0:T(8,128)(2,1)S(1)}, u32[]{:S(2)}, u32[]{:S(2)}) %collective-permute-start.19) | collective-permute-done | bytes 131104 | tf_op jit(solution)/shard_map/ppermute | solution.py:56
  143.1 1.9 collective-permute-done.23
  146.0 3.1 %collective-permute-done.51 = bf16[128,1024]{1,0:T(8,128)(2,1)S(1)} collective-permute-done((bf16[128,1024]{1,0:T(8,128)(2,1)S(1)}, bf16[128,1024]{1,0:T(8,128)(2,1)S(1)}, u32[]{:S(2)}, u32[]{:S(2)}) %collective-permute-start.51) | collective-permute-done | bytes 262176 | tf_op jit(solution)/shard_map/ppermute | solution.py:71
  149.9 4.1 %collective-permute-done.47 = bf16[128,1024]{1,0:T(8,128)(2,1)S(1)} collective-permute-done((bf16[128,1024]{1,0:T(8,128)(2,1)S(1)}, bf16[128,1024]{1,0:T(8,128)(2,1)S(1)}, u32[]{:S(2)}, u32[]{:S(2)}) %collective-permute-start.47) | collective-permute-done | bytes 262176 | tf_op jit(solution)/shard_map/ppermute | solution.py:70
  155.8 5.0 %collective-permute-done.20 = bf16[128,1024]{1,0:T(8,128)(2,1)S(1)} collective-permute-done((bf16[128,1024]{1,0:T(8,128)(2,1)S(1)}, bf16[128,1024]{1,0:T(8,128)(2,1)S(1)}, u32[]{:S(2)}, u32[]{:S(2)}) %collective-permute-start.20) | collective-permute-done | bytes 262176 | tf_op jit(solution)/shard_map/ppermute | solution.py:70
  160.8 2.2 %collective-permute-start.52 = (bf16[128,1024]{1,0:T(8,128)(2,1)S(1)}, bf16[128,1024]{1,0:T(8,128)(2,1)S(1)}, u32[]{:S(2)}, u32[]{:S(2)}) collective-permute-start(bf16[128,1024]{1,0:T(8,128)(2,1)S(1)} %get-tuple-element.37), channel_id=1, source_target_pairs={{4,0},{8,4},{12,8},{14,12},{10,14},{6,10},{2,6},{0,2},{5,1},{9,5},... | collective-permute-start | bytes 786440 | tf_op jit(solution)/shard_map/ppermute | solution.py:71
  163.2 2.9 %collective-permute-done.48 = bf16[128,1024]{1,0:T(8,128)(2,1)S(1)} collective-permute-done((bf16[128,1024]{1,0:T(8,128)(2,1)S(1)}, bf16[128,1024]{1,0:T(8,128)(2,1)S(1)}, u32[]{:S(2)}, u32[]{:S(2)}) %collective-permute-start.48) | collective-permute-done | bytes 262176 | tf_op jit(solution)/shard_map/ppermute | solution.py:70
  169.5 2.8 %collective-permute-done.21 = bf16[128,1024]{1,0:T(8,128)(2,1)S(1)} collective-permute-done((bf16[128,1024]{1,0:T(8,128)(2,1)S(1)}, bf16[128,1024]{1,0:T(8,128)(2,1)S(1)}, u32[]{:S(2)}, u32[]{:S(2)}) %collective-permute-start.21) | collective-permute-done | bytes 262176 | tf_op jit(solution)/shard_map/ppermute | solution.py:70
  172.4 1.9 %collective-permute-done.25 = bf16[128,1024]{1,0:T(8,128)(2,1)S(1)} collective-permute-done((bf16[128,1024]{1,0:T(8,128)(2,1)S(1)}, bf16[128,1024]{1,0:T(8,128)(2,1)S(1)}, u32[]{:S(2)}, u32[]{:S(2)}) %collective-permute-start.25) | collective-permute-done | bytes 262176 | tf_op jit(solution)/shard_map/ppermute | solution.py:71
  183.5 1.9 %fusion.16 = bf16[128,1024]{1,0:T(8,128)(2,1)} fusion(f32[128,1024]{1,0:T(8,128)S(1)} %copy-done.22, bf16[128,384]{1,0:T(8,128)(2,1)} %collective-permute-done.28, bf16[384,1024]{1,0:T(8,128)(2,1)S(1)} %collective-permute-done.29, bf16[128,1024]{1,0:T(8,128)(2,1)S(1)} %collective-permute-done.53, bf16[128,1024]{1,0:T(8,128)(2,1)S(1)} %collective-permute-done.49), kind=kOutput, calls=%fused_computation.37 | convolution fusion | flops 101449728 | bytes 2195456 | tf_op jit(solution)/shard_map/dot_general | solution.py:25
  (268 shorter events, 96.5 us)
Async XLA Ops:
  0.6 26.2 %collective-permute-start.27 = (bf16[128,1024]{1,0:T(8,128)(2,1)}, bf16[128,1024]{1,0:T(8,128)(2,1)}, u32[]{:S(2)}, u32[]{:S(2)}) collective-permute-start(bf16[128,1024]{1,0:T(8,128)(2,1)} %param.13), channel_id=1, source_target_pairs={{0,1},{1,0},{2,3},{3,2},{4,5},{5,4},{6,7},{7,6},{8,9},{9,8},{10,11... | collective-permute-start | bytes 786440 | tf_op jit(solution)/shard_map/ppermute | solution.py:17
  1.2 21.0 %collective-permute-start.30 = (bf16[128,1024]{1,0:T(8,128)(2,1)}, bf16[128,1024]{1,0:T(8,128)(2,1)S(1)}, u32[]{:S(2)}, u32[]{:S(2)}) collective-permute-start(bf16[128,1024]{1,0:T(8,128)(2,1)} %param.13), channel_id=1, source_target_pairs={{0,4},{4,8},{8,12},{12,14},{14,10},{10,6},{6,2},{2,0},{1,5},{5,9},... | collective-permute-start | bytes 786440 | tf_op jit(solution)/shard_map/ppermute | solution.py:41
  3.8 21.2 %collective-permute-start.31 = (bf16[128,1024]{1,0:T(8,128)(2,1)}, bf16[128,1024]{1,0:T(8,128)(2,1)}, u32[]{:S(2)}, u32[]{:S(2)}) collective-permute-start(bf16[128,1024]{1,0:T(8,128)(2,1)} %param.13), channel_id=1, source_target_pairs={{4,0},{8,4},{12,8},{14,12},{10,14},{6,10},{2,6},{0,2},{5,1},{9,5},... | collective-permute-start | bytes 786440 | tf_op jit(solution)/shard_map/ppermute | solution.py:42
  3.8 24.8 %collective-permute-start = (bf16[128,1024]{1,0:T(8,128)(2,1)}, bf16[128,1024]{1,0:T(8,128)(2,1)}, u32[]{:S(2)}, u32[]{:S(2)}) collective-permute-start(bf16[128,1024]{1,0:T(8,128)(2,1)} %param.8), channel_id=1, source_target_pairs={{0,1},{1,0},{2,3},{3,2},{4,5},{5,4},{6,7},{7,6},{8,9},{9,8},{10,11... | collective-permute-start | bytes 786440 | tf_op jit(solution)/shard_map/ppermute | solution.py:17
  4.0 29.3 %collective-permute-start.3 = (bf16[128,1024]{1,0:T(8,128)(2,1)}, bf16[128,1024]{1,0:T(8,128)(2,1)}, u32[]{:S(2)}, u32[]{:S(2)}) collective-permute-start(bf16[128,1024]{1,0:T(8,128)(2,1)} %param.8), channel_id=1, source_target_pairs={{0,4},{4,8},{8,12},{12,14},{14,10},{10,6},{6,2},{2,0},{1,5},{5,9},... | collective-permute-start | bytes 786440 | tf_op jit(solution)/shard_map/ppermute | solution.py:41
  7.1 14.5 %all-to-all-start = ((f32[8,1,128]{2,1,0:T(1,128)}), f32[8,1,128]{2,1,0:T(1,128)S(1)}, u32[]{:S(2)}, u32[]{:S(2)}) async-start(f32[8,1,128]{2,1,0:T(1,128)} %bitcast.3), calls=%async_computation | async-start | bytes 8192 | tf_op jit(solution)/shard_map/all_to_all | solution.py:95
  22.2 15.2 %collective-permute-start.4 = (bf16[128,1024]{1,0:T(8,128)(2,1)}, bf16[128,1024]{1,0:T(8,128)(2,1)S(1)}, u32[]{:S(2)}, u32[]{:S(2)}) collective-permute-start(bf16[128,1024]{1,0:T(8,128)(2,1)} %param.8), channel_id=1, source_target_pairs={{4,0},{8,4},{12,8},{14,12},{10,14},{6,10},{2,6},{0,2},{5,1},{9,5},... | collective-permute-start | bytes 786440 | tf_op jit(solution)/shard_map/ppermute | solution.py:42
  25.0 54.8 %collective-permute-start.29 = (bf16[384,1024]{1,0:T(8,128)(2,1)}, bf16[384,1024]{1,0:T(8,128)(2,1)S(1)}, u32[]{:S(2)}, u32[]{:S(2)}) collective-permute-start(bf16[384,1024]{1,0:T(8,128)(2,1)} %dynamic-slice_bitcast_fusion.1), channel_id=1, source_target_pairs={{0,1},{1,0},{2,3},{3,2},{4,5},{5,4},{6,7},{7,6},{8,9},{9,8},{10,11... | collective-permute-start | bytes 2359304 | tf_op jit(solution)/shard_map/ppermute | solution.py:17
  26.8 20.7 %collective-permute-start.32 = (bf16[256,1024]{1,0:T(8,128)(2,1)S(1)}, bf16[256,1024]{1,0:T(8,128)(2,1)S(1)}, u32[]{:S(2)}, u32[]{:S(2)}) collective-permute-start(bf16[256,1024]{1,0:T(8,128)(2,1)S(1)} %get-tuple-element.68), channel_id=1, source_target_pairs={{0,1},{1,0},{2,3},{3,2},{4,5},{5,4},{6,7},{7,6},{8,9},{9,8},{10,11... | collective-permute-start | bytes 1572872 | tf_op jit(solution)/shard_map/ppermute | solution.py:17
  28.7 11.0 %collective-permute-start.34 = (bf16[128,1024]{1,0:T(8,128)(2,1)S(1)}, bf16[128,1024]{1,0:T(8,128)(2,1)S(1)}, u32[]{:S(2)}, u32[]{:S(2)}) collective-permute-start(bf16[128,1024]{1,0:T(8,128)(2,1)S(1)} %copy-done.26), channel_id=1, source_target_pairs={{0,4},{4,8},{8,12},{12,14},{14,10},{10,6},{6,2},{2,0},{1,5},{5,9},... | collective-permute-start | bytes 786440 | tf_op jit(solution)/shard_map/ppermute | solution.py:41
  33.3 12.2 %collective-permute-start.35 = (bf16[128,1024]{1,0:T(8,128)(2,1)}, bf16[128,1024]{1,0:T(8,128)(2,1)S(1)}, u32[]{:S(2)}, u32[]{:S(2)}) collective-permute-start(bf16[128,1024]{1,0:T(8,128)(2,1)} %collective-permute-done.31), channel_id=1, source_target_pairs={{4,0},{8,4},{12,8},{14,12},{10,14},{6,10},{2,6},{0,2},{5,1},{9,5},... | collective-permute-start | bytes 786440 | tf_op jit(solution)/shard_map/ppermute | solution.py:42
  37.5 8.0 %collective-permute-start.7 = (bf16[128,1024]{1,0:T(8,128)(2,1)}, bf16[128,1024]{1,0:T(8,128)(2,1)S(1)}, u32[]{:S(2)}, u32[]{:S(2)}) collective-permute-start(bf16[128,1024]{1,0:T(8,128)(2,1)} %collective-permute-done.3), channel_id=1, source_target_pairs={{0,4},{4,8},{8,12},{12,14},{14,10},{10,6},{6,2},{2,0},{1,5},{5,9},... | collective-permute-start | bytes 786440 | tf_op jit(solution)/shard_map/ppermute | solution.py:41
  45.4 36.4 %collective-permute-start.2 = (bf16[384,1024]{1,0:T(8,128)(2,1)S(1)}, bf16[384,1024]{1,0:T(8,128)(2,1)S(1)}, u32[]{:S(2)}, u32[]{:S(2)}) collective-permute-start(bf16[384,1024]{1,0:T(8,128)(2,1)S(1)} %dynamic-slice_bitcast_fusion), channel_id=1, source_target_pairs={{0,1},{1,0},{2,3},{3,2},{4,5},{5,4},{6,7},{7,6},{8,9},{9,8},{10,11... | collective-permute-start | bytes 2359304 | tf_op jit(solution)/shard_map/ppermute | solution.py:17
  45.5 135.2 %collective-permute-start.28 = (bf16[128,384]{1,0:T(8,128)(2,1)}, bf16[128,384]{1,0:T(8,128)(2,1)}, u32[]{:S(2)}, u32[]{:S(2)}) collective-permute-start(bf16[128,384]{1,0:T(8,128)(2,1)} %get-tuple-element.29), channel_id=1, source_target_pairs={{0,1},{1,0},{2,3},{3,2},{4,5},{5,4},{6,7},{7,6},{8,9},{9,8},{10,11... | collective-permute-start | bytes 294920 | tf_op jit(solution)/shard_map/ppermute | solution.py:17
  47.5 9.2 %collective-permute-start.38 = (bf16[128,1024]{1,0:T(8,128)(2,1)S(1)}, bf16[128,1024]{1,0:T(8,128)(2,1)S(1)}, u32[]{:S(2)}, u32[]{:S(2)}) collective-permute-start(bf16[128,1024]{1,0:T(8,128)(2,1)S(1)} %collective-permute-done.34), channel_id=1, source_target_pairs={{0,4},{4,8},{8,12},{12,14},{14,10},{10,6},{6,2},{2,0},{1,5},{5,9},... | collective-permute-start | bytes 786440 | tf_op jit(solution)/shard_map/ppermute | solution.py:41
  50.2 11.7 %collective-permute-start.11 = (bf16[128,1024]{1,0:T(8,128)(2,1)S(1)}, bf16[128,1024]{1,0:T(8,128)(2,1)S(1)}, u32[]{:S(2)}, u32[]{:S(2)}) collective-permute-start(bf16[128,1024]{1,0:T(8,128)(2,1)S(1)} %collective-permute-done.7), channel_id=1, source_target_pairs={{0,4},{4,8},{8,12},{12,14},{14,10},{10,6},{6,2},{2,0},{1,5},{5,9},... | collective-permute-start | bytes 786440 | tf_op jit(solution)/shard_map/ppermute | solution.py:41
  81.9 10.9 %collective-permute-start.40 = (bf16[256,1024]{1,0:T(8,128)(2,1)S(1)}, bf16[256,1024]{1,0:T(8,128)(2,1)S(1)}, u32[]{:S(2)}, u32[]{:S(2)}) collective-permute-start(bf16[256,1024]{1,0:T(8,128)(2,1)S(1)} %get-tuple-element.60), channel_id=1, source_target_pairs={{0,1},{1,0},{2,3},{3,2},{4,5},{5,4},{6,7},{7,6},{8,9},{9,8},{10,11... | collective-permute-start | bytes 1572872 | tf_op jit(solution)/shard_map/ppermute | solution.py:17
  82.7 11.0 %collective-permute-start.13 = (bf16[256,1024]{1,0:T(8,128)(2,1)S(1)}, bf16[256,1024]{1,0:T(8,128)(2,1)S(1)}, u32[]{:S(2)}, u32[]{:S(2)}) collective-permute-start(bf16[256,1024]{1,0:T(8,128)(2,1)S(1)} %get-tuple-element.72), channel_id=1, source_target_pairs={{0,1},{1,0},{2,3},{3,2},{4,5},{5,4},{6,7},{7,6},{8,9},{9,8},{10,11... | collective-permute-start | bytes 1572872 | tf_op jit(solution)/shard_map/ppermute | solution.py:17
  98.7 29.0 %collective-permute-start.45 = (bf16[128,384]{1,0:T(8,128)(2,1)}, bf16[128,384]{1,0:T(8,128)(2,1)}, u32[]{:S(2)}, u32[]{:S(2)}) collective-permute-start(bf16[128,384]{1,0:T(8,128)(2,1)} %get-tuple-element.21), channel_id=1, source_target_pairs={{0,1},{1,0},{2,3},{3,2},{4,5},{5,4},{6,7},{7,6},{8,9},{9,8},{10,11... | collective-permute-start | bytes 294920 | tf_op jit(solution)/shard_map/ppermute | solution.py:17
  101.5 31.0 %collective-permute-start.41 = (bf16[256,384]{1,0:T(8,128)(2,1)}, bf16[256,384]{1,0:T(8,128)(2,1)S(1)}, u32[]{:S(2)}, u32[]{:S(2)}) collective-permute-start(bf16[256,384]{1,0:T(8,128)(2,1)} %get-tuple-element.23), channel_id=1, source_target_pairs={{0,1},{1,0},{2,3},{3,2},{4,5},{5,4},{6,7},{7,6},{8,9},{9,8},{10,11... | collective-permute-start | bytes 589832 | tf_op jit(solution)/shard_map/ppermute | solution.py:17
  103.6 27.0 %collective-permute-start.18 = (bf16[128,384]{1,0:T(8,128)(2,1)}, bf16[128,384]{1,0:T(8,128)(2,1)}, u32[]{:S(2)}, u32[]{:S(2)}) collective-permute-start(bf16[128,384]{1,0:T(8,128)(2,1)} %get-tuple-element.88), channel_id=1, source_target_pairs={{0,1},{1,0},{2,3},{3,2},{4,5},{5,4},{6,7},{7,6},{8,9},{9,8},{10,11... | collective-permute-start | bytes 294920 | tf_op jit(solution)/shard_map/ppermute | solution.py:17
  104.3 9.2 %collective-permute-start.54 = (f32[1024]{0:T(1024)S(1)}, f32[1024]{0:T(1024)S(1)}, u32[]{:S(2)}, u32[]{:S(2)}) collective-permute-start(f32[1024]{0:T(1024)S(1)} %constant_dynamic-update-slice_fusion.56), channel_id=1, source_target_pairs={{0,1},{1,0},{2,3},{3,2},{4,5},{5,4},{6,7},{7,6},{8,9},{9,8},{10,11... | collective-permute-start | bytes 12296 | tf_op jit(solution)/shard_map/ppermute | solution.py:17
  113.5 19.9 %collective-permute-start.14 = (bf16[256,384]{1,0:T(8,128)(2,1)}, bf16[256,384]{1,0:T(8,128)(2,1)S(1)}, u32[]{:S(2)}, u32[]{:S(2)}) collective-permute-start(bf16[256,384]{1,0:T(8,128)(2,1)} %get-tuple-element.51), channel_id=1, source_target_pairs={{0,1},{1,0},{2,3},{3,2},{4,5},{5,4},{6,7},{7,6},{8,9},{9,8},{10,11... | collective-permute-start | bytes 589832 | tf_op jit(solution)/shard_map/ppermute | solution.py:17
  115.1 12.0 %all-to-all-start.1 = ((f32[8,1,128]{2,1,0:T(1,128)}), f32[8,1,128]{2,1,0:T(1,128)S(1)}, u32[]{:S(2)}, u32[]{:S(2)}) async-start(f32[8,1,128]{2,1,0:T(1,128)} %bitcast.20), calls=%async_computation.1 | async-start | bytes 8192 | tf_op jit(solution)/shard_map/all_to_all | solution.py:172
  127.7 47.8 %collective-permute-start.56 = (bf16[384,1024]{1,0:T(8,128)(2,1)}, bf16[384,1024]{1,0:T(8,128)(2,1)S(1)}, u32[]{:S(2)}, u32[]{:S(2)}) collective-permute-start(bf16[384,1024]{1,0:T(8,128)(2,1)} %fusion.1), channel_id=1, source_target_pairs={{0,16},{16,0},{1,17},{17,1},{2,18},{18,2},{3,19},{19,3},{4,20},{20... | collective-permute-start | bytes 2359304 | tf_op jit(solution)/shard_map/ppermute | solution.py:159
  130.6 47.5 %collective-permute-start.55 = (bf16[384,1024]{1,0:T(8,128)(2,1)S(1)}, bf16[384,1024]{1,0:T(8,128)(2,1)S(1)}, u32[]{:S(2)}, u32[]{:S(2)}) collective-permute-start(bf16[384,1024]{1,0:T(8,128)(2,1)S(1)} %copy-done.24), channel_id=1, source_target_pairs={{0,16},{16,0},{1,17},{17,1},{2,18},{18,2},{3,19},{19,3},{4,20},{20... | collective-permute-start | bytes 2359304 | tf_op jit(solution)/shard_map/ppermute | solution.py:159
  144.9 9.1 %collective-permute-start.47 = (bf16[128,1024]{1,0:T(8,128)(2,1)S(1)}, bf16[128,1024]{1,0:T(8,128)(2,1)S(1)}, u32[]{:S(2)}, u32[]{:S(2)}) collective-permute-start(bf16[128,1024]{1,0:T(8,128)(2,1)S(1)} %pad_maximum_fusion.2), channel_id=1, source_target_pairs={{0,4},{4,8},{8,12},{12,14},{14,10},{10,6},{6,2},{2,0},{1,5},{5,9},... | collective-permute-start | bytes 786440 | tf_op jit(solution)/shard_map/ppermute | solution.py:70
  155.5 10.5 %collective-permute-start.48 = (bf16[128,1024]{1,0:T(8,128)(2,1)S(1)}, bf16[128,1024]{1,0:T(8,128)(2,1)S(1)}, u32[]{:S(2)}, u32[]{:S(2)}) collective-permute-start(bf16[128,1024]{1,0:T(8,128)(2,1)S(1)} %get-tuple-element.36), channel_id=1, source_target_pairs={{0,4},{4,8},{8,12},{12,14},{14,10},{10,6},{6,2},{2,0},{1,5},{5,9},... | collective-permute-start | bytes 786440 | tf_op jit(solution)/shard_map/ppermute | solution.py:70
  172.4 13.0 %collective-permute-start.1 = (bf16[128,384]{1,0:T(8,128)(2,1)S(1)}, bf16[128,384]{1,0:T(8,128)(2,1)S(1)}, u32[]{:S(2)}, u32[]{:S(2)}) collective-permute-start(bf16[128,384]{1,0:T(8,128)(2,1)S(1)} %copy-done.29), channel_id=1, source_target_pairs={{0,1},{1,0},{2,3},{3,2},{4,5},{5,4},{6,7},{7,6},{8,9},{9,8},{10,11... | collective-permute-start | bytes 294920 | tf_op jit(solution)/shard_map/ppermute | solution.py:17
  174.3 9.1 %collective-permute-start.49 = (bf16[128,1024]{1,0:T(8,128)(2,1)S(1)}, bf16[128,1024]{1,0:T(8,128)(2,1)S(1)}, u32[]{:S(2)}, u32[]{:S(2)}) collective-permute-start(bf16[128,1024]{1,0:T(8,128)(2,1)S(1)} %get-tuple-element.34), channel_id=1, source_target_pairs={{0,4},{4,8},{8,12},{12,14},{14,10},{10,6},{6,2},{2,0},{1,5},{5,9},... | collective-permute-start | bytes 786440 | tf_op jit(solution)/shard_map/ppermute | solution.py:70
  175.5 8.0 %collective-permute-start.53 = (bf16[128,1024]{1,0:T(8,128)(2,1)S(1)}, bf16[128,1024]{1,0:T(8,128)(2,1)S(1)}, u32[]{:S(2)}, u32[]{:S(2)}) collective-permute-start(bf16[128,1024]{1,0:T(8,128)(2,1)S(1)} %get-tuple-element.35), channel_id=1, source_target_pairs={{4,0},{8,4},{12,8},{14,12},{10,14},{6,10},{2,6},{0,2},{5,1},{9,5},... | collective-permute-start | bytes 786440 | tf_op jit(solution)/shard_map/ppermute | solution.py:71
  178.2 8.5 %collective-permute-start.22 = (bf16[128,1024]{1,0:T(8,128)(2,1)S(1)}, bf16[128,1024]{1,0:T(8,128)(2,1)S(1)}, u32[]{:S(2)}, u32[]{:S(2)}) collective-permute-start(bf16[128,1024]{1,0:T(8,128)(2,1)S(1)} %get-tuple-element.40), channel_id=1, source_target_pairs={{0,4},{4,8},{8,12},{12,14},{14,10},{10,6},{6,2},{2,0},{1,5},{5,9},... | collective-permute-start | bytes 786440 | tf_op jit(solution)/shard_map/ppermute | solution.py:70
  (59 other events, 398.0 us)

commit v2 on v1

v2 whole, which is shorter than its diff:
```python
import functools

import jax
import jax.numpy as jnp
from jax import lax
from jax.experimental import pallas as pl
from jax.experimental.pallas import tpu as pltpu
from jax.sharding import PartitionSpec as P

BF16 = jnp.bfloat16
F32 = jnp.float32
VMEM_LIMIT = 32 * 1024 * 1024


def ring_order(count):
    if count % 2:
        return list(range(count))
    return list(range(0, count, 2)) + list(range(count - 1, 0, -2))


def swap_cores(value):
    return lax.ppermute(value, "tensor", [(0, 1), (1, 0)])


def tied(values, others):
    out = lax.optimization_barrier((tuple(values), tuple(others)))
    return out[0]


def dot_units(rows, weights):
    return lax.dot_general(rows, weights, (((1,), (1,)), ((), ())), preferred_element_type=F32)


def dot_width(rows, weights):
    return lax.dot_general(rows, weights, (((1,), (0,)), ((), ())), preferred_element_type=F32)


def dot_rows(left, right):
    return lax.dot_general(left, right, (((0,), (0,)), ((), ())), preferred_element_type=F32)


def call(kernel, out_shape, operands, flops, scalars):
    moved = sum(v.size * v.dtype.itemsize for v in operands) + sum(
        v.size * v.dtype.itemsize for v in out_shape
    )
    return pl.pallas_call(
        kernel,
        out_shape=out_shape,
        in_specs=[pl.BlockSpec(memory_space=pltpu.SMEM)]
        + [pl.BlockSpec(memory_space=pltpu.VMEM)] * len(operands),
        out_specs=[pl.BlockSpec(memory_space=pltpu.VMEM)] * len(out_shape),
        compiler_params=pltpu.CompilerParams(vmem_limit_bytes=VMEM_LIMIT),
        cost_estimate=pl.CostEstimate(flops=flops, bytes_accessed=moved, transcendentals=0),
    )(scalars, *operands)


def stacked(refs):
    return jnp.concatenate([ref[...] for ref in refs], axis=0) if len(refs) > 1 else refs[0][...]


def column_of(row):
    count = row.shape[1]
    across = lax.broadcasted_iota(jnp.int32, (count, count), 0)
    along = lax.broadcasted_iota(jnp.int32, (count, count), 1)
    return jnp.sum(jnp.where(across == along, row, 0.0), axis=1, keepdims=True)


def row_of(column):
    count = column.shape[0]
    across = lax.broadcasted_iota(jnp.int32, (count, count), 0)
    along = lax.broadcasted_iota(jnp.int32, (count, count), 1)
    return jnp.sum(jnp.where(across == along, column, 0.0), axis=0, keepdims=True)


def halves_of(w_ref, core):
    width = w_ref.shape[1] // 2
    mine = w_ref[:, pl.ds(pl.multiple_of(core * width, width), width)]
    other = w_ref[:, pl.ds(pl.multiple_of((1 - core) * width, width), width)]
    return mine, other


def forward_kernel(n_rows, n_gates, scalars, *refs):
    mine, other = refs[:n_rows], refs[n_rows : 2 * n_rows]
    tables = refs[2 * n_rows : 2 * n_rows + n_gates]
    w_ref, hidden_ref, gated_ref, slope_ref = refs[2 * n_rows + n_gates :]
    w_mine, w_other = halves_of(w_ref, scalars[0])
    gate = jnp.concatenate([column_of(t[pl.ds(scalars[1], 1), :]) for t in tables], axis=0)
    pre = dot_units(stacked(mine), w_mine) + dot_units(stacked(other), w_other)
    logistic = 1.0 / (1.0 + jnp.exp(-pre))
    hidden = (pre * logistic).astype(BF16)
    hidden_ref[...] = hidden
    gated_ref[...] = (gate * hidden.astype(F32)).astype(BF16)
    slope_ref[...] = gate * (logistic * (1.0 + pre * (1.0 - logistic)))


def backward_kernel(n_rows, scalars, *refs):
    mine, other = refs[:n_rows], refs[n_rows : 2 * n_rows]
    w_ref, hidden_ref, slope_ref, grad_ref, dots_ref = refs[2 * n_rows :]
    w_mine, w_other = halves_of(w_ref, scalars[0])
    units = dot_units(stacked(mine), w_mine) + dot_units(stacked(other), w_other)
    grad_ref[...] = (slope_ref[...] * units).astype(BF16)
    sums = jnp.sum(hidden_ref[...].astype(F32) * units, axis=1, keepdims=True)
    count = dots_ref.shape[1]
    for i in range(dots_ref.shape[0]):
        dots_ref[i : i + 1, :] = row_of(sums[i * count : (i + 1) * count])


def return_kernel(kind, scalars, *refs):
    mine_ref, other_ref, w_ref, w_cols_ref = refs[:4]
    width = w_cols_ref.shape[1]
    w_mine = w_ref[:, pl.ds(pl.multiple_of(scalars[0] * width, width), width)]
    part = dot_width(mine_ref[...], w_mine) + dot_width(other_ref[...], w_cols_ref[...])
    count = part.shape[0] // 2
    if kind == "far":
        behind_ref, ahead_ref = refs[4:]
        behind_ref[...] = part[:count].astype(BF16)
        ahead_ref[...] = part[count:].astype(BF16)
    elif kind == "join":
        half = count // 2
        from_ahead, from_behind, behind_ref, ahead_ref = refs[4:]
        behind_ref[:half, :] = (part[:half] + from_ahead[...].astype(F32)).astype(BF16)
        behind_ref[half:, :] = part[half:count].astype(BF16)
        ahead_ref[:half, :] = part[count : count + half].astype(BF16)
        ahead_ref[half:, :] = (part[count + half :] + from_behind[...].astype(F32)).astype(BF16)
    elif kind == "add":
        from_ahead, from_behind, behind_ref, ahead_ref = refs[4:]
        behind_ref[...] = (part[:count] + from_ahead[...].astype(F32)).astype(BF16)
        ahead_ref[...] = (part[count:] + from_behind[...].astype(F32)).astype(BF16)
    else:
        from_ahead, from_behind, out_ref = refs[4:]
        total = part + from_ahead[...].astype(F32) + from_behind[...].astype(F32)
        out_ref[...] = total.astype(BF16)


def weight_kernel(n_left, n_right, scalars, *refs):
    left = refs[:n_left]
    mine = refs[n_left : n_left + n_right]
    other = refs[n_left + n_right : n_left + 2 * n_right]
    out_ref = refs[-1]

    @pl.when(scalars[0] == 0)
    def _():
        out_ref[...] = dot_rows(stacked(left), stacked(mine)).astype(out_ref.dtype)

    @pl.when(scalars[0] != 0)
    def _():
        out_ref[...] = dot_rows(stacked(left), stacked(other)).astype(out_ref.dtype)


def per_device(tokens, routes, gates, w_in, w_out, cotangent):
    size = lax.axis_size("expert")
    n_dp = lax.axis_size("dp")
    rows, half_width = tokens.shape
    half = rows // 2
    experts = size * w_in.shape[0]
    core = lax.axis_index("tensor")
    place = lax.axis_index("expert")
    group = lax.axis_index("dp")
    order = ring_order(size)
    onward_pairs = [(order[i], order[(i + 1) % size]) for i in range(size)]
    back_pairs = [(b, a) for a, b in onward_pairs]
    steps = size // 2
    scalars = jnp.stack([core, place]).astype(jnp.int32)
    w_in, w_out = w_in[0], w_out[0]
    units = w_in.shape[0]

    def onward(value):
        return lax.ppermute(value, "expert", onward_pairs)

    def back(value):
        return lax.ppermute(value, "expert", back_pairs)

    def other_columns(weights):
        return lax.dynamic_slice_in_dim(weights, (1 - core) * half_width, half_width, axis=1)

    table = jnp.sum(
        jnp.where(
            routes.T[None, :, :] == jnp.arange(experts, dtype=jnp.int32)[:, None, None],
            gates.T[None, :, :],
            0.0,
        ),
        axis=1,
    )

    def forward(mine, other, tables):
        count = sum(v.shape[0] for v in mine)
        shape = (count, units)
        return call(
            functools.partial(forward_kernel, len(mine), len(tables)),
            [
                jax.ShapeDtypeStruct(shape, BF16),
                jax.ShapeDtypeStruct(shape, BF16),
                jax.ShapeDtypeStruct(shape, F32),
            ],
            [*mine, *other, *tables, w_in],
            4 * count * units * half_width,
            scalars,
        )

    def backward(mine, other, hidden, slope):
        count = sum(v.shape[0] for v in mine)
        return call(
            functools.partial(backward_kernel, len(mine)),
            [
                jax.ShapeDtypeStruct((count, units), BF16),
                jax.ShapeDtypeStruct((count // rows, rows), F32),
            ],
            [*mine, *other, w_out, hidden, slope],
            4 * count * units * half_width,
            scalars,
        )

    def returned(kind, mine, other, weights, cols, arrived):
        count = mine.shape[0]
        if kind == "own":
            shapes = [(rows, half_width)]
        elif kind == "far":
            shapes = [(half, half_width)] * 2
        else:
            shapes = [(rows, half_width)] * 2
        return call(
            functools.partial(return_kernel, kind),
            [jax.ShapeDtypeStruct(s, BF16) for s in shapes],
            [mine, other, weights, cols, *arrived],
            4 * count * units * half_width,
            scalars,
        )

    def weight_part(which, left, mine, other, dtype):
        return call(
            functools.partial(weight_kernel, len(left), len(mine)),
            [jax.ShapeDtypeStruct((units, half_width), dtype)],
            [*left, *mine, *other],
            2 * size * rows * units * half_width,
            jnp.reshape(which, (1,)).astype(jnp.int32),
        )[0]

    tok_in = (onward(tokens), back(tokens))
    cot_in = (onward(cotangent), back(cotangent))
    table_in = (onward(table), back(table))
    in_cols = swap_cores(other_columns(w_in))
    out_cols = swap_cores(other_columns(w_out))

    def take_tokens(mine, tables):
        other = tuple(swap_cores(v) for v in mine)
        hidden, gated, slope = forward(mine, other, tables)
        return {
            "tok": (mine, other),
            "hidden": hidden,
            "slope": slope,
            "gated": gated,
            "gated_other": swap_cores(gated),
        }

    def take_cotangent(item, mine):
        other = tuple(swap_cores(v) for v in mine)
        grad, dots = backward(mine, other, item["hidden"], item["slope"])
        item["cot"] = (mine, other)
        item["grad"] = grad
        item["grad_other"] = swap_cores(grad)
        item["dots"] = dots + swap_cores(dots)
        return item

    items = [take_tokens((tokens,), (table,))]
    take_cotangent(items[0], (cotangent,))
    last = (items[0]["grad"], items[0]["gated"])
    for step in range(1, steps + 1):
        tok_now, cot_now, table_now = tok_in, cot_in, table_in
        tok_now = tied(tok_now, last)
        if step < steps - 1:
            tok_in = (onward(tok_now[0]), back(tok_now[1]))
            table_in = (onward(table_now[0]), back(table_now[1]))
        elif step == steps - 1:
            tok_in = (onward(tok_now[0][:half]), back(tok_now[1][half:]))
            table_in = (onward(table_now[0]),)
        item = take_tokens(tok_now, table_now)
        cot_now = tied(cot_now, (item["gated"],))
        if step < steps - 1:
            cot_in = (onward(cot_now[0]), back(cot_now[1]))
        elif step == steps - 1:
            cot_in = (onward(cot_now[0][:half]), back(cot_now[1][half:]))
        take_cotangent(item, cot_now)
        last = (item["grad"],)
        items.append(item)

    row_mask = jnp.arange(experts, dtype=jnp.int32)[:, None] == place

    def dots_table(row):
        return jnp.where(row_mask, row[None, :], 0.0)

    far = items[steps]
    to_behind, to_ahead = returned("far", far["gated"], far["gated_other"], w_out, out_cols, ())
    mixed_in = (back(to_behind), onward(to_ahead))
    to_behind, to_ahead = returned("far", far["grad"], far["grad_other"], w_in, in_cols, ())
    back_in = (back(to_behind), onward(to_ahead))
    dots_in = (None, onward(dots_table(far["dots"][0])))

    gated = [v["gated"] for v in items]
    grads = [v["grad"] for v in items]
    toks = [[x for v in items for x in v["tok"][i]] for i in (0, 1)]
    cots = [[x for v in items for x in v["cot"][i]] for i in (0, 1)]

    def weight_sent(left, right):
        if n_dp == 2:
            sent = weight_part((1 - group) != core, left, *right, BF16)
            return lax.ppermute(sent, "dp", [(0, 1), (1, 0)])
        part_mine = weight_part(jnp.int32(0), left, *right, F32)
        part_other = weight_part(jnp.int32(1), left, *right, F32)
        part = jnp.concatenate(
            [
                jnp.where(core == 0, part_mine, part_other),
                jnp.where(core == 0, part_other, part_mine),
            ],
            axis=1,
        )
        width = part.shape[1] // n_dp
        pieces = [
            lax.dynamic_slice_in_dim(part, ((group + shift) % n_dp) * width, width, axis=1)
            for shift in range(n_dp)
        ]
        total = pieces[0]
        for shift in range(1, n_dp):
            pairs = [(i, (i + shift) % n_dp) for i in range(n_dp)]
            total = total + lax.ppermute(pieces[shift].astype(BF16), "dp", pairs).astype(F32)
        return total

    def weight_total(left, right, arrived):
        if n_dp != 2:
            return arrived[None]
        own = weight_part(group != core, left, *right, F32)
        return (own + arrived.astype(F32))[None]

    out_arrived = weight_sent(gated, cots)
    in_arrived = weight_sent(grads, toks)

    for step in range(steps - 1, 0, -1):
        item = items[step]
        kind = "join" if step == steps - 1 else "add"
        to_behind, to_ahead = returned(
            kind, item["gated"], item["gated_other"], w_out, out_cols, mixed_in
        )
        mixed_in = (back(to_behind), onward(to_ahead))
        back_in = tied(back_in, (to_behind, to_ahead))
        to_behind, to_ahead = returned(
            kind, item["grad"], item["grad_other"], w_in, in_cols, back_in
        )
        back_in = (back(to_behind), onward(to_ahead))
        mixed_in = tied(mixed_in, (to_behind, to_ahead))
        table_behind, table_ahead = dots_table(item["dots"][0]), dots_table(item["dots"][1])
        if dots_in[0] is not None:
            table_behind = table_behind + dots_in[0]
        table_ahead = table_ahead + dots_in[1]
        dots_in = (back(table_behind), onward(table_ahead))

    own = items[0]
    mixed = returned("own", own["gated"], own["gated_other"], w_out, out_cols, mixed_in)[0]
    grad_tokens = returned("own", own["grad"], own["grad_other"], w_in, in_cols, back_in)[0]
    grad_out = weight_total(gated, cots, out_arrived)
    grad_in = weight_total(grads, toks, in_arrived)
    dots = dots_table(own["dots"][0]) + dots_in[0] + dots_in[1]
    grad_gates = jnp.sum(
        jnp.where(
            routes[:, :, None] == jnp.arange(experts, dtype=jnp.int32)[None, None, :],
            dots.T[:, None, :],
            0.0,
        ),
        axis=2,
    )
    return (mixed, grad_tokens, grad_gates, grad_in, grad_out)


def solution(mesh):
    placed = (
        P(("dp", "expert"), "tensor"),
        P(("dp", "expert"), None),
        P(("dp", "expert"), None),
        P("expert", "tensor", None),
        P("expert", "tensor", None),
        P(("dp", "expert"), "tensor"),
    )
    return jax.shard_map(
        per_device,
        mesh=mesh,
        in_specs=placed,
        out_specs=(
            P(("dp", "expert"), "tensor"),
            P(("dp", "expert"), "tensor"),
            P(("dp", "expert"), None),
            P("expert", "tensor", "dp"),
            P("expert", "tensor", "dp"),
        ),
        check_vma=False,
    )
```

time: 189 us -> 179 us (0.947)
  matrix products: 48.2 us -> 0 us
  Pallas kernels: 0 us -> 42.6 us
  waiting for transfers between devices: 60.5 us -> 50.5 us
  local copies, waits for them, and re-layouts: 12.2 us -> 18.6 us
  other arithmetic: 10.1 us -> 4.48 us
  starting transfers between devices: 56 us -> 60.1 us
    dot_general x44 -> x0, matrix products: 48.2 us -> none  [the longest x20 26 us: rows_by_width(): lax.dot_general(rows, weights, (((1,), (0,)), ((), ())), preferred_elemen...]
    pallas_call x0 -> x24, Pallas kernels: none -> 42.6 us  [call(): pl.pallas_call(kernel, out_shape=out_shape, in_specs=[pl.BlockSpec(memory...]
    ppermute x34 -> x48, starting transfers between devices: 39.9 us -> 51.6 us  [the longest x24 36.2 us: onward(): return lax.ppermute(value, 'expert', onward_pairs)]
    all_to_all x2 -> x0, starting transfers between devices: 10.4 us -> none  [the longest x1 5.57 us: per_device(): lax.all_to_all(dot_send, 'expert', split_axis=0, concat_axis=0, tiled=True)]
    ppermute x34 -> x48, waiting for transfers between devices: 54.8 us -> 48.4 us  [the longest x22 28.4 us: back(): return lax.ppermute(value, 'expert', back_pairs)]
    unnamed x92 -> x106, local copies, waits for them, and re-layouts: 8.61 us -> 14 us
    all_to_all x2 -> x0, waiting for transfers between devices: 5.2 us -> none  [the longest x1 5.2 us: per_device(): lax.all_to_all(dot_send, 'expert', split_axis=0, concat_axis=0, tiled=True)]
    convert_element_type x6 -> x0, other arithmetic: 3.13 us -> none  [the longest x2 2.51 us: weight_grad(): sent = piece((group + shift) % n_dp).astype(BF16)]
  transfers between devices with their start and end apart: 59 -> 83, of which waited for: 26 -> 24; matrix products, arithmetic and copies ran while one was open for 37% -> 5% of each run, Pallas kernels for 0% -> 23%
where the time goes in v2:
time: 179 us; the launch traced here: 178 us
  starting transfers between devices  60.1 us (34%)
  waiting for transfers between devices  50.5 us (28%)
  Pallas kernels  42.6 us (24%)
  local copies, waits for them, and re-layouts  18.6 us (10%)
  other arithmetic  4.48 us (3%)
    pallas_call x24, Pallas kernels, call(): pl.pallas_call(kernel, out_shape=out_shape, in_specs=[pl.BlockSpec(memory...  42.6 us
    ppermute x24, starting transfers between devices, onward(): return lax.ppermute(value, 'expert', onward_pairs)  36.2 us
    ppermute x22, waiting for transfers between devices, back(): return lax.ppermute(value, 'expert', back_pairs)  28.4 us
    ppermute x24, waiting for transfers between devices, onward(): return lax.ppermute(value, 'expert', onward_pairs)  18.6 us
    unnamed x106, local copies, waits for them, and re-layouts  14 us
    ppermute x22, starting transfers between devices, back(): return lax.ppermute(value, 'expert', back_pairs)  13.4 us
    ppermute x35, starting transfers between devices, swap_cores(): return lax.ppermute(value, 'tensor', [(0, 1), (1, 0)])  8.48 us
  transfers between devices with their start and end apart: 83, of which 24 were waited for; matrix products, arithmetic and copies ran while one was open for 5% of the time, Pallas kernels for 23%

profile of v2, /device:TPU:0, one launch (start us, length us, event | category | flops | bytes accessed | tf_op | source)
XLA Modules:
  0.0 177.8 jit_solution(1185146950457635420)
XLA Ops:
  1.2 3.0 %collective-permute-start.3 = (bf16[128,1024]{1,0:T(8,128)(2,1)}, bf16[128,1024]{1,0:T(8,128)(2,1)S(1)}, u32[]{:S(2)}, u32[]{:S(2)}) collective-permute-start(bf16[128,1024]{1,0:T(8,128)(2,1)} %refs_5_.5), channel_id=1, source_target_pairs={{0,4},{4,8},{8,12},{12,14},{14,10},{10,6},{6,2},{2,0},{1,5},{5,9},... | collective-permute-start | bytes 786440 | tf_op jit(solution)/shard_map/ppermute | solution.py:168
  10.0 1.8 shard_map.102
  16.7 4.7 %collective-permute-done.8.refs_4_ = f32[8,128]{1,0:T(8,128)S(1)} collective-permute-done((f32[8,128]{1,0:T(8,128)S(1)}, f32[8,128]{1,0:T(8,128)S(1)}, u32[]{:S(2)}, u32[]{:S(2)}) %collective-permute-start.8) | collective-permute-done | bytes 4128 | tf_op jit(solution)/shard_map/ppermute | solution.py:168
  22.7 2.3 %collective-permute-done.9.refs_5_ = f32[8,128]{1,0:T(8,128)S(1)} collective-permute-done((f32[8,128]{1,0:T(8,128)S(1)}, f32[8,128]{1,0:T(8,128)S(1)}, u32[]{:S(2)}, u32[]{:S(2)}) %collective-permute-start.9) | collective-permute-done | bytes 4128 | tf_op jit(solution)/shard_map/ppermute | solution.py:171
  25.0 2.0 %shard_map.103 = (bf16[256,384]{1,0:T(8,128)(2,1)S(1)}, bf16[256,384]{1,0:T(8,128)(2,1)S(1)}, f32[256,384]{1,0:T(8,128)S(1)}) custom-call(s32[2]{0:T(128)S(1)} %pad_add_fusion.scalars, bf16[128,1024]{1,0:T(8,128)(2,1)S(1)} %collective-permute-done.3.refs_0_.refs_6_, bf16[128,1024]{1,0:T(8,128)(2,1)} %collective-permute-done.4.refs_1_.refs_7_, ...), custom_call_target="tpu_custom_call" | custom-call | flops 402653184 | bytes 3416064 | tf_op jit(solution)/shard_map/pallas_call | solution.py:46
  28.3 1.6 collective-permute-start.11
  32.5 4.3 %collective-permute-done.11.refs_0_.refs_8_ = bf16[128,1024]{1,0:T(8,128)(2,1)} collective-permute-done((bf16[128,1024]{1,0:T(8,128)(2,1)S(1)}, bf16[128,1024]{1,0:T(8,128)(2,1)}, u32[]{:S(2)}, u32[]{:S(2)}) %collective-permute-start.11) | collective-permute-done | bytes 262176 | tf_op jit(solution)/shard_map/ppermute | solution.py:168
  40.8 1.6 collective-permute-start.19
  42.4 4.8 %collective-permute-done.19.refs_4_ = f32[8,128]{1,0:T(8,128)S(1)} collective-permute-done((f32[8,128]{1,0:T(8,128)S(1)}, f32[8,128]{1,0:T(8,128)S(1)}, u32[]{:S(2)}, u32[]{:S(2)}) %collective-permute-start.19) | collective-permute-done | bytes 4128 | tf_op jit(solution)/shard_map/ppermute | solution.py:168
  47.6 3.2 %collective-permute-done.20.refs_5_ = f32[8,128]{1,0:T(8,128)S(1)} collective-permute-done((f32[8,128]{1,0:T(8,128)S(1)}, f32[8,128]{1,0:T(8,128)S(1)}, u32[]{:S(2)}, u32[]{:S(2)}) %collective-permute-start.20) | collective-permute-done | bytes 4128 | tf_op jit(solution)/shard_map/ppermute | solution.py:171
  50.8 2.1 %shard_map.105 = (bf16[256,384]{1,0:T(8,128)(2,1)S(1)}, bf16[256,384]{1,0:T(8,128)(2,1)S(1)}, f32[256,384]{1,0:T(8,128)S(1)}) custom-call(s32[2]{0:T(128)S(1)} %pad_add_fusion.scalars, bf16[128,1024]{1,0:T(8,128)(2,1)} %collective-permute-done.11.refs_0_.refs_8_, bf16[128,1024]{1,0:T(8,128)(2,1)} %collective-permute-done.12.refs_1_.refs_9_, ...), custom_call_target="tpu_custom_call" | custom-call | flops 402653184 | bytes 3416064 | tf_op jit(solution)/shard_map/pallas_call | solution.py:46
  55.5 1.6 collective-permute-start.22
  57.5 1.6 collective-permute-start.30
  63.1 2.0 %shard_map.106 = (bf16[256,384]{1,0:T(8,128)(2,1)S(1)}, f32[2,128]{1,0:T(2,128)S(1)}) custom-call(s32[2]{0:T(128)S(1)} %pad_add_fusion.scalars, bf16[128,1024]{1,0:T(8,128)(2,1)} %collective-permute-done.24.refs_0_.refs_8_, bf16[128,1024]{1,0:T(8,128)(2,1)} %collective-permute-done.25.refs_1_.refs_9_, ...), custom_call_target="tpu_custom_call" | custom-call | flops 402653184 | bytes 3408896 | tf_op jit(solution)/shard_map/pallas_call | solution.py:46
  69.5 2.2 %collective-permute-done.31.refs_5_ = f32[8,128]{1,0:T(8,128)S(1)} collective-permute-done((f32[8,128]{1,0:T(8,128)S(1)}, f32[8,128]{1,0:T(8,128)S(1)}, u32[]{:S(2)}, u32[]{:S(2)}) %collective-permute-start.31) | collective-permute-done | bytes 4128 | tf_op jit(solution)/shard_map/ppermute | solution.py:171
  71.7 2.0 %shard_map.107 = (bf16[256,384]{1,0:T(8,128)(2,1)S(1)}, bf16[256,384]{1,0:T(8,128)(2,1)S(1)}, f32[256,384]{1,0:T(8,128)S(1)}) custom-call(s32[2]{0:T(128)S(1)} %pad_add_fusion.scalars, bf16[128,1024]{1,0:T(8,128)(2,1)S(1)} %collective-permute-done.22.refs_0_.refs_10_, bf16[128,1024]{1,0:T(8,128)(2,1)} %collective-permute-done.23.refs_1_.refs_11_, ...), custom_call_target="tpu_custom_call" | custom-call | flops 402653184 | bytes 3416064 | tf_op jit(solution)/shard_map/pallas_call | solution.py:46
  85.1 2.1 %shard_map.108 = (bf16[256,384]{1,0:T(8,128)(2,1)S(1)}, f32[2,128]{1,0:T(2,128)S(1)}) custom-call(s32[2]{0:T(128)S(1)} %pad_add_fusion.scalars, bf16[128,1024]{1,0:T(8,128)(2,1)} %collective-permute-done.35.refs_0_.refs_10_, bf16[128,1024]{1,0:T(8,128)(2,1)} %collective-permute-done.36.refs_1_.refs_11_, ...), custom_call_target="tpu_custom_call" | custom-call | flops 402653184 | bytes 3408896 | tf_op jit(solution)/shard_map/pallas_call | solution.py:46
  97.4 1.6 shard_map.110
  101.2 2.6 %shard_map.124 = bf16[384,1024]{1,0:T(8,128)(2,1)S(1)} custom-call(s32[1]{0:T(128)} %bitcast.18.scalars, bf16[128,384]{1,0:T(8,128)(2,1)S(1)} %copy-done.42, bf16[256,384]{1,0:T(8,128)(2,1)S(1)} %copy-done.34, bf16[256,384]{1,0:T(8,128)(2,1)S(1)} %copy-done.40, bf16[256,384]{1,0:T(8,128)(2,1)S(1)} %copy-done.32, ...), custom_call_target="tpu_custom_call" | custom-call | flops 805306368 | bytes 5767168 | tf_op jit(solution)/shard_map/pallas_call | solution.py:46
  103.9 2.8 %shard_map.123 = f32[384,1024]{1,0:T(8,128)S(1)} custom-call(s32[1]{0:T(128)} %bitcast.17.scalars, bf16[128,384]{1,0:T(8,128)(2,1)S(1)} %copy-done.42, bf16[256,384]{1,0:T(8,128)(2,1)S(1)} %copy-done.34, bf16[256,384]{1,0:T(8,128)(2,1)S(1)} %copy-done.40, bf16[256,384]{1,0:T(8,128)(2,1)S(1)} %copy-done.32, ...), custom_call_target="tpu_custom_call" | custom-call | flops 805306368 | bytes 6553600 | tf_op jit(solution)/shard_map/pallas_call | solution.py:46
  106.8 2.2 %shard_map.122 = bf16[384,1024]{1,0:T(8,128)(2,1)S(1)} custom-call(s32[1]{0:T(128)} %bitcast.18.scalars, bf16[128,384]{1,0:T(8,128)(2,1)S(1)} %get-tuple-element.77.refs_0_, bf16[256,384]{1,0:T(8,128)(2,1)S(1)} %copy-done.36, bf16[256,384]{1,0:T(8,128)(2,1)S(1)} %copy-done.38, bf16[256,384]{1,0:T(8,128)(2,1)S(1)} %get-tuple-element.101.refs_0_.refs_3_, ...), custom_call_target="tpu_custom_call" | custom-call | flops 805306368 | bytes 5767168 | tf_op jit(solution)/shard_map/pallas_call | solution.py:46
  118.8 1.8 %shard_map.111 = (bf16[128,1024]{1,0:T(8,128)(2,1)S(1)}, bf16[128,1024]{1,0:T(8,128)(2,1)S(1)}) custom-call(s32[2]{0:T(128)S(1)} %pad_add_fusion.scalars, bf16[256,384]{1,0:T(8,128)(2,1)S(1)} %copy-done.32, bf16[256,384]{1,0:T(8,128)(2,1)S(1)} %collective-permute-done.32.refs_1_, bf16[384,2048]{1,0:T(8,128)(2,1)S(1)} %bitcast.40, ...), custom_call_target="tpu_custom_call" | custom-call | flops 402653184 | bytes 3538944 | tf_op jit(solution)/shard_map/pallas_call | solution.py:46
  124.7 5.3 %collective-permute-done.45.refs_4_ = bf16[128,1024]{1,0:T(8,128)(2,1)S(1)} collective-permute-done((bf16[128,1024]{1,0:T(8,128)(2,1)S(1)}, bf16[128,1024]{1,0:T(8,128)(2,1)S(1)}, u32[]{:S(2)}, u32[]{:S(2)}) %collective-permute-start.45) | collective-permute-done | bytes 262176 | tf_op jit(solution)/shard_map/ppermute | solution.py:171
  135.6 1.8 %shard_map.115 = (bf16[128,1024]{1,0:T(8,128)(2,1)S(1)}, bf16[128,1024]{1,0:T(8,128)(2,1)S(1)}) custom-call(s32[2]{0:T(128)S(1)} %pad_add_fusion.scalars, bf16[256,384]{1,0:T(8,128)(2,1)S(1)} %copy-done.40, bf16[256,384]{1,0:T(8,128)(2,1)S(1)} %collective-permute-done.21.refs_1_, bf16[384,2048]{1,0:T(8,128)(2,1)S(1)} %bitcast.41, ...), custom_call_target="tpu_custom_call" | custom-call | flops 402653184 | bytes 3801088 | tf_op jit(solution)/shard_map/pallas_call | solution.py:46
  139.6 3.2 %collective-permute-done.59.refs_4_ = bf16[128,1024]{1,0:T(8,128)(2,1)S(1)} collective-permute-done((bf16[128,1024]{1,0:T(8,128)(2,1)S(1)}, bf16[128,1024]{1,0:T(8,128)(2,1)S(1)}, u32[]{:S(2)}, u32[]{:S(2)}) %collective-permute-start.59) | collective-permute-done | bytes 262176 | tf_op jit(solution)/shard_map/ppermute | solution.py:171
  144.0 2.2 %shard_map.121 = f32[384,1024]{1,0:T(8,128)S(1)} custom-call(s32[1]{0:T(128)} %bitcast.17.scalars, bf16[128,384]{1,0:T(8,128)(2,1)S(1)} %get-tuple-element.77.refs_0_, bf16[256,384]{1,0:T(8,128)(2,1)S(1)} %copy-done.36, bf16[256,384]{1,0:T(8,128)(2,1)S(1)} %copy-done.38, bf16[256,384]{1,0:T(8,128)(2,1)S(1)} %get-tuple-element.101.refs_0_.refs_3_, ...), custom_call_target="tpu_custom_call" | custom-call | flops 805306368 | bytes 6553600 | tf_op jit(solution)/shard_map/pallas_call | solution.py:46
  153.2 1.9 %shard_map.117 = (bf16[128,1024]{1,0:T(8,128)(2,1)S(1)}, bf16[128,1024]{1,0:T(8,128)(2,1)S(1)}) custom-call(s32[2]{0:T(128)S(1)} %pad_add_fusion.scalars, bf16[256,384]{1,0:T(8,128)(2,1)S(1)} %copy-done.34, bf16[256,384]{1,0:T(8,128)(2,1)S(1)} %collective-permute-done.10.refs_1_, bf16[384,2048]{1,0:T(8,128)(2,1)S(1)} %bitcast.42, ...), custom_call_target="tpu_custom_call" | custom-call | flops 402653184 | bytes 3801088 | tf_op jit(solution)/shard_map/pallas_call | solution.py:46
  155.1 4.2 %collective-permute-done.64.refs_4_ = bf16[128,1024]{1,0:T(8,128)(2,1)S(1)} collective-permute-done((bf16[128,1024]{1,0:T(8,128)(2,1)S(1)}, bf16[128,1024]{1,0:T(8,128)(2,1)S(1)}, u32[]{:S(2)}, u32[]{:S(2)}) %collective-permute-start.64) | collective-permute-done | bytes 262176 | tf_op jit(solution)/shard_map/ppermute | solution.py:171
  166.6 2.3 %collective-permute-done.61.refs_4_ = bf16[128,1024]{1,0:T(8,128)(2,1)S(1)} collective-permute-done((bf16[128,1024]{1,0:T(8,128)(2,1)S(1)}, bf16[128,1024]{1,0:T(8,128)(2,1)S(1)}, u32[]{:S(2)}, u32[]{:S(2)}) %collective-permute-start.61) | collective-permute-done | bytes 262176 | tf_op jit(solution)/shard_map/ppermute | solution.py:171
  171.6 2.3 %shard_map.119 = bf16[128,1024]{1,0:T(8,128)(2,1)} custom-call(s32[2]{0:T(128)S(1)} %pad_add_fusion.scalars, bf16[128,384]{1,0:T(8,128)(2,1)S(1)} %copy-done.42, bf16[128,384]{1,0:T(8,128)(2,1)S(1)} %collective-permute-done.1.refs_1_, bf16[384,2048]{1,0:T(8,128)(2,1)S(1)} %bitcast.43, bf16[384,1024]{1,0:T(8,128)(2,1)} %collective-permute-done.2.refs_3_, ...), custom_call_target="tpu_custom_call" | custom-call | flops 201326592 | bytes 3342336 | tf_op jit(solution)/shard_map/pallas_call | solution.py:46
  174.0 2.1 %collective-permute-done.68.refs_5_ = bf16[128,1024]{1,0:T(8,128)(2,1)S(1)} collective-permute-done((bf16[128,1024]{1,0:T(8,128)(2,1)S(1)}, bf16[128,1024]{1,0:T(8,128)(2,1)S(1)}, u32[]{:S(2)}, u32[]{:S(2)}) %collective-permute-start.68) | collective-permute-done | bytes 262176 | tf_op jit(solution)/shard_map/ppermute | solution.py:168
  176.1 1.7 shard_map.120
  (289 shorter events, 95.6 us)
Async XLA Ops:
  1.2 10.5 %collective-permute-start.3 = (bf16[128,1024]{1,0:T(8,128)(2,1)}, bf16[128,1024]{1,0:T(8,128)(2,1)S(1)}, u32[]{:S(2)}, u32[]{:S(2)}) collective-permute-start(bf16[128,1024]{1,0:T(8,128)(2,1)} %refs_5_.5), channel_id=1, source_target_pairs={{0,4},{4,8},{8,12},{12,14},{14,10},{10,6},{6,2},{2,0},{1,5},{5,9},... | collective-permute-start | bytes 786440 | tf_op jit(solution)/shard_map/ppermute | solution.py:168
  12.6 12.4 %collective-permute-start.6 = (bf16[128,1024]{1,0:T(8,128)(2,1)S(1)}, bf16[128,1024]{1,0:T(8,128)(2,1)S(1)}, u32[]{:S(2)}, u32[]{:S(2)}) collective-permute-start(bf16[128,1024]{1,0:T(8,128)(2,1)S(1)} %collective-permute-done.3.refs_0_.refs_6_), channel_id=1, source_target_pairs={{0,1},{1,0},{2,3},{3,2},{4,5},{5,4},{6,7},{7,6},{8,9},{9,8},{10,11... | collective-permute-start | bytes 786440 | tf_op jit(solution)/shard_map/ppermute | solution.py:22
  12.6 12.4 %collective-permute-start.7 = (bf16[128,1024]{1,0:T(8,128)(2,1)}, bf16[128,1024]{1,0:T(8,128)(2,1)S(1)}, u32[]{:S(2)}, u32[]{:S(2)}) collective-permute-start(bf16[128,1024]{1,0:T(8,128)(2,1)} %collective-permute-done.4.refs_1_.refs_7_), channel_id=1, source_target_pairs={{0,1},{1,0},{2,3},{3,2},{4,5},{5,4},{6,7},{7,6},{8,9},{9,8},{10,11... | collective-permute-start | bytes 786440 | tf_op jit(solution)/shard_map/ppermute | solution.py:22
  13.1 14.7 %collective-permute-start.13 = (bf16[128,1024]{1,0:T(8,128)(2,1)S(1)}, bf16[128,1024]{1,0:T(8,128)(2,1)S(1)}, u32[]{:S(2)}, u32[]{:S(2)}) collective-permute-start(bf16[128,1024]{1,0:T(8,128)(2,1)S(1)} %copy-done.21), channel_id=1, source_target_pairs={{0,4},{4,8},{8,12},{12,14},{14,10},{10,6},{6,2},{2,0},{1,5},{5,9},... | collective-permute-start | bytes 786440 | tf_op jit(solution)/shard_map/ppermute | solution.py:168
  14.7 13.1 %collective-permute-start.14 = (bf16[128,1024]{1,0:T(8,128)(2,1)S(1)}, bf16[128,1024]{1,0:T(8,128)(2,1)S(1)}, u32[]{:S(2)}, u32[]{:S(2)}) collective-permute-start(bf16[128,1024]{1,0:T(8,128)(2,1)S(1)} %copy-done.21), channel_id=1, source_target_pairs={{4,0},{8,4},{12,8},{14,12},{10,14},{6,10},{2,6},{0,2},{5,1},{9,5},... | collective-permute-start | bytes 786440 | tf_op jit(solution)/shard_map/ppermute | solution.py:171
  38.2 12.5 %collective-permute-start.17 = (bf16[128,1024]{1,0:T(8,128)(2,1)}, bf16[128,1024]{1,0:T(8,128)(2,1)S(1)}, u32[]{:S(2)}, u32[]{:S(2)}) collective-permute-start(bf16[128,1024]{1,0:T(8,128)(2,1)} %collective-permute-done.11.refs_0_.refs_8_), channel_id=1, source_target_pairs={{0,1},{1,0},{2,3},{3,2},{4,5},{5,4},{6,7},{7,6},{8,9},{9,8},{10,11... | collective-permute-start | bytes 786440 | tf_op jit(solution)/shard_map/ppermute | solution.py:22
  38.3 12.5 %collective-permute-start.18 = (bf16[128,1024]{1,0:T(8,128)(2,1)}, bf16[128,1024]{1,0:T(8,128)(2,1)S(1)}, u32[]{:S(2)}, u32[]{:S(2)}) collective-permute-start(bf16[128,1024]{1,0:T(8,128)(2,1)} %collective-permute-done.12.refs_1_.refs_9_), channel_id=1, source_target_pairs={{0,1},{1,0},{2,3},{3,2},{4,5},{5,4},{6,7},{7,6},{8,9},{9,8},{10,11... | collective-permute-start | bytes 786440 | tf_op jit(solution)/shard_map/ppermute | solution.py:22
  38.8 16.2 %collective-permute-start.24 = (bf16[128,1024]{1,0:T(8,128)(2,1)S(1)}, bf16[128,1024]{1,0:T(8,128)(2,1)}, u32[]{:S(2)}, u32[]{:S(2)}) collective-permute-start(bf16[128,1024]{1,0:T(8,128)(2,1)S(1)} %collective-permute-done.13.refs_0_.refs_6_), channel_id=1, source_target_pairs={{0,4},{4,8},{8,12},{12,14},{14,10},{10,6},{6,2},{2,0},{1,5},{5,9},... | collective-permute-start | bytes 786440 | tf_op jit(solution)/shard_map/ppermute | solution.py:168
  40.3 14.6 %collective-permute-start.25 = (bf16[128,1024]{1,0:T(8,128)(2,1)S(1)}, bf16[128,1024]{1,0:T(8,128)(2,1)}, u32[]{:S(2)}, u32[]{:S(2)}) collective-permute-start(bf16[128,1024]{1,0:T(8,128)(2,1)S(1)} %collective-permute-done.14.refs_1_.refs_7_), channel_id=1, source_target_pairs={{4,0},{8,4},{12,8},{14,12},{10,14},{6,10},{2,6},{0,2},{5,1},{9,5},... | collective-permute-start | bytes 786440 | tf_op jit(solution)/shard_map/ppermute | solution.py:171
  55.5 9.6 %collective-permute-start.22 = (bf16[128,1024]{1,0:T(8,128)(2,1)}, bf16[128,1024]{1,0:T(8,128)(2,1)S(1)}, u32[]{:S(2)}, u32[]{:S(2)}) collective-permute-start(bf16[128,1024]{1,0:T(8,128)(2,1)} %collective-permute-done.11.refs_0_.refs_8_), channel_id=1, source_target_pairs={{0,4},{4,8},{8,12},{12,14},{14,10},{10,6},{6,2},{2,0},{1,5},{5,9},... | collective-permute-start | bytes 786440 | tf_op jit(solution)/shard_map/ppermute | solution.py:168
  57.1 9.5 %collective-permute-start.23 = (bf16[128,1024]{1,0:T(8,128)(2,1)}, bf16[128,1024]{1,0:T(8,128)(2,1)}, u32[]{:S(2)}, u32[]{:S(2)}) collective-permute-start(bf16[128,1024]{1,0:T(8,128)(2,1)} %collective-permute-done.12.refs_1_.refs_9_), channel_id=1, source_target_pairs={{4,0},{8,4},{12,8},{14,12},{10,14},{6,10},{2,6},{0,2},{5,1},{9,5},... | collective-permute-start | bytes 786440 | tf_op jit(solution)/shard_map/ppermute | solution.py:171
  57.5 10.5 %collective-permute-start.30 = (f32[8,128]{1,0:T(8,128)S(1)}, f32[8,128]{1,0:T(8,128)S(1)}, u32[]{:S(2)}, u32[]{:S(2)}) collective-permute-start(f32[8,128]{1,0:T(8,128)S(1)} %collective-permute-done.19.refs_4_), channel_id=1, source_target_pairs={{0,4},{4,8},{8,12},{12,14},{14,10},{10,6},{6,2},{2,0},{1,5},{5,9},... | collective-permute-start | bytes 12296 | tf_op jit(solution)/shard_map/ppermute | solution.py:168
  59.1 17.4 %collective-permute-start.35 = (bf16[128,1024]{1,0:T(8,128)(2,1)}, bf16[128,1024]{1,0:T(8,128)(2,1)}, u32[]{:S(2)}, u32[]{:S(2)}) collective-permute-start(bf16[128,1024]{1,0:T(8,128)(2,1)} %collective-permute-done.24.refs_0_.refs_8_), channel_id=1, source_target_pairs={{0,4},{4,8},{8,12},{12,14},{14,10},{10,6},{6,2},{2,0},{1,5},{5,9},... | collective-permute-start | bytes 786440 | tf_op jit(solution)/shard_map/ppermute | solution.py:168
  60.6 15.9 %collective-permute-start.36 = (bf16[128,1024]{1,0:T(8,128)(2,1)}, bf16[128,1024]{1,0:T(8,128)(2,1)}, u32[]{:S(2)}, u32[]{:S(2)}) collective-permute-start(bf16[128,1024]{1,0:T(8,128)(2,1)} %collective-permute-done.25.refs_1_.refs_9_), channel_id=1, source_target_pairs={{4,0},{8,4},{12,8},{14,12},{10,14},{6,10},{2,6},{0,2},{5,1},{9,5},... | collective-permute-start | bytes 786440 | tf_op jit(solution)/shard_map/ppermute | solution.py:171
  71.7 25.1 %collective-permute-start.2 = (bf16[384,1024]{1,0:T(8,128)(2,1)}, bf16[384,1024]{1,0:T(8,128)(2,1)}, u32[]{:S(2)}, u32[]{:S(2)}) collective-permute-start(bf16[384,1024]{1,0:T(8,128)(2,1)} %dynamic-slice_bitcast_fusion.1), channel_id=1, source_target_pairs={{0,1},{1,0},{2,3},{3,2},{4,5},{5,4},{6,7},{7,6},{8,9},{9,8},{10,11... | collective-permute-start | bytes 2359304 | tf_op jit(solution)/shard_map/ppermute | solution.py:22
  77.5 14.2 %collective-permute-start.41 = (f32[8,128]{1,0:T(8,128)S(1)}, f32[8,128]{1,0:T(8,128)S(1)}, u32[]{:S(2)}, u32[]{:S(2)}) collective-permute-start(f32[8,128]{1,0:T(8,128)S(1)} %collective-permute-done.30.refs_4_), channel_id=1, source_target_pairs={{0,4},{4,8},{8,12},{12,14},{14,10},{10,6},{6,2},{2,0},{1,5},{5,9},... | collective-permute-start | bytes 12296 | tf_op jit(solution)/shard_map/ppermute | solution.py:168
  93.1 16.7 %collective-permute-start.48 = (bf16[384,1024]{1,0:T(8,128)(2,1)S(1)}, bf16[384,1024]{1,0:T(8,128)(2,1)S(1)}, u32[]{:S(2)}, u32[]{:S(2)}) collective-permute-start(bf16[384,1024]{1,0:T(8,128)(2,1)S(1)} %copy-done.51), channel_id=1, source_target_pairs={{0,1},{1,0},{2,3},{3,2},{4,5},{5,4},{6,7},{7,6},{8,9},{9,8},{10,11... | collective-permute-start | bytes 2359304 | tf_op jit(solution)/shard_map/ppermute | solution.py:22
  96.8 16.4 %collective-permute-start.32 = (bf16[256,384]{1,0:T(8,128)(2,1)S(1)}, bf16[256,384]{1,0:T(8,128)(2,1)S(1)}, u32[]{:S(2)}, u32[]{:S(2)}) collective-permute-start(bf16[256,384]{1,0:T(8,128)(2,1)S(1)} %copy-done.32), channel_id=1, source_target_pairs={{0,1},{1,0},{2,3},{3,2},{4,5},{5,4},{6,7},{7,6},{8,9},{9,8},{10,11... | collective-permute-start | bytes 589832 | tf_op jit(solution)/shard_map/ppermute | solution.py:22
  96.9 23.8 %collective-permute-start.47 = (bf16[256,384]{1,0:T(8,128)(2,1)S(1)}, bf16[256,384]{1,0:T(8,128)(2,1)S(1)}, u32[]{:S(2)}, u32[]{:S(2)}) collective-permute-start(bf16[256,384]{1,0:T(8,128)(2,1)S(1)} %get-tuple-element.101.refs_0_.refs_3_), channel_id=1, source_target_pairs={{0,1},{1,0},{2,3},{3,2},{4,5},{5,4},{6,7},{7,6},{8,9},{9,8},{10,11... | collective-permute-start | bytes 589832 | tf_op jit(solution)/shard_map/ppermute | solution.py:22
  99.1 17.7 %collective-permute-start.43 = (bf16[64,1024]{1,0:T(8,128)(2,1)S(1)}, bf16[64,1024]{1,0:T(8,128)(2,1)S(1)}, u32[]{:S(2)}, u32[]{:S(2)}) collective-permute-start(bf16[64,1024]{1,0:T(8,128)(2,1)S(1)} %get-tuple-element.105), channel_id=1, source_target_pairs={{4,0},{8,4},{12,8},{14,12},{10,14},{6,10},{2,6},{0,2},{5,1},{9,5},... | collective-permute-start | bytes 393224 | tf_op jit(solution)/shard_map/ppermute | solution.py:171
  120.7 11.5 %collective-permute-start.10 = (bf16[256,384]{1,0:T(8,128)(2,1)S(1)}, bf16[256,384]{1,0:T(8,128)(2,1)S(1)}, u32[]{:S(2)}, u32[]{:S(2)}) collective-permute-start(bf16[256,384]{1,0:T(8,128)(2,1)S(1)} %copy-done.34), channel_id=1, source_target_pairs={{0,1},{1,0},{2,3},{3,2},{4,5},{5,4},{6,7},{7,6},{8,9},{9,8},{10,11... | collective-permute-start | bytes 589832 | tf_op jit(solution)/shard_map/ppermute | solution.py:22
  120.8 12.8 %collective-permute-start.21 = (bf16[256,384]{1,0:T(8,128)(2,1)S(1)}, bf16[256,384]{1,0:T(8,128)(2,1)S(1)}, u32[]{:S(2)}, u32[]{:S(2)}) collective-permute-start(bf16[256,384]{1,0:T(8,128)(2,1)S(1)} %copy-done.40), channel_id=1, source_target_pairs={{0,1},{1,0},{2,3},{3,2},{4,5},{5,4},{6,7},{7,6},{8,9},{9,8},{10,11... | collective-permute-start | bytes 589832 | tf_op jit(solution)/shard_map/ppermute | solution.py:22
  121.3 12.9 %collective-permute-start.58 = (bf16[256,384]{1,0:T(8,128)(2,1)S(1)}, bf16[256,384]{1,0:T(8,128)(2,1)S(1)}, u32[]{:S(2)}, u32[]{:S(2)}) collective-permute-start(bf16[256,384]{1,0:T(8,128)(2,1)S(1)} %copy-done.38), channel_id=1, source_target_pairs={{0,1},{1,0},{2,3},{3,2},{4,5},{5,4},{6,7},{7,6},{8,9},{9,8},{10,11... | collective-permute-start | bytes 589832 | tf_op jit(solution)/shard_map/ppermute | solution.py:22
  122.0 9.5 %collective-permute-start.46 = (bf16[128,1024]{1,0:T(8,128)(2,1)S(1)}, bf16[128,1024]{1,0:T(8,128)(2,1)S(1)}, u32[]{:S(2)}, u32[]{:S(2)}) collective-permute-start(bf16[128,1024]{1,0:T(8,128)(2,1)S(1)} %get-tuple-element.108), channel_id=1, source_target_pairs={{0,4},{4,8},{8,12},{12,14},{14,10},{10,6},{6,2},{2,0},{1,5},{5,9},... | collective-permute-start | bytes 786440 | tf_op jit(solution)/shard_map/ppermute | solution.py:168
  130.0 31.7 %collective-permute-start.82 = (bf16[384,1024]{1,0:T(8,128)(2,1)S(1)}, bf16[384,1024]{1,0:T(8,128)(2,1)S(1)}, u32[]{:S(2)}, u32[]{:S(2)}) collective-permute-start(bf16[384,1024]{1,0:T(8,128)(2,1)S(1)} %shard_map.124), channel_id=1, source_target_pairs={{0,16},{16,0},{1,17},{17,1},{2,18},{18,2},{3,19},{19,3},{4,20},{20... | collective-permute-start | bytes 2359304 | tf_op jit(solution)/shard_map/ppermute | solution.py:306
  137.4 13.1 %collective-permute-start.56 = (bf16[128,1024]{1,0:T(8,128)(2,1)S(1)}, bf16[128,1024]{1,0:T(8,128)(2,1)S(1)}, u32[]{:S(2)}, u32[]{:S(2)}) collective-permute-start(bf16[128,1024]{1,0:T(8,128)(2,1)S(1)} %get-tuple-element.122), channel_id=1, source_target_pairs={{4,0},{8,4},{12,8},{14,12},{10,14},{6,10},{2,6},{0,2},{5,1},{9,5},... | collective-permute-start | bytes 786440 | tf_op jit(solution)/shard_map/ppermute | solution.py:171
  138.1 13.0 %collective-permute-start.57 = (bf16[128,1024]{1,0:T(8,128)(2,1)S(1)}, bf16[128,1024]{1,0:T(8,128)(2,1)S(1)}, u32[]{:S(2)}, u32[]{:S(2)}) collective-permute-start(bf16[128,1024]{1,0:T(8,128)(2,1)S(1)} %get-tuple-element.123), channel_id=1, source_target_pairs={{0,4},{4,8},{8,12},{12,14},{14,10},{10,6},{6,2},{2,0},{1,5},{5,9},... | collective-permute-start | bytes 786440 | tf_op jit(solution)/shard_map/ppermute | solution.py:168
  142.8 23.2 %collective-permute-start.81 = (bf16[384,1024]{1,0:T(8,128)(2,1)S(1)}, bf16[384,1024]{1,0:T(8,128)(2,1)S(1)}, u32[]{:S(2)}, u32[]{:S(2)}) collective-permute-start(bf16[384,1024]{1,0:T(8,128)(2,1)S(1)} %shard_map.122), channel_id=1, source_target_pairs={{0,16},{16,0},{1,17},{17,1},{2,18},{18,2},{3,19},{19,3},{4,20},{20... | collective-permute-start | bytes 2359304 | tf_op jit(solution)/shard_map/ppermute | solution.py:306
  150.5 9.2 %collective-permute-start.63 = (bf16[256,384]{1,0:T(8,128)(2,1)S(1)}, bf16[256,384]{1,0:T(8,128)(2,1)S(1)}, u32[]{:S(2)}, u32[]{:S(2)}) collective-permute-start(bf16[256,384]{1,0:T(8,128)(2,1)S(1)} %copy-done.36), channel_id=1, source_target_pairs={{0,1},{1,0},{2,3},{3,2},{4,5},{5,4},{6,7},{7,6},{8,9},{9,8},{10,11... | collective-permute-start | bytes 589832 | tf_op jit(solution)/shard_map/ppermute | solution.py:22
  159.3 14.6 %collective-permute-start.66 = (bf16[128,384]{1,0:T(8,128)(2,1)S(1)}, bf16[128,384]{1,0:T(8,128)(2,1)S(1)}, u32[]{:S(2)}, u32[]{:S(2)}) collective-permute-start(bf16[128,384]{1,0:T(8,128)(2,1)S(1)} %get-tuple-element.77.refs_0_), channel_id=1, source_target_pairs={{0,1},{1,0},{2,3},{3,2},{4,5},{5,4},{6,7},{7,6},{8,9},{9,8},{10,11... | collective-permute-start | bytes 294920 | tf_op jit(solution)/shard_map/ppermute | solution.py:22
  159.6 12.0 %collective-permute-start.1 = (bf16[128,384]{1,0:T(8,128)(2,1)S(1)}, bf16[128,384]{1,0:T(8,128)(2,1)S(1)}, u32[]{:S(2)}, u32[]{:S(2)}) collective-permute-start(bf16[128,384]{1,0:T(8,128)(2,1)S(1)} %copy-done.42), channel_id=1, source_target_pairs={{0,1},{1,0},{2,3},{3,2},{4,5},{5,4},{6,7},{7,6},{8,9},{9,8},{10,11... | collective-permute-start | bytes 294920 | tf_op jit(solution)/shard_map/ppermute | solution.py:22
  161.7 9.9 %collective-permute-start.62 = (bf16[128,1024]{1,0:T(8,128)(2,1)S(1)}, bf16[128,1024]{1,0:T(8,128)(2,1)S(1)}, u32[]{:S(2)}, u32[]{:S(2)}) collective-permute-start(bf16[128,1024]{1,0:T(8,128)(2,1)S(1)} %get-tuple-element.131), channel_id=1, source_target_pairs={{0,4},{4,8},{8,12},{12,14},{14,10},{10,6},{6,2},{2,0},{1,5},{5,9},... | collective-permute-start | bytes 786440 | tf_op jit(solution)/shard_map/ppermute | solution.py:168
  (104 other events, 462.6 us)

commit v3 on v0

v3 whole, which is shorter than its diff:
```python
import functools

import jax
import jax.numpy as jnp
from jax import lax
from jax.experimental import pallas as pl
from jax.experimental.pallas import tpu as pltpu
from jax.sharding import PartitionSpec as P

BF16 = jnp.bfloat16
F32 = jnp.float32
VMEM_LIMIT = 16 * 1024 * 1024
LANES = 128
EXTRA = 16


def ring_order(count):
    if count % 2:
        return list(range(count))
    return list(range(0, count, 2)) + list(range(count - 1, 0, -2))


def swap_cores(value, name):
    with jax.named_scope("swap_" + name):
        return lax.ppermute(value, "tensor", [(0, 1), (1, 0)])


def tied(values, others):
    return lax.optimization_barrier((tuple(values), tuple(others)))[0]


def dot_units(rows, weights):
    return lax.dot_general(rows, weights, (((1,), (1,)), ((), ())), preferred_element_type=F32)


def dot_width(rows, weights):
    return lax.dot_general(rows, weights, (((1,), (0,)), ((), ())), preferred_element_type=F32)


def dot_rows(left, right):
    return lax.dot_general(left, right, (((0,), (0,)), ((), ())), preferred_element_type=F32)


def call(kernel, out_shape, operands, scalars, work=4 * 10**9):
    return pl.pallas_call(
        kernel,
        out_shape=out_shape,
        in_specs=[pl.BlockSpec(memory_space=pltpu.SMEM)]
        + [pl.BlockSpec(memory_space=pltpu.VMEM)] * len(operands),
        out_specs=[pl.BlockSpec(memory_space=pltpu.VMEM)] * len(out_shape),
        compiler_params=pltpu.CompilerParams(vmem_limit_bytes=VMEM_LIMIT),
        cost_estimate=pl.CostEstimate(flops=work, bytes_accessed=0, transcendentals=0),
    )(scalars, *operands)


def picked(core, first, second):
    return jnp.where(core == 0, first, second)


def diagonal(count):
    across = lax.broadcasted_iota(jnp.int32, (count, count), 0)
    along = lax.broadcasted_iota(jnp.int32, (count, count), 1)
    return across == along


def column_of(row):
    return jnp.sum(jnp.where(diagonal(row.shape[1]), row, 0.0), axis=1, keepdims=True)


def row_of(column):
    return jnp.sum(jnp.where(diagonal(column.shape[0]), column, 0.0), axis=0, keepdims=True)


def pieces_of(value):
    high = value.astype(BF16).astype(F32)
    middle = (value - high).astype(BF16).astype(F32)
    return high, middle, value - high - middle


def prepare_kernel(scalars, local_ref, arrived_ref, mine_ref, other_ref):
    core = scalars[0]
    units, width = local_ref.shape[0], local_ref.shape[1] // 2
    for ref, where in ((local_ref, core), (arrived_ref, 1 - core)):
        at = pl.ds(pl.multiple_of(where * units, units), units)
        mine_ref[at, :] = ref[:, pl.ds(pl.multiple_of(core * width, width), width)]
        other_ref[at, :] = ref[:, pl.ds(pl.multiple_of((1 - core) * width, width), width)]


def stacked(values):
    return jnp.concatenate(values, axis=0) if len(values) > 1 else values[0]


def units_of(core, rows_refs, w_ref, w_other_ref):
    mine = stacked([picked(core, f[...], s[...]) for f, s, _ in rows_refs])
    other = stacked([a[...] for _, _, a in rows_refs])
    return dot_units(mine, w_ref[...]) + dot_units(other, w_other_ref[...])


def forward_kernel(slots, with_next, scalars, *refs):
    if with_next:
        refs = give_next(scalars[0], refs)
    rows_refs = [refs[3 * i : 3 * i + 3] for i in range(len(slots))]
    gates_ref, w_ref, w_other_ref, hidden_ref, gated_ref, slope_ref = refs[3 * len(slots) :]
    core = scalars[0]
    columns = []
    for slot, piece in zip(slots, rows_refs):
        count = piece[2].shape[0]
        gate = column_of(gates_ref[pl.ds(scalars[2 + slot], 1), :])
        if count < gate.shape[0]:
            gate = picked(core, gate[:count], gate[count:])
        columns.append(gate)
    gate = stacked(columns)
    pre = units_of(core, rows_refs, w_ref, w_other_ref)
    logistic = 1.0 / (1.0 + jnp.exp(-pre))
    hidden = (pre * logistic).astype(BF16)
    hidden_ref[...] = hidden
    gated_ref[...] = (gate * hidden.astype(F32)).astype(BF16)
    slope_ref[...] = gate * (logistic * (1.0 + pre * (1.0 - logistic)))


def give_next(core, refs):
    refs[-1][...] = picked(core, refs[1][...], refs[0][...])
    return refs[2:-1]


def backward_kernel(pieces, with_next, scalars, *refs):
    if with_next:
        refs = give_next(scalars[0], refs)
    rows_refs = [refs[3 * i : 3 * i + 3] for i in range(pieces)]
    w_ref, w_other_ref, hidden_ref, gated_ref, slope_ref, out_ref = refs[3 * pieces :]
    count, units = hidden_ref.shape
    wide = units_of(scalars[0], rows_refs, w_ref, w_other_ref)
    out_ref[:, :units] = gated_ref[...]
    out_ref[:, units : 2 * units] = (slope_ref[...] * wide).astype(BF16)
    sums = jnp.sum(hidden_ref[...].astype(F32) * wide, axis=1, keepdims=True)
    lane = lax.broadcasted_iota(jnp.int32, (count, LANES), 1)
    kept = jnp.zeros((count, LANES), F32)
    for i, piece in enumerate(pieces_of(sums)):
        kept = jnp.where(lane == i, piece, kept)
    out_ref[:, 2 * units :] = kept.astype(BF16)


def dots_rows(expert, dots, start, rows, width, experts):
    count = dots.shape[0]
    row = row_of(dots)
    if count < rows:
        blank = jnp.zeros((1, count), F32)
        row = jnp.concatenate([row, blank] if start == 0 else [blank, row], axis=1)
    per_row = width // rows
    deep = -(-experts // per_row)
    line = lax.broadcasted_iota(jnp.int32, (EXTRA, width), 0)
    lane = lax.broadcasted_iota(jnp.int32, (EXTRA, width), 1)
    chosen = lane // rows == lax.rem(expert, per_row)
    out = jnp.zeros((EXTRA, width), F32)
    for i, piece in enumerate(pieces_of(row)):
        spread = jnp.concatenate([piece] * per_row, axis=1)
        out = jnp.where(chosen & (line == i * deep + expert // per_row), spread, out)
    return out


def return_kernel(kind, at, first_row, count, experts, rows, scalars, mine_ref, arrived_ref, w_ref, *refs):
    core, expert = scalars[0], scalars[1]
    units, width = w_ref.shape
    lines = slice(first_row, first_row + count)
    mine, arrived = mine_ref[lines, at : at + units], arrived_ref[lines, at : at + units]
    both = jnp.concatenate([picked(core, mine, arrived), picked(core, arrived, mine)], axis=0)
    part = dot_width(both, w_ref[...])
    with_dots = at > 0
    extra = [None, None]
    if with_dots:
        mine = jnp.sum(mine_ref[lines, 2 * units :].astype(F32), axis=1, keepdims=True)
        arrived = jnp.sum(arrived_ref[lines, 2 * units :].astype(F32), axis=1, keepdims=True)
        dots = [picked(core, mine, arrived), picked(core, arrived, mine)]
        starts = (0, count if count < rows else 0)
        extra = [
            dots_rows(expert, d, start, rows, width, experts) for d, start in zip(dots, starts)
        ]
    if kind == "far":
        for i, out_ref in enumerate(refs):
            out_ref[:count, :] = part[i * count : (i + 1) * count].astype(BF16)
            if with_dots:
                out_ref[count:, :] = extra[i].astype(BF16)
        return
    from_ahead, from_behind = refs[:2]
    if kind == "own":
        total = part + from_ahead[:rows, :].astype(F32) + from_behind[:rows, :].astype(F32)
        if not with_dots:
            refs[2][...] = total.astype(BF16)
            return
        routes_ref, out_ref, gates_ref = refs[2:]
        out_ref[...] = total.astype(BF16)
        table = extra[0] + extra[1]
        table = table + from_ahead[rows:, :].astype(F32) + from_behind[rows:, :].astype(F32)
        per_row = width // rows
        deep = -(-experts // per_row)
        routes = routes_ref[...]
        grads = jnp.zeros(routes.shape, F32)
        for e in range(experts):
            lanes = slice((e % per_row) * rows, (e % per_row + 1) * rows)
            line = e // per_row
            row = sum(table[i * deep + line : i * deep + line + 1, lanes] for i in range(3))
            grads = jnp.where(routes == e, column_of(row), grads)
        gates_ref[...] = grads
        return
    behind_ref, ahead_ref = refs[2:]
    behind, ahead = part[:count], part[count:]
    if kind == "join":
        half = count // 2
        behind_ref[:half, :] = (behind[:half] + from_ahead[:half, :].astype(F32)).astype(BF16)
        behind_ref[half:count, :] = behind[half:].astype(BF16)
        ahead_ref[:half, :] = ahead[:half].astype(BF16)
        ahead_ref[half:count, :] = (ahead[half:] + from_behind[:half, :].astype(F32)).astype(BF16)
    else:
        half = count
        behind_ref[:count, :] = (behind + from_ahead[:count, :].astype(F32)).astype(BF16)
        ahead_ref[:count, :] = (ahead + from_behind[:count, :].astype(F32)).astype(BF16)
    if with_dots:
        behind_ref[count:, :] = (extra[0] + from_ahead[half:, :].astype(F32)).astype(BF16)
        ahead_ref[count:, :] = (extra[1] + from_behind[half:, :].astype(F32)).astype(BF16)


def weight_kernel(pieces, at, scalars, *refs):
    core = scalars[0]
    lefts, rights = [], []
    mine_ref, other_ref = refs[-2:]
    units = mine_ref.shape[0]
    taken = 0
    for count in pieces:
        mine, arrived = refs[taken : taken + 2]
        firsts = refs[taken + 2 : taken + 2 + count]
        seconds = refs[taken + 2 + count : taken + 2 + 2 * count]
        taken += 2 + 2 * count
        own, came = mine[:, at : at + 2 * units], arrived[:, at : at + 2 * units]
        lefts += [picked(core, own, came), picked(core, came, own)]
        rights += [*firsts, *seconds]
    part = dot_rows(stacked(lefts), stacked([v[...] for v in rights]))
    mine_ref[...] = picked(core, part[:units], part[units:]).astype(BF16)
    other_ref[...] = picked(core, part[units:], part[:units]).astype(BF16)


def add_kernel(scalars, *refs):
    first, second, came, first_out, second_out = refs
    count = first.shape[0]
    first_out[...] = first[...].astype(F32) + came[:count, :].astype(F32)
    second_out[...] = second[...].astype(F32) + came[count:, :].astype(F32)


def send_kernel(scalars, first_mine, first_came, second_mine, second_came, sent, first, second):
    count = first.shape[0]

    @pl.when(scalars[0] == 0)
    def _():
        sent[:count, :] = first_came[...]
        sent[count:, :] = second_came[...]
        first[...] = first_mine[...]
        second[...] = second_mine[...]

    @pl.when(scalars[0] != 0)
    def _():
        sent[:count, :] = first_mine[...]
        sent[count:, :] = second_mine[...]
        first[...] = first_came[...]
        second[...] = second_came[...]


def per_device(tokens, routes, gates, w_in, w_out, cotangent):
    size = lax.axis_size("expert")
    n_dp = lax.axis_size("dp")
    rows, width = tokens.shape
    half = rows // 2
    experts = size * w_in.shape[0]
    core = lax.axis_index("tensor")
    place = lax.axis_index("expert")
    group = lax.axis_index("dp")
    order = ring_order(size)
    onward_pairs = [(order[i], order[(i + 1) % size]) for i in range(size)]
    back_pairs = [(b, a) for a, b in onward_pairs]
    steps = size // 2
    w_in, w_out = w_in[0], w_out[0]
    local_units = w_in.shape[0]
    units = 2 * local_units

    def both_ways(forth_value, back_value, name):
        with jax.named_scope("onward_" + name):
            forth = lax.ppermute(forth_value, "expert", onward_pairs)
        with jax.named_scope("back_" + name):
            return forth, lax.ppermute(back_value, "expert", back_pairs)

    table = jnp.sum(
        jnp.where(
            routes.T[None, :, :] == jnp.arange(experts, dtype=jnp.int32)[:, None, None],
            gates.T[None, :, :],
            0.0,
        ),
        axis=1,
    )
    gate_rows = lax.all_to_all(table, "expert", split_axis=0, concat_axis=0, tiled=True)

    position = jnp.where(place % 2 == 0, place // 2, size - 1 - place // 2)
    shifts = jnp.array([0, *range(1, steps), steps], dtype=jnp.int32)
    at_ring = (position + picked(core, -shifts, shifts) + size) % size
    sources = jnp.where(at_ring < steps, 2 * at_ring, 2 * (size - 1 - at_ring) + 1)
    scalars = jnp.concatenate([jnp.stack([core, place]), sources]).astype(jnp.int32)

    def next_shape(following):
        return [jax.ShapeDtypeStruct(v.shape, BF16) for v in following[:1]]

    def forward(slots, pieces, following=()):
        count = sum(p[2].shape[0] for p in pieces)
        shape = (count, units)
        return call(
            functools.partial(forward_kernel, slots, len(following) > 0),
            [
                jax.ShapeDtypeStruct(shape, BF16),
                jax.ShapeDtypeStruct(shape, BF16),
                jax.ShapeDtypeStruct(shape, F32),
                *next_shape(following),
            ],
            [*following, *(v for p in pieces for v in p), gate_rows, *in_all],
            scalars,
        )

    def backward(pieces, hidden, gated, slope, following=()):
        count = hidden.shape[0]
        return call(
            functools.partial(backward_kernel, len(pieces), len(following) > 0),
            [jax.ShapeDtypeStruct((count, 2 * units + LANES), BF16), *next_shape(following)],
            [*following, *(v for p in pieces for v in p), *out_all, hidden, gated, slope],
            scalars,
        )

    def returned(kind, at, mine, arrived, weights, sums, more=()):
        count = rows if kind in ("join", "add") else half
        first_row = half if kind == "far" and mine.shape[0] > half else 0
        extra = EXTRA if at else 0
        if kind == "own":
            shapes = [jax.ShapeDtypeStruct((rows, width), BF16)]
            if at:
                shapes.append(jax.ShapeDtypeStruct(routes.shape, F32))
        else:
            shapes = [jax.ShapeDtypeStruct((count + extra, width), BF16)] * 2
        return call(
            functools.partial(return_kernel, kind, at, first_row, count, experts, rows),
            shapes,
            [mine, arrived, weights, *sums, *more],
            scalars,
        )

    ring = [both_ways(tokens, tokens, "tok1"), both_ways(cotangent, cotangent, "cot1")]

    def prepared(weights):
        return call(
            prepare_kernel,
            [jax.ShapeDtypeStruct((units, width), BF16)] * 2,
            [weights, swap_cores(weights, "weights")],
            scalars,
        )

    in_all = prepared(w_in)
    out_all = prepared(tied((w_out,), ring[0])[0])

    own_sent = jnp.concatenate(
        [
            lax.dynamic_slice_in_dim(v, (1 - core) * half, half, axis=0)
            for v in (tokens, cotangent)
        ],
        axis=0,
    )

    arrivals, outputs, lefts, lefts_arrived = [], [], [], []
    own_arrived = None
    for turn in range(2 * steps):
        now = ring[turn]
        step = turn // 2 + 1
        name = ("tok", "cot")[turn % 2]
        picked_rows = None
        if 1 <= turn < 2 * steps - 1:
            done = turn - 1
            at_end = turn == 2 * steps - 3
            first, second, other = arrivals[done]
            if done % 2 == 0 and len(lefts) > len(lefts_arrived) + 1:
                index = len(lefts_arrived)
                sent = tied((lefts[index],), outputs[-1])[0]
                lefts_arrived.append(swap_cores(sent, "left" + str(index + 1)))
            elif done % 2 == 1 and lefts_arrived:
                other = tied((other,), lefts_arrived[-1:])[0]
            if at_end:
                other = tied((other,), now)[0]
            pieces = [(first, second, other)]
            following = () if at_end else now
            if done % 2 == 0:
                result = forward((done // 2 + 1,), pieces, following)
            else:
                result = backward(pieces, *outputs[done - 1], following)
                lefts.append(result[0])
            if not at_end:
                *result, picked_rows = result
                now = tied(now, (picked_rows,))
            outputs.append(result)
        if picked_rows is None:
            picked_rows = picked(core, now[1], now[0])
        if step < steps - 1:
            ring.append(both_ways(now[0], now[1], name + str(step + 1)))
        elif step == steps - 1:
            ring.append(both_ways(ring[turn][0][:half], ring[turn][1][half:], name + str(step + 1)))
        if turn == 1:
            both = swap_cores(jnp.concatenate([picked_rows, own_sent], axis=0), name + str(step))
            other, own_arrived = both[:rows], both[rows:]
        else:
            other = swap_cores(picked_rows, name + str(step))
        arrivals.append((*now, other))
    tok_pieces = [(tokens[:half], tokens[half:], own_arrived[:half]), arrivals[2 * steps - 2]]
    cot_pieces = [(cotangent[:half], cotangent[half:], own_arrived[half:]), arrivals[2 * steps - 1]]
    tok_pieces[1] = tied(tok_pieces[1], (*lefts, *lefts_arrived))
    hidden, gated, slope = forward((0, steps), tok_pieces)
    gated_arrived = swap_cores(gated, "gated")
    ends = backward(cot_pieces, hidden, gated, slope)[0]
    ends_arrived = swap_cores(ends, "ends")
    for index in range(len(lefts_arrived), steps - 1):
        sent = tied((lefts[index],), (ends_arrived,))[0]
        lefts_arrived.append(swap_cores(sent, "left" + str(index + 1)))

    sent = returned("far", 0, gated, gated_arrived, out_all[0], ())
    mixed_in = both_ways(sent[1], sent[0], "mixed")[::-1]
    sent = returned("far", units, ends, ends_arrived, in_all[0], ())
    back_in = both_ways(sent[1], sent[0], "grad")[::-1]

    def weight_part(at, which, after):
        operands = []
        for s in range(steps - 1):
            operands += [lefts[s], lefts_arrived[s], *arrivals[2 * s + which][:2]]
        pieces = (tok_pieces, cot_pieces)[which]
        operands += [ends, tied((ends_arrived,), after)[0]]
        operands += [p[0] for p in pieces] + [p[1] for p in pieces]
        return call(
            functools.partial(weight_kernel, [1] * (steps - 1) + [2], at),
            [jax.ShapeDtypeStruct((local_units, width), BF16)] * 2,
            operands,
            scalars,
        )

    out_mine, out_other = weight_part(0, 1, sent)
    out_other = swap_cores(out_other, "grad_out")
    in_mine, in_other = weight_part(units, 0, (out_mine,))
    in_other = swap_cores(in_other, "grad_in")
    if n_dp == 2:
        away = jnp.reshape(jnp.where(group == core, 0, 1), (1,)).astype(jnp.int32)
        parts_sent, *kept = call(
            send_kernel,
            [jax.ShapeDtypeStruct((2 * local_units, width), BF16)]
            + [jax.ShapeDtypeStruct((local_units, width), BF16)] * 2,
            [out_mine, out_other, in_mine, in_other],
            away,
        )
        parts_came = lax.ppermute(parts_sent, "dp", [(0, 1), (1, 0)])
        after_parts = (parts_sent,)
    else:
        kept, parts_came = [], []
        after_parts = ()
        for mine, arrived in ((out_mine, out_other), (in_mine, in_other)):
            part = jnp.concatenate(
                [picked(core, mine, arrived), picked(core, arrived, mine)], axis=1
            )
            across = part.shape[1] // n_dp
            slices = [
                lax.dynamic_slice_in_dim(part, ((group + shift) % n_dp) * across, across, axis=1)
                for shift in range(n_dp)
            ]
            total = 0.0
            for shift in range(1, n_dp):
                pairs = [(i, (i + shift) % n_dp) for i in range(n_dp)]
                total = total + lax.ppermute(slices[shift], "dp", pairs).astype(F32)
            kept.append(slices[0])
            parts_came.append(total)
        parts_came = jnp.concatenate(parts_came, axis=0)

    first_ties = {steps - 1: ((out_mine,), (in_mine,)), steps - 2: (after_parts, ())}
    for step in range(steps - 1, 0, -1):
        kind = "join" if step == steps - 1 else "add"
        left, left_arrived = lefts[step - 1], lefts_arrived[step - 1]
        mixed_ties, back_ties = first_ties.get(step, ((), ()))
        mixed_in = tied(mixed_in, (*sent, *mixed_ties))
        sent = returned(kind, 0, left, left_arrived, out_all[0], mixed_in)
        mixed_in = both_ways(sent[1], sent[0], "mixed")[::-1]
        back_in = tied(back_in, (*sent, *back_ties))
        sent = returned(kind, units, left, left_arrived, in_all[0], back_in)
        back_in = both_ways(sent[1], sent[0], "grad")[::-1]
    mixed_in = tied(mixed_in, sent)

    mixed = returned("own", 0, ends, ends_arrived, out_all[0], mixed_in)[0]
    grad_tokens, grad_gates = returned(
        "own", units, ends, ends_arrived, in_all[0], back_in, (routes,)
    )

    grad_out, grad_in = call(
        add_kernel,
        [jax.ShapeDtypeStruct(v.shape, F32) for v in kept],
        [*kept, parts_came],
        scalars,
    )
    return (mixed, grad_tokens, grad_gates, grad_in[None], grad_out[None])


def solution(mesh):
    placed = (
        P(("dp", "expert"), "tensor"),
        P(("dp", "expert"), None),
        P(("dp", "expert"), None),
        P("expert", "tensor", None),
        P("expert", "tensor", None),
        P(("dp", "expert"), "tensor"),
    )
    return jax.shard_map(
        per_device,
        mesh=mesh,
        in_specs=placed,
        out_specs=(
            P(("dp", "expert"), "tensor"),
            P(("dp", "expert"), "tensor"),
            P(("dp", "expert"), None),
            P("expert", "tensor", "dp"),
            P("expert", "tensor", "dp"),
        ),
        check_vma=False,
    )
```

time: 327 us -> 142 us (0.43)
  other arithmetic: 82.6 us -> 2.2 us
  local copies, waits for them, and re-layouts: 62.2 us -> 15.1 us
  Pallas kernels: 0 us -> 44.1 us
  blocking collectives: 44.1 us -> 0 us
  waiting for transfers between devices: 76.1 us -> 34.1 us
  matrix products: 19.8 us -> 0 us
  starting transfers between devices: 26.6 us -> 45.2 us
  between operations: 14 us -> 1.18 us
    all_to_all x5 -> x1, waiting for transfers between devices: 70.3 us -> 0.01 us  [per_device(): lax.all_to_all(table, 'expert', split_axis=0, concat_axis=0, tiled=True)]
    unnamed x2 -> x0, other arithmetic: 68.8 us -> none
    pallas_call x0 -> x24, Pallas kernels: none -> 44.1 us  [call(): pl.pallas_call(kernel, out_shape=out_shape, in_specs=[pl.BlockSpec(memory...]
    ppermute x0 -> x50, starting transfers between devices: none -> 39 us  [the longest x16 26.7 us: both_ways(): forth = lax.ppermute(forth_value, 'expert', onward_pairs)]
    all_to_all x1 -> x0, blocking collectives: 35.2 us -> none  [to_owner(): lax.all_to_all(slot_rows, 'expert', split_axis=0, concat_axis=0, tiled=True)]
    ppermute x0 -> x50, waiting for transfers between devices: none -> 34 us  [the longest x16 20 us: both_ways(): return (forth, lax.ppermute(back_value, 'expert', back_pairs))]
    unnamed x36 -> x74, local copies, waits for them, and re-layouts: 35.5 us -> 12.3 us
    all_to_all x5 -> x1, starting transfers between devices: 26.3 us -> 6.26 us  [per_device(): lax.all_to_all(table, 'expert', split_axis=0, concat_axis=0, tiled=True)]
  transfers between devices with their start and end apart: 9 -> 51, of which waited for: 4 -> 22; matrix products, arithmetic and copies ran while one was open for 44% -> 4% of each run, Pallas kernels for 0% -> 28%
where the time goes in v3:
time: 142 us
  starting transfers between devices  45.2 us (32%)
  Pallas kernels  44.1 us (31%)
  waiting for transfers between devices  34.1 us (24%)
  local copies, waits for them, and re-layouts  15.1 us (11%)
  other arithmetic  2.2 us (2%)
    pallas_call x24, Pallas kernels, call(): pl.pallas_call(kernel, out_shape=out_shape, in_specs=[pl.BlockSpec(memory...  44.1 us
    ppermute x16, starting transfers between devices, both_ways(): forth = lax.ppermute(forth_value, 'expert', onward_pairs)  26.7 us
    ppermute x16, waiting for transfers between devices, both_ways(): return (forth, lax.ppermute(back_value, 'expert', back_pairs))  20 us
    unnamed x74, local copies, waits for them, and re-layouts  12.3 us
    ppermute x16, waiting for transfers between devices, both_ways(): forth = lax.ppermute(forth_value, 'expert', onward_pairs)  10.2 us
    ppermute x16, starting transfers between devices, both_ways(): return (forth, lax.ppermute(back_value, 'expert', back_pairs))  7.08 us
    all_to_all x1, starting transfers between devices, per_device(): lax.all_to_all(table, 'expert', split_axis=0, concat_axis=0, tiled=True)  6.26 us
    ppermute x17, starting transfers between devices, swap_cores(): return lax.ppermute(value, 'tensor', [(0, 1), (1, 0)])  3.67 us
  transfers between devices with their start and end apart: 51, of which 22 were waited for; matrix products, arithmetic and copies ran while one was open for 4% of the time, Pallas kernels for 28%

profile of v3, /device:TPU:0, one launch (start us, length us, event | category | flops | bytes accessed | tf_op | source)
XLA Modules:
  0.0 141.9 jit_solution(3807611952709610617)
XLA Ops:
  1.2 2.6 %collective-permute-start = (bf16[128,1024]{1,0:T(8,128)(2,1)}, bf16[128,1024]{1,0:T(8,128)(2,1)S(1)}, u32[]{:S(2)}, u32[]{:S(2)}) collective-permute-start(bf16[128,1024]{1,0:T(8,128)(2,1)} %param.12), channel_id=1, source_target_pairs={{0,4},{4,8},{8,12},{12,14},{14,10},{10,6},{6,2},{2,0},{1,5},{5,9},... | collective-permute-start | bytes 786440 | tf_op jit(solution)/shard_map/onward_cot1/ppermute | solution.py:285
  3.8 2.0 %collective-permute-start.2 = (bf16[128,1024]{1,0:T(8,128)(2,1)}, bf16[128,1024]{1,0:T(8,128)(2,1)S(1)}, u32[]{:S(2)}, u32[]{:S(2)}) collective-permute-start(bf16[128,1024]{1,0:T(8,128)(2,1)} %param.7), channel_id=1, source_target_pairs={{0,4},{4,8},{8,12},{12,14},{14,10},{10,6},{6,2},{2,0},{1,5},{5,9},... | collective-permute-start | bytes 786440 | tf_op jit(solution)/shard_map/onward_tok1/ppermute | solution.py:285
  7.2 6.3 %all-to-all-start = ((f32[8,1,128]{2,1,0:T(1,128)}), f32[8,1,128]{2,1,0:T(1,128)S(1)}, u32[]{:S(2)}, u32[]{:S(2)}) async-start(f32[8,1,128]{2,1,0:T(1,128)} %bitcast.5), calls=%async_computation | async-start | bytes 8192 | tf_op jit(solution)/shard_map/all_to_all | solution.py:297
  14.5 2.0 %collective-permute-done.2.refs_2_ = bf16[128,1024]{1,0:T(8,128)(2,1)S(1)} collective-permute-done((bf16[128,1024]{1,0:T(8,128)(2,1)}, bf16[128,1024]{1,0:T(8,128)(2,1)S(1)}, u32[]{:S(2)}, u32[]{:S(2)}) %collective-permute-start.2) | collective-permute-done | bytes 262176 | tf_op jit(solution)/shard_map/onward_tok1/ppermute | solution.py:285
  18.1 1.7 %fusion.3 = (bf16[64,1024]{1,0:T(8,128)(2,1)S(1)}, bf16[64,1024]{1,0:T(8,128)(2,1)}, bf16[64,1024]{1,0:T(8,128)(2,1)S(1)}) fusion(bf16[128,1024]{1,0:T(8,128)(2,1)} %param.7, s32[]{:T(128)S(6)} %select_n.75), kind=kLoop, calls=%fused_computation.17 | loop fusion | bytes 786436 | tf_op jit(solution)/shard_map/slice | solution.py:412
  27.8 1.8 %shard_map.111 = (bf16[128,768]{1,0:T(8,128)(2,1)S(1)}, bf16[128,768]{1,0:T(8,128)(2,1)S(1)}, f32[128,768]{1,0:T(8,128)S(1)}, bf16[128,1024]{1,0:T(8,128)(2,1)S(1)}) custom-call(s32[7]{0:T(128)S(1)} %pad_add_fusion.scalars, bf16[128,1024]{1,0:T(8,128)(2,1)S(1)} %collective-permute-done.refs_0_.refs_2_, ...), custom_call_target="tpu_custom_call" | custom-call | flops 4000000000 | tf_op jit(solution)/shard_map/pallas_call | solution.py:45
  29.8 1.6 %collective-permute-start.9 = (bf16[128,1024]{1,0:T(8,128)(2,1)S(1)}, bf16[128,1024]{1,0:T(8,128)(2,1)S(1)}, u32[]{:S(2)}, u32[]{:S(2)}) collective-permute-start(bf16[128,1024]{1,0:T(8,128)(2,1)S(1)} %collective-permute-done.2.refs_2_), channel_id=1, source_target_pairs={{0,4},{4,8},{8,12},{12,14},{14,10},{10,6},{6,2},{2,0},{1,5},{5,9},... | collective-permute-start | bytes 786440 | tf_op jit(solution)/shard_map/onward_tok2/ppermute | solution.py:285
  35.6 3.4 %collective-permute-done.9.refs_0_.refs_2_.refs_6_ = bf16[128,1024]{1,0:T(8,128)(2,1)S(1)} collective-permute-done((bf16[128,1024]{1,0:T(8,128)(2,1)S(1)}, bf16[128,1024]{1,0:T(8,128)(2,1)S(1)}, u32[]{:S(2)}, u32[]{:S(2)}) %collective-permute-start.9) | collective-permute-done | bytes 262176 | tf_op jit(solution)/shard_map/onward_tok2/ppermute | solution.py:285
  40.6 1.8 %shard_map.113 = (bf16[128,1664]{1,0:T(8,128)(2,1)S(1)}, bf16[128,1024]{1,0:T(8,128)(2,1)S(1)}) custom-call(s32[7]{0:T(128)S(1)} %pad_add_fusion.scalars, bf16[128,1024]{1,0:T(8,128)(2,1)S(1)} %collective-permute-done.9.refs_0_.refs_2_.refs_6_, bf16[128,1024]{1,0:T(8,128)(2,1)S(1)} %collective-permute-done.10.refs_1_.refs_3_.refs_7_, ...), custom_call_target="tpu_custom_call" | custom-call | flops 4000000000 | tf_op jit(solution)/shard_map/pallas_call | solution.py:45
  42.5 1.6 %collective-permute-start.18 = (bf16[128,1024]{1,0:T(8,128)(2,1)S(1)}, bf16[128,1024]{1,0:T(8,128)(2,1)S(1)}, u32[]{:S(2)}, u32[]{:S(2)}) collective-permute-start(bf16[128,1024]{1,0:T(8,128)(2,1)S(1)} %collective-permute-done.9.refs_0_.refs_2_.refs_6_), channel_id=1, source_target_pairs={{0,4},{4,8},{8,12},{12,14},{14,10},{10,6},{6,2},{2,0},{1,5},{5,9},... | collective-permute-start | bytes 786440 | tf_op jit(solution)/shard_map/onward_tok3/ppermute | solution.py:285
  45.4 1.8 %shard_map.114 = (bf16[128,768]{1,0:T(8,128)(2,1)S(1)}, bf16[128,768]{1,0:T(8,128)(2,1)S(1)}, f32[128,768]{1,0:T(8,128)S(1)}, bf16[128,1024]{1,0:T(8,128)(2,1)S(1)}) custom-call(s32[7]{0:T(128)S(1)} %pad_add_fusion.scalars, bf16[128,1024]{1,0:T(8,128)(2,1)S(1)} %collective-permute-done.7.refs_0_.refs_2_.refs_6_, ...), custom_call_target="tpu_custom_call" | custom-call | flops 4000000000 | tf_op jit(solution)/shard_map/pallas_call | solution.py:45
  47.4 1.6 %collective-permute-start.13 = (bf16[128,1024]{1,0:T(8,128)(2,1)S(1)}, bf16[128,1024]{1,0:T(8,128)(2,1)S(1)}, u32[]{:S(2)}, u32[]{:S(2)}) collective-permute-start(bf16[128,1024]{1,0:T(8,128)(2,1)S(1)} %collective-permute-done.7.refs_0_.refs_2_.refs_6_), channel_id=1, source_target_pairs={{0,4},{4,8},{8,12},{12,14},{14,10},{10,6},{6,2},{2,0},{1,5},{5,9},... | collective-permute-start | bytes 786440 | tf_op jit(solution)/shard_map/onward_cot3/ppermute | solution.py:285
  49.4 2.2 %collective-permute-done.18.refs_0_.refs_10_ = bf16[128,1024]{1,0:T(8,128)(2,1)S(1)} collective-permute-done((bf16[128,1024]{1,0:T(8,128)(2,1)S(1)}, bf16[128,1024]{1,0:T(8,128)(2,1)S(1)}, u32[]{:S(2)}, u32[]{:S(2)}) %collective-permute-start.18) | collective-permute-done | bytes 262176 | tf_op jit(solution)/shard_map/onward_tok3/ppermute | solution.py:285
  53.2 1.8 %shard_map.115 = (bf16[128,1664]{1,0:T(8,128)(2,1)S(1)}, bf16[128,1024]{1,0:T(8,128)(2,1)S(1)}) custom-call(s32[7]{0:T(128)S(1)} %pad_add_fusion.scalars, bf16[128,1024]{1,0:T(8,128)(2,1)S(1)} %collective-permute-done.18.refs_0_.refs_10_, bf16[128,1024]{1,0:T(8,128)(2,1)S(1)} %collective-permute-done.20.refs_1_.refs_11_, ...), custom_call_target="tpu_custom_call" | custom-call | flops 4000000000 | tf_op jit(solution)/shard_map/pallas_call | solution.py:45
  59.5 1.8 %shard_map.116 = (bf16[128,768]{1,0:T(8,128)(2,1)S(1)}, bf16[128,768]{1,0:T(8,128)(2,1)S(1)}, f32[128,768]{1,0:T(8,128)S(1)}) custom-call(s32[7]{0:T(128)S(1)} %pad_add_fusion.scalars, bf16[128,1024]{1,0:T(8,128)(2,1)S(1)} %collective-permute-done.18.refs_0_.refs_10_, bf16[128,1024]{1,0:T(8,128)(2,1)S(1)} %collective-permute-done.20.refs_1_.refs_11_, ...), custom_call_target="tpu_custom_call" | custom-call | flops 4000000000 | tf_op jit(solution)/shard_map/pallas_call | solution.py:45
  62.4 1.8 %shard_map.117 = (bf16[128,1664]{1,0:T(8,128)(2,1)S(1)}, bf16[64,1024]{1,0:T(8,128)(2,1)S(1)}) custom-call(s32[7]{0:T(128)S(1)} %pad_add_fusion.scalars, bf16[64,1024]{1,0:T(8,128)(2,1)S(1)} %collective-permute-done.19.refs_0_.refs_3_.refs_15_, bf16[64,1024]{1,0:T(8,128)(2,1)S(1)} %collective-permute-done.21.refs_1_.refs_4_.refs_17_, ...), custom_call_target="tpu_custom_call" | custom-call | flops 4000000000 | tf_op jit(solution)/shard_map/pallas_call | solution.py:45
  64.3 2.5 %collective-permute-done.16.refs_4_.refs_17_ = bf16[64,1024]{1,0:T(8,128)(2,1)S(1)} collective-permute-done((bf16[64,1024]{1,0:T(8,128)(2,1)S(1)}, bf16[64,1024]{1,0:T(8,128)(2,1)S(1)}, u32[]{:S(2)}, u32[]{:S(2)}) %collective-permute-start.16) | collective-permute-done | bytes 131104 | tf_op jit(solution)/shard_map/back_cot4/ppermute | solution.py:287
  67.0 1.8 %shard_map.118 = (bf16[128,768]{1,0:T(8,128)(2,1)S(1)}, bf16[128,768]{1,0:T(8,128)(2,1)S(1)}, f32[128,768]{1,0:T(8,128)S(1)}) custom-call(s32[7]{0:T(128)S(1)} %pad_add_fusion.scalars, bf16[64,1024]{1,0:T(8,128)(2,1)S(1)} %get-tuple-element.196.refs_0_.refs_14_, bf16[64,1024]{1,0:T(8,128)(2,1)S(1)} %get-tuple-element.194.refs_1_.refs_16_, ...), custom_call_target="tpu_custom_call" | custom-call | flops 4000000000 | tf_op jit(solution)/shard_map/pallas_call | solution.py:45
  68.8 1.8 %shard_map.119.mine_ref.refs_12_ = bf16[128,1664]{1,0:T(8,128)(2,1)S(1)} custom-call(s32[7]{0:T(128)S(1)} %pad_add_fusion.scalars, bf16[64,1024]{1,0:T(8,128)(2,1)S(1)} %get-tuple-element.199.refs_0_.refs_14_, bf16[64,1024]{1,0:T(8,128)(2,1)S(1)} %get-tuple-element.198.refs_1_.refs_16_, bf16[64,1024]{1,0:T(8,128)(2,1)S(1)} %get-tuple-element.193.refs_2_, ...), custom_call_target="tpu_custom_call" | custom-call | flops 4000000000 | tf_op jit(solution)/shard_map/pallas_call | solution.py:45
  76.7 1.6 %shard_map.121 = (bf16[80,1024]{1,0:T(8,128)(2,1)}, bf16[80,1024]{1,0:T(8,128)(2,1)}) custom-call(s32[7]{0:T(128)S(1)} %pad_add_fusion.scalars, bf16[128,1664]{1,0:T(8,128)(2,1)S(1)} %shard_map.119.mine_ref.refs_12_, bf16[128,1664]{1,0:T(8,128)(2,1)S(1)} %collective-permute-done.27.arrived_ref.refs_13_, bf16[768,1024]{1,0:T(8,128)(2,1)S(1)} %copy-done.22), custom_call_target="tpu_custom_call" | custom-call | flops 4000000000 | tf_op jit(solution)/shard_map/pallas_call | solution.py:45
  78.3 3.3 %shard_map.122 = (bf16[384,1024]{1,0:T(8,128)(2,1)S(1)}, bf16[384,1024]{1,0:T(8,128)(2,1)}) custom-call(s32[7]{0:T(128)S(1)} %pad_add_fusion.scalars, bf16[128,1664]{1,0:T(8,128)(2,1)S(1)} %get-tuple-element.113.refs_0_.mine_ref, bf16[128,1664]{1,0:T(8,128)(2,1)S(1)} %collective-permute-done.24.refs_1_.arrived_ref, ...), custom_call_target="tpu_custom_call" | custom-call | flops 4000000000 | tf_op jit(solution)/shard_map/pallas_call | solution.py:45
  82.6 3.3 %shard_map.124 = (bf16[384,1024]{1,0:T(8,128)(2,1)S(1)}, bf16[384,1024]{1,0:T(8,128)(2,1)}) custom-call(s32[7]{0:T(128)S(1)} %pad_add_fusion.scalars, bf16[128,1664]{1,0:T(8,128)(2,1)S(1)} %get-tuple-element.113.refs_0_.mine_ref, bf16[128,1664]{1,0:T(8,128)(2,1)S(1)} %collective-permute-done.24.refs_1_.arrived_ref, ...), custom_call_target="tpu_custom_call" | custom-call | flops 4000000000 | tf_op jit(solution)/shard_map/pallas_call | solution.py:45
  99.9 2.6 %shard_map.126 = (bf16[768,1024]{1,0:T(8,128)(2,1)}, bf16[384,1024]{1,0:T(8,128)(2,1)S(1)}, bf16[384,1024]{1,0:T(8,128)(2,1)S(1)}) custom-call(s32[1]{0:T(128)} %bitcast.9.scalars, bf16[384,1024]{1,0:T(8,128)(2,1)S(1)} %copy-done.27, bf16[384,1024]{1,0:T(8,128)(2,1)S(1)} %collective-permute-done.37.first_came, bf16[384,1024]{1,0:T(8,128)(2,1)S(1)} %copy-done.29, ...), custom_call_target="tpu_custom_call" | custom-call | flops 4000000000 | tf_op jit(solution)/shard_map/pallas_call | solution.py:45
  107.6 2.5 %collective-permute-done.41.refs_0_ = bf16[144,1024]{1,0:T(8,128)(2,1)S(1)} collective-permute-done((bf16[144,1024]{1,0:T(8,128)(2,1)S(1)}, bf16[144,1024]{1,0:T(8,128)(2,1)S(1)}, u32[]{:S(2)}, u32[]{:S(2)}) %collective-permute-start.41) | collective-permute-done | bytes 294944 | tf_op jit(solution)/shard_map/back_grad/ppermute | solution.py:287
  113.9 1.9 %collective-permute-done.39.refs_0_ = bf16[128,1024]{1,0:T(8,128)(2,1)S(1)} collective-permute-done((bf16[128,1024]{1,0:T(8,128)(2,1)S(1)}, bf16[128,1024]{1,0:T(8,128)(2,1)S(1)}, u32[]{:S(2)}, u32[]{:S(2)}) %collective-permute-start.39) | collective-permute-done | bytes 262176 | tf_op jit(solution)/shard_map/back_mixed/ppermute | solution.py:287
  119.5 2.6 %collective-permute-done.45.refs_0_ = bf16[144,1024]{1,0:T(8,128)(2,1)S(1)} collective-permute-done((bf16[144,1024]{1,0:T(8,128)(2,1)S(1)}, bf16[144,1024]{1,0:T(8,128)(2,1)S(1)}, u32[]{:S(2)}, u32[]{:S(2)}) %collective-permute-start.45) | collective-permute-done | bytes 294944 | tf_op jit(solution)/shard_map/back_grad/ppermute | solution.py:287
  125.8 1.9 %collective-permute-done.43.refs_0_ = bf16[128,1024]{1,0:T(8,128)(2,1)S(1)} collective-permute-done((bf16[128,1024]{1,0:T(8,128)(2,1)S(1)}, bf16[128,1024]{1,0:T(8,128)(2,1)S(1)}, u32[]{:S(2)}, u32[]{:S(2)}) %collective-permute-start.43) | collective-permute-done | bytes 262176 | tf_op jit(solution)/shard_map/back_mixed/ppermute | solution.py:287
  128.2 1.6 %shard_map.131 = bf16[128,1024]{1,0:T(8,128)(2,1)} custom-call(s32[7]{0:T(128)S(1)} %pad_add_fusion.scalars, bf16[128,1664]{1,0:T(8,128)(2,1)S(1)} %copy-done.9, bf16[128,1664]{1,0:T(8,128)(2,1)S(1)} %copy-done.11, bf16[768,1024]{1,0:T(8,128)(2,1)S(1)} %copy-done.20, bf16[128,1024]{1,0:T(8,128)(2,1)S(1)} %collective-permute-done.43.refs_0_, ...), custom_call_target="tpu_custom_call" | custom-call | flops 4000000000 | tf_op jit(solution)/shard_map/pallas_call | solution.py:45
  129.9 2.6 %collective-permute-done.47.refs_0_ = bf16[144,1024]{1,0:T(8,128)(2,1)S(1)} collective-permute-done((bf16[144,1024]{1,0:T(8,128)(2,1)S(1)}, bf16[144,1024]{1,0:T(8,128)(2,1)S(1)}, u32[]{:S(2)}, u32[]{:S(2)}) %collective-permute-start.47) | collective-permute-done | bytes 294944 | tf_op jit(solution)/shard_map/back_grad/ppermute | solution.py:287
  132.7 1.7 %shard_map.132 = (bf16[128,1024]{1,0:T(8,128)(2,1)}, f32[128,4]{1,0:T(8,128)S(1)}) custom-call(s32[7]{0:T(128)S(1)} %pad_add_fusion.scalars, bf16[128,1664]{1,0:T(8,128)(2,1)S(1)} %copy-done.9, bf16[128,1664]{1,0:T(8,128)(2,1)S(1)} %copy-done.11, bf16[768,1024]{1,0:T(8,128)(2,1)S(1)} %copy-done.23, bf16[144,1024]{1,0:T(8,128)(2,1)S(1)} %collective-permute-done.47.refs_0_, ...), custom_call_target="tpu_custom_call" | custom-call | flops 4000000000 | tf_op jit(solution)/shard_map/pallas_call | solution.py:45
  135.0 2.5 %collective-permute-done.49.refs_2_ = bf16[768,1024]{1,0:T(8,128)(2,1)} collective-permute-done((bf16[768,1024]{1,0:T(8,128)(2,1)}, bf16[768,1024]{1,0:T(8,128)(2,1)}, u32[]{:S(2)}, u32[]{:S(2)}) %collective-permute-start.49) | collective-permute-done | bytes 1572896 | tf_op jit(solution)/shard_map/ppermute | solution.py:455
  138.6 3.3 %shard_map.133 = (f32[384,1024]{1,0:T(8,128)}, f32[384,1024]{1,0:T(8,128)}) custom-call(s32[7]{0:T(128)S(1)} %pad_add_fusion.scalars, bf16[384,1024]{1,0:T(8,128)(2,1)S(1)} %copy-done.31, bf16[384,1024]{1,0:T(8,128)(2,1)S(1)} %copy-done.33, bf16[768,1024]{1,0:T(8,128)(2,1)} %collective-permute-done.49.refs_2_), custom_call_target="tpu_custom_call" | custom-call | flops 4000000000 | tf_op jit(solution)/shard_map/pallas_call | solution.py:45
  (183 shorter events, 67.1 us)
Async XLA Ops:
  0.6 20.4 %collective-permute-start.5 = (bf16[384,2048]{1,0:T(8,128)(2,1)}, bf16[384,2048]{1,0:T(8,128)(2,1)}, u32[]{:S(2)}, u32[]{:S(2)}) collective-permute-start(bf16[384,2048]{1,0:T(8,128)(2,1)} %bitcast.17), channel_id=1, source_target_pairs={{0,1},{1,0},{2,3},{3,2},{4,5},{5,4},{6,7},{7,6},{8,9},{9,8},{10,11... | collective-permute-start | bytes 4718600 | tf_op jit(solution)/shard_map/swap_weights/ppermute | solution.py:25
  1.2 23.8 %collective-permute-start = (bf16[128,1024]{1,0:T(8,128)(2,1)}, bf16[128,1024]{1,0:T(8,128)(2,1)S(1)}, u32[]{:S(2)}, u32[]{:S(2)}) collective-permute-start(bf16[128,1024]{1,0:T(8,128)(2,1)} %param.12), channel_id=1, source_target_pairs={{0,4},{4,8},{8,12},{12,14},{14,10},{10,6},{6,2},{2,0},{1,5},{5,9},... | collective-permute-start | bytes 786440 | tf_op jit(solution)/shard_map/onward_cot1/ppermute | solution.py:285
  3.8 21.2 %collective-permute-start.1 = (bf16[128,1024]{1,0:T(8,128)(2,1)}, bf16[128,1024]{1,0:T(8,128)(2,1)S(1)}, u32[]{:S(2)}, u32[]{:S(2)}) collective-permute-start(bf16[128,1024]{1,0:T(8,128)(2,1)} %param.12), channel_id=1, source_target_pairs={{4,0},{8,4},{12,8},{14,12},{10,14},{6,10},{2,6},{0,2},{5,1},{9,5},... | collective-permute-start | bytes 786440 | tf_op jit(solution)/shard_map/back_cot1/ppermute | solution.py:287
  3.8 12.7 %collective-permute-start.2 = (bf16[128,1024]{1,0:T(8,128)(2,1)}, bf16[128,1024]{1,0:T(8,128)(2,1)S(1)}, u32[]{:S(2)}, u32[]{:S(2)}) collective-permute-start(bf16[128,1024]{1,0:T(8,128)(2,1)} %param.7), channel_id=1, source_target_pairs={{0,4},{4,8},{8,12},{12,14},{14,10},{10,6},{6,2},{2,0},{1,5},{5,9},... | collective-permute-start | bytes 786440 | tf_op jit(solution)/shard_map/onward_tok1/ppermute | solution.py:285
  5.8 12.2 %collective-permute-start.3 = (bf16[128,1024]{1,0:T(8,128)(2,1)}, bf16[128,1024]{1,0:T(8,128)(2,1)S(1)}, u32[]{:S(2)}, u32[]{:S(2)}) collective-permute-start(bf16[128,1024]{1,0:T(8,128)(2,1)} %param.7), channel_id=1, source_target_pairs={{4,0},{8,4},{12,8},{14,12},{10,14},{6,10},{2,6},{0,2},{5,1},{9,5},... | collective-permute-start | bytes 786440 | tf_op jit(solution)/shard_map/back_tok1/ppermute | solution.py:287
  7.2 17.8 %all-to-all-start = ((f32[8,1,128]{2,1,0:T(1,128)}), f32[8,1,128]{2,1,0:T(1,128)S(1)}, u32[]{:S(2)}, u32[]{:S(2)}) async-start(f32[8,1,128]{2,1,0:T(1,128)} %bitcast.5), calls=%async_computation | async-start | bytes 8192 | tf_op jit(solution)/shard_map/all_to_all | solution.py:297
  18.0 15.5 %collective-permute-start.11 = (bf16[384,2048]{1,0:T(8,128)(2,1)}, bf16[384,2048]{1,0:T(8,128)(2,1)}, u32[]{:S(2)}, u32[]{:S(2)}) collective-permute-start(bf16[384,2048]{1,0:T(8,128)(2,1)} %bitcast.19), channel_id=1, source_target_pairs={{0,1},{1,0},{2,3},{3,2},{4,5},{5,4},{6,7},{7,6},{8,9},{9,8},{10,11... | collective-permute-start | bytes 4718600 | tf_op jit(solution)/shard_map/swap_weights/ppermute | solution.py:25
  29.8 9.2 %collective-permute-start.9 = (bf16[128,1024]{1,0:T(8,128)(2,1)S(1)}, bf16[128,1024]{1,0:T(8,128)(2,1)S(1)}, u32[]{:S(2)}, u32[]{:S(2)}) collective-permute-start(bf16[128,1024]{1,0:T(8,128)(2,1)S(1)} %collective-permute-done.2.refs_2_), channel_id=1, source_target_pairs={{0,4},{4,8},{8,12},{12,14},{14,10},{10,6},{6,2},{2,0},{1,5},{5,9},... | collective-permute-start | bytes 786440 | tf_op jit(solution)/shard_map/onward_tok2/ppermute | solution.py:285
  31.4 9.1 %collective-permute-start.10 = (bf16[128,1024]{1,0:T(8,128)(2,1)S(1)}, bf16[128,1024]{1,0:T(8,128)(2,1)S(1)}, u32[]{:S(2)}, u32[]{:S(2)}) collective-permute-start(bf16[128,1024]{1,0:T(8,128)(2,1)S(1)} %collective-permute-done.3.refs_3_), channel_id=1, source_target_pairs={{4,0},{8,4},{12,8},{14,12},{10,14},{6,10},{2,6},{0,2},{5,1},{9,5},... | collective-permute-start | bytes 786440 | tf_op jit(solution)/shard_map/back_tok2/ppermute | solution.py:287
  31.9 12.7 %collective-permute-start.7 = (bf16[128,1024]{1,0:T(8,128)(2,1)S(1)}, bf16[128,1024]{1,0:T(8,128)(2,1)S(1)}, u32[]{:S(2)}, u32[]{:S(2)}) collective-permute-start(bf16[128,1024]{1,0:T(8,128)(2,1)S(1)} %collective-permute-done.refs_0_.refs_2_), channel_id=1, source_target_pairs={{0,4},{4,8},{8,12},{12,14},{14,10},{10,6},{6,2},{2,0},{1,5},{5,9},... | collective-permute-start | bytes 786440 | tf_op jit(solution)/shard_map/onward_cot2/ppermute | solution.py:285
  33.5 12.0 %collective-permute-start.8 = (bf16[128,1024]{1,0:T(8,128)(2,1)S(1)}, bf16[128,1024]{1,0:T(8,128)(2,1)S(1)}, u32[]{:S(2)}, u32[]{:S(2)}) collective-permute-start(bf16[128,1024]{1,0:T(8,128)(2,1)S(1)} %collective-permute-done.1.refs_1_.refs_3_), channel_id=1, source_target_pairs={{4,0},{8,4},{12,8},{14,12},{10,14},{6,10},{2,6},{0,2},{5,1},{9,5},... | collective-permute-start | bytes 786440 | tf_op jit(solution)/shard_map/back_cot2/ppermute | solution.py:287
  42.5 9.2 %collective-permute-start.18 = (bf16[128,1024]{1,0:T(8,128)(2,1)S(1)}, bf16[128,1024]{1,0:T(8,128)(2,1)S(1)}, u32[]{:S(2)}, u32[]{:S(2)}) collective-permute-start(bf16[128,1024]{1,0:T(8,128)(2,1)S(1)} %collective-permute-done.9.refs_0_.refs_2_.refs_6_), channel_id=1, source_target_pairs={{0,4},{4,8},{8,12},{12,14},{14,10},{10,6},{6,2},{2,0},{1,5},{5,9},... | collective-permute-start | bytes 786440 | tf_op jit(solution)/shard_map/onward_tok3/ppermute | solution.py:285
  44.1 9.1 %collective-permute-start.20 = (bf16[128,1024]{1,0:T(8,128)(2,1)S(1)}, bf16[128,1024]{1,0:T(8,128)(2,1)S(1)}, u32[]{:S(2)}, u32[]{:S(2)}) collective-permute-start(bf16[128,1024]{1,0:T(8,128)(2,1)S(1)} %collective-permute-done.10.refs_1_.refs_3_.refs_7_), channel_id=1, source_target_pairs={{4,0},{8,4},{12,8},{14,12},{10,14},{6,10},{2,6},{0,2},{5,1},{9,5},... | collective-permute-start | bytes 786440 | tf_op jit(solution)/shard_map/back_tok3/ppermute | solution.py:287
  47.4 9.9 %collective-permute-start.13 = (bf16[128,1024]{1,0:T(8,128)(2,1)S(1)}, bf16[128,1024]{1,0:T(8,128)(2,1)S(1)}, u32[]{:S(2)}, u32[]{:S(2)}) collective-permute-start(bf16[128,1024]{1,0:T(8,128)(2,1)S(1)} %collective-permute-done.7.refs_0_.refs_2_.refs_6_), channel_id=1, source_target_pairs={{0,4},{4,8},{8,12},{12,14},{14,10},{10,6},{6,2},{2,0},{1,5},{5,9},... | collective-permute-start | bytes 786440 | tf_op jit(solution)/shard_map/onward_cot3/ppermute | solution.py:285
  49.0 9.9 %collective-permute-start.15 = (bf16[128,1024]{1,0:T(8,128)(2,1)S(1)}, bf16[128,1024]{1,0:T(8,128)(2,1)S(1)}, u32[]{:S(2)}, u32[]{:S(2)}) collective-permute-start(bf16[128,1024]{1,0:T(8,128)(2,1)S(1)} %collective-permute-done.8.refs_1_.refs_3_.refs_7_), channel_id=1, source_target_pairs={{4,0},{8,4},{12,8},{14,12},{10,14},{6,10},{2,6},{0,2},{5,1},{9,5},... | collective-permute-start | bytes 786440 | tf_op jit(solution)/shard_map/back_cot3/ppermute | solution.py:287
  74.6 13.3 %collective-permute-start.31 = (bf16[64,1024]{1,0:T(8,128)(2,1)}, bf16[64,1024]{1,0:T(8,128)(2,1)S(1)}, u32[]{:S(2)}, u32[]{:S(2)}) collective-permute-start(bf16[64,1024]{1,0:T(8,128)(2,1)} %get-tuple-element.134), channel_id=1, source_target_pairs={{4,0},{8,4},{12,8},{14,12},{10,14},{6,10},{2,6},{0,2},{5,1},{9,5},... | collective-permute-start | bytes 393224 | tf_op jit(solution)/shard_map/back_mixed/ppermute | solution.py:287
  75.2 14.3 %collective-permute-start.32 = (bf16[64,1024]{1,0:T(8,128)(2,1)S(1)}, bf16[64,1024]{1,0:T(8,128)(2,1)}, u32[]{:S(2)}, u32[]{:S(2)}) collective-permute-start(bf16[64,1024]{1,0:T(8,128)(2,1)S(1)} %get-tuple-element.135), channel_id=1, source_target_pairs={{0,4},{4,8},{8,12},{12,14},{14,10},{10,6},{6,2},{2,0},{1,5},{5,9},... | collective-permute-start | bytes 393224 | tf_op jit(solution)/shard_map/onward_mixed/ppermute | solution.py:285
  82.5 15.8 %collective-permute-start.37 = (bf16[384,1024]{1,0:T(8,128)(2,1)}, bf16[384,1024]{1,0:T(8,128)(2,1)S(1)}, u32[]{:S(2)}, u32[]{:S(2)}) collective-permute-start(bf16[384,1024]{1,0:T(8,128)(2,1)} %get-tuple-element.150), channel_id=1, source_target_pairs={{0,1},{1,0},{2,3},{3,2},{4,5},{5,4},{6,7},{7,6},{8,9},{9,8},{10,11... | collective-permute-start | bytes 2359304 | tf_op jit(solution)/shard_map/swap_grad_out/ppermute | solution.py:25
  86.8 13.1 %collective-permute-start.38 = (bf16[384,1024]{1,0:T(8,128)(2,1)}, bf16[384,1024]{1,0:T(8,128)(2,1)}, u32[]{:S(2)}, u32[]{:S(2)}) collective-permute-start(bf16[384,1024]{1,0:T(8,128)(2,1)} %get-tuple-element.151), channel_id=1, source_target_pairs={{0,1},{1,0},{2,3},{3,2},{4,5},{5,4},{6,7},{7,6},{8,9},{9,8},{10,11... | collective-permute-start | bytes 2359304 | tf_op jit(solution)/shard_map/swap_grad_in/ppermute | solution.py:25
  88.0 8.7 %collective-permute-start.36 = (bf16[80,1024]{1,0:T(8,128)(2,1)}, bf16[80,1024]{1,0:T(8,128)(2,1)S(1)}, u32[]{:S(2)}, u32[]{:S(2)}) collective-permute-start(bf16[80,1024]{1,0:T(8,128)(2,1)} %get-tuple-element.137), channel_id=1, source_target_pairs={{0,4},{4,8},{8,12},{12,14},{14,10},{10,6},{6,2},{2,0},{1,5},{5,9},... | collective-permute-start | bytes 491528 | tf_op jit(solution)/shard_map/onward_grad/ppermute | solution.py:285
  94.5 9.5 %collective-permute-start.33 = (bf16[128,1024]{1,0:T(8,128)(2,1)S(1)}, bf16[128,1024]{1,0:T(8,128)(2,1)S(1)}, u32[]{:S(2)}, u32[]{:S(2)}) collective-permute-start(bf16[128,1024]{1,0:T(8,128)(2,1)S(1)} %get-tuple-element.142), channel_id=1, source_target_pairs={{4,0},{8,4},{12,8},{14,12},{10,14},{6,10},{2,6},{0,2},{5,1},{9,5},... | collective-permute-start | bytes 786440 | tf_op jit(solution)/shard_map/back_mixed/ppermute | solution.py:287
  95.1 9.2 %collective-permute-start.34 = (bf16[128,1024]{1,0:T(8,128)(2,1)S(1)}, bf16[128,1024]{1,0:T(8,128)(2,1)S(1)}, u32[]{:S(2)}, u32[]{:S(2)}) collective-permute-start(bf16[128,1024]{1,0:T(8,128)(2,1)S(1)} %get-tuple-element.143), channel_id=1, source_target_pairs={{0,4},{4,8},{8,12},{12,14},{14,10},{10,6},{6,2},{2,0},{1,5},{5,9},... | collective-permute-start | bytes 786440 | tf_op jit(solution)/shard_map/onward_mixed/ppermute | solution.py:285
  97.8 12.4 %collective-permute-start.41 = (bf16[144,1024]{1,0:T(8,128)(2,1)S(1)}, bf16[144,1024]{1,0:T(8,128)(2,1)S(1)}, u32[]{:S(2)}, u32[]{:S(2)}) collective-permute-start(bf16[144,1024]{1,0:T(8,128)(2,1)S(1)} %get-tuple-element.148), channel_id=1, source_target_pairs={{4,0},{8,4},{12,8},{14,12},{10,14},{6,10},{2,6},{0,2},{5,1},{9,5},... | collective-permute-start | bytes 884744 | tf_op jit(solution)/shard_map/back_grad/ppermute | solution.py:287
  98.3 12.3 %collective-permute-start.42 = (bf16[144,1024]{1,0:T(8,128)(2,1)S(1)}, bf16[144,1024]{1,0:T(8,128)(2,1)S(1)}, u32[]{:S(2)}, u32[]{:S(2)}) collective-permute-start(bf16[144,1024]{1,0:T(8,128)(2,1)S(1)} %get-tuple-element.149), channel_id=1, source_target_pairs={{0,4},{4,8},{8,12},{12,14},{14,10},{10,6},{6,2},{2,0},{1,5},{5,9},... | collective-permute-start | bytes 884744 | tf_op jit(solution)/shard_map/onward_grad/ppermute | solution.py:285
  102.5 35.0 %collective-permute-start.49 = (bf16[768,1024]{1,0:T(8,128)(2,1)}, bf16[768,1024]{1,0:T(8,128)(2,1)}, u32[]{:S(2)}, u32[]{:S(2)}) collective-permute-start(bf16[768,1024]{1,0:T(8,128)(2,1)} %get-tuple-element.152), channel_id=1, source_target_pairs={{0,16},{16,0},{1,17},{17,1},{2,18},{18,2},{3,19},{19,3},{4,20},{20... | collective-permute-start | bytes 4718600 | tf_op jit(solution)/shard_map/ppermute | solution.py:455
  105.5 10.2 %collective-permute-start.39 = (bf16[128,1024]{1,0:T(8,128)(2,1)S(1)}, bf16[128,1024]{1,0:T(8,128)(2,1)S(1)}, u32[]{:S(2)}, u32[]{:S(2)}) collective-permute-start(bf16[128,1024]{1,0:T(8,128)(2,1)S(1)} %get-tuple-element.155), channel_id=1, source_target_pairs={{4,0},{8,4},{12,8},{14,12},{10,14},{6,10},{2,6},{0,2},{5,1},{9,5},... | collective-permute-start | bytes 786440 | tf_op jit(solution)/shard_map/back_mixed/ppermute | solution.py:287
  106.0 10.3 %collective-permute-start.40 = (bf16[128,1024]{1,0:T(8,128)(2,1)S(1)}, bf16[128,1024]{1,0:T(8,128)(2,1)S(1)}, u32[]{:S(2)}, u32[]{:S(2)}) collective-permute-start(bf16[128,1024]{1,0:T(8,128)(2,1)S(1)} %get-tuple-element.156), channel_id=1, source_target_pairs={{0,4},{4,8},{8,12},{12,14},{14,10},{10,6},{6,2},{2,0},{1,5},{5,9},... | collective-permute-start | bytes 786440 | tf_op jit(solution)/shard_map/onward_mixed/ppermute | solution.py:285
  111.8 10.3 %collective-permute-start.45 = (bf16[144,1024]{1,0:T(8,128)(2,1)S(1)}, bf16[144,1024]{1,0:T(8,128)(2,1)S(1)}, u32[]{:S(2)}, u32[]{:S(2)}) collective-permute-start(bf16[144,1024]{1,0:T(8,128)(2,1)S(1)} %get-tuple-element.159), channel_id=1, source_target_pairs={{4,0},{8,4},{12,8},{14,12},{10,14},{6,10},{2,6},{0,2},{5,1},{9,5},... | collective-permute-start | bytes 884744 | tf_op jit(solution)/shard_map/back_grad/ppermute | solution.py:287
  112.3 10.3 %collective-permute-start.46 = (bf16[144,1024]{1,0:T(8,128)(2,1)S(1)}, bf16[144,1024]{1,0:T(8,128)(2,1)S(1)}, u32[]{:S(2)}, u32[]{:S(2)}) collective-permute-start(bf16[144,1024]{1,0:T(8,128)(2,1)S(1)} %get-tuple-element.160), channel_id=1, source_target_pairs={{0,4},{4,8},{8,12},{12,14},{14,10},{10,6},{6,2},{2,0},{1,5},{5,9},... | collective-permute-start | bytes 884744 | tf_op jit(solution)/shard_map/onward_grad/ppermute | solution.py:285
  117.4 10.3 %collective-permute-start.43 = (bf16[128,1024]{1,0:T(8,128)(2,1)S(1)}, bf16[128,1024]{1,0:T(8,128)(2,1)S(1)}, u32[]{:S(2)}, u32[]{:S(2)}) collective-permute-start(bf16[128,1024]{1,0:T(8,128)(2,1)S(1)} %get-tuple-element.163), channel_id=1, source_target_pairs={{4,0},{8,4},{12,8},{14,12},{10,14},{6,10},{2,6},{0,2},{5,1},{9,5},... | collective-permute-start | bytes 786440 | tf_op jit(solution)/shard_map/back_mixed/ppermute | solution.py:287
  117.9 10.3 %collective-permute-start.44 = (bf16[128,1024]{1,0:T(8,128)(2,1)S(1)}, bf16[128,1024]{1,0:T(8,128)(2,1)S(1)}, u32[]{:S(2)}, u32[]{:S(2)}) collective-permute-start(bf16[128,1024]{1,0:T(8,128)(2,1)S(1)} %get-tuple-element.164), channel_id=1, source_target_pairs={{0,4},{4,8},{8,12},{12,14},{14,10},{10,6},{6,2},{2,0},{1,5},{5,9},... | collective-permute-start | bytes 786440 | tf_op jit(solution)/shard_map/onward_mixed/ppermute | solution.py:285
  123.7 8.7 %collective-permute-start.47 = (bf16[144,1024]{1,0:T(8,128)(2,1)S(1)}, bf16[144,1024]{1,0:T(8,128)(2,1)S(1)}, u32[]{:S(2)}, u32[]{:S(2)}) collective-permute-start(bf16[144,1024]{1,0:T(8,128)(2,1)S(1)} %get-tuple-element.167), channel_id=1, source_target_pairs={{4,0},{8,4},{12,8},{14,12},{10,14},{6,10},{2,6},{0,2},{5,1},{9,5},... | collective-permute-start | bytes 884744 | tf_op jit(solution)/shard_map/back_grad/ppermute | solution.py:287
  (55 other events, 386.6 us)

commit v4 on v3

v4 whole, which is shorter than its diff:
```python
import functools

import jax
import jax.numpy as jnp
from jax import lax
from jax.experimental import pallas as pl
from jax.experimental.pallas import tpu as pltpu
from jax.sharding import PartitionSpec as P

BF16 = jnp.bfloat16
F32 = jnp.float32
VMEM_LIMIT = 16 * 1024 * 1024
LANES = 128
EXTRA = 16


def ring_order(count):
    if count % 2:
        return list(range(count))
    return list(range(0, count, 2)) + list(range(count - 1, 0, -2))


def swap_cores(value, name):
    with jax.named_scope("swap_" + name):
        return lax.ppermute(value, "tensor", [(0, 1), (1, 0)])


def tied(values, others):
    return lax.optimization_barrier((tuple(values), tuple(others)))[0]


def dot_width(rows, weights):
    return lax.dot_general(rows, weights, (((1,), (0,)), ((), ())), preferred_element_type=F32)


def dot_rows(left, right):
    return lax.dot_general(left, right, (((0,), (0,)), ((), ())), preferred_element_type=F32)


def call(kernel, out_shape, operands, scalars, work=4 * 10**9, unmoved=0, scratch=()):
    return pl.pallas_call(
        kernel,
        out_shape=out_shape,
        in_specs=[pl.BlockSpec(memory_space=pltpu.SMEM)]
        + [pl.BlockSpec(memory_space=pltpu.HBM)] * unmoved
        + [pl.BlockSpec(memory_space=pltpu.VMEM)] * (len(operands) - unmoved),
        out_specs=[pl.BlockSpec(memory_space=pltpu.VMEM)] * len(out_shape),
        scratch_shapes=list(scratch),
        compiler_params=pltpu.CompilerParams(vmem_limit_bytes=VMEM_LIMIT),
        cost_estimate=pl.CostEstimate(flops=work, bytes_accessed=0, transcendentals=0),
    )(scalars, *operands)


def picked(core, first, second):
    return jnp.where(core == 0, first, second)


def diagonal(count):
    across = lax.broadcasted_iota(jnp.int32, (count, count), 0)
    along = lax.broadcasted_iota(jnp.int32, (count, count), 1)
    return across == along


def column_of(row):
    return jnp.sum(jnp.where(diagonal(row.shape[1]), row, 0.0), axis=1, keepdims=True)


def row_of(column):
    return jnp.sum(jnp.where(diagonal(column.shape[0]), column, 0.0), axis=0, keepdims=True)


def pieces_of(value):
    high = value.astype(BF16).astype(F32)
    middle = (value - high).astype(BF16).astype(F32)
    return high, middle, value - high - middle


def prepare(core, local_ref, arrived_ref, flat_ref, mine_ref, other_ref):
    units, width = local_ref.shape[0], local_ref.shape[1] // 2
    at = pl.ds(pl.multiple_of(core * units, units), units)
    mine = pl.ds(pl.multiple_of(core * width, width), width)
    other = pl.ds(pl.multiple_of((1 - core) * width, width), width)
    block = local_ref[:, mine]
    flat_ref[at, :] = block
    mine_ref[:, at] = block.T
    other_ref[:, at] = local_ref[:, other].T
    came = pl.ds(pl.multiple_of((1 - core) * units, units), units)
    if arrived_ref.shape[1] > width:
        block, beside = arrived_ref[:, mine], arrived_ref[:, other]
    else:
        start = arrived_ref.shape[0] - 2 * units
        mine = pl.ds(pl.multiple_of(start + core * units, LANES), units)
        other = pl.ds(pl.multiple_of(start + (1 - core) * units, LANES), units)
        block, beside = arrived_ref[mine, :], arrived_ref[other, :]
    flat_ref[came, :] = block
    mine_ref[:, came] = block.T
    other_ref[:, came] = beside.T


def stacked(values):
    return jnp.concatenate(values, axis=0) if len(values) > 1 else values[0]


def give_next(core, refs):
    out_ref = refs[-1]
    half = out_ref.shape[0] // 2
    cut = refs[0].shape[0] - 2 * half
    out_ref[:half, :] = picked(core, refs[1][:half, :], refs[0][:half, :])
    out_ref[half:, :] = picked(core, refs[1][half + cut :, :], refs[0][half + cut :, :])
    return refs[2:-1]


def table_parts(expert, rows, width, experts):
    per_row = width // rows
    deep = -(-experts // per_row)
    line = lax.broadcasted_iota(jnp.int32, (EXTRA, width), 0)
    lane = lax.broadcasted_iota(jnp.int32, (EXTRA, width), 1)
    lanes = lane // rows == lax.rem(expert, per_row)
    return [lanes & (line == i * deep + expert // per_row) for i in range(3)]


def payload_kernel(experts, scalars, routes_hbm, gates_hbm, cotangent_hbm, out_ref, routes_ref, gates_ref, sems):
    rows, width = cotangent_hbm.shape
    half = rows // 2
    copies = [
        pltpu.make_async_copy(routes_hbm, routes_ref, sems.at[0]),
        pltpu.make_async_copy(gates_hbm, gates_ref, sems.at[1]),
        pltpu.make_async_copy(
            cotangent_hbm.at[pl.ds(0, half), :], out_ref.at[pl.ds(0, half), :], sems.at[2]
        ),
        pltpu.make_async_copy(
            cotangent_hbm.at[pl.ds(half, half), :],
            out_ref.at[pl.ds(half + EXTRA, half), :],
            sems.at[3],
        ),
    ]
    for copy in copies:
        copy.start()
    copies[0].wait()
    copies[1].wait()
    table = jnp.zeros((EXTRA, width), F32)
    for expert in range(experts):
        named = jnp.where(routes_ref[...] == expert, gates_ref[...], 0.0)
        row = jnp.sum(named, axis=0, keepdims=True)
        for piece, place in zip(pieces_of(row), table_parts(expert, rows, width, experts)):
            spread = jnp.concatenate([piece] * (width // rows), axis=1)
            table = jnp.where(place, spread, table)
    out_ref[half : half + EXTRA, :] = table.astype(BF16)
    copies[2].wait()
    copies[3].wait()


def gate_column(extra, expert, rows, experts):
    width = extra.shape[1]
    places = table_parts(expert, rows, width, experts)
    values = extra.astype(F32)
    row = sum(jnp.sum(jnp.where(p, values, 0.0), axis=0, keepdims=True) for p in places)
    row = sum(row[:, i * rows : (i + 1) * rows] for i in range(width // rows))
    return column_of(row)


def first_tokens_kernel(scalars, first, second, tokens, cotangent, out_ref):
    core = scalars[0]
    rows = first.shape[0]
    half = rows // 2
    out_ref[:rows, :] = picked(core, second[...], first[...])
    for i, ref in enumerate((tokens, cotangent)):
        at = rows + i * half
        out_ref[at : at + half, :] = picked(core, ref[half:rows, :], ref[:half, :])


def first_cotangent_kernel(scalars, first, second, w_ref, out_ref, sems):
    core = scalars[0]
    units, width = w_ref.shape[0], out_ref.shape[1]
    rows = out_ref.shape[0] - 2 * units
    half = rows // 2
    copies = [
        pltpu.make_async_copy(
            w_ref.at[:, pl.ds(i * width, width)],
            out_ref.at[pl.ds(rows + i * units, units), :],
            sems.at[i],
        )
        for i in range(2)
    ]
    for copy in copies:
        copy.start()
    out_ref[:half, :] = picked(core, second[:half, :], first[:half, :])
    out_ref[half:rows, :] = picked(core, second[half + EXTRA :, :], first[half + EXTRA :, :])
    for copy in copies:
        copy.wait()


def pick_kernel(scalars, first, second, out_ref):
    out_ref[...] = picked(scalars[0], second[...], first[...])


def taken(kinds, refs):
    pieces = []
    for kind in kinds:
        count = 2 if isinstance(kind, int) else 3
        pieces.append((kind, refs[:count]))
        refs = refs[count:]
    return pieces, refs


def rows_of(core, piece, rows):
    kind, refs = piece
    half = rows // 2
    if kind == "full":
        first, second, other = refs
        mine, there = picked(core, first[...], second[...]), other[...]
        if mine.shape[0] == rows:
            return mine, there, None
        extra = mine[half : half + EXTRA]
        mine = stacked([mine[:half], mine[half + EXTRA :]])
        if there.shape[0] > rows:
            there = stacked([there[:half], there[half + EXTRA :]])
        return mine, there, extra
    if kind == "far":
        first, second, other = refs
        if first.shape[0] == half:
            return picked(core, first[...], second[...]), other[...], None
        there = picked(core, other[:half, :], other[EXTRA:, :])
    else:
        block, arrived = refs
        there = arrived[kind : kind + half, :]
        if block.shape[0] == rows:
            return picked(core, block[:half, :], block[half:, :]), there, None
        first, second = block.at[: half + EXTRA, :], block.at[half:, :]
    mine = picked(core, first[:half, :], second[EXTRA:, :])
    return mine, there, picked(core, first[half:, :], second[:EXTRA, :])


def units_of(core, pieces, rows, w_ref, w_other_ref):
    here, there, extra = zip(*(rows_of(core, p, rows) for p in pieces))
    wide = dot_width(stacked(here), w_ref[...]) + dot_width(stacked(there), w_other_ref[...])
    return wide, extra


def forward_kernel(kinds, rows, with_next, with_weights, scalars, *refs):
    core = scalars[0]
    if with_weights:
        weights = refs[-2:]
        prepare(core, *refs[:2], *refs[-3:])
        refs = refs[2:-3]
    if with_next:
        refs = give_next(core, refs)
    hidden_ref, slope_ref = refs[-2:]
    pieces, refs = taken(kinds, refs)
    if not with_weights:
        weights = refs[:2]
    pre = units_of(core, pieces, rows, *weights)[0]
    logistic = 1.0 / (1.0 + jnp.exp(-pre))
    hidden_ref[...] = (pre * logistic).astype(BF16)
    slope_ref[...] = logistic * (1.0 + pre * (1.0 - logistic))


def backward_kernel(kinds, rows, experts, with_next, with_weights, before, scalars, *refs):
    core, expert = scalars[0], scalars[1]
    if with_weights:
        weights = refs[-2:]
        prepare(core, *refs[:2], *refs[-3:])
        refs = refs[2:-3]
    if with_next:
        refs = give_next(core, refs)
    if before:
        lines = refs[0].shape[0]
        for i in range(before):
            refs[-1][i * lines : (i + 1) * lines, :] = refs[i][...]
        refs = (*refs[before:-1], refs[-1].at[before * lines :, :])
    hidden_ref, slope_ref, out_ref = refs[-3:]
    pieces, refs = taken(kinds, refs)
    if not with_weights:
        weights = refs[:2]
    lines, units = hidden_ref.shape
    wide, extras = units_of(core, pieces, rows, *weights)
    columns = []
    for extra in extras:
        column = gate_column(extra, expert, rows, experts)
        if len(kinds) > 1:
            column = picked(core, column[: rows // 2], column[rows // 2 :])
        columns.append(column)
    gate = stacked(columns)
    hidden = hidden_ref[...].astype(F32)
    out_ref[:, :units] = (gate * hidden).astype(BF16)
    out_ref[:, units : 2 * units] = (gate * slope_ref[...] * wide).astype(BF16)
    sums = jnp.sum(hidden * wide, axis=1, keepdims=True)
    lane = lax.broadcasted_iota(jnp.int32, (lines, LANES), 1)
    kept = jnp.zeros((lines, LANES), F32)
    for i, piece in enumerate(pieces_of(sums)):
        kept = jnp.where(lane == i, piece, kept)
    out_ref[:, 2 * units : 2 * units + LANES] = kept.astype(BF16)


def dots_rows(expert, dots, start, rows, width, experts):
    count = dots.shape[0]
    row = row_of(dots)
    if count < rows:
        blank = jnp.zeros((1, count), F32)
        row = jnp.concatenate([row, blank] if start == 0 else [blank, row], axis=1)
    out = jnp.zeros((EXTRA, width), F32)
    for piece, place in zip(pieces_of(row), table_parts(expert, rows, width, experts)):
        out = jnp.where(place, jnp.concatenate([piece] * (width // rows), axis=1), out)
    return out


def return_kernel(kind, at, first_row, count, experts, rows, scalars, mine_ref, arrived_ref, w_ref, *refs):
    core, expert = scalars[0], scalars[1]
    units, width = w_ref.shape
    if kind == "far":
        lanes = slice(at, at + units + (LANES if at else 0))
        mine_all = mine_ref[first_row : first_row + count, lanes]
        arrived_all = arrived_ref[first_row : first_row + count, lanes]
    else:
        mine_here, arrived_here, w_here, sems = refs[-4:]
        refs = refs[:-4]
        window = (pl.ds(first_row, count), pl.ds(at, mine_here.shape[1]))
        copies = [
            pltpu.make_async_copy(mine_ref.at[window], mine_here, sems.at[0]),
            pltpu.make_async_copy(arrived_ref.at[window], arrived_here, sems.at[1]),
            pltpu.make_async_copy(w_ref, w_here, sems.at[2]),
        ]
        for copy in copies:
            copy.start()
        for copy in copies:
            copy.wait()
        mine_all, arrived_all, w_ref = mine_here[...], arrived_here[...], w_here
    mine, arrived = mine_all[:, :units], arrived_all[:, :units]
    both = jnp.concatenate([picked(core, mine, arrived), picked(core, arrived, mine)], axis=0)
    part = dot_width(both, w_ref[...])
    with_dots = at > 0
    extra = [None, None]
    if with_dots:
        mine = jnp.sum(mine_all[:, units:].astype(F32), axis=1, keepdims=True)
        arrived = jnp.sum(arrived_all[:, units:].astype(F32), axis=1, keepdims=True)
        dots = [picked(core, mine, arrived), picked(core, arrived, mine)]
        starts = (0, count if count < rows else 0)
        extra = [
            dots_rows(expert, d, start, rows, width, experts) for d, start in zip(dots, starts)
        ]
    if kind == "far":
        for i, out_ref in enumerate(refs):
            out_ref[:count, :] = part[i * count : (i + 1) * count].astype(BF16)
            if with_dots:
                out_ref[count:, :] = extra[i].astype(BF16)
        return
    from_ahead, from_behind = refs[:2]
    if kind == "own":
        total = part + from_ahead[:rows, :].astype(F32) + from_behind[:rows, :].astype(F32)
        if not with_dots:
            refs[2][...] = total.astype(BF16)
            return
        routes_ref, out_ref, gates_ref = refs[2:]
        out_ref[...] = total.astype(BF16)
        table = extra[0] + extra[1]
        table = table + from_ahead[rows:, :].astype(F32) + from_behind[rows:, :].astype(F32)
        per_row = width // rows
        deep = -(-experts // per_row)
        routes = routes_ref[...]
        grads = jnp.zeros(routes.shape, F32)
        for e in range(experts):
            lanes = slice((e % per_row) * rows, (e % per_row + 1) * rows)
            line = e // per_row
            row = sum(table[i * deep + line : i * deep + line + 1, lanes] for i in range(3))
            grads = jnp.where(routes == e, row, grads)
        gates_ref[...] = grads
        return
    behind_ref, ahead_ref = refs[2:]
    behind, ahead = part[:count], part[count:]
    if kind == "join":
        half = count // 2
        behind_ref[:half, :] = (behind[:half] + from_ahead[:half, :].astype(F32)).astype(BF16)
        behind_ref[half:count, :] = behind[half:].astype(BF16)
        ahead_ref[:half, :] = ahead[:half].astype(BF16)
        ahead_ref[half:count, :] = (ahead[half:] + from_behind[:half, :].astype(F32)).astype(BF16)
    else:
        half = count
        behind_ref[:count, :] = (behind + from_ahead[:count, :].astype(F32)).astype(BF16)
        ahead_ref[:count, :] = (ahead + from_behind[:count, :].astype(F32)).astype(BF16)
    if with_dots:
        behind_ref[count:, :] = (extra[0] + from_ahead[half:, :].astype(F32)).astype(BF16)
        ahead_ref[count:, :] = (extra[1] + from_behind[half:, :].astype(F32)).astype(BF16)


def weight_kernel(at, rows, scalars, *refs):
    core = scalars[0]
    lefts = []
    mine_ref, other_ref = refs[-2:]
    taken = 0
    if at:
        taken = 2
        units = refs[0].shape[0]
        mine_ref[:units, :] = refs[0][...]
        other_ref[:units, :] = refs[1][...]
        mine_ref, other_ref = mine_ref.at[units:, :], other_ref.at[units:, :]
    units = mine_ref.shape[0]
    above, above_came, ends, ends_came = refs[taken : taken + 4]
    rights = refs[taken + 4 : -2]
    for left, came in ((above, above_came), (ends, ends_came)):
        count = ends.shape[0]
        for i in range(left.shape[0] // count):
            lines = slice(i * count, (i + 1) * count)
            here, there = left[lines, at : at + 2 * units], came[lines, at : at + 2 * units]
            lefts += [picked(core, here, there), picked(core, there, here)]
    half = rows // 2
    block, far_first, far_second = rights[-3:]
    cut = block.shape[0] - rows
    blocks = []
    for ref in rights[:-3]:
        blocks += [ref[:half, :], ref[half + cut :, :]] if cut else [ref[...]]
    blocks += [block[:half, :], far_first[:half, :]]
    blocks += [block[half + cut :, :], far_second[cut:, :]]
    part = dot_rows(stacked(lefts), stacked(blocks))
    mine_ref[...] = picked(core, part[:units], part[units:]).astype(BF16)
    other_ref[...] = picked(core, part[units:], part[:units]).astype(BF16)


def send_kernel(scalars, mine_ref, came_ref, sent_ref, kept_ref):
    @pl.when(scalars[2] == 0)
    def _():
        sent_ref[...] = came_ref[...]
        kept_ref[...] = mine_ref[...]

    @pl.when(scalars[2] != 0)
    def _():
        sent_ref[...] = mine_ref[...]
        kept_ref[...] = came_ref[...]


def add_kernel(*refs):
    for i in range(2):
        refs[4 + i][...] = refs[2 * i][...].astype(F32) + refs[2 * i + 1][...].astype(F32)


def per_device(tokens, routes, gates, w_in, w_out, cotangent):
    size = lax.axis_size("expert")
    n_dp = lax.axis_size("dp")
    rows, width = tokens.shape
    half = rows // 2
    experts = size * w_in.shape[0]
    core = lax.axis_index("tensor")
    place = lax.axis_index("expert")
    group = lax.axis_index("dp")
    order = ring_order(size)
    onward_pairs = [(order[i], order[(i + 1) % size]) for i in range(size)]
    back_pairs = [(b, a) for a, b in onward_pairs]
    steps = size // 2
    w_in, w_out = w_in[0], w_out[0]
    local_units = w_in.shape[0]
    units = 2 * local_units

    def both_ways(forth_value, back_value, name):
        with jax.named_scope("onward_" + name):
            forth = lax.ppermute(forth_value, "expert", onward_pairs)
        with jax.named_scope("back_" + name):
            return forth, lax.ppermute(back_value, "expert", back_pairs)

    scalars = jnp.stack([core, place, (core + group) % 2]).astype(jnp.int32)

    weight_shapes = [
        jax.ShapeDtypeStruct((units, width), BF16),
        jax.ShapeDtypeStruct((width, units), BF16),
        jax.ShapeDtypeStruct((width, units), BF16),
    ]

    def split(pieces):
        return tuple(p[0] for p in pieces), [v for p in pieces for v in p[1:]]

    def forward(pieces, weights, following=()):
        shape = (rows, units)
        raw = weights[0] is w_in
        kinds, operands = split(pieces)
        result = call(
            functools.partial(forward_kernel, kinds, rows, len(following) > 0, raw),
            [
                jax.ShapeDtypeStruct(shape, BF16),
                jax.ShapeDtypeStruct(shape, F32),
                *[jax.ShapeDtypeStruct((rows, width), BF16) for _ in following[:1]],
                *(weight_shapes if raw else ()),
            ],
            [
                *(weights if raw else ()),
                *following,
                *operands,
                *(() if raw else weights[1:]),
            ],
            scalars,
        )
        return (result[:-3], result[-3:]) if raw else (result, weights)

    def backward(pieces, weights, hidden, slope, following=(), before=()):
        count = hidden.shape[0] * (1 + len(before))
        raw = weights[0] is w_out
        kinds, operands = split(pieces)
        result = call(
            functools.partial(
                backward_kernel, kinds, rows, experts, len(following) > 0, raw, len(before)
            ),
            [
                jax.ShapeDtypeStruct((count, 2 * units + LANES), BF16),
                *[jax.ShapeDtypeStruct((rows, width), BF16) for _ in following[:1]],
                *(weight_shapes if raw else ()),
            ],
            [
                *(weights if raw else ()),
                *following,
                *before,
                *operands,
                *(() if raw else weights[1:]),
                hidden,
                slope,
            ],
            scalars,
        )
        return (result[:-3], result[-3:]) if raw else (result, weights)

    def returned(kind, at, first_row, mine, arrived, weights, sums, more=()):
        count = rows if kind in ("join", "add") else half
        extra = EXTRA if at else 0
        if kind == "own":
            shapes = [jax.ShapeDtypeStruct((rows, width), BF16)]
            if at:
                shapes.append(jax.ShapeDtypeStruct(routes.shape[::-1], F32))
        else:
            shapes = [jax.ShapeDtypeStruct((count + extra, width), BF16)] * 2
        kernel = functools.partial(return_kernel, kind, at, first_row, count, experts, rows)
        operands = [mine, arrived, weights, *sums, *more]
        if kind == "far":
            return call(kernel, shapes, operands, scalars, 3 * 10**9)
        held = (count, units + (LANES if at else 0))
        scratch = [
            pltpu.VMEM(held, BF16),
            pltpu.VMEM(held, BF16),
            pltpu.VMEM((units, width), BF16),
            pltpu.SemaphoreType.DMA((3,)),
        ]
        return call(kernel, shapes, operands, scalars, 2 * 10**9, 3, scratch)

    payload = pl.pallas_call(
        functools.partial(payload_kernel, experts),
        out_shape=jax.ShapeDtypeStruct((rows + EXTRA, width), BF16),
        in_specs=[pl.BlockSpec(memory_space=pltpu.SMEM)]
        + [pl.BlockSpec(memory_space=pltpu.HBM)] * 3,
        out_specs=pl.BlockSpec(memory_space=pltpu.VMEM),
        scratch_shapes=[
            pltpu.VMEM(routes.shape[::-1], jnp.int32),
            pltpu.VMEM(gates.shape[::-1], F32),
            pltpu.SemaphoreType.DMA((4,)),
        ],
        compiler_params=pltpu.CompilerParams(vmem_limit_bytes=VMEM_LIMIT),
        cost_estimate=pl.CostEstimate(flops=10**9, bytes_accessed=0, transcendentals=0),
    )(scalars, routes.T, gates.T, cotangent)
    ring = [both_ways(tokens, tokens, "tok1"), both_ways(payload, payload, "cot1")]

    in_all, out_all = (w_in, swap_cores(w_in, "weights")), ()

    arrivals, outputs, lefts = [], [], []
    for turn in range(2 * steps):
        now = ring[turn]
        step = turn // 2 + 1
        name = ("tok", "cot")[turn % 2]
        sent = None
        if turn == 0:
            sent = call(
                first_tokens_kernel,
                [jax.ShapeDtypeStruct((2 * rows, width), BF16)],
                [*now, tokens, cotangent],
                scalars,
                2 * 10**9,
            )[0]
        elif turn == 1:
            seen = tied((*now, w_out), (*in_all, sent_first))
            cot_sent = pl.pallas_call(
                first_cotangent_kernel,
                out_shape=jax.ShapeDtypeStruct((rows + units, width), BF16),
                in_specs=[pl.BlockSpec(memory_space=pltpu.SMEM)]
                + [pl.BlockSpec(memory_space=pltpu.VMEM)] * 2
                + [pl.BlockSpec(memory_space=pltpu.HBM)],
                out_specs=pl.BlockSpec(memory_space=pltpu.VMEM),
                scratch_shapes=[pltpu.SemaphoreType.DMA((2,))],
                compiler_params=pltpu.CompilerParams(vmem_limit_bytes=VMEM_LIMIT),
                cost_estimate=pl.CostEstimate(flops=10**9, bytes_accessed=0, transcendentals=0),
            )(scalars, *seen)
            result, in_all = forward([("full", *arrivals[0])], in_all)
            outputs.append(result)
        elif turn < 2 * steps - 1:
            done = turn - 1
            first, second, other = arrivals[done]
            following = now if turn < 2 * steps - 3 else ()
            if turn == 2 * steps - 3:
                other = tied((other,), now)[0]
            pieces = [("full", first, second, other)]
            if done % 2 == 0:
                result, in_all = forward(pieces, in_all, following)
                if following:
                    *result, sent = result
                outputs.append(result)
            else:
                before = lefts if turn == 2 * steps - 2 else ()
                result, out_all = backward(
                    pieces, out_all, *outputs[done - 1], following, before
                )
                if following:
                    *result, sent = result
                lefts.append(result[0])
                outputs.append(result)
            if turn != 2 * steps - 3:
                now = tied(now, outputs[-1][:1])
        else:
            now = tied(now, outputs[-1])
        if turn == 0:
            sent_first = sent
        elif turn == 1:
            sent = cot_sent
        elif sent is None:
            shape = [jax.ShapeDtypeStruct(now[0].shape, BF16)]
            sent = call(pick_kernel, shape, [*now], scalars, 10**8)[0]
        if step < steps - 1:
            ring.append(both_ways(now[0], now[1], name + str(step + 1)))
        elif step == steps - 1:
            cut = half + (EXTRA if turn % 2 else 0)
            ends = ring[turn][0][:cut], ring[turn][1][half:]
            ring.append(both_ways(*ends, name + str(step + 1)))
        other = swap_cores(sent, name + str(step))
        if turn == 0:
            own_arrived, other = other, other[:rows]
        elif turn == 1:
            out_all, other = (w_out, other), other[:rows]
        arrivals.append((*now, other))
    tok_pieces = [(rows, tokens, own_arrived), ("far", *arrivals[2 * steps - 2])]
    cot_pieces = [(rows + half, payload, own_arrived), ("far", *arrivals[2 * steps - 1])]
    lefts = lefts[-1]
    lefts_arrived = swap_cores(lefts, "lefts")
    hidden, slope = forward(tok_pieces, in_all)[0]
    ends = backward(cot_pieces, out_all, hidden, slope)[0][0]
    ends_arrived = swap_cores(ends, "ends")

    sent = returned("far", 0, half, ends, ends_arrived, out_all[0], ())
    mixed_in = both_ways(sent[1], sent[0], "mixed")[::-1]
    ends_after = tied((ends_arrived,), sent)[0]
    sent = returned("far", units, half, ends, ends_after, in_all[0], ())
    back_in = both_ways(sent[1], sent[0], "grad")[::-1]

    def weight_part(at, which, after, above):
        operands = [*above, lefts, lefts_arrived, ends, tied((ends_arrived,), after)[0]]
        for s in range(steps - 1):
            operands += arrivals[2 * s + which][:2]
        own, far_ends = (tok_pieces, cot_pieces)[which]
        operands += [own[1], *far_ends[1:3]]
        deep = local_units * (1 + len(above) // 2)
        return call(
            functools.partial(weight_kernel, at, rows),
            [jax.ShapeDtypeStruct((deep, width), BF16)] * 2,
            operands,
            scalars,
            2 * 10**9,
        )

    part_out = weight_part(0, 1, sent, ())
    parts, parts_other = weight_part(units, 0, (*part_out, *mixed_in, *back_in), part_out)
    parts_other = swap_cores(parts_other, "grad")
    for step in range(steps - 1, 0, -1):
        kind = "join" if step == steps - 1 else "add"
        line = (step - 1) * rows
        mixed_in = tied(mixed_in, (*sent, *((parts,) if kind == "join" else ())))
        sent = returned(kind, 0, line, lefts, lefts_arrived, out_all[0], mixed_in)
        mixed_in = both_ways(sent[1], sent[0], "mixed")[::-1]
        back_in = tied(back_in, sent)
        sent = returned(kind, units, line, lefts, lefts_arrived, in_all[0], back_in)
        back_in = both_ways(sent[1], sent[0], "grad")[::-1]
        if kind == "join":
            parts_other = tied((parts_other,), sent)[0]
            if n_dp == 2:
                tile = units // 4
                block = pl.BlockSpec((tile, width), lambda i: (i, 0))
                parts_sent, parts_kept = pl.pallas_call(
                    send_kernel,
                    grid=(4,),
                    out_shape=[jax.ShapeDtypeStruct(parts.shape, BF16)] * 2,
                    in_specs=[pl.BlockSpec(memory_space=pltpu.SMEM), block, block],
                    out_specs=[block] * 2,
                    compiler_params=pltpu.CompilerParams(vmem_limit_bytes=VMEM_LIMIT),
                    cost_estimate=pl.CostEstimate(flops=10**9, bytes_accessed=0, transcendentals=0),
                )(scalars, parts, parts_other)
                parts_came = lax.ppermute(parts_sent, "dp", [(0, 1), (1, 0)])
            else:
                totals = []
                for i in range(2):
                    piece = slice(i * local_units, (i + 1) * local_units)
                    mine, arrived = parts[piece], parts_other[piece]
                    part = jnp.concatenate(
                        [picked(core, mine, arrived), picked(core, arrived, mine)], axis=1
                    )
                    across = part.shape[1] // n_dp
                    slices = [
                        lax.dynamic_slice_in_dim(part, ((group + shift) % n_dp) * across, across, axis=1)
                        for shift in range(n_dp)
                    ]
                    total = slices[0].astype(F32)
                    for shift in range(1, n_dp):
                        pairs = [(i, (i + shift) % n_dp) for i in range(n_dp)]
                        total = total + lax.ppermute(slices[shift], "dp", pairs).astype(F32)
                    totals.append(total)
            if n_dp == 2:
                sent = (*sent, parts_sent)
    mixed_in = tied(mixed_in, sent)
    if n_dp == 2:
        tiles = 3 if local_units % 48 == 0 else 1
        block = (local_units // tiles, width)
        upper = pl.BlockSpec(block, lambda i: (i, 0))
        lower = pl.BlockSpec(block, lambda i: (i + tiles, 0))
        totals = pl.pallas_call(
            add_kernel,
            grid=(tiles,),
            out_shape=[jax.ShapeDtypeStruct((local_units, width), F32)] * 2,
            in_specs=[upper] * 2 + [lower] * 2,
            out_specs=[upper] * 2,
            compiler_params=pltpu.CompilerParams(vmem_limit_bytes=VMEM_LIMIT),
            cost_estimate=pl.CostEstimate(flops=10**9, bytes_accessed=0, transcendentals=0),
        )(*([parts_kept, parts_came] * 2))
    back_in = tied(back_in, totals)
    mixed = returned("own", 0, 0, ends, ends_arrived, out_all[0], mixed_in)[0]
    grad_tokens, grad_gates = returned(
        "own", units, 0, ends, ends_arrived, in_all[0], back_in, (routes.T,)
    )
    grad_gates = grad_gates.T

    grad_out, grad_in = totals
    return (mixed, grad_tokens, grad_gates, grad_in[None], grad_out[None])


def solution(mesh):
    placed = (
        P(("dp", "expert"), "tensor"),
        P(("dp", "expert"), None),
        P(("dp", "expert"), None),
        P("expert", "tensor", None),
        P("expert", "tensor", None),
        P(("dp", "expert"), "tensor"),
    )
    return jax.shard_map(
        per_device,
        mesh=mesh,
        in_specs=placed,
        out_specs=(
            P(("dp", "expert"), "tensor"),
            P(("dp", "expert"), "tensor"),
            P(("dp", "expert"), None),
            P("expert", "tensor", "dp"),
            P("expert", "tensor", "dp"),
        ),
        check_vma=False,
    )
```

time: 142 us -> 123 us (0.87)
  local copies, waits for them, and re-layouts: 15.1 us -> 2.42 us
  waiting for transfers between devices: 34.1 us -> 44.5 us
  Pallas kernels: 44.1 us -> 36.7 us
  starting transfers between devices: 45.2 us -> 37.9 us
  other arithmetic: 2.2 us -> 0.08 us
    pallas_call x24, Pallas kernels: 44.1 us -> 32.1 us  [call(): pl.pallas_call(kernel, out_shape=out_shape, in_specs=[pl.BlockSpec(memory...]
    unnamed x74 -> x16, local copies, waits for them, and re-layouts: 12.3 us -> 2.34 us
    ppermute x16, waiting for transfers between devices: 20 us -> 28 us  [both_ways(): return (forth, lax.ppermute(back_value, 'expert', back_pairs))]
    all_to_all x1 -> x0, starting transfers between devices: 6.26 us -> none  [per_device(): lax.all_to_all(table, 'expert', split_axis=0, concat_axis=0, tiled=True)]
    pallas_call x0 -> x4, Pallas kernels: none -> 4.64 us  [the longest x1 2.07 us: per_device(): pl.pallas_call(add_kernel, grid=(tiles,), out_shape=[jax.ShapeDtypeStruct...]
    ppermute x16, waiting for transfers between devices: 10.2 us -> 13.7 us  [both_ways(): forth = lax.ppermute(forth_value, 'expert', onward_pairs)]
    ppermute x1, waiting for transfers between devices: 2.49 us -> 0.01 us  [per_device(): parts_came = lax.ppermute(parts_sent, 'dp', [(0, 1), (1, 0)])]
    ppermute x16, starting transfers between devices: 26.7 us -> 29 us  [both_ways(): forth = lax.ppermute(forth_value, 'expert', onward_pairs)]
  transfers between devices with their start and end apart: 51 -> 45, of which waited for: 22 -> 30; matrix products, arithmetic and copies ran while one was open for 4% -> 0% of each run, Pallas kernels for 28% -> 25%
where the time goes in v4:
time: 123 us
  waiting for transfers between devices  44.5 us (36%)
  starting transfers between devices  37.9 us (31%)
  Pallas kernels  36.7 us (30%)
  local copies, waits for them, and re-layouts  2.42 us (2%)
  between operations  1.23 us (1%)
    pallas_call x24, Pallas kernels, call(): pl.pallas_call(kernel, out_shape=out_shape, in_specs=[pl.BlockSpec(memory...  32.1 us
    ppermute x16, starting transfers between devices, both_ways(): forth = lax.ppermute(forth_value, 'expert', onward_pairs)  29 us
    ppermute x16, waiting for transfers between devices, both_ways(): return (forth, lax.ppermute(back_value, 'expert', back_pairs))  28 us
    ppermute x16, waiting for transfers between devices, both_ways(): forth = lax.ppermute(forth_value, 'expert', onward_pairs)  13.7 us
    ppermute x16, starting transfers between devices, both_ways(): return (forth, lax.ppermute(back_value, 'expert', back_pairs))  4.81 us
    ppermute x12, waiting for transfers between devices, swap_cores(): return lax.ppermute(value, 'tensor', [(0, 1), (1, 0)])  2.79 us
    ppermute x12, starting transfers between devices, swap_cores(): return lax.ppermute(value, 'tensor', [(0, 1), (1, 0)])  2.52 us
  transfers between devices with their start and end apart: 45, of which 30 were waited for; matrix products, arithmetic and copies ran while one was open for 0% of the time, Pallas kernels for 25%

profile of v4, /device:TPU:0, one launch (start us, length us, event | category | flops | bytes accessed | tf_op | source)
XLA Modules:
  0.0 122.8 jit_solution(14530341614441898845)
XLA Ops:
  1.1 2.6 %collective-permute-start = (bf16[128,1024]{1,0:T(8,128)(2,1)}, bf16[128,1024]{1,0:T(8,128)(2,1)S(1)}, u32[]{:S(2)}, u32[]{:S(2)}) collective-permute-start(bf16[128,1024]{1,0:T(8,128)(2,1)} %refs_12_.1), channel_id=1, source_target_pairs={{0,4},{4,8},{8,12},{12,14},{14,10},{10,6},{6,2},{2,0},{1,5},{5,9},... | collective-permute-start | bytes 786440 | tf_op jit(solution)/shard_map/onward_tok1/ppermute | solution.py:454
  7.2 2.1 %collective-permute-start.3 = (bf16[144,1024]{1,0:T(8,128)(2,1)S(1)}, bf16[144,1024]{1,0:T(8,128)(2,1)S(1)}, u32[]{:S(2)}, u32[]{:S(2)}) collective-permute-start(bf16[144,1024]{1,0:T(8,128)(2,1)S(1)} %shard_map.101.refs_0_.refs_10_), channel_id=1, source_target_pairs={{0,4},{4,8},{8,12},{12,14},{14,10},{10,6},{6,2},{2,0},{1,5},{5,9},... | collective-permute-start | bytes 884744 | tf_op jit(solution)/shard_map/onward_cot1/ppermute | solution.py:454
  9.3 1.8 %collective-permute-done.first.refs_2_.refs_6_ = bf16[128,1024]{1,0:T(8,128)(2,1)S(1)} collective-permute-done((bf16[128,1024]{1,0:T(8,128)(2,1)}, bf16[128,1024]{1,0:T(8,128)(2,1)S(1)}, u32[]{:S(2)}, u32[]{:S(2)}) %collective-permute-start) | collective-permute-done | bytes 262176 | tf_op jit(solution)/shard_map/onward_tok1/ppermute | solution.py:454
  11.1 2.0 %collective-permute-done.1.second.refs_3_.refs_7_ = bf16[128,1024]{1,0:T(8,128)(2,1)S(1)} collective-permute-done((bf16[128,1024]{1,0:T(8,128)(2,1)}, bf16[128,1024]{1,0:T(8,128)(2,1)S(1)}, u32[]{:S(2)}, u32[]{:S(2)}) %collective-permute-start.1) | collective-permute-done | bytes 262176 | tf_op jit(solution)/shard_map/back_tok1/ppermute | solution.py:456
  13.8 3.4 %collective-permute-done.3.first.refs_4_ = bf16[144,1024]{1,0:T(8,128)(2,1)S(1)} collective-permute-done((bf16[144,1024]{1,0:T(8,128)(2,1)S(1)}, bf16[144,1024]{1,0:T(8,128)(2,1)S(1)}, u32[]{:S(2)}, u32[]{:S(2)}) %collective-permute-start.3) | collective-permute-done | bytes 294944 | tf_op jit(solution)/shard_map/onward_cot1/ppermute | solution.py:454
  24.4 2.0 %shard_map.104 = (bf16[128,768]{1,0:T(8,128)(2,1)S(1)}, f32[128,768]{1,0:T(8,128)S(1)}, bf16[768,1024]{1,0:T(8,128)(2,1)S(1)}, bf16[1024,768]{1,0:T(8,128)(2,1)S(1)}, bf16[1024,768]{1,0:T(8,128)(2,1)S(1)}) custom-call(s32[3]{0:T(128)S(1)} %pad_add_fusion.scalars, bf16[384,2048]{1,0:T(8,128)(2,1)S(1)} %bitcast.13, ...), custom_call_target="tpu_custom_call" | custom-call | flops 4000000000 | tf_op jit(solution)/shard_map/pallas_call | solution.py:41
  26.4 2.8 %collective-permute-done.7.refs_2_.refs_8_ = bf16[128,1024]{1,0:T(8,128)(2,1)S(1)} collective-permute-done((bf16[128,1024]{1,0:T(8,128)(2,1)S(1)}, bf16[128,1024]{1,0:T(8,128)(2,1)S(1)}, u32[]{:S(2)}, u32[]{:S(2)}) %collective-permute-start.7) | collective-permute-done | bytes 262176 | tf_op jit(solution)/shard_map/onward_tok2/ppermute | solution.py:454
  30.8 2.1 %shard_map.105 = (bf16[128,1664]{1,0:T(8,128)(2,1)S(1)}, bf16[128,1024]{1,0:T(8,128)(2,1)S(1)}, bf16[768,1024]{1,0:T(8,128)(2,1)S(1)}, bf16[1024,768]{1,0:T(8,128)(2,1)S(1)}, bf16[1024,768]{1,0:T(8,128)(2,1)S(1)}) custom-call(s32[3]{0:T(128)S(1)} %pad_add_fusion.scalars, bf16[384,2048]{1,0:T(8,128)(2,1)S(1)} %bitcast.11, ...), custom_call_target="tpu_custom_call" | custom-call | flops 4000000000 | tf_op jit(solution)/shard_map/pallas_call | solution.py:41
  33.0 1.6 %collective-permute-start.16 = (bf16[128,1024]{1,0:T(8,128)(2,1)S(1)}, bf16[128,1024]{1,0:T(8,128)(2,1)S(1)}, u32[]{:S(2)}, u32[]{:S(2)}) collective-permute-start(bf16[128,1024]{1,0:T(8,128)(2,1)S(1)} %collective-permute-done.7.refs_2_.refs_8_), channel_id=1, source_target_pairs={{0,4},{4,8},{8,12},{12,14},{14,10},{10,6},{6,2},{2,0},{1,5},{5,9},... | collective-permute-start | bytes 786440 | tf_op jit(solution)/shard_map/onward_tok3/ppermute | solution.py:454
  37.3 1.6 %collective-permute-start.12 = (bf16[144,1024]{1,0:T(8,128)(2,1)S(1)}, bf16[144,1024]{1,0:T(8,128)(2,1)S(1)}, u32[]{:S(2)}, u32[]{:S(2)}) collective-permute-start(bf16[144,1024]{1,0:T(8,128)(2,1)S(1)} %collective-permute-done.4.refs_0_.refs_2_.refs_6_), channel_id=1, source_target_pairs={{0,4},{4,8},{8,12},{12,14},{14,10},{10,6},{6,2},{2,0},{1,5},{5,9},... | collective-permute-start | bytes 884744 | tf_op jit(solution)/shard_map/onward_cot3/ppermute | solution.py:454
  39.3 2.8 %collective-permute-done.16.refs_0_.refs_10_ = bf16[128,1024]{1,0:T(8,128)(2,1)S(1)} collective-permute-done((bf16[128,1024]{1,0:T(8,128)(2,1)S(1)}, bf16[128,1024]{1,0:T(8,128)(2,1)S(1)}, u32[]{:S(2)}, u32[]{:S(2)}) %collective-permute-start.16) | collective-permute-done | bytes 262176 | tf_op jit(solution)/shard_map/onward_tok3/ppermute | solution.py:454
  50.0 2.3 %collective-permute-start.13 = (bf16[80,1024]{1,0:T(8,128)(2,1)S(1)}, bf16[80,1024]{1,0:T(8,128)(2,1)S(1)}, u32[]{:S(2)}, u32[]{:S(2)}) collective-permute-start(bf16[80,1024]{1,0:T(8,128)(2,1)S(1)} %slice.26), channel_id=1, source_target_pairs={{0,4},{4,8},{8,12},{12,14},{14,10},{10,6},{6,2},{2,0},{1,5},{5,9},... | collective-permute-start | bytes 491528 | tf_op jit(solution)/shard_map/onward_cot4/ppermute | solution.py:454
  56.6 2.0 %collective-permute-done.15.second.refs_3_.refs_12_ = bf16[80,1024]{1,0:T(8,128)(2,1)S(1)} collective-permute-done((bf16[80,1024]{1,0:T(8,128)(2,1)S(1)}, bf16[80,1024]{1,0:T(8,128)(2,1)S(1)}, u32[]{:S(2)}, u32[]{:S(2)}) %collective-permute-start.15) | collective-permute-done | bytes 163872 | tf_op jit(solution)/shard_map/back_cot4/ppermute | solution.py:456
  65.1 1.7 %collective-permute-start.28 = (bf16[64,1024]{1,0:T(8,128)(2,1)S(1)}, bf16[64,1024]{1,0:T(8,128)(2,1)S(1)}, u32[]{:S(2)}, u32[]{:S(2)}) collective-permute-start(bf16[64,1024]{1,0:T(8,128)(2,1)S(1)} %get-tuple-element.117), channel_id=1, source_target_pairs={{0,4},{4,8},{8,12},{12,14},{14,10},{10,6},{6,2},{2,0},{1,5},{5,9},... | collective-permute-start | bytes 393224 | tf_op jit(solution)/shard_map/onward_mixed/ppermute | solution.py:454
  68.1 1.7 %collective-permute-start.30 = (bf16[80,1024]{1,0:T(8,128)(2,1)S(1)}, bf16[80,1024]{1,0:T(8,128)(2,1)S(1)}, u32[]{:S(2)}, u32[]{:S(2)}) collective-permute-start(bf16[80,1024]{1,0:T(8,128)(2,1)S(1)} %get-tuple-element.121), channel_id=1, source_target_pairs={{0,4},{4,8},{8,12},{12,14},{14,10},{10,6},{6,2},{2,0},{1,5},{5,9},... | collective-permute-start | bytes 491528 | tf_op jit(solution)/shard_map/onward_grad/ppermute | solution.py:454
  69.9 2.4 %shard_map.117 = (bf16[384,1024]{1,0:T(8,128)(2,1)S(1)}, bf16[384,1024]{1,0:T(8,128)(2,1)S(1)}) custom-call(s32[3]{0:T(128)S(1)} %pad_add_fusion.scalars, bf16[384,1664]{1,0:T(8,128)(2,1)S(1)} %shard_map.110.refs_0_.refs_2_.mine_ref, bf16[384,1664]{1,0:T(8,128)(2,1)S(1)} %collective-permute-done.26.refs_1_.refs_3_.arrived_ref, ...), custom_call_target="tpu_custom_call" | custom-call | flops 2000000000 | tf_op jit(solution)/shard_map/pallas_call | solution.py:41
  72.3 1.8 %collective-permute-done.29.refs_0_ = bf16[80,1024]{1,0:T(8,128)(2,1)S(1)} collective-permute-done((bf16[80,1024]{1,0:T(8,128)(2,1)S(1)}, bf16[80,1024]{1,0:T(8,128)(2,1)S(1)}, u32[]{:S(2)}, u32[]{:S(2)}) %collective-permute-start.29) | collective-permute-done | bytes 163872 | tf_op jit(solution)/shard_map/back_grad/ppermute | solution.py:456
  74.2 2.5 %shard_map.118 = (bf16[768,1024]{1,0:T(8,128)(2,1)S(1)}, bf16[768,1024]{1,0:T(8,128)(2,1)S(1)}) custom-call(s32[3]{0:T(128)S(1)} %pad_add_fusion.scalars, bf16[384,1024]{1,0:T(8,128)(2,1)S(1)} %get-tuple-element.123.refs_0_, bf16[384,1024]{1,0:T(8,128)(2,1)S(1)} %get-tuple-element.124.refs_1_, bf16[384,1664]{1,0:T(8,128)(2,1)S(1)} %shard_map.110.refs_0_.refs_2_.mine_ref, ...), custom_call_target="tpu_custom_call" | custom-call | flops 2000000000 | tf_op jit(solution)/shard_map/pallas_call | solution.py:41
  82.8 1.8 %collective-permute-start.32 = (bf16[128,1024]{1,0:T(8,128)(2,1)S(1)}, bf16[128,1024]{1,0:T(8,128)(2,1)S(1)}, u32[]{:S(2)}, u32[]{:S(2)}) collective-permute-start(bf16[128,1024]{1,0:T(8,128)(2,1)S(1)} %get-tuple-element.130), channel_id=1, source_target_pairs={{0,4},{4,8},{8,12},{12,14},{14,10},{10,6},{6,2},{2,0},{1,5},{5,9},... | collective-permute-start | bytes 786440 | tf_op jit(solution)/shard_map/onward_mixed/ppermute | solution.py:454
  84.8 1.8 %collective-permute-start.37 = (bf16[144,1024]{1,0:T(8,128)(2,1)S(1)}, bf16[144,1024]{1,0:T(8,128)(2,1)S(1)}, u32[]{:S(2)}, u32[]{:S(2)}) collective-permute-start(bf16[144,1024]{1,0:T(8,128)(2,1)S(1)} %get-tuple-element.134), channel_id=1, source_target_pairs={{0,4},{4,8},{8,12},{12,14},{14,10},{10,6},{6,2},{2,0},{1,5},{5,9},... | collective-permute-start | bytes 884744 | tf_op jit(solution)/shard_map/onward_grad/ppermute | solution.py:454
  86.6 5.1 %collective-permute-done.31.refs_0_ = bf16[128,1024]{1,0:T(8,128)(2,1)S(1)} collective-permute-done((bf16[128,1024]{1,0:T(8,128)(2,1)S(1)}, bf16[128,1024]{1,0:T(8,128)(2,1)S(1)}, u32[]{:S(2)}, u32[]{:S(2)}) %collective-permute-start.31) | collective-permute-done | bytes 262176 | tf_op jit(solution)/shard_map/back_mixed/ppermute | solution.py:456
  93.6 1.8 %collective-permute-start.35 = (bf16[128,1024]{1,0:T(8,128)(2,1)S(1)}, bf16[128,1024]{1,0:T(8,128)(2,1)S(1)}, u32[]{:S(2)}, u32[]{:S(2)}) collective-permute-start(bf16[128,1024]{1,0:T(8,128)(2,1)S(1)} %get-tuple-element.141), channel_id=1, source_target_pairs={{0,4},{4,8},{8,12},{12,14},{14,10},{10,6},{6,2},{2,0},{1,5},{5,9},... | collective-permute-start | bytes 786440 | tf_op jit(solution)/shard_map/onward_mixed/ppermute | solution.py:454
  95.4 2.6 %collective-permute-done.36.refs_0_ = bf16[144,1024]{1,0:T(8,128)(2,1)S(1)} collective-permute-done((bf16[144,1024]{1,0:T(8,128)(2,1)S(1)}, bf16[144,1024]{1,0:T(8,128)(2,1)S(1)}, u32[]{:S(2)}, u32[]{:S(2)}) %collective-permute-start.36) | collective-permute-done | bytes 294944 | tf_op jit(solution)/shard_map/back_grad/ppermute | solution.py:456
  99.9 1.8 %collective-permute-start.41 = (bf16[144,1024]{1,0:T(8,128)(2,1)S(1)}, bf16[144,1024]{1,0:T(8,128)(2,1)S(1)}, u32[]{:S(2)}, u32[]{:S(2)}) collective-permute-start(bf16[144,1024]{1,0:T(8,128)(2,1)S(1)} %get-tuple-element.145), channel_id=1, source_target_pairs={{0,4},{4,8},{8,12},{12,14},{14,10},{10,6},{6,2},{2,0},{1,5},{5,9},... | collective-permute-start | bytes 884744 | tf_op jit(solution)/shard_map/onward_grad/ppermute | solution.py:454
  101.7 1.9 %collective-permute-done.34.refs_0_ = bf16[128,1024]{1,0:T(8,128)(2,1)S(1)} collective-permute-done((bf16[128,1024]{1,0:T(8,128)(2,1)S(1)}, bf16[128,1024]{1,0:T(8,128)(2,1)S(1)}, u32[]{:S(2)}, u32[]{:S(2)}) %collective-permute-start.34) | collective-permute-done | bytes 262176 | tf_op jit(solution)/shard_map/back_mixed/ppermute | solution.py:456
  105.5 1.8 %collective-permute-start.39 = (bf16[128,1024]{1,0:T(8,128)(2,1)S(1)}, bf16[128,1024]{1,0:T(8,128)(2,1)S(1)}, u32[]{:S(2)}, u32[]{:S(2)}) collective-permute-start(bf16[128,1024]{1,0:T(8,128)(2,1)S(1)} %get-tuple-element.149), channel_id=1, source_target_pairs={{0,4},{4,8},{8,12},{12,14},{14,10},{10,6},{6,2},{2,0},{1,5},{5,9},... | collective-permute-start | bytes 786440 | tf_op jit(solution)/shard_map/onward_mixed/ppermute | solution.py:454
  107.3 2.6 %collective-permute-done.40.refs_0_ = bf16[144,1024]{1,0:T(8,128)(2,1)S(1)} collective-permute-done((bf16[144,1024]{1,0:T(8,128)(2,1)S(1)}, bf16[144,1024]{1,0:T(8,128)(2,1)S(1)}, u32[]{:S(2)}, u32[]{:S(2)}) %collective-permute-start.40) | collective-permute-done | bytes 294944 | tf_op jit(solution)/shard_map/back_grad/ppermute | solution.py:456
  112.0 1.7 %collective-permute-start.43 = (bf16[144,1024]{1,0:T(8,128)(2,1)S(1)}, bf16[144,1024]{1,0:T(8,128)(2,1)S(1)}, u32[]{:S(2)}, u32[]{:S(2)}) collective-permute-start(bf16[144,1024]{1,0:T(8,128)(2,1)S(1)} %get-tuple-element.153), channel_id=1, source_target_pairs={{0,4},{4,8},{8,12},{12,14},{14,10},{10,6},{6,2},{2,0},{1,5},{5,9},... | collective-permute-start | bytes 884744 | tf_op jit(solution)/shard_map/onward_grad/ppermute | solution.py:454
  113.7 1.9 %collective-permute-done.38.refs_0_ = bf16[128,1024]{1,0:T(8,128)(2,1)S(1)} collective-permute-done((bf16[128,1024]{1,0:T(8,128)(2,1)S(1)}, bf16[128,1024]{1,0:T(8,128)(2,1)S(1)}, u32[]{:S(2)}, u32[]{:S(2)}) %collective-permute-start.38) | collective-permute-done | bytes 262176 | tf_op jit(solution)/shard_map/back_mixed/ppermute | solution.py:456
  115.9 1.8 %shard_map.126 = bf16[128,1024]{1,0:T(8,128)(2,1)} custom-call(s32[3]{0:T(128)S(1)} %pad_add_fusion.scalars, bf16[128,1664]{1,0:T(8,128)(2,1)S(1)} %shard_map.114.mine_ref.refs_2_.refs_4_, bf16[128,1664]{1,0:T(8,128)(2,1)S(1)} %collective-permute-done.25.arrived_ref.refs_3_.refs_5_, bf16[768,1024]{1,0:T(8,128)(2,1)S(1)} %get-tuple-element.115.w_ref, ...), custom_call_target="tpu_custom_call" | custom-call | flops 2000000000 | tf_op jit(solution)/shard_map/pallas_call | solution.py:41
  117.7 2.1 %shard_map.127 = (f32[384,1024]{1,0:T(8,128)}, f32[384,1024]{1,0:T(8,128)}) custom-call(bf16[768,1024]{1,0:T(8,128)(2,1)S(1)} %get-tuple-element.156.refs_0_.refs_2_, bf16[768,1024]{1,0:T(8,128)(2,1)S(1)} %collective-permute-done.44.refs_1_.refs_3_, bf16[768,1024]{1,0:T(8,128)(2,1)S(1)} %get-tuple-element.156.refs_0_.refs_2_, ...), custom_call_target="tpu_custom_call" | custom-call | flops 1000000000 | tf_op jit(solution)/shard_map/pallas_call | solution.py:712
  120.8 1.8 %shard_map.128 = (bf16[128,1024]{1,0:T(8,128)(2,1)}, f32[4,128]{1,0:T(4,128)}) custom-call(s32[3]{0:T(128)S(1)} %pad_add_fusion.scalars, bf16[128,1664]{1,0:T(8,128)(2,1)S(1)} %shard_map.114.mine_ref.refs_2_.refs_4_, bf16[128,1664]{1,0:T(8,128)(2,1)S(1)} %collective-permute-done.25.arrived_ref.refs_3_.refs_5_, ...), custom_call_target="tpu_custom_call" | custom-call | flops 2000000000 | tf_op jit(solution)/shard_map/pallas_call | solution.py:41
  (109 shorter events, 51.8 us)
Async XLA Ops:
  0.6 18.1 %collective-permute-start.9 = (bf16[384,2048]{1,0:T(8,128)(2,1)}, bf16[384,2048]{1,0:T(8,128)(2,1)S(1)}, u32[]{:S(2)}, u32[]{:S(2)}) collective-permute-start(bf16[384,2048]{1,0:T(8,128)(2,1)} %bitcast.12), channel_id=1, source_target_pairs={{0,1},{1,0},{2,3},{3,2},{4,5},{5,4},{6,7},{7,6},{8,9},{9,8},{10,11... | collective-permute-start | bytes 4718600 | tf_op jit(solution)/shard_map/swap_weights/ppermute | solution.py:25
  1.1 10.0 %collective-permute-start = (bf16[128,1024]{1,0:T(8,128)(2,1)}, bf16[128,1024]{1,0:T(8,128)(2,1)S(1)}, u32[]{:S(2)}, u32[]{:S(2)}) collective-permute-start(bf16[128,1024]{1,0:T(8,128)(2,1)} %refs_12_.1), channel_id=1, source_target_pairs={{0,4},{4,8},{8,12},{12,14},{14,10},{10,6},{6,2},{2,0},{1,5},{5,9},... | collective-permute-start | bytes 786440 | tf_op jit(solution)/shard_map/onward_tok1/ppermute | solution.py:454
  3.8 9.4 %collective-permute-start.1 = (bf16[128,1024]{1,0:T(8,128)(2,1)}, bf16[128,1024]{1,0:T(8,128)(2,1)S(1)}, u32[]{:S(2)}, u32[]{:S(2)}) collective-permute-start(bf16[128,1024]{1,0:T(8,128)(2,1)} %refs_12_.1), channel_id=1, source_target_pairs={{4,0},{8,4},{12,8},{14,12},{10,14},{6,10},{2,6},{0,2},{5,1},{9,5},... | collective-permute-start | bytes 786440 | tf_op jit(solution)/shard_map/back_tok1/ppermute | solution.py:456
  7.2 10.0 %collective-permute-start.3 = (bf16[144,1024]{1,0:T(8,128)(2,1)S(1)}, bf16[144,1024]{1,0:T(8,128)(2,1)S(1)}, u32[]{:S(2)}, u32[]{:S(2)}) collective-permute-start(bf16[144,1024]{1,0:T(8,128)(2,1)S(1)} %shard_map.101.refs_0_.refs_10_), channel_id=1, source_target_pairs={{0,4},{4,8},{8,12},{12,14},{14,10},{10,6},{6,2},{2,0},{1,5},{5,9},... | collective-permute-start | bytes 884744 | tf_op jit(solution)/shard_map/onward_cot1/ppermute | solution.py:454
  9.2 9.4 %collective-permute-start.5 = (bf16[144,1024]{1,0:T(8,128)(2,1)S(1)}, bf16[144,1024]{1,0:T(8,128)(2,1)S(1)}, u32[]{:S(2)}, u32[]{:S(2)}) collective-permute-start(bf16[144,1024]{1,0:T(8,128)(2,1)S(1)} %shard_map.101.refs_0_.refs_10_), channel_id=1, source_target_pairs={{4,0},{8,4},{12,8},{14,12},{10,14},{6,10},{2,6},{0,2},{5,1},{9,5},... | collective-permute-start | bytes 884744 | tf_op jit(solution)/shard_map/back_cot1/ppermute | solution.py:456
  20.0 9.2 %collective-permute-start.7 = (bf16[128,1024]{1,0:T(8,128)(2,1)S(1)}, bf16[128,1024]{1,0:T(8,128)(2,1)S(1)}, u32[]{:S(2)}, u32[]{:S(2)}) collective-permute-start(bf16[128,1024]{1,0:T(8,128)(2,1)S(1)} %collective-permute-done.first.refs_2_.refs_6_), channel_id=1, source_target_pairs={{0,4},{4,8},{8,12},{12,14},{14,10},{10,6},{6,2},{2,0},{1,5},{5,9},... | collective-permute-start | bytes 786440 | tf_op jit(solution)/shard_map/onward_tok2/ppermute | solution.py:454
  21.6 9.2 %collective-permute-start.8 = (bf16[128,1024]{1,0:T(8,128)(2,1)S(1)}, bf16[128,1024]{1,0:T(8,128)(2,1)S(1)}, u32[]{:S(2)}, u32[]{:S(2)}) collective-permute-start(bf16[128,1024]{1,0:T(8,128)(2,1)S(1)} %collective-permute-done.1.second.refs_3_.refs_7_), channel_id=1, source_target_pairs={{4,0},{8,4},{12,8},{14,12},{10,14},{6,10},{2,6},{0,2},{5,1},{9,5},... | collective-permute-start | bytes 786440 | tf_op jit(solution)/shard_map/back_tok2/ppermute | solution.py:456
  22.1 13.0 %collective-permute-start.4 = (bf16[144,1024]{1,0:T(8,128)(2,1)S(1)}, bf16[144,1024]{1,0:T(8,128)(2,1)S(1)}, u32[]{:S(2)}, u32[]{:S(2)}) collective-permute-start(bf16[144,1024]{1,0:T(8,128)(2,1)S(1)} %collective-permute-done.3.first.refs_4_), channel_id=1, source_target_pairs={{0,4},{4,8},{8,12},{12,14},{14,10},{10,6},{6,2},{2,0},{1,5},{5,9},... | collective-permute-start | bytes 884744 | tf_op jit(solution)/shard_map/onward_cot2/ppermute | solution.py:454
  24.0 11.9 %collective-permute-start.6 = (bf16[144,1024]{1,0:T(8,128)(2,1)S(1)}, bf16[144,1024]{1,0:T(8,128)(2,1)S(1)}, u32[]{:S(2)}, u32[]{:S(2)}) collective-permute-start(bf16[144,1024]{1,0:T(8,128)(2,1)S(1)} %collective-permute-done.5.second.refs_5_), channel_id=1, source_target_pairs={{4,0},{8,4},{12,8},{14,12},{10,14},{6,10},{2,6},{0,2},{5,1},{9,5},... | collective-permute-start | bytes 884744 | tf_op jit(solution)/shard_map/back_cot2/ppermute | solution.py:456
  33.0 9.2 %collective-permute-start.16 = (bf16[128,1024]{1,0:T(8,128)(2,1)S(1)}, bf16[128,1024]{1,0:T(8,128)(2,1)S(1)}, u32[]{:S(2)}, u32[]{:S(2)}) collective-permute-start(bf16[128,1024]{1,0:T(8,128)(2,1)S(1)} %collective-permute-done.7.refs_2_.refs_8_), channel_id=1, source_target_pairs={{0,4},{4,8},{8,12},{12,14},{14,10},{10,6},{6,2},{2,0},{1,5},{5,9},... | collective-permute-start | bytes 786440 | tf_op jit(solution)/shard_map/onward_tok3/ppermute | solution.py:454
  34.6 9.1 %collective-permute-start.17 = (bf16[128,1024]{1,0:T(8,128)(2,1)S(1)}, bf16[128,1024]{1,0:T(8,128)(2,1)S(1)}, u32[]{:S(2)}, u32[]{:S(2)}) collective-permute-start(bf16[128,1024]{1,0:T(8,128)(2,1)S(1)} %collective-permute-done.8.refs_3_.refs_9_), channel_id=1, source_target_pairs={{4,0},{8,4},{12,8},{14,12},{10,14},{6,10},{2,6},{0,2},{5,1},{9,5},... | collective-permute-start | bytes 786440 | tf_op jit(solution)/shard_map/back_tok3/ppermute | solution.py:456
  37.3 10.7 %collective-permute-start.12 = (bf16[144,1024]{1,0:T(8,128)(2,1)S(1)}, bf16[144,1024]{1,0:T(8,128)(2,1)S(1)}, u32[]{:S(2)}, u32[]{:S(2)}) collective-permute-start(bf16[144,1024]{1,0:T(8,128)(2,1)S(1)} %collective-permute-done.4.refs_0_.refs_2_.refs_6_), channel_id=1, source_target_pairs={{0,4},{4,8},{8,12},{12,14},{14,10},{10,6},{6,2},{2,0},{1,5},{5,9},... | collective-permute-start | bytes 884744 | tf_op jit(solution)/shard_map/onward_cot3/ppermute | solution.py:454
  38.9 10.4 %collective-permute-start.14 = (bf16[144,1024]{1,0:T(8,128)(2,1)S(1)}, bf16[144,1024]{1,0:T(8,128)(2,1)S(1)}, u32[]{:S(2)}, u32[]{:S(2)}) collective-permute-start(bf16[144,1024]{1,0:T(8,128)(2,1)S(1)} %collective-permute-done.6.refs_1_.refs_3_.refs_7_), channel_id=1, source_target_pairs={{4,0},{8,4},{12,8},{14,12},{10,14},{6,10},{2,6},{0,2},{5,1},{9,5},... | collective-permute-start | bytes 884744 | tf_op jit(solution)/shard_map/back_cot3/ppermute | solution.py:456
  45.1 7.2 %collective-permute-start.20 = (bf16[128,1024]{1,0:T(8,128)(2,1)S(1)}, bf16[128,1024]{1,0:T(8,128)(2,1)S(1)}, u32[]{:S(2)}, u32[]{:S(2)}) collective-permute-start(bf16[128,1024]{1,0:T(8,128)(2,1)S(1)} %get-tuple-element.105), channel_id=1, source_target_pairs={{0,1},{1,0},{2,3},{3,2},{4,5},{5,4},{6,7},{7,6},{8,9},{9,8},{10,11... | collective-permute-start | bytes 786440 | tf_op jit(solution)/shard_map/swap_tok3/ppermute | solution.py:25
  45.2 9.7 %collective-permute-start.22 = (bf16[64,1024]{1,0:T(8,128)(2,1)S(1)}, bf16[64,1024]{1,0:T(8,128)(2,1)S(1)}, u32[]{:S(2)}, u32[]{:S(2)}) collective-permute-start(bf16[64,1024]{1,0:T(8,128)(2,1)S(1)} %slice.28), channel_id=1, source_target_pairs={{0,4},{4,8},{8,12},{12,14},{14,10},{10,6},{6,2},{2,0},{1,5},{5,9},... | collective-permute-start | bytes 393224 | tf_op jit(solution)/shard_map/onward_tok4/ppermute | solution.py:454
  46.7 8.2 %collective-permute-start.23 = (bf16[64,1024]{1,0:T(8,128)(2,1)S(1)}, bf16[64,1024]{1,0:T(8,128)(2,1)S(1)}, u32[]{:S(2)}, u32[]{:S(2)}) collective-permute-start(bf16[64,1024]{1,0:T(8,128)(2,1)S(1)} %slice.29), channel_id=1, source_target_pairs={{4,0},{8,4},{12,8},{14,12},{10,14},{6,10},{2,6},{0,2},{5,1},{9,5},... | collective-permute-start | bytes 393224 | tf_op jit(solution)/shard_map/back_tok4/ppermute | solution.py:456
  55.8 14.1 %collective-permute-start.26 = (bf16[384,1664]{1,0:T(8,128)(2,1)S(1)}, bf16[384,1664]{1,0:T(8,128)(2,1)S(1)}, u32[]{:S(2)}, u32[]{:S(2)}) collective-permute-start(bf16[384,1664]{1,0:T(8,128)(2,1)S(1)} %shard_map.110.refs_0_.refs_2_.mine_ref), channel_id=1, source_target_pairs={{0,1},{1,0},{2,3},{3,2},{4,5},{5,4},{6,7},{7,6},{8,9},{9,8},{10,11... | collective-permute-start | bytes 3833864 | tf_op jit(solution)/shard_map/swap_lefts/ppermute | solution.py:25
  64.8 7.5 %collective-permute-start.27 = (bf16[64,1024]{1,0:T(8,128)(2,1)S(1)}, bf16[64,1024]{1,0:T(8,128)(2,1)S(1)}, u32[]{:S(2)}, u32[]{:S(2)}) collective-permute-start(bf16[64,1024]{1,0:T(8,128)(2,1)S(1)} %get-tuple-element.116), channel_id=1, source_target_pairs={{4,0},{8,4},{12,8},{14,12},{10,14},{6,10},{2,6},{0,2},{5,1},{9,5},... | collective-permute-start | bytes 393224 | tf_op jit(solution)/shard_map/back_mixed/ppermute | solution.py:456
  65.1 7.2 %collective-permute-start.28 = (bf16[64,1024]{1,0:T(8,128)(2,1)S(1)}, bf16[64,1024]{1,0:T(8,128)(2,1)S(1)}, u32[]{:S(2)}, u32[]{:S(2)}) collective-permute-start(bf16[64,1024]{1,0:T(8,128)(2,1)S(1)} %get-tuple-element.117), channel_id=1, source_target_pairs={{0,4},{4,8},{8,12},{12,14},{14,10},{10,6},{6,2},{2,0},{1,5},{5,9},... | collective-permute-start | bytes 393224 | tf_op jit(solution)/shard_map/onward_mixed/ppermute | solution.py:454
  81.0 36.7 %collective-permute-start.44 = (bf16[768,1024]{1,0:T(8,128)(2,1)S(1)}, bf16[768,1024]{1,0:T(8,128)(2,1)S(1)}, u32[]{:S(2)}, u32[]{:S(2)}) collective-permute-start(bf16[768,1024]{1,0:T(8,128)(2,1)S(1)} %get-tuple-element.137), channel_id=1, source_target_pairs={{0,16},{16,0},{1,17},{17,1},{2,18},{18,2},{3,19},{19,3},{4,20},{20... | collective-permute-start | bytes 4718600 | tf_op jit(solution)/shard_map/ppermute | solution.py:685
  82.5 9.2 %collective-permute-start.31 = (bf16[128,1024]{1,0:T(8,128)(2,1)S(1)}, bf16[128,1024]{1,0:T(8,128)(2,1)S(1)}, u32[]{:S(2)}, u32[]{:S(2)}) collective-permute-start(bf16[128,1024]{1,0:T(8,128)(2,1)S(1)} %get-tuple-element.129), channel_id=1, source_target_pairs={{4,0},{8,4},{12,8},{14,12},{10,14},{6,10},{2,6},{0,2},{5,1},{9,5},... | collective-permute-start | bytes 786440 | tf_op jit(solution)/shard_map/back_mixed/ppermute | solution.py:456
  82.8 9.2 %collective-permute-start.32 = (bf16[128,1024]{1,0:T(8,128)(2,1)S(1)}, bf16[128,1024]{1,0:T(8,128)(2,1)S(1)}, u32[]{:S(2)}, u32[]{:S(2)}) collective-permute-start(bf16[128,1024]{1,0:T(8,128)(2,1)S(1)} %get-tuple-element.130), channel_id=1, source_target_pairs={{0,4},{4,8},{8,12},{12,14},{14,10},{10,6},{6,2},{2,0},{1,5},{5,9},... | collective-permute-start | bytes 786440 | tf_op jit(solution)/shard_map/onward_mixed/ppermute | solution.py:454
  84.6 13.5 %collective-permute-start.36 = (bf16[144,1024]{1,0:T(8,128)(2,1)S(1)}, bf16[144,1024]{1,0:T(8,128)(2,1)S(1)}, u32[]{:S(2)}, u32[]{:S(2)}) collective-permute-start(bf16[144,1024]{1,0:T(8,128)(2,1)S(1)} %get-tuple-element.133), channel_id=1, source_target_pairs={{4,0},{8,4},{12,8},{14,12},{10,14},{6,10},{2,6},{0,2},{5,1},{9,5},... | collective-permute-start | bytes 884744 | tf_op jit(solution)/shard_map/back_grad/ppermute | solution.py:456
  84.8 13.5 %collective-permute-start.37 = (bf16[144,1024]{1,0:T(8,128)(2,1)S(1)}, bf16[144,1024]{1,0:T(8,128)(2,1)S(1)}, u32[]{:S(2)}, u32[]{:S(2)}) collective-permute-start(bf16[144,1024]{1,0:T(8,128)(2,1)S(1)} %get-tuple-element.134), channel_id=1, source_target_pairs={{0,4},{4,8},{8,12},{12,14},{14,10},{10,6},{6,2},{2,0},{1,5},{5,9},... | collective-permute-start | bytes 884744 | tf_op jit(solution)/shard_map/onward_grad/ppermute | solution.py:454
  93.3 10.3 %collective-permute-start.34 = (bf16[128,1024]{1,0:T(8,128)(2,1)S(1)}, bf16[128,1024]{1,0:T(8,128)(2,1)S(1)}, u32[]{:S(2)}, u32[]{:S(2)}) collective-permute-start(bf16[128,1024]{1,0:T(8,128)(2,1)S(1)} %get-tuple-element.140), channel_id=1, source_target_pairs={{4,0},{8,4},{12,8},{14,12},{10,14},{6,10},{2,6},{0,2},{5,1},{9,5},... | collective-permute-start | bytes 786440 | tf_op jit(solution)/shard_map/back_mixed/ppermute | solution.py:456
  93.6 10.4 %collective-permute-start.35 = (bf16[128,1024]{1,0:T(8,128)(2,1)S(1)}, bf16[128,1024]{1,0:T(8,128)(2,1)S(1)}, u32[]{:S(2)}, u32[]{:S(2)}) collective-permute-start(bf16[128,1024]{1,0:T(8,128)(2,1)S(1)} %get-tuple-element.141), channel_id=1, source_target_pairs={{0,4},{4,8},{8,12},{12,14},{14,10},{10,6},{6,2},{2,0},{1,5},{5,9},... | collective-permute-start | bytes 786440 | tf_op jit(solution)/shard_map/onward_mixed/ppermute | solution.py:454
  99.7 10.3 %collective-permute-start.40 = (bf16[144,1024]{1,0:T(8,128)(2,1)S(1)}, bf16[144,1024]{1,0:T(8,128)(2,1)S(1)}, u32[]{:S(2)}, u32[]{:S(2)}) collective-permute-start(bf16[144,1024]{1,0:T(8,128)(2,1)S(1)} %get-tuple-element.144), channel_id=1, source_target_pairs={{4,0},{8,4},{12,8},{14,12},{10,14},{6,10},{2,6},{0,2},{5,1},{9,5},... | collective-permute-start | bytes 884744 | tf_op jit(solution)/shard_map/back_grad/ppermute | solution.py:456
  99.9 10.4 %collective-permute-start.41 = (bf16[144,1024]{1,0:T(8,128)(2,1)S(1)}, bf16[144,1024]{1,0:T(8,128)(2,1)S(1)}, u32[]{:S(2)}, u32[]{:S(2)}) collective-permute-start(bf16[144,1024]{1,0:T(8,128)(2,1)S(1)} %get-tuple-element.145), channel_id=1, source_target_pairs={{0,4},{4,8},{8,12},{12,14},{14,10},{10,6},{6,2},{2,0},{1,5},{5,9},... | collective-permute-start | bytes 884744 | tf_op jit(solution)/shard_map/onward_grad/ppermute | solution.py:454
  105.3 10.3 %collective-permute-start.38 = (bf16[128,1024]{1,0:T(8,128)(2,1)S(1)}, bf16[128,1024]{1,0:T(8,128)(2,1)S(1)}, u32[]{:S(2)}, u32[]{:S(2)}) collective-permute-start(bf16[128,1024]{1,0:T(8,128)(2,1)S(1)} %get-tuple-element.148), channel_id=1, source_target_pairs={{4,0},{8,4},{12,8},{14,12},{10,14},{6,10},{2,6},{0,2},{5,1},{9,5},... | collective-permute-start | bytes 786440 | tf_op jit(solution)/shard_map/back_mixed/ppermute | solution.py:456
  105.5 10.4 %collective-permute-start.39 = (bf16[128,1024]{1,0:T(8,128)(2,1)S(1)}, bf16[128,1024]{1,0:T(8,128)(2,1)S(1)}, u32[]{:S(2)}, u32[]{:S(2)}) collective-permute-start(bf16[128,1024]{1,0:T(8,128)(2,1)S(1)} %get-tuple-element.149), channel_id=1, source_target_pairs={{0,4},{4,8},{8,12},{12,14},{14,10},{10,6},{6,2},{2,0},{1,5},{5,9},... | collective-permute-start | bytes 786440 | tf_op jit(solution)/shard_map/onward_mixed/ppermute | solution.py:454
  111.6 9.2 %collective-permute-start.42 = (bf16[144,1024]{1,0:T(8,128)(2,1)S(1)}, bf16[144,1024]{1,0:T(8,128)(2,1)S(1)}, u32[]{:S(2)}, u32[]{:S(2)}) collective-permute-start(bf16[144,1024]{1,0:T(8,128)(2,1)S(1)} %get-tuple-element.152), channel_id=1, source_target_pairs={{4,0},{8,4},{12,8},{14,12},{10,14},{6,10},{2,6},{0,2},{5,1},{9,5},... | collective-permute-start | bytes 884744 | tf_op jit(solution)/shard_map/back_grad/ppermute | solution.py:456
  112.0 8.8 %collective-permute-start.43 = (bf16[144,1024]{1,0:T(8,128)(2,1)S(1)}, bf16[144,1024]{1,0:T(8,128)(2,1)S(1)}, u32[]{:S(2)}, u32[]{:S(2)}) collective-permute-start(bf16[144,1024]{1,0:T(8,128)(2,1)S(1)} %get-tuple-element.153), channel_id=1, source_target_pairs={{0,4},{4,8},{8,12},{12,14},{14,10},{10,6},{6,2},{2,0},{1,5},{5,9},... | collective-permute-start | bytes 884744 | tf_op jit(solution)/shard_map/onward_grad/ppermute | solution.py:454
  (21 other events, 97.1 us)

commit v5 on v4

--- a/solution.py
+++ b/solution.py
@@ -37,15 +37,13 @@
     return lax.dot_general(left, right, (((0,), (0,)), ((), ())), preferred_element_type=F32)
 
 
-def call(kernel, out_shape, operands, scalars, work=4 * 10**9, unmoved=0, scratch=()):
+def call(kernel, out_shape, operands, scalars, work=4 * 10**9):
     return pl.pallas_call(
         kernel,
         out_shape=out_shape,
         in_specs=[pl.BlockSpec(memory_space=pltpu.SMEM)]
-        + [pl.BlockSpec(memory_space=pltpu.HBM)] * unmoved
-        + [pl.BlockSpec(memory_space=pltpu.VMEM)] * (len(operands) - unmoved),
+        + [pl.BlockSpec(memory_space=pltpu.VMEM)] * len(operands),
         out_specs=[pl.BlockSpec(memory_space=pltpu.VMEM)] * len(out_shape),
-        scratch_shapes=list(scratch),
         compiler_params=pltpu.CompilerParams(vmem_limit_bytes=VMEM_LIMIT),
         cost_estimate=pl.CostEstimate(flops=work, bytes_accessed=0, transcendentals=0),
     )(scalars, *operands)
@@ -119,7 +117,7 @@
     return [lanes & (line == i * deep + expert // per_row) for i in range(3)]
 
 
-def payload_kernel(experts, scalars, routes_hbm, gates_hbm, cotangent_hbm, out_ref, routes_ref, gates_ref, sems):
+def payload_kernel(experts, routes_hbm, gates_hbm, cotangent_hbm, out_ref, routes_ref, gates_ref, sems):
     rows, width = cotangent_hbm.shape
     half = rows // 2
     copies = [
@@ -188,10 +186,6 @@
     out_ref[half:rows, :] = picked(core, second[half + EXTRA :, :], first[half + EXTRA :, :])
     for copy in copies:
         copy.wait()
-
-
-def pick_kernel(scalars, first, second, out_ref):
-    out_ref[...] = picked(scalars[0], second[...], first[...])
 
 
 def taken(kinds, refs):
@@ -307,24 +301,9 @@
 def return_kernel(kind, at, first_row, count, experts, rows, scalars, mine_ref, arrived_ref, w_ref, *refs):
     core, expert = scalars[0], scalars[1]
     units, width = w_ref.shape
-    if kind == "far":
-        lanes = slice(at, at + units + (LANES if at else 0))
-        mine_all = mine_ref[first_row : first_row + count, lanes]
-        arrived_all = arrived_ref[first_row : first_row + count, lanes]
-    else:
-        mine_here, arrived_here, w_here, sems = refs[-4:]
-        refs = refs[:-4]
-        window = (pl.ds(first_row, count), pl.ds(at, mine_here.shape[1]))
-        copies = [
-            pltpu.make_async_copy(mine_ref.at[window], mine_here, sems.at[0]),
-            pltpu.make_async_copy(arrived_ref.at[window], arrived_here, sems.at[1]),
-            pltpu.make_async_copy(w_ref, w_here, sems.at[2]),
-        ]
-        for copy in copies:
-            copy.start()
-        for copy in copies:
-            copy.wait()
-        mine_all, arrived_all, w_ref = mine_here[...], arrived_here[...], w_here
+    lanes = slice(at, at + units + (LANES if at else 0))
+    mine_all = mine_ref[first_row : first_row + count, lanes]
+    arrived_all = arrived_ref[first_row : first_row + count, lanes]
     mine, arrived = mine_all[:, :units], arrived_all[:, :units]
     both = jnp.concatenate([picked(core, mine, arrived), picked(core, arrived, mine)], axis=0)
     part = dot_width(both, w_ref[...])
@@ -427,9 +406,19 @@
         kept_ref[...] = came_ref[...]
 
 
-def add_kernel(*refs):
-    for i in range(2):
-        refs[4 + i][...] = refs[2 * i][...].astype(F32) + refs[2 * i + 1][...].astype(F32)
+def add_kernel(kept_ref, came_ref, first_hbm, second_hbm, held_ref, sems):
+    tiles, rows = held_ref.shape[0], held_ref.shape[1]
+    copies = []
+    for i in range(tiles):
+        at = slice(i * rows, (i + 1) * rows)
+        held_ref[i] = kept_ref[at, :].astype(F32) + came_ref[at, :].astype(F32)
+        out = first_hbm if i < tiles // 2 else second_hbm
+        start = (i % (tiles // 2)) * rows
+        copy = pltpu.make_async_copy(held_ref.at[i], out.at[pl.ds(start, rows), :], sems.at[i])
+        copy.start()
+        copies.append(copy)
+    for copy in copies:
+        copy.wait()
 
 
 def per_device(tokens, routes, gates, w_in, w_out, cotangent):
@@ -455,7 +444,9 @@
         with jax.named_scope("back_" + name):
             return forth, lax.ppermute(back_value, "expert", back_pairs)
 
-    scalars = jnp.stack([core, place, (core + group) % 2]).astype(jnp.int32)
+    first_core = lax.optimization_barrier(core == 0)
+    core_now = jnp.where(first_core, 0, 1)
+    scalars = jnp.stack([core_now, place, (core + group) % 2]).astype(jnp.int32)
 
     weight_shapes = [
         jax.ShapeDtypeStruct((units, width), BF16),
@@ -525,22 +516,12 @@
             shapes = [jax.ShapeDtypeStruct((count + extra, width), BF16)] * 2
         kernel = functools.partial(return_kernel, kind, at, first_row, count, experts, rows)
         operands = [mine, arrived, weights, *sums, *more]
-        if kind == "far":
-            return call(kernel, shapes, operands, scalars, 3 * 10**9)
-        held = (count, units + (LANES if at else 0))
-        scratch = [
-            pltpu.VMEM(held, BF16),
-            pltpu.VMEM(held, BF16),
-            pltpu.VMEM((units, width), BF16),
-            pltpu.SemaphoreType.DMA((3,)),
-        ]
-        return call(kernel, shapes, operands, scalars, 2 * 10**9, 3, scratch)
+        return call(kernel, shapes, operands, scalars, 22 * 10**8)
 
     payload = pl.pallas_call(
         functools.partial(payload_kernel, experts),
         out_shape=jax.ShapeDtypeStruct((rows + EXTRA, width), BF16),
-        in_specs=[pl.BlockSpec(memory_space=pltpu.SMEM)]
-        + [pl.BlockSpec(memory_space=pltpu.HBM)] * 3,
+        in_specs=[pl.BlockSpec(memory_space=pltpu.HBM)] * 3,
         out_specs=pl.BlockSpec(memory_space=pltpu.VMEM),
         scratch_shapes=[
             pltpu.VMEM(routes.shape[::-1], jnp.int32),
@@ -549,8 +530,9 @@
         ],
         compiler_params=pltpu.CompilerParams(vmem_limit_bytes=VMEM_LIMIT),
         cost_estimate=pl.CostEstimate(flops=10**9, bytes_accessed=0, transcendentals=0),
-    )(scalars, routes.T, gates.T, cotangent)
-    ring = [both_ways(tokens, tokens, "tok1"), both_ways(payload, payload, "cot1")]
+    )(routes.T, gates.T, cotangent)
+    tokens_now = tied((tokens,), (scalars,))[0]
+    ring = [both_ways(tokens_now, tokens_now, "tok1"), both_ways(payload, payload, "cot1")]
 
     in_all, out_all = (w_in, swap_cores(w_in, "weights")), ()
 
@@ -613,8 +595,7 @@
         elif turn == 1:
             sent = cot_sent
         elif sent is None:
-            shape = [jax.ShapeDtypeStruct(now[0].shape, BF16)]
-            sent = call(pick_kernel, shape, [*now], scalars, 10**8)[0]
+            sent = jnp.where(first_core, now[1], now[0])
         if step < steps - 1:
             ring.append(both_ways(now[0], now[1], name + str(step + 1)))
         elif step == steps - 1:
@@ -635,13 +616,7 @@
     ends = backward(cot_pieces, out_all, hidden, slope)[0][0]
     ends_arrived = swap_cores(ends, "ends")
 
-    sent = returned("far", 0, half, ends, ends_arrived, out_all[0], ())
-    mixed_in = both_ways(sent[1], sent[0], "mixed")[::-1]
-    ends_after = tied((ends_arrived,), sent)[0]
-    sent = returned("far", units, half, ends, ends_after, in_all[0], ())
-    back_in = both_ways(sent[1], sent[0], "grad")[::-1]
-
-    def weight_part(at, which, after, above):
+    def weight_part(at, which, above, after):
         operands = [*above, lefts, lefts_arrived, ends, tied((ends_arrived,), after)[0]]
         for s in range(steps - 1):
             operands += arrivals[2 * s + which][:2]
@@ -656,77 +631,92 @@
             2 * 10**9,
         )
 
-    part_out = weight_part(0, 1, sent, ())
-    parts, parts_other = weight_part(units, 0, (*part_out, *mixed_in, *back_in), part_out)
-    parts_other = swap_cores(parts_other, "grad")
-    for step in range(steps - 1, 0, -1):
+    def over_groups(mine, other):
+        if n_dp == 2:
+            block = pl.BlockSpec((units // 4, width), lambda i: (i, 0))
+            sent, kept = pl.pallas_call(
+                send_kernel,
+                grid=(4,),
+                out_shape=[jax.ShapeDtypeStruct(mine.shape, BF16)] * 2,
+                in_specs=[pl.BlockSpec(memory_space=pltpu.SMEM), block, block],
+                out_specs=[block] * 2,
+                compiler_params=pltpu.CompilerParams(vmem_limit_bytes=VMEM_LIMIT),
+                cost_estimate=pl.CostEstimate(flops=10**9, bytes_accessed=0, transcendentals=0),
+            )(scalars, mine, other)
+            with jax.named_scope("groups"):
+                return (sent,), kept, lax.ppermute(sent, "dp", [(0, 1), (1, 0)])
+        part = jnp.concatenate([picked(core, mine, other), picked(core, other, mine)], axis=1)
+        across = part.shape[1] // n_dp
+        slices = [
+            lax.dynamic_slice_in_dim(part, ((group + shift) % n_dp) * across, across, axis=1)
+            for shift in range(n_dp)
+        ]
+        total = 0.0
+        for shift in range(1, n_dp):
+            pairs = [(i, (i + shift) % n_dp) for i in range(n_dp)]
+            total = total + lax.ppermute(slices[shift], "dp", pairs).astype(F32)
+        return (), slices[0], total
+
+    def summed(kept, came):
+        if n_dp != 2:
+            total = kept.astype(F32) + came
+            return total[:local_units], total[local_units:]
+        tiles = 8
+        return pl.pallas_call(
+            add_kernel,
+            out_shape=[jax.ShapeDtypeStruct((local_units, width), F32)] * 2,
+            in_specs=[pl.BlockSpec(memory_space=pltpu.VMEM)] * 2,
+            out_specs=[pl.BlockSpec(memory_space=pl.ANY)] * 2,
+            scratch_shapes=[
+                pltpu.VMEM((tiles, units // tiles, width), F32),
+                pltpu.SemaphoreType.DMA((tiles,)),
+            ],
+            compiler_params=pltpu.CompilerParams(vmem_limit_bytes=VMEM_LIMIT),
+            cost_estimate=pl.CostEstimate(flops=10**9, bytes_accessed=0, transcendentals=0),
+        )(kept, came)
+
+    def mixed_far(after):
+        came = tied((ends_arrived,), after)[0]
+        sent = returned("far", 0, half, ends, came, out_all[0], ())
+        return sent, both_ways(sent[1], sent[0], "mixed")[::-1]
+
+    def back_far(after):
+        came = tied((ends_arrived,), after)[0]
+        sent = returned("far", units, half, ends, came, in_all[0], ())
+        return sent, both_ways(sent[1], sent[0], "grad")[::-1]
+
+    def mixed_step(step, sums, after):
         kind = "join" if step == steps - 1 else "add"
         line = (step - 1) * rows
-        mixed_in = tied(mixed_in, (*sent, *((parts,) if kind == "join" else ())))
-        sent = returned(kind, 0, line, lefts, lefts_arrived, out_all[0], mixed_in)
-        mixed_in = both_ways(sent[1], sent[0], "mixed")[::-1]
-        back_in = tied(back_in, sent)
-        sent = returned(kind, units, line, lefts, lefts_arrived, in_all[0], back_in)
-        back_in = both_ways(sent[1], sent[0], "grad")[::-1]
-        if kind == "join":
-            parts_other = tied((parts_other,), sent)[0]
-            if n_dp == 2:
-                tile = units // 4
-                block = pl.BlockSpec((tile, width), lambda i: (i, 0))
-                parts_sent, parts_kept = pl.pallas_call(
-                    send_kernel,
-                    grid=(4,),
-                    out_shape=[jax.ShapeDtypeStruct(parts.shape, BF16)] * 2,
-                    in_specs=[pl.BlockSpec(memory_space=pltpu.SMEM), block, block],
-                    out_specs=[block] * 2,
-                    compiler_params=pltpu.CompilerParams(vmem_limit_bytes=VMEM_LIMIT),
-                    cost_estimate=pl.CostEstimate(flops=10**9, bytes_accessed=0, transcendentals=0),
-                )(scalars, parts, parts_other)
-                parts_came = lax.ppermute(parts_sent, "dp", [(0, 1), (1, 0)])
-            else:
-                totals = []
-                for i in range(2):
-                    piece = slice(i * local_units, (i + 1) * local_units)
-                    mine, arrived = parts[piece], parts_other[piece]
-                    part = jnp.concatenate(
-                        [picked(core, mine, arrived), picked(core, arrived, mine)], axis=1
-                    )
-                    across = part.shape[1] // n_dp
-                    slices = [
-                        lax.dynamic_slice_in_dim(part, ((group + shift) % n_dp) * across, across, axis=1)
-                        for shift in range(n_dp)
-                    ]
-                    total = slices[0].astype(F32)
-                    for shift in range(1, n_dp):
-                        pairs = [(i, (i + shift) % n_dp) for i in range(n_dp)]
-                        total = total + lax.ppermute(slices[shift], "dp", pairs).astype(F32)
-                    totals.append(total)
-            if n_dp == 2:
-                sent = (*sent, parts_sent)
-    mixed_in = tied(mixed_in, sent)
-    if n_dp == 2:
-        tiles = 3 if local_units % 48 == 0 else 1
-        block = (local_units // tiles, width)
-        upper = pl.BlockSpec(block, lambda i: (i, 0))
-        lower = pl.BlockSpec(block, lambda i: (i + tiles, 0))
-        totals = pl.pallas_call(
-            add_kernel,
-            grid=(tiles,),
-            out_shape=[jax.ShapeDtypeStruct((local_units, width), F32)] * 2,
-            in_specs=[upper] * 2 + [lower] * 2,
-            out_specs=[upper] * 2,
-            compiler_params=pltpu.CompilerParams(vmem_limit_bytes=VMEM_LIMIT),
-            cost_estimate=pl.CostEstimate(flops=10**9, bytes_accessed=0, transcendentals=0),
-        )(*([parts_kept, parts_came] * 2))
-    back_in = tied(back_in, totals)
-    mixed = returned("own", 0, 0, ends, ends_arrived, out_all[0], mixed_in)[0]
+        sums = tied(sums, after)
+        sent = returned(kind, 0, line, lefts, lefts_arrived, out_all[0], sums)
+        return sent, both_ways(sent[1], sent[0], "mixed")[::-1]
+
+    def back_step(step, sums, after):
+        kind = "join" if step == steps - 1 else "add"
+        line = (step - 1) * rows
+        sums = tied(sums, after)
+        sent = returned(kind, units, line, lefts, lefts_arrived, in_all[0], sums)
+        return sent, both_ways(sent[1], sent[0], "grad")[::-1]
+
+    part_out = weight_part(0, 1, (), ())
+    parts, parts_other = weight_part(units, 0, part_out, ())
+    parts_other = swap_cores(parts_other, "grad")
+    sent, mixed_in = mixed_far((parts,))
+    sent, back_in = back_far(sent)
+    sent, mixed_in = mixed_step(steps - 1, mixed_in, sent)
+    parts_sent, kept, came = over_groups(parts, tied((parts_other,), sent)[0])
+    sent, back_in = back_step(steps - 1, back_in, (*sent, *parts_sent))
+    for step in range(steps - 2, 0, -1):
+        sent, mixed_in = mixed_step(step, mixed_in, sent)
+        sent, back_in = back_step(step, back_in, sent)
+    own = (0, ends, ends_arrived)
+    mixed = returned("own", 0, *own, out_all[0], tied(mixed_in, sent))[0]
     grad_tokens, grad_gates = returned(
-        "own", units, 0, ends, ends_arrived, in_all[0], back_in, (routes.T,)
+        "own", units, *own, in_all[0], tied(back_in, (mixed,)), (routes.T,)
     )
-    grad_gates = grad_gates.T
-
-    grad_out, grad_in = totals
-    return (mixed, grad_tokens, grad_gates, grad_in[None], grad_out[None])
+    grad_out, grad_in = summed(kept, tied((came,), (grad_tokens,))[0])
+    return (mixed, grad_tokens, grad_gates.T, grad_in[None], grad_out[None])
 
 
 def solution(mesh):

time: 123 us -> 118 us (0.959)
  Pallas kernels: 36.7 us -> 32.9 us
  waiting for transfers between devices: 44.5 us -> 42.9 us
    pallas_call x24 -> x21, Pallas kernels: 32.1 us -> 29.1 us  [call(): pl.pallas_call(kernel, out_shape=out_shape, in_specs=[pl.BlockSpec(memory...]
    ppermute x16, waiting for transfers between devices: 28 us -> 26.6 us  [both_ways(): return (forth, lax.ppermute(back_value, 'expert', back_pairs))]
  transfers between devices with their start and end apart: 45 -> 45, of which waited for: 30 -> 30; matrix products, arithmetic and copies ran while one was open for 0% -> 0% of each run, Pallas kernels for 25% -> 22%
where the time goes in v5:
time: 118 us
  waiting for transfers between devices  42.9 us (36%)
  starting transfers between devices  38.4 us (33%)
  Pallas kernels  32.9 us (28%)
  local copies, waits for them, and re-layouts  2.41 us (2%)
    pallas_call x21, Pallas kernels, call(): pl.pallas_call(kernel, out_shape=out_shape, in_specs=[pl.BlockSpec(memory...  29.1 us
    ppermute x16, starting transfers between devices, both_ways(): forth = lax.ppermute(forth_value, 'expert', onward_pairs)  28.3 us
    ppermute x16, waiting for transfers between devices, both_ways(): return (forth, lax.ppermute(back_value, 'expert', back_pairs))  26.6 us
    ppermute x16, waiting for transfers between devices, both_ways(): forth = lax.ppermute(forth_value, 'expert', onward_pairs)  14.2 us
    ppermute x16, starting transfers between devices, both_ways(): return (forth, lax.ppermute(back_value, 'expert', back_pairs))  5.72 us
    ppermute x12, starting transfers between devices, swap_cores(): return lax.ppermute(value, 'tensor', [(0, 1), (1, 0)])  2.86 us
  transfers between devices with their start and end apart: 45, of which 30 were waited for; matrix products, arithmetic and copies ran while one was open for 0% of the time, Pallas kernels for 22%

profile of v5, /device:TPU:0, one launch (start us, length us, event | category | flops | bytes accessed | tf_op | source)
XLA Modules:
  0.0 117.9 jit_solution(11943373357886265705)
XLA Ops:
  1.2 2.6 %collective-permute-start = (bf16[128,1024]{1,0:T(8,128)(2,1)}, bf16[128,1024]{1,0:T(8,128)(2,1)S(1)}, u32[]{:S(2)}, u32[]{:S(2)}) collective-permute-start(bf16[128,1024]{1,0:T(8,128)(2,1)} %refs_12_.1), channel_id=1, source_target_pairs={{0,4},{4,8},{8,12},{12,14},{14,10},{10,6},{6,2},{2,0},{1,5},{5,9},... | collective-permute-start | bytes 786440 | tf_op jit(solution)/shard_map/onward_tok1/ppermute | solution.py:443
  6.6 2.1 %collective-permute-start.3 = (bf16[144,1024]{1,0:T(8,128)(2,1)S(1)}, bf16[144,1024]{1,0:T(8,128)(2,1)S(1)}, u32[]{:S(2)}, u32[]{:S(2)}) collective-permute-start(bf16[144,1024]{1,0:T(8,128)(2,1)S(1)} %shard_map.101.refs_0_.refs_10_), channel_id=1, source_target_pairs={{0,4},{4,8},{8,12},{12,14},{14,10},{10,6},{6,2},{2,0},{1,5},{5,9},... | collective-permute-start | bytes 884744 | tf_op jit(solution)/shard_map/onward_cot1/ppermute | solution.py:443
  8.7 2.5 %collective-permute-done.first.refs_2_.refs_6_ = bf16[128,1024]{1,0:T(8,128)(2,1)S(1)} collective-permute-done((bf16[128,1024]{1,0:T(8,128)(2,1)}, bf16[128,1024]{1,0:T(8,128)(2,1)S(1)}, u32[]{:S(2)}, u32[]{:S(2)}) %collective-permute-start) | collective-permute-done | bytes 262176 | tf_op jit(solution)/shard_map/onward_tok1/ppermute | solution.py:443
  11.1 2.0 %collective-permute-done.1.second.refs_3_.refs_7_ = bf16[128,1024]{1,0:T(8,128)(2,1)S(1)} collective-permute-done((bf16[128,1024]{1,0:T(8,128)(2,1)}, bf16[128,1024]{1,0:T(8,128)(2,1)S(1)}, u32[]{:S(2)}, u32[]{:S(2)}) %collective-permute-start.1) | collective-permute-done | bytes 262176 | tf_op jit(solution)/shard_map/back_tok1/ppermute | solution.py:445
  13.8 3.5 %collective-permute-done.3.first.refs_4_ = bf16[144,1024]{1,0:T(8,128)(2,1)S(1)} collective-permute-done((bf16[144,1024]{1,0:T(8,128)(2,1)S(1)}, bf16[144,1024]{1,0:T(8,128)(2,1)S(1)}, u32[]{:S(2)}, u32[]{:S(2)}) %collective-permute-start.3) | collective-permute-done | bytes 294944 | tf_op jit(solution)/shard_map/onward_cot1/ppermute | solution.py:443
  24.5 1.9 %shard_map.104 = (bf16[128,768]{1,0:T(8,128)(2,1)S(1)}, f32[128,768]{1,0:T(8,128)S(1)}, bf16[768,1024]{1,0:T(8,128)(2,1)S(1)}, bf16[1024,768]{1,0:T(8,128)(2,1)S(1)}, bf16[1024,768]{1,0:T(8,128)(2,1)S(1)}) custom-call(s32[3]{0:T(128)S(1)} %pad_add_fusion.scalars, bf16[384,2048]{1,0:T(8,128)(2,1)S(1)} %bitcast.13, ...), custom_call_target="tpu_custom_call" | custom-call | flops 4000000000 | tf_op jit(solution)/shard_map/pallas_call | solution.py:41
  26.5 2.8 %collective-permute-done.7.refs_2_.refs_8_ = bf16[128,1024]{1,0:T(8,128)(2,1)S(1)} collective-permute-done((bf16[128,1024]{1,0:T(8,128)(2,1)S(1)}, bf16[128,1024]{1,0:T(8,128)(2,1)S(1)}, u32[]{:S(2)}, u32[]{:S(2)}) %collective-permute-start.7) | collective-permute-done | bytes 262176 | tf_op jit(solution)/shard_map/onward_tok2/ppermute | solution.py:443
  29.3 1.6 %collective-permute-done.8.refs_3_.refs_9_ = bf16[128,1024]{1,0:T(8,128)(2,1)S(1)} collective-permute-done((bf16[128,1024]{1,0:T(8,128)(2,1)S(1)}, bf16[128,1024]{1,0:T(8,128)(2,1)S(1)}, u32[]{:S(2)}, u32[]{:S(2)}) %collective-permute-start.8) | collective-permute-done | bytes 262176 | tf_op jit(solution)/shard_map/back_tok2/ppermute | solution.py:445
  30.9 2.1 %shard_map.105 = (bf16[128,1664]{1,0:T(8,128)(2,1)S(1)}, bf16[128,1024]{1,0:T(8,128)(2,1)S(1)}, bf16[768,1024]{1,0:T(8,128)(2,1)S(1)}, bf16[1024,768]{1,0:T(8,128)(2,1)S(1)}, bf16[1024,768]{1,0:T(8,128)(2,1)S(1)}) custom-call(s32[3]{0:T(128)S(1)} %pad_add_fusion.scalars, bf16[384,2048]{1,0:T(8,128)(2,1)S(1)} %bitcast.11, ...), custom_call_target="tpu_custom_call" | custom-call | flops 4000000000 | tf_op jit(solution)/shard_map/pallas_call | solution.py:41
  33.0 1.6 %collective-permute-start.16 = (bf16[128,1024]{1,0:T(8,128)(2,1)S(1)}, bf16[128,1024]{1,0:T(8,128)(2,1)S(1)}, u32[]{:S(2)}, u32[]{:S(2)}) collective-permute-start(bf16[128,1024]{1,0:T(8,128)(2,1)S(1)} %collective-permute-done.7.refs_2_.refs_8_), channel_id=1, source_target_pairs={{0,4},{4,8},{8,12},{12,14},{14,10},{10,6},{6,2},{2,0},{1,5},{5,9},... | collective-permute-start | bytes 786440 | tf_op jit(solution)/shard_map/onward_tok3/ppermute | solution.py:443
  37.3 1.6 %collective-permute-start.12 = (bf16[144,1024]{1,0:T(8,128)(2,1)S(1)}, bf16[144,1024]{1,0:T(8,128)(2,1)S(1)}, u32[]{:S(2)}, u32[]{:S(2)}) collective-permute-start(bf16[144,1024]{1,0:T(8,128)(2,1)S(1)} %collective-permute-done.4.refs_0_.refs_2_.refs_6_), channel_id=1, source_target_pairs={{0,4},{4,8},{8,12},{12,14},{14,10},{10,6},{6,2},{2,0},{1,5},{5,9},... | collective-permute-start | bytes 884744 | tf_op jit(solution)/shard_map/onward_cot3/ppermute | solution.py:443
  39.4 2.8 %collective-permute-done.16.refs_0_.refs_10_ = bf16[128,1024]{1,0:T(8,128)(2,1)S(1)} collective-permute-done((bf16[128,1024]{1,0:T(8,128)(2,1)S(1)}, bf16[128,1024]{1,0:T(8,128)(2,1)S(1)}, u32[]{:S(2)}, u32[]{:S(2)}) %collective-permute-start.16) | collective-permute-done | bytes 262176 | tf_op jit(solution)/shard_map/onward_tok3/ppermute | solution.py:443
  42.2 1.6 %collective-permute-done.17.refs_1_.refs_11_ = bf16[128,1024]{1,0:T(8,128)(2,1)S(1)} collective-permute-done((bf16[128,1024]{1,0:T(8,128)(2,1)S(1)}, bf16[128,1024]{1,0:T(8,128)(2,1)S(1)}, u32[]{:S(2)}, u32[]{:S(2)}) %collective-permute-start.17) | collective-permute-done | bytes 262176 | tf_op jit(solution)/shard_map/back_tok3/ppermute | solution.py:445
  49.5 2.3 %collective-permute-start.13 = (bf16[80,1024]{1,0:T(8,128)(2,1)S(1)}, bf16[80,1024]{1,0:T(8,128)(2,1)S(1)}, u32[]{:S(2)}, u32[]{:S(2)}) collective-permute-start(bf16[80,1024]{1,0:T(8,128)(2,1)S(1)} %slice.26), channel_id=1, source_target_pairs={{0,4},{4,8},{8,12},{12,14},{14,10},{10,6},{6,2},{2,0},{1,5},{5,9},... | collective-permute-start | bytes 491528 | tf_op jit(solution)/shard_map/onward_cot4/ppermute | solution.py:443
  56.2 2.2 %collective-permute-done.15.refs_3_.refs_12_ = bf16[80,1024]{1,0:T(8,128)(2,1)S(1)} collective-permute-done((bf16[80,1024]{1,0:T(8,128)(2,1)S(1)}, bf16[80,1024]{1,0:T(8,128)(2,1)S(1)}, u32[]{:S(2)}, u32[]{:S(2)}) %collective-permute-start.15) | collective-permute-done | bytes 163872 | tf_op jit(solution)/shard_map/back_cot4/ppermute | solution.py:445
  63.0 2.4 %shard_map.112 = (bf16[384,1024]{1,0:T(8,128)(2,1)S(1)}, bf16[384,1024]{1,0:T(8,128)(2,1)S(1)}) custom-call(s32[3]{0:T(128)S(1)} %pad_add_fusion.scalars, bf16[384,1664]{1,0:T(8,128)(2,1)S(1)} %shard_map.109.refs_0_.refs_2_.mine_ref, bf16[384,1664]{1,0:T(8,128)(2,1)S(1)} %collective-permute-done.26.refs_1_.refs_3_.arrived_ref, ...), custom_call_target="tpu_custom_call" | custom-call | flops 2000000000 | tf_op jit(solution)/shard_map/pallas_call | solution.py:41
  65.4 2.5 %shard_map.113 = (bf16[768,1024]{1,0:T(8,128)(2,1)S(1)}, bf16[768,1024]{1,0:T(8,128)(2,1)S(1)}) custom-call(s32[3]{0:T(128)S(1)} %pad_add_fusion.scalars, bf16[384,1024]{1,0:T(8,128)(2,1)S(1)} %get-tuple-element.118.refs_0_, bf16[384,1024]{1,0:T(8,128)(2,1)S(1)} %get-tuple-element.119.refs_1_, bf16[384,1664]{1,0:T(8,128)(2,1)S(1)} %shard_map.109.refs_0_.refs_2_.mine_ref, ...), custom_call_target="tpu_custom_call" | custom-call | flops 2000000000 | tf_op jit(solution)/shard_map/pallas_call | solution.py:41
  69.6 1.7 %collective-permute-start.28 = (bf16[64,1024]{1,0:T(8,128)(2,1)S(1)}, bf16[64,1024]{1,0:T(8,128)(2,1)S(1)}, u32[]{:S(2)}, u32[]{:S(2)}) collective-permute-start(bf16[64,1024]{1,0:T(8,128)(2,1)S(1)} %get-tuple-element.123), channel_id=1, source_target_pairs={{0,4},{4,8},{8,12},{12,14},{14,10},{10,6},{6,2},{2,0},{1,5},{5,9},... | collective-permute-start | bytes 393224 | tf_op jit(solution)/shard_map/onward_mixed/ppermute | solution.py:443
  72.6 1.7 %collective-permute-start.32 = (bf16[80,1024]{1,0:T(8,128)(2,1)S(1)}, bf16[80,1024]{1,0:T(8,128)(2,1)S(1)}, u32[]{:S(2)}, u32[]{:S(2)}) collective-permute-start(bf16[80,1024]{1,0:T(8,128)(2,1)S(1)} %get-tuple-element.127), channel_id=1, source_target_pairs={{0,4},{4,8},{8,12},{12,14},{14,10},{10,6},{6,2},{2,0},{1,5},{5,9},... | collective-permute-start | bytes 491528 | tf_op jit(solution)/shard_map/onward_grad/ppermute | solution.py:443
  76.6 1.9 %collective-permute-start.30 = (bf16[128,1024]{1,0:T(8,128)(2,1)S(1)}, bf16[128,1024]{1,0:T(8,128)(2,1)S(1)}, u32[]{:S(2)}, u32[]{:S(2)}) collective-permute-start(bf16[128,1024]{1,0:T(8,128)(2,1)S(1)} %get-tuple-element.131), channel_id=1, source_target_pairs={{0,4},{4,8},{8,12},{12,14},{14,10},{10,6},{6,2},{2,0},{1,5},{5,9},... | collective-permute-start | bytes 786440 | tf_op jit(solution)/shard_map/onward_mixed/ppermute | solution.py:443
  82.3 1.8 %collective-permute-start.37 = (bf16[144,1024]{1,0:T(8,128)(2,1)S(1)}, bf16[144,1024]{1,0:T(8,128)(2,1)S(1)}, u32[]{:S(2)}, u32[]{:S(2)}) collective-permute-start(bf16[144,1024]{1,0:T(8,128)(2,1)S(1)} %get-tuple-element.138), channel_id=1, source_target_pairs={{0,4},{4,8},{8,12},{12,14},{14,10},{10,6},{6,2},{2,0},{1,5},{5,9},... | collective-permute-start | bytes 884744 | tf_op jit(solution)/shard_map/onward_grad/ppermute | solution.py:443
  86.6 1.9 %collective-permute-start.35 = (bf16[128,1024]{1,0:T(8,128)(2,1)S(1)}, bf16[128,1024]{1,0:T(8,128)(2,1)S(1)}, u32[]{:S(2)}, u32[]{:S(2)}) collective-permute-start(bf16[128,1024]{1,0:T(8,128)(2,1)S(1)} %get-tuple-element.142), channel_id=1, source_target_pairs={{0,4},{4,8},{8,12},{12,14},{14,10},{10,6},{6,2},{2,0},{1,5},{5,9},... | collective-permute-start | bytes 786440 | tf_op jit(solution)/shard_map/onward_mixed/ppermute | solution.py:443
  88.4 3.6 %collective-permute-done.36.refs_0_ = bf16[144,1024]{1,0:T(8,128)(2,1)S(1)} collective-permute-done((bf16[144,1024]{1,0:T(8,128)(2,1)S(1)}, bf16[144,1024]{1,0:T(8,128)(2,1)S(1)}, u32[]{:S(2)}, u32[]{:S(2)}) %collective-permute-start.36) | collective-permute-done | bytes 294944 | tf_op jit(solution)/shard_map/back_grad/ppermute | solution.py:445
  93.6 1.8 %collective-permute-start.41 = (bf16[144,1024]{1,0:T(8,128)(2,1)S(1)}, bf16[144,1024]{1,0:T(8,128)(2,1)S(1)}, u32[]{:S(2)}, u32[]{:S(2)}) collective-permute-start(bf16[144,1024]{1,0:T(8,128)(2,1)S(1)} %get-tuple-element.146), channel_id=1, source_target_pairs={{0,4},{4,8},{8,12},{12,14},{14,10},{10,6},{6,2},{2,0},{1,5},{5,9},... | collective-permute-start | bytes 884744 | tf_op jit(solution)/shard_map/onward_grad/ppermute | solution.py:443
  95.4 2.2 %collective-permute-done.34.refs_0_ = bf16[128,1024]{1,0:T(8,128)(2,1)S(1)} collective-permute-done((bf16[128,1024]{1,0:T(8,128)(2,1)S(1)}, bf16[128,1024]{1,0:T(8,128)(2,1)S(1)}, u32[]{:S(2)}, u32[]{:S(2)}) %collective-permute-start.34) | collective-permute-done | bytes 262176 | tf_op jit(solution)/shard_map/back_mixed/ppermute | solution.py:445
  99.3 1.8 %collective-permute-start.39 = (bf16[128,1024]{1,0:T(8,128)(2,1)S(1)}, bf16[128,1024]{1,0:T(8,128)(2,1)S(1)}, u32[]{:S(2)}, u32[]{:S(2)}) collective-permute-start(bf16[128,1024]{1,0:T(8,128)(2,1)S(1)} %get-tuple-element.150), channel_id=1, source_target_pairs={{0,4},{4,8},{8,12},{12,14},{14,10},{10,6},{6,2},{2,0},{1,5},{5,9},... | collective-permute-start | bytes 786440 | tf_op jit(solution)/shard_map/onward_mixed/ppermute | solution.py:443
  101.1 2.9 %collective-permute-done.40.refs_0_ = bf16[144,1024]{1,0:T(8,128)(2,1)S(1)} collective-permute-done((bf16[144,1024]{1,0:T(8,128)(2,1)S(1)}, bf16[144,1024]{1,0:T(8,128)(2,1)S(1)}, u32[]{:S(2)}, u32[]{:S(2)}) %collective-permute-start.40) | collective-permute-done | bytes 294944 | tf_op jit(solution)/shard_map/back_grad/ppermute | solution.py:445
  107.4 2.2 %collective-permute-done.38.refs_0_ = bf16[128,1024]{1,0:T(8,128)(2,1)S(1)} collective-permute-done((bf16[128,1024]{1,0:T(8,128)(2,1)S(1)}, bf16[128,1024]{1,0:T(8,128)(2,1)S(1)}, u32[]{:S(2)}, u32[]{:S(2)}) %collective-permute-start.38) | collective-permute-done | bytes 262176 | tf_op jit(solution)/shard_map/back_mixed/ppermute | solution.py:445
  109.8 1.6 %shard_map.123 = bf16[128,1024]{1,0:T(8,128)(2,1)} custom-call(s32[3]{0:T(128)S(1)} %pad_add_fusion.scalars, bf16[128,1664]{1,0:T(8,128)(2,1)S(1)} %shard_map.111.refs_2_.refs_4_.mine_ref, bf16[128,1664]{1,0:T(8,128)(2,1)S(1)} %collective-permute-done.25.refs_3_.refs_5_.arrived_ref, bf16[768,1024]{1,0:T(8,128)(2,1)S(1)} %get-tuple-element.117.w_ref, ...), custom_call_target="tpu_custom_call" | custom-call | flops 2200000000 | tf_op jit(solution)/shard_map/pallas_call | solution.py:41
  111.4 2.8 %collective-permute-done.42.refs_0_ = bf16[144,1024]{1,0:T(8,128)(2,1)S(1)} collective-permute-done((bf16[144,1024]{1,0:T(8,128)(2,1)S(1)}, bf16[144,1024]{1,0:T(8,128)(2,1)S(1)}, u32[]{:S(2)}, u32[]{:S(2)}) %collective-permute-start.42) | collective-permute-done | bytes 294944 | tf_op jit(solution)/shard_map/back_grad/ppermute | solution.py:445
  114.3 1.7 %shard_map.124 = (bf16[128,1024]{1,0:T(8,128)(2,1)}, f32[4,128]{1,0:T(4,128)}) custom-call(s32[3]{0:T(128)S(1)} %pad_add_fusion.scalars, bf16[128,1664]{1,0:T(8,128)(2,1)S(1)} %shard_map.111.refs_2_.refs_4_.mine_ref, bf16[128,1664]{1,0:T(8,128)(2,1)S(1)} %collective-permute-done.25.refs_3_.refs_5_.arrived_ref, ...), custom_call_target="tpu_custom_call" | custom-call | flops 2200000000 | tf_op jit(solution)/shard_map/pallas_call | solution.py:41
  115.9 1.8 %shard_map.125 = (f32[384,1024]{1,0:T(8,128)}, f32[384,1024]{1,0:T(8,128)}) custom-call(bf16[768,1024]{1,0:T(8,128)(2,1)S(1)} %get-tuple-element.161.kept_ref, bf16[768,1024]{1,0:T(8,128)(2,1)S(1)} %collective-permute-done.44.came_ref), custom_call_target="tpu_custom_call" | custom-call | flops 1000000000 | tf_op jit(solution)/shard_map/pallas_call | solution.py:665
  (107 shorter events, 47.5 us)
Async XLA Ops:
  0.6 18.1 %collective-permute-start.9 = (bf16[384,2048]{1,0:T(8,128)(2,1)}, bf16[384,2048]{1,0:T(8,128)(2,1)S(1)}, u32[]{:S(2)}, u32[]{:S(2)}) collective-permute-start(bf16[384,2048]{1,0:T(8,128)(2,1)} %bitcast.12), channel_id=1, source_target_pairs={{0,1},{1,0},{2,3},{3,2},{4,5},{5,4},{6,7},{7,6},{8,9},{9,8},{10,11... | collective-permute-start | bytes 4718600 | tf_op jit(solution)/shard_map/swap_weights/ppermute | solution.py:25
  1.2 9.9 %collective-permute-start = (bf16[128,1024]{1,0:T(8,128)(2,1)}, bf16[128,1024]{1,0:T(8,128)(2,1)S(1)}, u32[]{:S(2)}, u32[]{:S(2)}) collective-permute-start(bf16[128,1024]{1,0:T(8,128)(2,1)} %refs_12_.1), channel_id=1, source_target_pairs={{0,4},{4,8},{8,12},{12,14},{14,10},{10,6},{6,2},{2,0},{1,5},{5,9},... | collective-permute-start | bytes 786440 | tf_op jit(solution)/shard_map/onward_tok1/ppermute | solution.py:443
  3.8 9.4 %collective-permute-start.1 = (bf16[128,1024]{1,0:T(8,128)(2,1)}, bf16[128,1024]{1,0:T(8,128)(2,1)S(1)}, u32[]{:S(2)}, u32[]{:S(2)}) collective-permute-start(bf16[128,1024]{1,0:T(8,128)(2,1)} %refs_12_.1), channel_id=1, source_target_pairs={{4,0},{8,4},{12,8},{14,12},{10,14},{6,10},{2,6},{0,2},{5,1},{9,5},... | collective-permute-start | bytes 786440 | tf_op jit(solution)/shard_map/back_tok1/ppermute | solution.py:445
  6.6 10.7 %collective-permute-start.3 = (bf16[144,1024]{1,0:T(8,128)(2,1)S(1)}, bf16[144,1024]{1,0:T(8,128)(2,1)S(1)}, u32[]{:S(2)}, u32[]{:S(2)}) collective-permute-start(bf16[144,1024]{1,0:T(8,128)(2,1)S(1)} %shard_map.101.refs_0_.refs_10_), channel_id=1, source_target_pairs={{0,4},{4,8},{8,12},{12,14},{14,10},{10,6},{6,2},{2,0},{1,5},{5,9},... | collective-permute-start | bytes 884744 | tf_op jit(solution)/shard_map/onward_cot1/ppermute | solution.py:443
  8.7 10.1 %collective-permute-start.5 = (bf16[144,1024]{1,0:T(8,128)(2,1)S(1)}, bf16[144,1024]{1,0:T(8,128)(2,1)S(1)}, u32[]{:S(2)}, u32[]{:S(2)}) collective-permute-start(bf16[144,1024]{1,0:T(8,128)(2,1)S(1)} %shard_map.101.refs_0_.refs_10_), channel_id=1, source_target_pairs={{4,0},{8,4},{12,8},{14,12},{10,14},{6,10},{2,6},{0,2},{5,1},{9,5},... | collective-permute-start | bytes 884744 | tf_op jit(solution)/shard_map/back_cot1/ppermute | solution.py:445
  20.1 9.2 %collective-permute-start.7 = (bf16[128,1024]{1,0:T(8,128)(2,1)S(1)}, bf16[128,1024]{1,0:T(8,128)(2,1)S(1)}, u32[]{:S(2)}, u32[]{:S(2)}) collective-permute-start(bf16[128,1024]{1,0:T(8,128)(2,1)S(1)} %collective-permute-done.first.refs_2_.refs_6_), channel_id=1, source_target_pairs={{0,4},{4,8},{8,12},{12,14},{14,10},{10,6},{6,2},{2,0},{1,5},{5,9},... | collective-permute-start | bytes 786440 | tf_op jit(solution)/shard_map/onward_tok2/ppermute | solution.py:443
  21.7 9.2 %collective-permute-start.8 = (bf16[128,1024]{1,0:T(8,128)(2,1)S(1)}, bf16[128,1024]{1,0:T(8,128)(2,1)S(1)}, u32[]{:S(2)}, u32[]{:S(2)}) collective-permute-start(bf16[128,1024]{1,0:T(8,128)(2,1)S(1)} %collective-permute-done.1.second.refs_3_.refs_7_), channel_id=1, source_target_pairs={{4,0},{8,4},{12,8},{14,12},{10,14},{6,10},{2,6},{0,2},{5,1},{9,5},... | collective-permute-start | bytes 786440 | tf_op jit(solution)/shard_map/back_tok2/ppermute | solution.py:445
  22.1 13.0 %collective-permute-start.4 = (bf16[144,1024]{1,0:T(8,128)(2,1)S(1)}, bf16[144,1024]{1,0:T(8,128)(2,1)S(1)}, u32[]{:S(2)}, u32[]{:S(2)}) collective-permute-start(bf16[144,1024]{1,0:T(8,128)(2,1)S(1)} %collective-permute-done.3.first.refs_4_), channel_id=1, source_target_pairs={{0,4},{4,8},{8,12},{12,14},{14,10},{10,6},{6,2},{2,0},{1,5},{5,9},... | collective-permute-start | bytes 884744 | tf_op jit(solution)/shard_map/onward_cot2/ppermute | solution.py:443
  24.1 11.9 %collective-permute-start.6 = (bf16[144,1024]{1,0:T(8,128)(2,1)S(1)}, bf16[144,1024]{1,0:T(8,128)(2,1)S(1)}, u32[]{:S(2)}, u32[]{:S(2)}) collective-permute-start(bf16[144,1024]{1,0:T(8,128)(2,1)S(1)} %collective-permute-done.5.second.refs_5_), channel_id=1, source_target_pairs={{4,0},{8,4},{12,8},{14,12},{10,14},{6,10},{2,6},{0,2},{5,1},{9,5},... | collective-permute-start | bytes 884744 | tf_op jit(solution)/shard_map/back_cot2/ppermute | solution.py:445
  33.0 9.2 %collective-permute-start.16 = (bf16[128,1024]{1,0:T(8,128)(2,1)S(1)}, bf16[128,1024]{1,0:T(8,128)(2,1)S(1)}, u32[]{:S(2)}, u32[]{:S(2)}) collective-permute-start(bf16[128,1024]{1,0:T(8,128)(2,1)S(1)} %collective-permute-done.7.refs_2_.refs_8_), channel_id=1, source_target_pairs={{0,4},{4,8},{8,12},{12,14},{14,10},{10,6},{6,2},{2,0},{1,5},{5,9},... | collective-permute-start | bytes 786440 | tf_op jit(solution)/shard_map/onward_tok3/ppermute | solution.py:443
  34.7 9.1 %collective-permute-start.17 = (bf16[128,1024]{1,0:T(8,128)(2,1)S(1)}, bf16[128,1024]{1,0:T(8,128)(2,1)S(1)}, u32[]{:S(2)}, u32[]{:S(2)}) collective-permute-start(bf16[128,1024]{1,0:T(8,128)(2,1)S(1)} %collective-permute-done.8.refs_3_.refs_9_), channel_id=1, source_target_pairs={{4,0},{8,4},{12,8},{14,12},{10,14},{6,10},{2,6},{0,2},{5,1},{9,5},... | collective-permute-start | bytes 786440 | tf_op jit(solution)/shard_map/back_tok3/ppermute | solution.py:445
  37.3 10.7 %collective-permute-start.12 = (bf16[144,1024]{1,0:T(8,128)(2,1)S(1)}, bf16[144,1024]{1,0:T(8,128)(2,1)S(1)}, u32[]{:S(2)}, u32[]{:S(2)}) collective-permute-start(bf16[144,1024]{1,0:T(8,128)(2,1)S(1)} %collective-permute-done.4.refs_0_.refs_2_.refs_6_), channel_id=1, source_target_pairs={{0,4},{4,8},{8,12},{12,14},{14,10},{10,6},{6,2},{2,0},{1,5},{5,9},... | collective-permute-start | bytes 884744 | tf_op jit(solution)/shard_map/onward_cot3/ppermute | solution.py:443
  39.0 10.4 %collective-permute-start.14 = (bf16[144,1024]{1,0:T(8,128)(2,1)S(1)}, bf16[144,1024]{1,0:T(8,128)(2,1)S(1)}, u32[]{:S(2)}, u32[]{:S(2)}) collective-permute-start(bf16[144,1024]{1,0:T(8,128)(2,1)S(1)} %collective-permute-done.6.refs_1_.refs_3_.refs_7_), channel_id=1, source_target_pairs={{4,0},{8,4},{12,8},{14,12},{10,14},{6,10},{2,6},{0,2},{5,1},{9,5},... | collective-permute-start | bytes 884744 | tf_op jit(solution)/shard_map/back_cot3/ppermute | solution.py:445
  45.2 9.7 %collective-permute-start.22 = (bf16[64,1024]{1,0:T(8,128)(2,1)S(1)}, bf16[64,1024]{1,0:T(8,128)(2,1)S(1)}, u32[]{:S(2)}, u32[]{:S(2)}) collective-permute-start(bf16[64,1024]{1,0:T(8,128)(2,1)S(1)} %slice.28), channel_id=1, source_target_pairs={{0,4},{4,8},{8,12},{12,14},{14,10},{10,6},{6,2},{2,0},{1,5},{5,9},... | collective-permute-start | bytes 393224 | tf_op jit(solution)/shard_map/onward_tok4/ppermute | solution.py:443
  46.8 8.1 %collective-permute-start.23 = (bf16[64,1024]{1,0:T(8,128)(2,1)S(1)}, bf16[64,1024]{1,0:T(8,128)(2,1)S(1)}, u32[]{:S(2)}, u32[]{:S(2)}) collective-permute-start(bf16[64,1024]{1,0:T(8,128)(2,1)S(1)} %slice.29), channel_id=1, source_target_pairs={{4,0},{8,4},{12,8},{14,12},{10,14},{6,10},{2,6},{0,2},{5,1},{9,5},... | collective-permute-start | bytes 393224 | tf_op jit(solution)/shard_map/back_tok4/ppermute | solution.py:445
  54.6 8.4 %collective-permute-start.26 = (bf16[384,1664]{1,0:T(8,128)(2,1)S(1)}, bf16[384,1664]{1,0:T(8,128)(2,1)S(1)}, u32[]{:S(2)}, u32[]{:S(2)}) collective-permute-start(bf16[384,1664]{1,0:T(8,128)(2,1)S(1)} %shard_map.109.refs_0_.refs_2_.mine_ref), channel_id=1, source_target_pairs={{0,1},{1,0},{2,3},{3,2},{4,5},{5,4},{6,7},{7,6},{8,9},{9,8},{10,11... | collective-permute-start | bytes 3833864 | tf_op jit(solution)/shard_map/swap_lefts/ppermute | solution.py:25
  67.9 10.5 %collective-permute-start.33 = (bf16[768,1024]{1,0:T(8,128)(2,1)S(1)}, bf16[768,1024]{1,0:T(8,128)(2,1)S(1)}, u32[]{:S(2)}, u32[]{:S(2)}) collective-permute-start(bf16[768,1024]{1,0:T(8,128)(2,1)S(1)} %get-tuple-element.132), channel_id=1, source_target_pairs={{0,1},{1,0},{2,3},{3,2},{4,5},{5,4},{6,7},{7,6},{8,9},{9,8},{10,11... | collective-permute-start | bytes 4718600 | tf_op jit(solution)/shard_map/swap_grad/ppermute | solution.py:25
  72.3 8.6 %collective-permute-start.31 = (bf16[80,1024]{1,0:T(8,128)(2,1)S(1)}, bf16[80,1024]{1,0:T(8,128)(2,1)S(1)}, u32[]{:S(2)}, u32[]{:S(2)}) collective-permute-start(bf16[80,1024]{1,0:T(8,128)(2,1)S(1)} %get-tuple-element.126), channel_id=1, source_target_pairs={{4,0},{8,4},{12,8},{14,12},{10,14},{6,10},{2,6},{0,2},{5,1},{9,5},... | collective-permute-start | bytes 491528 | tf_op jit(solution)/shard_map/back_grad/ppermute | solution.py:445
  72.6 8.2 %collective-permute-start.32 = (bf16[80,1024]{1,0:T(8,128)(2,1)S(1)}, bf16[80,1024]{1,0:T(8,128)(2,1)S(1)}, u32[]{:S(2)}, u32[]{:S(2)}) collective-permute-start(bf16[80,1024]{1,0:T(8,128)(2,1)S(1)} %get-tuple-element.127), channel_id=1, source_target_pairs={{0,4},{4,8},{8,12},{12,14},{14,10},{10,6},{6,2},{2,0},{1,5},{5,9},... | collective-permute-start | bytes 491528 | tf_op jit(solution)/shard_map/onward_grad/ppermute | solution.py:443
  76.4 8.8 %collective-permute-start.29 = (bf16[128,1024]{1,0:T(8,128)(2,1)S(1)}, bf16[128,1024]{1,0:T(8,128)(2,1)S(1)}, u32[]{:S(2)}, u32[]{:S(2)}) collective-permute-start(bf16[128,1024]{1,0:T(8,128)(2,1)S(1)} %get-tuple-element.130), channel_id=1, source_target_pairs={{4,0},{8,4},{12,8},{14,12},{10,14},{6,10},{2,6},{0,2},{5,1},{9,5},... | collective-permute-start | bytes 786440 | tf_op jit(solution)/shard_map/back_mixed/ppermute | solution.py:445
  76.6 8.6 %collective-permute-start.30 = (bf16[128,1024]{1,0:T(8,128)(2,1)S(1)}, bf16[128,1024]{1,0:T(8,128)(2,1)S(1)}, u32[]{:S(2)}, u32[]{:S(2)}) collective-permute-start(bf16[128,1024]{1,0:T(8,128)(2,1)S(1)} %get-tuple-element.131), channel_id=1, source_target_pairs={{0,4},{4,8},{8,12},{12,14},{14,10},{10,6},{6,2},{2,0},{1,5},{5,9},... | collective-permute-start | bytes 786440 | tf_op jit(solution)/shard_map/onward_mixed/ppermute | solution.py:443
  79.3 36.6 %collective-permute-start.44 = (bf16[768,1024]{1,0:T(8,128)(2,1)S(1)}, bf16[768,1024]{1,0:T(8,128)(2,1)S(1)}, u32[]{:S(2)}, u32[]{:S(2)}) collective-permute-start(bf16[768,1024]{1,0:T(8,128)(2,1)S(1)} %get-tuple-element.134), channel_id=1, source_target_pairs={{0,16},{16,0},{1,17},{17,1},{2,18},{18,2},{3,19},{19,3},{4,20},{20... | collective-permute-start | bytes 4718600 | tf_op jit(solution)/shard_map/groups/ppermute | solution.py:647
  82.0 10.0 %collective-permute-start.36 = (bf16[144,1024]{1,0:T(8,128)(2,1)S(1)}, bf16[144,1024]{1,0:T(8,128)(2,1)S(1)}, u32[]{:S(2)}, u32[]{:S(2)}) collective-permute-start(bf16[144,1024]{1,0:T(8,128)(2,1)S(1)} %get-tuple-element.137), channel_id=1, source_target_pairs={{4,0},{8,4},{12,8},{14,12},{10,14},{6,10},{2,6},{0,2},{5,1},{9,5},... | collective-permute-start | bytes 884744 | tf_op jit(solution)/shard_map/back_grad/ppermute | solution.py:445
  82.3 9.9 %collective-permute-start.37 = (bf16[144,1024]{1,0:T(8,128)(2,1)S(1)}, bf16[144,1024]{1,0:T(8,128)(2,1)S(1)}, u32[]{:S(2)}, u32[]{:S(2)}) collective-permute-start(bf16[144,1024]{1,0:T(8,128)(2,1)S(1)} %get-tuple-element.138), channel_id=1, source_target_pairs={{0,4},{4,8},{8,12},{12,14},{14,10},{10,6},{6,2},{2,0},{1,5},{5,9},... | collective-permute-start | bytes 884744 | tf_op jit(solution)/shard_map/onward_grad/ppermute | solution.py:443
  86.3 11.3 %collective-permute-start.34 = (bf16[128,1024]{1,0:T(8,128)(2,1)S(1)}, bf16[128,1024]{1,0:T(8,128)(2,1)S(1)}, u32[]{:S(2)}, u32[]{:S(2)}) collective-permute-start(bf16[128,1024]{1,0:T(8,128)(2,1)S(1)} %get-tuple-element.141), channel_id=1, source_target_pairs={{4,0},{8,4},{12,8},{14,12},{10,14},{6,10},{2,6},{0,2},{5,1},{9,5},... | collective-permute-start | bytes 786440 | tf_op jit(solution)/shard_map/back_mixed/ppermute | solution.py:445
  86.6 11.3 %collective-permute-start.35 = (bf16[128,1024]{1,0:T(8,128)(2,1)S(1)}, bf16[128,1024]{1,0:T(8,128)(2,1)S(1)}, u32[]{:S(2)}, u32[]{:S(2)}) collective-permute-start(bf16[128,1024]{1,0:T(8,128)(2,1)S(1)} %get-tuple-element.142), channel_id=1, source_target_pairs={{0,4},{4,8},{8,12},{12,14},{14,10},{10,6},{6,2},{2,0},{1,5},{5,9},... | collective-permute-start | bytes 786440 | tf_op jit(solution)/shard_map/onward_mixed/ppermute | solution.py:443
  93.4 10.6 %collective-permute-start.40 = (bf16[144,1024]{1,0:T(8,128)(2,1)S(1)}, bf16[144,1024]{1,0:T(8,128)(2,1)S(1)}, u32[]{:S(2)}, u32[]{:S(2)}) collective-permute-start(bf16[144,1024]{1,0:T(8,128)(2,1)S(1)} %get-tuple-element.145), channel_id=1, source_target_pairs={{4,0},{8,4},{12,8},{14,12},{10,14},{6,10},{2,6},{0,2},{5,1},{9,5},... | collective-permute-start | bytes 884744 | tf_op jit(solution)/shard_map/back_grad/ppermute | solution.py:445
  93.6 10.5 %collective-permute-start.41 = (bf16[144,1024]{1,0:T(8,128)(2,1)S(1)}, bf16[144,1024]{1,0:T(8,128)(2,1)S(1)}, u32[]{:S(2)}, u32[]{:S(2)}) collective-permute-start(bf16[144,1024]{1,0:T(8,128)(2,1)S(1)} %get-tuple-element.146), channel_id=1, source_target_pairs={{0,4},{4,8},{8,12},{12,14},{14,10},{10,6},{6,2},{2,0},{1,5},{5,9},... | collective-permute-start | bytes 884744 | tf_op jit(solution)/shard_map/onward_grad/ppermute | solution.py:443
  99.0 10.6 %collective-permute-start.38 = (bf16[128,1024]{1,0:T(8,128)(2,1)S(1)}, bf16[128,1024]{1,0:T(8,128)(2,1)S(1)}, u32[]{:S(2)}, u32[]{:S(2)}) collective-permute-start(bf16[128,1024]{1,0:T(8,128)(2,1)S(1)} %get-tuple-element.149), channel_id=1, source_target_pairs={{4,0},{8,4},{12,8},{14,12},{10,14},{6,10},{2,6},{0,2},{5,1},{9,5},... | collective-permute-start | bytes 786440 | tf_op jit(solution)/shard_map/back_mixed/ppermute | solution.py:445
  99.3 10.5 %collective-permute-start.39 = (bf16[128,1024]{1,0:T(8,128)(2,1)S(1)}, bf16[128,1024]{1,0:T(8,128)(2,1)S(1)}, u32[]{:S(2)}, u32[]{:S(2)}) collective-permute-start(bf16[128,1024]{1,0:T(8,128)(2,1)S(1)} %get-tuple-element.150), channel_id=1, source_target_pairs={{0,4},{4,8},{8,12},{12,14},{14,10},{10,6},{6,2},{2,0},{1,5},{5,9},... | collective-permute-start | bytes 786440 | tf_op jit(solution)/shard_map/onward_mixed/ppermute | solution.py:443
  105.3 8.9 %collective-permute-start.42 = (bf16[144,1024]{1,0:T(8,128)(2,1)S(1)}, bf16[144,1024]{1,0:T(8,128)(2,1)S(1)}, u32[]{:S(2)}, u32[]{:S(2)}) collective-permute-start(bf16[144,1024]{1,0:T(8,128)(2,1)S(1)} %get-tuple-element.153), channel_id=1, source_target_pairs={{4,0},{8,4},{12,8},{14,12},{10,14},{6,10},{2,6},{0,2},{5,1},{9,5},... | collective-permute-start | bytes 884744 | tf_op jit(solution)/shard_map/back_grad/ppermute | solution.py:445
  106.5 7.7 %collective-permute-start.43 = (bf16[144,1024]{1,0:T(8,128)(2,1)S(1)}, bf16[144,1024]{1,0:T(8,128)(2,1)S(1)}, u32[]{:S(2)}, u32[]{:S(2)}) collective-permute-start(bf16[144,1024]{1,0:T(8,128)(2,1)S(1)} %get-tuple-element.154), channel_id=1, source_target_pairs={{0,4},{4,8},{8,12},{12,14},{14,10},{10,6},{6,2},{2,0},{1,5},{5,9},... | collective-permute-start | bytes 884744 | tf_op jit(solution)/shard_map/onward_grad/ppermute | solution.py:443
  (20 other events, 98.1 us)

commit v6 on v5

--- a/solution.py
+++ b/solution.py
@@ -97,15 +97,6 @@
 
 def stacked(values):
     return jnp.concatenate(values, axis=0) if len(values) > 1 else values[0]
-
-
-def give_next(core, refs):
-    out_ref = refs[-1]
-    half = out_ref.shape[0] // 2
-    cut = refs[0].shape[0] - 2 * half
-    out_ref[:half, :] = picked(core, refs[1][:half, :], refs[0][:half, :])
-    out_ref[half:, :] = picked(core, refs[1][half + cut :, :], refs[0][half + cut :, :])
-    return refs[2:-1]
 
 
 def table_parts(expert, rows, width, experts):
@@ -157,88 +148,84 @@
     return column_of(row)
 
 
-def first_tokens_kernel(scalars, first, second, tokens, cotangent, out_ref):
-    core = scalars[0]
-    rows = first.shape[0]
-    half = rows // 2
-    out_ref[:rows, :] = picked(core, second[...], first[...])
-    for i, ref in enumerate((tokens, cotangent)):
-        at = rows + i * half
-        out_ref[at : at + half, :] = picked(core, ref[half:rows, :], ref[:half, :])
-
-
-def first_cotangent_kernel(scalars, first, second, w_ref, out_ref, sems):
+def first_tokens_kernel(scalars, first, second, out_ref):
+    out_ref[...] = picked(scalars[0], second[...], first[...])
+
+
+def first_cotangent_kernel(scalars, first, second, tokens, cotangent, w_ref, out_ref, sems):
     core = scalars[0]
     units, width = w_ref.shape[0], out_ref.shape[1]
-    rows = out_ref.shape[0] - 2 * units
-    half = rows // 2
+    rows, half = first.shape[0], tokens.shape[0] // 2
+    start = out_ref.shape[0] - 2 * units
     copies = [
         pltpu.make_async_copy(
             w_ref.at[:, pl.ds(i * width, width)],
-            out_ref.at[pl.ds(rows + i * units, units), :],
+            out_ref.at[pl.ds(start + i * units, units), :],
             sems.at[i],
         )
         for i in range(2)
     ]
     for copy in copies:
         copy.start()
-    out_ref[:half, :] = picked(core, second[:half, :], first[:half, :])
-    out_ref[half:rows, :] = picked(core, second[half + EXTRA :, :], first[half + EXTRA :, :])
+    out_ref[:rows, :] = picked(core, second[...], first[...])
+    for i, ref in enumerate((tokens, cotangent)):
+        at = rows + i * half
+        out_ref[at : at + half, :] = picked(core, ref[half:, :], ref[:half, :])
     for copy in copies:
         copy.wait()
+
+
+def whole_kernel(scalars, first, second, other, out_ref):
+    rows, width = first.shape
+    out_ref[:, :width] = picked(scalars[0], first[...], second[...])
+    out_ref[:, width:] = other[:rows, :]
 
 
 def taken(kinds, refs):
     pieces = []
     for kind in kinds:
-        count = 2 if isinstance(kind, int) else 3
+        count = 2 if isinstance(kind, int) else 1
         pieces.append((kind, refs[:count]))
         refs = refs[count:]
     return pieces, refs
 
 
-def rows_of(core, piece, rows):
+def rows_of(core, piece, rows, width):
     kind, refs = piece
     half = rows // 2
-    if kind == "full":
-        first, second, other = refs
-        mine, there = picked(core, first[...], second[...]), other[...]
-        if mine.shape[0] == rows:
-            return mine, there, None
-        extra = mine[half : half + EXTRA]
-        mine = stacked([mine[:half], mine[half + EXTRA :]])
-        if there.shape[0] > rows:
-            there = stacked([there[:half], there[half + EXTRA :]])
-        return mine, there, extra
-    if kind == "far":
-        first, second, other = refs
-        if first.shape[0] == half:
-            return picked(core, first[...], second[...]), other[...], None
-        there = picked(core, other[:half, :], other[EXTRA:, :])
-    else:
+    if isinstance(kind, int):
         block, arrived = refs
         there = arrived[kind : kind + half, :]
         if block.shape[0] == rows:
             return picked(core, block[:half, :], block[half:, :]), there, None
-        first, second = block.at[: half + EXTRA, :], block.at[half:, :]
-    mine = picked(core, first[:half, :], second[EXTRA:, :])
-    return mine, there, picked(core, first[half:, :], second[:EXTRA, :])
+        here = picked(core, block[:half, :], block[half + EXTRA :, :])
+        return here, there, block[half : half + EXTRA, :]
+    (block,) = refs
+    count = block.shape[0]
+    if count in (rows, half):
+        lines, extra = block[...], None
+    elif count > rows:
+        lines = stacked([block[:half, :], block[half + EXTRA :, :]])
+        extra = block[half : half + EXTRA, :width]
+    else:
+        lines = picked(core, block[:half, :], block[EXTRA:, :])
+        extra = picked(core, block[half:, :width], block[:EXTRA, :width])
+    return lines[:, :width], lines[:, width:], extra
 
 
 def units_of(core, pieces, rows, w_ref, w_other_ref):
-    here, there, extra = zip(*(rows_of(core, p, rows) for p in pieces))
+    width = w_ref.shape[0]
+    here, there, extra = zip(*(rows_of(core, p, rows, width) for p in pieces))
     wide = dot_width(stacked(here), w_ref[...]) + dot_width(stacked(there), w_other_ref[...])
     return wide, extra
 
 
-def forward_kernel(kinds, rows, with_next, with_weights, scalars, *refs):
+def forward_kernel(kinds, rows, with_weights, scalars, *refs):
     core = scalars[0]
     if with_weights:
         weights = refs[-2:]
         prepare(core, *refs[:2], *refs[-3:])
         refs = refs[2:-3]
-    if with_next:
-        refs = give_next(core, refs)
     hidden_ref, slope_ref = refs[-2:]
     pieces, refs = taken(kinds, refs)
     if not with_weights:
@@ -249,14 +236,12 @@
     slope_ref[...] = logistic * (1.0 + pre * (1.0 - logistic))
 
 
-def backward_kernel(kinds, rows, experts, with_next, with_weights, before, scalars, *refs):
+def backward_kernel(kinds, rows, experts, with_weights, before, scalars, *refs):
     core, expert = scalars[0], scalars[1]
     if with_weights:
         weights = refs[-2:]
         prepare(core, *refs[:2], *refs[-3:])
         refs = refs[2:-3]
-    if with_next:
-        refs = give_next(core, refs)
     if before:
         lines = refs[0].shape[0]
         for i in range(before):
@@ -361,57 +346,40 @@
         ahead_ref[count:, :] = (extra[1] + from_behind[half:, :].astype(F32)).astype(BF16)
 
 
-def weight_kernel(at, rows, scalars, *refs):
+def weight_kernel(blocks, rows, scalars, *refs):
     core = scalars[0]
-    lefts = []
-    mine_ref, other_ref = refs[-2:]
-    taken = 0
-    if at:
-        taken = 2
-        units = refs[0].shape[0]
-        mine_ref[:units, :] = refs[0][...]
-        other_ref[:units, :] = refs[1][...]
-        mine_ref, other_ref = mine_ref.at[units:, :], other_ref.at[units:, :]
-    units = mine_ref.shape[0]
-    above, above_came, ends, ends_came = refs[taken : taken + 4]
-    rights = refs[taken + 4 : -2]
-    for left, came in ((above, above_came), (ends, ends_came)):
-        count = ends.shape[0]
-        for i in range(left.shape[0] // count):
-            lines = slice(i * count, (i + 1) * count)
-            here, there = left[lines, at : at + 2 * units], came[lines, at : at + 2 * units]
-            lefts += [picked(core, here, there), picked(core, there, here)]
-    half = rows // 2
-    block, far_first, far_second = rights[-3:]
-    cut = block.shape[0] - rows
-    blocks = []
-    for ref in rights[:-3]:
-        blocks += [ref[:half, :], ref[half + cut :, :]] if cut else [ref[...]]
-    blocks += [block[:half, :], far_first[:half, :]]
-    blocks += [block[half + cut :, :], far_second[cut:, :]]
-    part = dot_rows(stacked(lefts), stacked(blocks))
-    mine_ref[...] = picked(core, part[:units], part[units:]).astype(BF16)
-    other_ref[...] = picked(core, part[units:], part[:units]).astype(BF16)
-
-
-def send_kernel(scalars, mine_ref, came_ref, sent_ref, kept_ref):
-    @pl.when(scalars[2] == 0)
-    def _():
-        sent_ref[...] = came_ref[...]
-        kept_ref[...] = mine_ref[...]
-
-    @pl.when(scalars[2] != 0)
-    def _():
-        sent_ref[...] = mine_ref[...]
-        kept_ref[...] = came_ref[...]
-
-
-def add_kernel(kept_ref, came_ref, first_hbm, second_hbm, held_ref, sems):
+    above, ends, own_other = refs[:3]
+    own_ref, other_ref = refs[-2:]
+    units, width = own_ref.shape[0] // 4, own_ref.shape[1]
+    for i in range(2):
+        lanes = slice(2 * i * units, 2 * (i + 1) * units)
+        left = stacked([above[:, lanes], ends[:, lanes]])
+        pieces = [("block", (ref,)) for ref in refs[3 + i * blocks : 3 + (i + 1) * blocks]]
+        first_row = rows + EXTRA + (1 - i) * (rows // 2)
+        pieces[-2] = (first_row, (pieces[-2][1][0], own_other))
+        here, there, _ = zip(*(rows_of(core, p, rows, width) for p in pieces))
+        for side, right in enumerate((here, there)):
+            part = dot_rows(left, stacked(right))
+            own = picked(core, part[:units], part[units:]).astype(BF16)
+            other = picked(core, part[units:], part[:units]).astype(BF16)
+            kept = jnp.where(scalars[2] == side, 1, 0)
+            at = pl.ds(pl.multiple_of(kept * 2 * units + i * units, units), units)
+            own_ref[at, :] = own
+            other_ref[at, :] = other
+
+
+def send_kernel(own_ref, came_ref, out_ref):
+    out_ref[...] = (own_ref[...].astype(F32) + came_ref[...].astype(F32)).astype(BF16)
+
+
+def add_kernel(own_ref, other_ref, came_ref, first_hbm, second_hbm, held_ref, sems):
     tiles, rows = held_ref.shape[0], held_ref.shape[1]
     copies = []
     for i in range(tiles):
         at = slice(i * rows, (i + 1) * rows)
-        held_ref[i] = kept_ref[at, :].astype(F32) + came_ref[at, :].astype(F32)
+        below = slice((tiles + i) * rows, (tiles + i + 1) * rows)
+        kept = own_ref[below, :].astype(F32) + other_ref[below, :].astype(F32)
+        held_ref[i] = kept + came_ref[at, :].astype(F32)
         out = first_hbm if i < tiles // 2 else second_hbm
         start = (i % (tiles // 2)) * rows
         copy = pltpu.make_async_copy(held_ref.at[i], out.at[pl.ds(start, rows), :], sems.at[i])
@@ -457,44 +425,35 @@
     def split(pieces):
         return tuple(p[0] for p in pieces), [v for p in pieces for v in p[1:]]
 
-    def forward(pieces, weights, following=()):
+    def forward(pieces, weights):
         shape = (rows, units)
         raw = weights[0] is w_in
         kinds, operands = split(pieces)
         result = call(
-            functools.partial(forward_kernel, kinds, rows, len(following) > 0, raw),
+            functools.partial(forward_kernel, kinds, rows, raw),
             [
                 jax.ShapeDtypeStruct(shape, BF16),
                 jax.ShapeDtypeStruct(shape, F32),
-                *[jax.ShapeDtypeStruct((rows, width), BF16) for _ in following[:1]],
+                *(weight_shapes if raw else ()),
+            ],
+            [*(weights if raw else ()), *operands, *(() if raw else weights[1:])],
+            scalars,
+            10**9,
+        )
+        return (result[:-3], result[-3:]) if raw else (result, weights)
+
+    def backward(pieces, weights, hidden, slope, before=()):
+        count = hidden.shape[0] * (1 + len(before))
+        raw = weights[0] is w_out
+        kinds, operands = split(pieces)
+        result = call(
+            functools.partial(backward_kernel, kinds, rows, experts, raw, len(before)),
+            [
+                jax.ShapeDtypeStruct((count, 2 * units + LANES), BF16),
                 *(weight_shapes if raw else ()),
             ],
             [
                 *(weights if raw else ()),
-                *following,
-                *operands,
-                *(() if raw else weights[1:]),
-            ],
-            scalars,
-        )
-        return (result[:-3], result[-3:]) if raw else (result, weights)
-
-    def backward(pieces, weights, hidden, slope, following=(), before=()):
-        count = hidden.shape[0] * (1 + len(before))
-        raw = weights[0] is w_out
-        kinds, operands = split(pieces)
-        result = call(
-            functools.partial(
-                backward_kernel, kinds, rows, experts, len(following) > 0, raw, len(before)
-            ),
-            [
-                jax.ShapeDtypeStruct((count, 2 * units + LANES), BF16),
-                *[jax.ShapeDtypeStruct((rows, width), BF16) for _ in following[:1]],
-                *(weight_shapes if raw else ()),
-            ],
-            [
-                *(weights if raw else ()),
-                *following,
                 *before,
                 *operands,
                 *(() if raw else weights[1:]),
@@ -502,6 +461,7 @@
                 slope,
             ],
             scalars,
+            10**9,
         )
         return (result[:-3], result[-3:]) if raw else (result, weights)
 
@@ -517,6 +477,13 @@
         kernel = functools.partial(return_kernel, kind, at, first_row, count, experts, rows)
         operands = [mine, arrived, weights, *sums, *more]
         return call(kernel, shapes, operands, scalars, 22 * 10**8)
+
+    apart_pairs = [(2 * i, 2 * j) for i, j in onward_pairs]
+    apart_pairs += [(2 * i + 1, 2 * j + 1) for i, j in back_pairs]
+
+    def apart(value, name):
+        with jax.named_scope("onward_" + name):
+            return lax.ppermute(value, ("expert", "tensor"), apart_pairs)
 
     payload = pl.pallas_call(
         functools.partial(payload_kernel, experts),
@@ -536,136 +503,116 @@
 
     in_all, out_all = (w_in, swap_cores(w_in, "weights")), ()
 
-    arrivals, outputs, lefts = [], [], []
+    tok_sent = call(
+        first_tokens_kernel,
+        [jax.ShapeDtypeStruct((rows, width), BF16)],
+        [*ring[0]],
+        scalars,
+        2 * 10**9,
+    )[0]
+    tok_came = swap_cores(tok_sent, "tok1")
+    def whole(pair, other):
+        count = pair[0].shape[0]
+        shape = [jax.ShapeDtypeStruct((count, 2 * width), BF16)]
+        return call(whole_kernel, shape, [*pair, other], scalars, 10**6)[0]
+
+    tok_whole = whole(ring[0], tok_came)
+    seen = tied((*ring[1], w_out), (*in_all, tok_whole))
+    cot_sent = pl.pallas_call(
+        first_cotangent_kernel,
+        out_shape=jax.ShapeDtypeStruct((2 * rows + EXTRA + units, width), BF16),
+        in_specs=[pl.BlockSpec(memory_space=pltpu.SMEM)]
+        + [pl.BlockSpec(memory_space=pltpu.VMEM)] * 4
+        + [pl.BlockSpec(memory_space=pltpu.HBM)],
+        out_specs=pl.BlockSpec(memory_space=pltpu.VMEM),
+        scratch_shapes=[pltpu.SemaphoreType.DMA((2,))],
+        compiler_params=pltpu.CompilerParams(vmem_limit_bytes=VMEM_LIMIT),
+        cost_estimate=pl.CostEstimate(flops=10**9, bytes_accessed=0, transcendentals=0),
+    )(scalars, *seen[:2], tokens, cotangent, seen[2])
+    own_arrived = swap_cores(cot_sent, "cot1")
+    out_all = (w_out, own_arrived)
+
+    arrivals = [tok_whole, whole(ring[1], out_all[1])]
+    outputs, lefts = [], []
     for turn in range(2 * steps):
-        now = ring[turn]
         step = turn // 2 + 1
-        name = ("tok", "cot")[turn % 2]
-        sent = None
-        if turn == 0:
-            sent = call(
-                first_tokens_kernel,
-                [jax.ShapeDtypeStruct((2 * rows, width), BF16)],
-                [*now, tokens, cotangent],
-                scalars,
-                2 * 10**9,
-            )[0]
-        elif turn == 1:
-            seen = tied((*now, w_out), (*in_all, sent_first))
-            cot_sent = pl.pallas_call(
-                first_cotangent_kernel,
-                out_shape=jax.ShapeDtypeStruct((rows + units, width), BF16),
-                in_specs=[pl.BlockSpec(memory_space=pltpu.SMEM)]
-                + [pl.BlockSpec(memory_space=pltpu.VMEM)] * 2
-                + [pl.BlockSpec(memory_space=pltpu.HBM)],
-                out_specs=pl.BlockSpec(memory_space=pltpu.VMEM),
-                scratch_shapes=[pltpu.SemaphoreType.DMA((2,))],
-                compiler_params=pltpu.CompilerParams(vmem_limit_bytes=VMEM_LIMIT),
-                cost_estimate=pl.CostEstimate(flops=10**9, bytes_accessed=0, transcendentals=0),
-            )(scalars, *seen)
-            result, in_all = forward([("full", *arrivals[0])], in_all)
-            outputs.append(result)
-        elif turn < 2 * steps - 1:
-            done = turn - 1
-            first, second, other = arrivals[done]
-            following = now if turn < 2 * steps - 3 else ()
-            if turn == 2 * steps - 3:
-                other = tied((other,), now)[0]
-            pieces = [("full", first, second, other)]
-            if done % 2 == 0:
-                result, in_all = forward(pieces, in_all, following)
-                if following:
-                    *result, sent = result
-                outputs.append(result)
-            else:
-                before = lefts if turn == 2 * steps - 2 else ()
-                result, out_all = backward(
-                    pieces, out_all, *outputs[done - 1], following, before
-                )
-                if following:
-                    *result, sent = result
-                lefts.append(result[0])
-                outputs.append(result)
-            if turn != 2 * steps - 3:
-                now = tied(now, outputs[-1][:1])
-        else:
-            now = tied(now, outputs[-1])
-        if turn == 0:
-            sent_first = sent
-        elif turn == 1:
-            sent = cot_sent
-        elif sent is None:
-            sent = jnp.where(first_core, now[1], now[0])
+        name = ("tok", "cot")[turn % 2] + str(step + 1)
+        now = arrivals[turn]
+        if turn >= 2:
+            now = arrivals[turn] = tied((now,), outputs[turn - 2])[0]
         if step < steps - 1:
-            ring.append(both_ways(now[0], now[1], name + str(step + 1)))
+            arrivals.append(apart(now, name))
         elif step == steps - 1:
             cut = half + (EXTRA if turn % 2 else 0)
-            ends = ring[turn][0][:cut], ring[turn][1][half:]
-            ring.append(both_ways(*ends, name + str(step + 1)))
-        other = swap_cores(sent, name + str(step))
-        if turn == 0:
-            own_arrived, other = other, other[:rows]
-        elif turn == 1:
-            out_all, other = (w_out, other), other[:rows]
-        arrivals.append((*now, other))
-    tok_pieces = [(rows, tokens, own_arrived), ("far", *arrivals[2 * steps - 2])]
-    cot_pieces = [(rows + half, payload, own_arrived), ("far", *arrivals[2 * steps - 1])]
-    lefts = lefts[-1]
-    lefts_arrived = swap_cores(lefts, "lefts")
-    hidden, slope = forward(tok_pieces, in_all)[0]
-    ends = backward(cot_pieces, out_all, hidden, slope)[0][0]
+            arrivals.append(apart(jnp.where(first_core, now[:cut], now[half:]), name))
+        pieces = [("block", now)]
+        if turn % 2 == 0:
+            if step == steps:
+                pieces = [(rows + EXTRA, tokens, own_arrived), *pieces]
+            result, in_all = forward(pieces, in_all)
+        else:
+            if step == steps:
+                pieces = [(rows + EXTRA + half, payload, own_arrived), *pieces]
+            before = lefts if step == steps - 1 else ()
+            result, out_all = backward(pieces, out_all, *outputs[-1], before)
+            lefts.append(result[0])
+        outputs.append(result)
+    ends = lefts[steps - 1]
+    lefts = lefts[steps - 2]
+    lefts_arrived = swap_cores(tied((lefts,), (ends,))[0], "lefts")
     ends_arrived = swap_cores(ends, "ends")
 
-    def weight_part(at, which, above, after):
-        operands = [*above, lefts, lefts_arrived, ends, tied((ends_arrived,), after)[0]]
-        for s in range(steps - 1):
-            operands += arrivals[2 * s + which][:2]
-        own, far_ends = (tok_pieces, cot_pieces)[which]
-        operands += [own[1], *far_ends[1:3]]
-        deep = local_units * (1 + len(above) // 2)
-        return call(
-            functools.partial(weight_kernel, at, rows),
-            [jax.ShapeDtypeStruct((deep, width), BF16)] * 2,
-            operands,
-            scalars,
-            2 * 10**9,
-        )
-
-    def over_groups(mine, other):
-        if n_dp == 2:
-            block = pl.BlockSpec((units // 4, width), lambda i: (i, 0))
-            sent, kept = pl.pallas_call(
-                send_kernel,
-                grid=(4,),
-                out_shape=[jax.ShapeDtypeStruct(mine.shape, BF16)] * 2,
-                in_specs=[pl.BlockSpec(memory_space=pltpu.SMEM), block, block],
-                out_specs=[block] * 2,
-                compiler_params=pltpu.CompilerParams(vmem_limit_bytes=VMEM_LIMIT),
-                cost_estimate=pl.CostEstimate(flops=10**9, bytes_accessed=0, transcendentals=0),
-            )(scalars, mine, other)
-            with jax.named_scope("groups"):
-                return (sent,), kept, lax.ppermute(sent, "dp", [(0, 1), (1, 0)])
+    def weight_parts(after):
+        operands = [lefts, tied((ends,), after)[0], own_arrived]
+        for which in (1, 0):
+            blocks = [arrivals[2 * step + which] for step in range(steps)]
+            own = (tokens, payload)[which]
+            operands += [*blocks[:-1], own, blocks[-1]]
+        return pl.pallas_call(
+            functools.partial(weight_kernel, steps + 1, rows),
+            out_shape=[jax.ShapeDtypeStruct((2 * units, width), BF16)] * 2,
+            in_specs=[pl.BlockSpec(memory_space=pltpu.SMEM)]
+            + [pl.BlockSpec(memory_space=pltpu.VMEM)] * len(operands),
+            out_specs=[pl.BlockSpec(memory_space=pltpu.VMEM)] * 2,
+            compiler_params=pltpu.CompilerParams(vmem_limit_bytes=2 * VMEM_LIMIT),
+            cost_estimate=pl.CostEstimate(flops=4 * 10**9, bytes_accessed=0, transcendentals=0),
+        )(scalars, *operands)
+
+    def over_groups(own, came):
+        block = pl.BlockSpec((units // 4, width), lambda i: (i, 0))
+        sent = pl.pallas_call(
+            send_kernel,
+            grid=(4,),
+            out_shape=jax.ShapeDtypeStruct((units, width), BF16),
+            in_specs=[block] * 2,
+            out_specs=block,
+            compiler_params=pltpu.CompilerParams(vmem_limit_bytes=VMEM_LIMIT),
+            cost_estimate=pl.CostEstimate(flops=10**9, bytes_accessed=0, transcendentals=0),
+        )(own, came)
+        with jax.named_scope("groups"):
+            return (sent,), lax.ppermute(sent, "dp", [(0, 1), (1, 0)])
+
+    def over_many_groups(away, kept):
+        mine = picked((core + group) % 2, kept, away)
+        other = picked((core + group) % 2, away, kept)
         part = jnp.concatenate([picked(core, mine, other), picked(core, other, mine)], axis=1)
         across = part.shape[1] // n_dp
         slices = [
             lax.dynamic_slice_in_dim(part, ((group + shift) % n_dp) * across, across, axis=1)
             for shift in range(n_dp)
         ]
-        total = 0.0
+        total = slices[0]
         for shift in range(1, n_dp):
             pairs = [(i, (i + shift) % n_dp) for i in range(n_dp)]
-            total = total + lax.ppermute(slices[shift], "dp", pairs).astype(F32)
-        return (), slices[0], total
-
-    def summed(kept, came):
-        if n_dp != 2:
-            total = kept.astype(F32) + came
-            return total[:local_units], total[local_units:]
+            total = total + lax.ppermute(slices[shift].astype(BF16), "dp", pairs).astype(F32)
+        return total[:local_units], total[local_units:]
+
+    def summed(own, kept, came):
         tiles = 8
         return pl.pallas_call(
             add_kernel,
             out_shape=[jax.ShapeDtypeStruct((local_units, width), F32)] * 2,
-            in_specs=[pl.BlockSpec(memory_space=pltpu.VMEM)] * 2,
+            in_specs=[pl.BlockSpec(memory_space=pltpu.VMEM)] * 3,
             out_specs=[pl.BlockSpec(memory_space=pl.ANY)] * 2,
             scratch_shapes=[
                 pltpu.VMEM((tiles, units // tiles, width), F32),
@@ -673,7 +620,7 @@
             ],
             compiler_params=pltpu.CompilerParams(vmem_limit_bytes=VMEM_LIMIT),
             cost_estimate=pl.CostEstimate(flops=10**9, bytes_accessed=0, transcendentals=0),
-        )(kept, came)
+        )(own, kept, came)
 
     def mixed_far(after):
         came = tied((ends_arrived,), after)[0]
@@ -699,14 +646,16 @@
         sent = returned(kind, units, line, lefts, lefts_arrived, in_all[0], sums)
         return sent, both_ways(sent[1], sent[0], "grad")[::-1]
 
-    part_out = weight_part(0, 1, (), ())
-    parts, parts_other = weight_part(units, 0, part_out, ())
-    parts_other = swap_cores(parts_other, "grad")
-    sent, mixed_in = mixed_far((parts,))
+    parts, parts_other = weight_parts(())
+    sent, mixed_in = mixed_far((parts, lefts_arrived))
+    parts_came = swap_cores(tied((parts_other,), sent)[0], "parts")
     sent, back_in = back_far(sent)
     sent, mixed_in = mixed_step(steps - 1, mixed_in, sent)
-    parts_sent, kept, came = over_groups(parts, tied((parts_other,), sent)[0])
-    sent, back_in = back_step(steps - 1, back_in, (*sent, *parts_sent))
+    after = sent
+    if n_dp == 2:
+        parts_sent, came = over_groups(parts, tied((parts_came,), sent)[0])
+        after = (*sent, *parts_sent)
+    sent, back_in = back_step(steps - 1, back_in, after)
     for step in range(steps - 2, 0, -1):
         sent, mixed_in = mixed_step(step, mixed_in, sent)
         sent, back_in = back_step(step, back_in, sent)
@@ -715,7 +664,12 @@
     grad_tokens, grad_gates = returned(
         "own", units, *own, in_all[0], tied(back_in, (mixed,)), (routes.T,)
     )
-    grad_out, grad_in = summed(kept, tied((came,), (grad_tokens,))[0])
+    if n_dp == 2:
+        came = tied((came,), (grad_tokens,))[0]
+        grad_out, grad_in = summed(parts, parts_came, came)
+    else:
+        both = parts.astype(F32) + parts_came.astype(F32)
+        grad_out, grad_in = over_many_groups(both[:units], both[units:])
     return (mixed, grad_tokens, grad_gates.T, grad_in[None], grad_out[None])
 
 

time: 118 us -> 112 us (0.949)
  starting transfers between devices: 38.4 us -> 27 us
  waiting for transfers between devices: 42.9 us -> 49.2 us
    ppermute x16 -> x10, starting transfers between devices: 28.3 us -> 4.59 us  [both_ways(): forth = lax.ppermute(forth_value, 'expert', onward_pairs)]
    ppermute x1 -> x7, waiting for transfers between devices: 0.01 us -> 17.5 us  [the longest x6 17.5 us: apart(): return lax.ppermute(value, ('expert', 'tensor'), apart_pairs)]
    ppermute x16 -> x10, waiting for transfers between devices: 26.6 us -> 13.3 us  [both_ways(): return (forth, lax.ppermute(back_value, 'expert', back_pairs))]
    ppermute x16 -> x10, starting transfers between devices: 5.72 us -> 16.9 us  [both_ways(): return (forth, lax.ppermute(back_value, 'expert', back_pairs))]
    pallas_call x21, Pallas kernels: 29.1 us -> 25.1 us  [call(): pl.pallas_call(kernel, out_shape=out_shape, in_specs=[pl.BlockSpec(memory...]
    pallas_call x2 -> x3, Pallas kernels: 1.61 us -> 5.23 us  [the longest x1 4.05 us: weight_parts(): pl.pallas_call(functools.partial(weight_kernel, steps + 1, rows), out_sha...]
    ppermute x12 -> x6, waiting for transfers between devices: 2.05 us -> 5.28 us  [swap_cores(): return lax.ppermute(value, 'tensor', [(0, 1), (1, 0)])]
    ppermute x1 -> x7, starting transfers between devices: 1.51 us -> 4.11 us  [the longest x6 2.56 us: apart(): return lax.ppermute(value, ('expert', 'tensor'), apart_pairs)]
  transfers between devices with their start and end apart: 45 -> 33, of which waited for: 30 -> 26; matrix products, arithmetic and copies ran while one was open for 0% -> 0% of each run, Pallas kernels for 22% -> 25%
where the time goes in v6:
time: 112 us
  waiting for transfers between devices  49.2 us (44%)
  Pallas kernels  32.5 us (29%)
  starting transfers between devices  27 us (24%)
  local copies, waits for them, and re-layouts  2.34 us (2%)
    pallas_call x21, Pallas kernels, call(): pl.pallas_call(kernel, out_shape=out_shape, in_specs=[pl.BlockSpec(memory...  25.1 us
    ppermute x6, waiting for transfers between devices, apart(): return lax.ppermute(value, ('expert', 'tensor'), apart_pairs)  17.5 us
    ppermute x10, starting transfers between devices, both_ways(): return (forth, lax.ppermute(back_value, 'expert', back_pairs))  16.9 us
    ppermute x10, waiting for transfers between devices, both_ways(): return (forth, lax.ppermute(back_value, 'expert', back_pairs))  13.3 us
    ppermute x10, waiting for transfers between devices, both_ways(): forth = lax.ppermute(forth_value, 'expert', onward_pairs)  13.1 us
    ppermute x6, waiting for transfers between devices, swap_cores(): return lax.ppermute(value, 'tensor', [(0, 1), (1, 0)])  5.28 us
    ppermute x10, starting transfers between devices, both_ways(): forth = lax.ppermute(forth_value, 'expert', onward_pairs)  4.59 us
    pallas_call x1, Pallas kernels, weight_parts(): pl.pallas_call(functools.partial(weight_kernel, steps + 1, rows), out_sha...  4.05 us
  transfers between devices with their start and end apart: 33, of which 26 were waited for; matrix products, arithmetic and copies ran while one was open for 0% of the time, Pallas kernels for 25%

profile of v6, /device:TPU:0, one launch (start us, length us, event | category | flops | bytes accessed | tf_op | source)
XLA Modules:
  0.0 112.3 jit_solution(18291463397439166622)
XLA Ops:
  1.2 2.5 %collective-permute-start.4 = (bf16[128,1024]{1,0:T(8,128)(2,1)}, bf16[128,1024]{1,0:T(8,128)(2,1)S(1)}, u32[]{:S(2)}, u32[]{:S(2)}) collective-permute-start(bf16[128,1024]{1,0:T(8,128)(2,1)} %refs_11_.1), channel_id=1, source_target_pairs={{4,0},{8,4},{12,8},{14,12},{10,14},{6,10},{2,6},{0,2},{5,1},{9,5},... | collective-permute-start | bytes 786440 | tf_op jit(solution)/shard_map/back_tok1/ppermute | solution.py:413
  6.6 2.0 %collective-permute-start.1 = (bf16[144,1024]{1,0:T(8,128)(2,1)S(1)}, bf16[144,1024]{1,0:T(8,128)(2,1)S(1)}, u32[]{:S(2)}, u32[]{:S(2)}) collective-permute-start(bf16[144,1024]{1,0:T(8,128)(2,1)S(1)} %shard_map.101.refs_0_.refs_6_), channel_id=1, source_target_pairs={{4,0},{8,4},{12,8},{14,12},{10,14},{6,10},{2,6},{0,2},{5,1},{9,5},... | collective-permute-start | bytes 884744 | tf_op jit(solution)/shard_map/back_cot1/ppermute | solution.py:413
  8.7 2.5 %collective-permute-done.4.second = bf16[128,1024]{1,0:T(8,128)(2,1)S(1)} collective-permute-done((bf16[128,1024]{1,0:T(8,128)(2,1)}, bf16[128,1024]{1,0:T(8,128)(2,1)S(1)}, u32[]{:S(2)}, u32[]{:S(2)}) %collective-permute-start.4) | collective-permute-done | bytes 262176 | tf_op jit(solution)/shard_map/back_tok1/ppermute | solution.py:413
  11.2 1.9 %collective-permute-done.3.first = bf16[128,1024]{1,0:T(8,128)(2,1)S(1)} collective-permute-done((bf16[128,1024]{1,0:T(8,128)(2,1)}, bf16[128,1024]{1,0:T(8,128)(2,1)S(1)}, u32[]{:S(2)}, u32[]{:S(2)}) %collective-permute-start.3) | collective-permute-done | bytes 262176 | tf_op jit(solution)/shard_map/onward_tok1/ppermute | solution.py:411
  13.8 1.5 %collective-permute-done.5.other = bf16[128,1024]{1,0:T(8,128)(2,1)S(1)} collective-permute-done((bf16[128,1024]{1,0:T(8,128)(2,1)S(1)}, bf16[128,1024]{1,0:T(8,128)(2,1)S(1)}, u32[]{:S(2)}, u32[]{:S(2)}) %collective-permute-start.5) | collective-permute-done | bytes 262176 | tf_op jit(solution)/shard_map/swap_tok1/ppermute | solution.py:25
  15.9 1.4 %collective-permute-done.1.second = bf16[144,1024]{1,0:T(8,128)(2,1)S(1)} collective-permute-done((bf16[144,1024]{1,0:T(8,128)(2,1)S(1)}, bf16[144,1024]{1,0:T(8,128)(2,1)S(1)}, u32[]{:S(2)}, u32[]{:S(2)}) %collective-permute-start.1) | collective-permute-done | bytes 294944 | tf_op jit(solution)/shard_map/back_cot1/ppermute | solution.py:413
  17.3 1.4 %collective-permute-done.first = bf16[144,1024]{1,0:T(8,128)(2,1)S(1)} collective-permute-done((bf16[144,1024]{1,0:T(8,128)(2,1)S(1)}, bf16[144,1024]{1,0:T(8,128)(2,1)S(1)}, u32[]{:S(2)}, u32[]{:S(2)}) %collective-permute-start) | collective-permute-done | bytes 294944 | tf_op jit(solution)/shard_map/onward_cot1/ppermute | solution.py:411
  20.0 3.7 %collective-permute-done.6.other.refs_1_.refs_2_ = bf16[1040,1024]{1,0:T(8,128)(2,1)S(1)} collective-permute-done((bf16[1040,1024]{1,0:T(8,128)(2,1)S(1)}, bf16[1040,1024]{1,0:T(8,128)(2,1)S(1)}, u32[]{:S(2)}, u32[]{:S(2)}) %collective-permute-start.6) | collective-permute-done | bytes 2129952 | tf_op jit(solution)/shard_map/swap_cot1/ppermute | solution.py:25
  24.8 1.9 %shard_map.106 = (bf16[128,768]{1,0:T(8,128)(2,1)S(1)}, f32[128,768]{1,0:T(8,128)S(1)}, bf16[768,1024]{1,0:T(8,128)(2,1)S(1)}, bf16[1024,768]{1,0:T(8,128)(2,1)S(1)}, bf16[1024,768]{1,0:T(8,128)(2,1)S(1)}) custom-call(s32[3]{0:T(128)S(1)} %pad_add_fusion.scalars, bf16[384,2048]{1,0:T(8,128)(2,1)S(1)} %bitcast.13, ...), custom_call_target="tpu_custom_call" | custom-call | flops 1000000000 | tf_op jit(solution)/shard_map/pallas_call | solution.py:41
  26.8 2.1 %collective-permute-done.9.refs_0_.refs_9_ = bf16[128,2048]{1,0:T(8,128)(2,1)S(1)} collective-permute-done((bf16[128,2048]{1,0:T(8,128)(2,1)S(1)}, bf16[128,2048]{1,0:T(8,128)(2,1)S(1)}, u32[]{:S(2)}, u32[]{:S(2)}) %collective-permute-start.9) | collective-permute-done | bytes 524320 | tf_op jit(solution)/shard_map/onward_tok2/ppermute | solution.py:486
  29.2 2.0 %shard_map.107 = (bf16[128,1664]{1,0:T(8,128)(2,1)S(1)}, bf16[768,1024]{1,0:T(8,128)(2,1)S(1)}, bf16[1024,768]{1,0:T(8,128)(2,1)S(1)}, bf16[1024,768]{1,0:T(8,128)(2,1)S(1)}) custom-call(s32[3]{0:T(128)S(1)} %pad_add_fusion.scalars, bf16[384,2048]{1,0:T(8,128)(2,1)S(1)} %bitcast.11, bf16[1040,1024]{1,0:T(8,128)(2,1)S(1)} %collective-permute-done.6.other.refs_1_.refs_2_, ...), custom_call_target="tpu_custom_call" | custom-call | flops 1000000000 | tf_op jit(solution)/shard_map/pallas_call | solution.py:41
  31.3 3.9 %collective-permute-done.7.refs_0_.refs_4_ = bf16[144,2048]{1,0:T(8,128)(2,1)S(1)} collective-permute-done((bf16[144,2048]{1,0:T(8,128)(2,1)S(1)}, bf16[144,2048]{1,0:T(8,128)(2,1)S(1)}, u32[]{:S(2)}, u32[]{:S(2)}) %collective-permute-start.7) | collective-permute-done | bytes 589856 | tf_op jit(solution)/shard_map/onward_cot2/ppermute | solution.py:486
  36.8 4.0 %collective-permute-done.11.refs_0_.refs_10_ = bf16[128,2048]{1,0:T(8,128)(2,1)S(1)} collective-permute-done((bf16[128,2048]{1,0:T(8,128)(2,1)S(1)}, bf16[128,2048]{1,0:T(8,128)(2,1)S(1)}, u32[]{:S(2)}, u32[]{:S(2)}) %collective-permute-start.11) | collective-permute-done | bytes 524320 | tf_op jit(solution)/shard_map/onward_tok3/ppermute | solution.py:486
  42.5 4.6 %collective-permute-done.8.refs_2_.refs_5_ = bf16[144,2048]{1,0:T(8,128)(2,1)S(1)} collective-permute-done((bf16[144,2048]{1,0:T(8,128)(2,1)S(1)}, bf16[144,2048]{1,0:T(8,128)(2,1)S(1)}, u32[]{:S(2)}, u32[]{:S(2)}) %collective-permute-start.8) | collective-permute-done | bytes 589856 | tf_op jit(solution)/shard_map/onward_cot3/ppermute | solution.py:486
  52.4 1.8 %collective-permute-done.10.refs_2_.refs_7_ = bf16[80,2048]{1,0:T(8,128)(2,1)S(1)} collective-permute-done((bf16[80,2048]{1,0:T(8,128)(2,1)S(1)}, bf16[80,2048]{1,0:T(8,128)(2,1)S(1)}, u32[]{:S(2)}, u32[]{:S(2)}) %collective-permute-start.10) | collective-permute-done | bytes 327712 | tf_op jit(solution)/shard_map/onward_cot4/ppermute | solution.py:486
  56.1 4.0 %shard_map.114 = (bf16[1536,1024]{1,0:T(8,128)(2,1)S(1)}, bf16[1536,1024]{1,0:T(8,128)(2,1)S(1)}) custom-call(s32[3]{0:T(128)S(1)} %pad_add_fusion.scalars, bf16[384,1664]{1,0:T(8,128)(2,1)S(1)} %shard_map.111.refs_0_.mine_ref, bf16[128,1664]{1,0:T(8,128)(2,1)S(1)} %shard_map.113.refs_1_.mine_ref, ...), custom_call_target="tpu_custom_call" | custom-call | flops 4000000000 | tf_op jit(solution)/shard_map/pallas_call | solution.py:571
  61.3 1.6 %collective-permute-start.15 = (bf16[64,1024]{1,0:T(8,128)(2,1)S(1)}, bf16[64,1024]{1,0:T(8,128)(2,1)S(1)}, u32[]{:S(2)}, u32[]{:S(2)}) collective-permute-start(bf16[64,1024]{1,0:T(8,128)(2,1)S(1)} %get-tuple-element.101), channel_id=1, source_target_pairs={{4,0},{8,4},{12,8},{14,12},{10,14},{6,10},{2,6},{0,2},{5,1},{9,5},... | collective-permute-start | bytes 393224 | tf_op jit(solution)/shard_map/back_mixed/ppermute | solution.py:413
  64.3 1.8 %collective-permute-start.19 = (bf16[80,1024]{1,0:T(8,128)(2,1)S(1)}, bf16[80,1024]{1,0:T(8,128)(2,1)S(1)}, u32[]{:S(2)}, u32[]{:S(2)}) collective-permute-start(bf16[80,1024]{1,0:T(8,128)(2,1)S(1)} %get-tuple-element.105), channel_id=1, source_target_pairs={{4,0},{8,4},{12,8},{14,12},{10,14},{6,10},{2,6},{0,2},{5,1},{9,5},... | collective-permute-start | bytes 491528 | tf_op jit(solution)/shard_map/back_grad/ppermute | solution.py:413
  69.7 1.6 %collective-permute-start.17 = (bf16[128,1024]{1,0:T(8,128)(2,1)S(1)}, bf16[128,1024]{1,0:T(8,128)(2,1)S(1)}, u32[]{:S(2)}, u32[]{:S(2)}) collective-permute-start(bf16[128,1024]{1,0:T(8,128)(2,1)S(1)} %get-tuple-element.109), channel_id=1, source_target_pairs={{4,0},{8,4},{12,8},{14,12},{10,14},{6,10},{2,6},{0,2},{5,1},{9,5},... | collective-permute-start | bytes 786440 | tf_op jit(solution)/shard_map/back_mixed/ppermute | solution.py:413
  72.2 1.6 %collective-permute-start.32 = (bf16[768,1024]{1,0:T(8,128)(2,1)S(1)}, bf16[768,1024]{1,0:T(8,128)(2,1)S(1)}, u32[]{:S(2)}, u32[]{:S(2)}) collective-permute-start(bf16[768,1024]{1,0:T(8,128)(2,1)S(1)} %shard_map.118), channel_id=1, source_target_pairs={{0,16},{16,0},{1,17},{17,1},{2,18},{18,2},{3,19},{19,3},{4,20},{20... | collective-permute-start | bytes 4718600 | tf_op jit(solution)/shard_map/groups/ppermute | solution.py:593
  74.9 1.6 %collective-permute-start.24 = (bf16[144,1024]{1,0:T(8,128)(2,1)S(1)}, bf16[144,1024]{1,0:T(8,128)(2,1)S(1)}, u32[]{:S(2)}, u32[]{:S(2)}) collective-permute-start(bf16[144,1024]{1,0:T(8,128)(2,1)S(1)} %get-tuple-element.116), channel_id=1, source_target_pairs={{4,0},{8,4},{12,8},{14,12},{10,14},{6,10},{2,6},{0,2},{5,1},{9,5},... | collective-permute-start | bytes 884744 | tf_op jit(solution)/shard_map/back_grad/ppermute | solution.py:413
  80.8 1.6 %collective-permute-start.22 = (bf16[128,1024]{1,0:T(8,128)(2,1)S(1)}, bf16[128,1024]{1,0:T(8,128)(2,1)S(1)}, u32[]{:S(2)}, u32[]{:S(2)}) collective-permute-start(bf16[128,1024]{1,0:T(8,128)(2,1)S(1)} %get-tuple-element.120), channel_id=1, source_target_pairs={{4,0},{8,4},{12,8},{14,12},{10,14},{6,10},{2,6},{0,2},{5,1},{9,5},... | collective-permute-start | bytes 786440 | tf_op jit(solution)/shard_map/back_mixed/ppermute | solution.py:413
  82.9 2.0 %collective-permute-done.24.refs_0_ = bf16[144,1024]{1,0:T(8,128)(2,1)S(1)} collective-permute-done((bf16[144,1024]{1,0:T(8,128)(2,1)S(1)}, bf16[144,1024]{1,0:T(8,128)(2,1)S(1)}, u32[]{:S(2)}, u32[]{:S(2)}) %collective-permute-start.24) | collective-permute-done | bytes 294944 | tf_op jit(solution)/shard_map/back_grad/ppermute | solution.py:413
  84.9 1.6 %collective-permute-done.25.refs_1_ = bf16[144,1024]{1,0:T(8,128)(2,1)S(1)} collective-permute-done((bf16[144,1024]{1,0:T(8,128)(2,1)S(1)}, bf16[144,1024]{1,0:T(8,128)(2,1)S(1)}, u32[]{:S(2)}, u32[]{:S(2)}) %collective-permute-start.25) | collective-permute-done | bytes 294944 | tf_op jit(solution)/shard_map/onward_grad/ppermute | solution.py:411
  87.6 1.6 %collective-permute-start.28 = (bf16[144,1024]{1,0:T(8,128)(2,1)S(1)}, bf16[144,1024]{1,0:T(8,128)(2,1)S(1)}, u32[]{:S(2)}, u32[]{:S(2)}) collective-permute-start(bf16[144,1024]{1,0:T(8,128)(2,1)S(1)} %get-tuple-element.124), channel_id=1, source_target_pairs={{4,0},{8,4},{12,8},{14,12},{10,14},{6,10},{2,6},{0,2},{5,1},{9,5},... | collective-permute-start | bytes 884744 | tf_op jit(solution)/shard_map/back_grad/ppermute | solution.py:413
  90.5 1.6 %collective-permute-done.23.refs_1_ = bf16[128,1024]{1,0:T(8,128)(2,1)S(1)} collective-permute-done((bf16[128,1024]{1,0:T(8,128)(2,1)S(1)}, bf16[128,1024]{1,0:T(8,128)(2,1)S(1)}, u32[]{:S(2)}, u32[]{:S(2)}) %collective-permute-start.23) | collective-permute-done | bytes 262176 | tf_op jit(solution)/shard_map/onward_mixed/ppermute | solution.py:411
  93.2 1.6 %collective-permute-start.26 = (bf16[128,1024]{1,0:T(8,128)(2,1)S(1)}, bf16[128,1024]{1,0:T(8,128)(2,1)S(1)}, u32[]{:S(2)}, u32[]{:S(2)}) collective-permute-start(bf16[128,1024]{1,0:T(8,128)(2,1)S(1)} %get-tuple-element.128), channel_id=1, source_target_pairs={{4,0},{8,4},{12,8},{14,12},{10,14},{6,10},{2,6},{0,2},{5,1},{9,5},... | collective-permute-start | bytes 786440 | tf_op jit(solution)/shard_map/back_mixed/ppermute | solution.py:413
  95.3 2.3 %collective-permute-done.28.refs_0_ = bf16[144,1024]{1,0:T(8,128)(2,1)S(1)} collective-permute-done((bf16[144,1024]{1,0:T(8,128)(2,1)S(1)}, bf16[144,1024]{1,0:T(8,128)(2,1)S(1)}, u32[]{:S(2)}, u32[]{:S(2)}) %collective-permute-start.28) | collective-permute-done | bytes 294944 | tf_op jit(solution)/shard_map/back_grad/ppermute | solution.py:413
  97.6 1.6 %collective-permute-done.29.refs_1_ = bf16[144,1024]{1,0:T(8,128)(2,1)S(1)} collective-permute-done((bf16[144,1024]{1,0:T(8,128)(2,1)S(1)}, bf16[144,1024]{1,0:T(8,128)(2,1)S(1)}, u32[]{:S(2)}, u32[]{:S(2)}) %collective-permute-start.29) | collective-permute-done | bytes 294944 | tf_op jit(solution)/shard_map/onward_grad/ppermute | solution.py:411
  104.4 1.6 %shard_map.124 = bf16[128,1024]{1,0:T(8,128)(2,1)} custom-call(s32[3]{0:T(128)S(1)} %pad_add_fusion.scalars, bf16[128,1664]{1,0:T(8,128)(2,1)S(1)} %shard_map.113.refs_1_.mine_ref, bf16[128,1664]{1,0:T(8,128)(2,1)S(1)} %collective-permute-done.13.arrived_ref, bf16[768,1024]{1,0:T(8,128)(2,1)S(1)} %get-tuple-element.97.w_ref, ...), custom_call_target="tpu_custom_call" | custom-call | flops 2200000000 | tf_op jit(solution)/shard_map/pallas_call | solution.py:41
  108.7 1.7 %shard_map.125 = (bf16[128,1024]{1,0:T(8,128)(2,1)}, f32[4,128]{1,0:T(4,128)}) custom-call(s32[3]{0:T(128)S(1)} %pad_add_fusion.scalars, bf16[128,1664]{1,0:T(8,128)(2,1)S(1)} %shard_map.113.refs_1_.mine_ref, bf16[128,1664]{1,0:T(8,128)(2,1)S(1)} %collective-permute-done.13.arrived_ref, bf16[768,1024]{1,0:T(8,128)(2,1)S(1)} %get-tuple-element.104.w_ref, ...), custom_call_target="tpu_custom_call" | custom-call | flops 2200000000 | tf_op jit(solution)/shard_map/pallas_call | solution.py:41
  110.3 1.8 %shard_map.126 = (f32[384,1024]{1,0:T(8,128)}, f32[384,1024]{1,0:T(8,128)}) custom-call(bf16[1536,1024]{1,0:T(8,128)(2,1)S(1)} %get-tuple-element.99.own_ref, bf16[1536,1024]{1,0:T(8,128)(2,1)S(1)} %collective-permute-done.21.came_ref.other_ref, bf16[768,1024]{1,0:T(8,128)(2,1)S(1)} %collective-permute-done.32.came_ref), custom_call_target="tpu_custom_call" | custom-call | flops 1000000000 | tf_op jit(solution)/shard_map/pallas_call | solution.py:612
  (79 shorter events, 42.6 us)
Async XLA Ops:
  0.6 18.1 %collective-permute-start.2 = (bf16[384,2048]{1,0:T(8,128)(2,1)}, bf16[384,2048]{1,0:T(8,128)(2,1)S(1)}, u32[]{:S(2)}, u32[]{:S(2)}) collective-permute-start(bf16[384,2048]{1,0:T(8,128)(2,1)} %bitcast.12), channel_id=1, source_target_pairs={{0,1},{1,0},{2,3},{3,2},{4,5},{5,4},{6,7},{7,6},{8,9},{9,8},{10,11... | collective-permute-start | bytes 4718600 | tf_op jit(solution)/shard_map/swap_weights/ppermute | solution.py:25
  1.2 10.0 %collective-permute-start.4 = (bf16[128,1024]{1,0:T(8,128)(2,1)}, bf16[128,1024]{1,0:T(8,128)(2,1)S(1)}, u32[]{:S(2)}, u32[]{:S(2)}) collective-permute-start(bf16[128,1024]{1,0:T(8,128)(2,1)} %refs_11_.1), channel_id=1, source_target_pairs={{4,0},{8,4},{12,8},{14,12},{10,14},{6,10},{2,6},{0,2},{5,1},{9,5},... | collective-permute-start | bytes 786440 | tf_op jit(solution)/shard_map/back_tok1/ppermute | solution.py:413
  3.8 9.4 %collective-permute-start.3 = (bf16[128,1024]{1,0:T(8,128)(2,1)}, bf16[128,1024]{1,0:T(8,128)(2,1)S(1)}, u32[]{:S(2)}, u32[]{:S(2)}) collective-permute-start(bf16[128,1024]{1,0:T(8,128)(2,1)} %refs_11_.1), channel_id=1, source_target_pairs={{0,4},{4,8},{8,12},{12,14},{14,10},{10,6},{6,2},{2,0},{1,5},{5,9},... | collective-permute-start | bytes 786440 | tf_op jit(solution)/shard_map/onward_tok1/ppermute | solution.py:411
  6.6 10.7 %collective-permute-start.1 = (bf16[144,1024]{1,0:T(8,128)(2,1)S(1)}, bf16[144,1024]{1,0:T(8,128)(2,1)S(1)}, u32[]{:S(2)}, u32[]{:S(2)}) collective-permute-start(bf16[144,1024]{1,0:T(8,128)(2,1)S(1)} %shard_map.101.refs_0_.refs_6_), channel_id=1, source_target_pairs={{4,0},{8,4},{12,8},{14,12},{10,14},{6,10},{2,6},{0,2},{5,1},{9,5},... | collective-permute-start | bytes 884744 | tf_op jit(solution)/shard_map/back_cot1/ppermute | solution.py:413
  8.6 10.1 %collective-permute-start = (bf16[144,1024]{1,0:T(8,128)(2,1)S(1)}, bf16[144,1024]{1,0:T(8,128)(2,1)S(1)}, u32[]{:S(2)}, u32[]{:S(2)}) collective-permute-start(bf16[144,1024]{1,0:T(8,128)(2,1)S(1)} %shard_map.101.refs_0_.refs_6_), channel_id=1, source_target_pairs={{0,4},{4,8},{8,12},{12,14},{14,10},{10,6},{6,2},{2,0},{1,5},{5,9},... | collective-permute-start | bytes 884744 | tf_op jit(solution)/shard_map/onward_cot1/ppermute | solution.py:411
  19.5 4.3 %collective-permute-start.6 = (bf16[1040,1024]{1,0:T(8,128)(2,1)S(1)}, bf16[1040,1024]{1,0:T(8,128)(2,1)S(1)}, u32[]{:S(2)}, u32[]{:S(2)}) collective-permute-start(bf16[1040,1024]{1,0:T(8,128)(2,1)S(1)} %shard_map.104), channel_id=1, source_target_pairs={{0,1},{1,0},{2,3},{3,2},{4,5},{5,4},{6,7},{7,6},{8,9},{9,8},{10,11... | collective-permute-start | bytes 6389768 | tf_op jit(solution)/shard_map/swap_cot1/ppermute | solution.py:25
  19.6 9.2 %collective-permute-start.9 = (bf16[128,2048]{1,0:T(8,128)(2,1)S(1)}, bf16[128,2048]{1,0:T(8,128)(2,1)S(1)}, u32[]{:S(2)}, u32[]{:S(2)}) collective-permute-start(bf16[128,2048]{1,0:T(8,128)(2,1)S(1)} %shard_map.103.refs_2_.refs_8_), channel_id=1, source_target_pairs={{0,4},{4,8},{8,12},{12,14},{14,10},{10,6},{6,2},{2,0},{5,1},{9,5},... | collective-permute-start | bytes 1572872 | tf_op jit(solution)/shard_map/onward_tok2/ppermute | solution.py:486
  24.4 10.8 %collective-permute-start.7 = (bf16[144,2048]{1,0:T(8,128)(2,1)S(1)}, bf16[144,2048]{1,0:T(8,128)(2,1)S(1)}, u32[]{:S(2)}, u32[]{:S(2)}) collective-permute-start(bf16[144,2048]{1,0:T(8,128)(2,1)S(1)} %shard_map.105.refs_2_.refs_3_), channel_id=1, source_target_pairs={{0,4},{4,8},{8,12},{12,14},{14,10},{10,6},{6,2},{2,0},{5,1},{9,5},... | collective-permute-start | bytes 1769480 | tf_op jit(solution)/shard_map/onward_cot2/ppermute | solution.py:486
  28.8 11.9 %collective-permute-start.11 = (bf16[128,2048]{1,0:T(8,128)(2,1)S(1)}, bf16[128,2048]{1,0:T(8,128)(2,1)S(1)}, u32[]{:S(2)}, u32[]{:S(2)}) collective-permute-start(bf16[128,2048]{1,0:T(8,128)(2,1)S(1)} %collective-permute-done.9.refs_0_.refs_9_), channel_id=1, source_target_pairs={{0,4},{4,8},{8,12},{12,14},{14,10},{10,6},{6,2},{2,0},{5,1},{9,5},... | collective-permute-start | bytes 1572872 | tf_op jit(solution)/shard_map/onward_tok3/ppermute | solution.py:486
  35.2 11.9 %collective-permute-start.8 = (bf16[144,2048]{1,0:T(8,128)(2,1)S(1)}, bf16[144,2048]{1,0:T(8,128)(2,1)S(1)}, u32[]{:S(2)}, u32[]{:S(2)}) collective-permute-start(bf16[144,2048]{1,0:T(8,128)(2,1)S(1)} %collective-permute-done.7.refs_0_.refs_4_), channel_id=1, source_target_pairs={{0,4},{4,8},{8,12},{12,14},{14,10},{10,6},{6,2},{2,0},{5,1},{9,5},... | collective-permute-start | bytes 1769480 | tf_op jit(solution)/shard_map/onward_cot3/ppermute | solution.py:486
  40.8 9.1 %collective-permute-start.12 = (bf16[64,2048]{1,0:T(8,128)(2,1)S(1)}, bf16[64,2048]{1,0:T(8,128)(2,1)S(1)}, u32[]{:S(2)}, u32[]{:S(2)}) collective-permute-start(bf16[64,2048]{1,0:T(8,128)(2,1)S(1)} %slice_select_fusion.1), channel_id=1, source_target_pairs={{0,4},{4,8},{8,12},{12,14},{14,10},{10,6},{6,2},{2,0},{5,1},{9,5},... | collective-permute-start | bytes 786440 | tf_op jit(solution)/shard_map/onward_tok4/ppermute | solution.py:486
  47.1 7.1 %collective-permute-start.10 = (bf16[80,2048]{1,0:T(8,128)(2,1)S(1)}, bf16[80,2048]{1,0:T(8,128)(2,1)S(1)}, u32[]{:S(2)}, u32[]{:S(2)}) collective-permute-start(bf16[80,2048]{1,0:T(8,128)(2,1)S(1)} %slice_select_fusion), channel_id=1, source_target_pairs={{0,4},{4,8},{8,12},{12,14},{14,10},{10,6},{6,2},{2,0},{5,1},{9,5},... | collective-permute-start | bytes 983048 | tf_op jit(solution)/shard_map/onward_cot4/ppermute | solution.py:486
  55.6 4.6 %collective-permute-start.14 = (bf16[384,1664]{1,0:T(8,128)(2,1)S(1)}, bf16[384,1664]{1,0:T(8,128)(2,1)S(1)}, u32[]{:S(2)}, u32[]{:S(2)}) collective-permute-start(bf16[384,1664]{1,0:T(8,128)(2,1)S(1)} %shard_map.111.refs_0_.mine_ref), channel_id=1, source_target_pairs={{0,1},{1,0},{2,3},{3,2},{4,5},{5,4},{6,7},{7,6},{8,9},{9,8},{10,11... | collective-permute-start | bytes 3833864 | tf_op jit(solution)/shard_map/swap_lefts/ppermute | solution.py:25
  55.6 4.6 %collective-permute-start.13 = (bf16[128,1664]{1,0:T(8,128)(2,1)S(1)}, bf16[128,1664]{1,0:T(8,128)(2,1)S(1)}, u32[]{:S(2)}, u32[]{:S(2)}) collective-permute-start(bf16[128,1664]{1,0:T(8,128)(2,1)S(1)} %shard_map.113.refs_1_.mine_ref), channel_id=1, source_target_pairs={{0,1},{1,0},{2,3},{3,2},{4,5},{5,4},{6,7},{7,6},{8,9},{9,8},{10,11... | collective-permute-start | bytes 1277960 | tf_op jit(solution)/shard_map/swap_ends/ppermute | solution.py:25
  61.2 10.6 %collective-permute-start.21 = (bf16[1536,1024]{1,0:T(8,128)(2,1)S(1)}, bf16[1536,1024]{1,0:T(8,128)(2,1)S(1)}, u32[]{:S(2)}, u32[]{:S(2)}) collective-permute-start(bf16[1536,1024]{1,0:T(8,128)(2,1)S(1)} %get-tuple-element.112), channel_id=1, source_target_pairs={{0,1},{1,0},{2,3},{3,2},{4,5},{5,4},{6,7},{7,6},{8,9},{9,8},{10,11... | collective-permute-start | bytes 9437192 | tf_op jit(solution)/shard_map/swap_parts/ppermute | solution.py:25
  61.3 6.0 %collective-permute-start.15 = (bf16[64,1024]{1,0:T(8,128)(2,1)S(1)}, bf16[64,1024]{1,0:T(8,128)(2,1)S(1)}, u32[]{:S(2)}, u32[]{:S(2)}) collective-permute-start(bf16[64,1024]{1,0:T(8,128)(2,1)S(1)} %get-tuple-element.101), channel_id=1, source_target_pairs={{4,0},{8,4},{12,8},{14,12},{10,14},{6,10},{2,6},{0,2},{5,1},{9,5},... | collective-permute-start | bytes 393224 | tf_op jit(solution)/shard_map/back_mixed/ppermute | solution.py:413
  62.9 5.7 %collective-permute-start.16 = (bf16[64,1024]{1,0:T(8,128)(2,1)S(1)}, bf16[64,1024]{1,0:T(8,128)(2,1)S(1)}, u32[]{:S(2)}, u32[]{:S(2)}) collective-permute-start(bf16[64,1024]{1,0:T(8,128)(2,1)S(1)} %get-tuple-element.102), channel_id=1, source_target_pairs={{0,4},{4,8},{8,12},{12,14},{14,10},{10,6},{6,2},{2,0},{1,5},{5,9},... | collective-permute-start | bytes 393224 | tf_op jit(solution)/shard_map/onward_mixed/ppermute | solution.py:411
  64.3 9.5 %collective-permute-start.19 = (bf16[80,1024]{1,0:T(8,128)(2,1)S(1)}, bf16[80,1024]{1,0:T(8,128)(2,1)S(1)}, u32[]{:S(2)}, u32[]{:S(2)}) collective-permute-start(bf16[80,1024]{1,0:T(8,128)(2,1)S(1)} %get-tuple-element.105), channel_id=1, source_target_pairs={{4,0},{8,4},{12,8},{14,12},{10,14},{6,10},{2,6},{0,2},{5,1},{9,5},... | collective-permute-start | bytes 491528 | tf_op jit(solution)/shard_map/back_grad/ppermute | solution.py:413
  66.1 7.7 %collective-permute-start.20 = (bf16[80,1024]{1,0:T(8,128)(2,1)S(1)}, bf16[80,1024]{1,0:T(8,128)(2,1)S(1)}, u32[]{:S(2)}, u32[]{:S(2)}) collective-permute-start(bf16[80,1024]{1,0:T(8,128)(2,1)S(1)} %get-tuple-element.106), channel_id=1, source_target_pairs={{0,4},{4,8},{8,12},{12,14},{14,10},{10,6},{6,2},{2,0},{1,5},{5,9},... | collective-permute-start | bytes 491528 | tf_op jit(solution)/shard_map/onward_grad/ppermute | solution.py:411
  69.7 8.7 %collective-permute-start.17 = (bf16[128,1024]{1,0:T(8,128)(2,1)S(1)}, bf16[128,1024]{1,0:T(8,128)(2,1)S(1)}, u32[]{:S(2)}, u32[]{:S(2)}) collective-permute-start(bf16[128,1024]{1,0:T(8,128)(2,1)S(1)} %get-tuple-element.109), channel_id=1, source_target_pairs={{4,0},{8,4},{12,8},{14,12},{10,14},{6,10},{2,6},{0,2},{5,1},{9,5},... | collective-permute-start | bytes 786440 | tf_op jit(solution)/shard_map/back_mixed/ppermute | solution.py:413
  71.3 8.3 %collective-permute-start.18 = (bf16[128,1024]{1,0:T(8,128)(2,1)S(1)}, bf16[128,1024]{1,0:T(8,128)(2,1)S(1)}, u32[]{:S(2)}, u32[]{:S(2)}) collective-permute-start(bf16[128,1024]{1,0:T(8,128)(2,1)S(1)} %get-tuple-element.110), channel_id=1, source_target_pairs={{0,4},{4,8},{8,12},{12,14},{14,10},{10,6},{6,2},{2,0},{1,5},{5,9},... | collective-permute-start | bytes 786440 | tf_op jit(solution)/shard_map/onward_mixed/ppermute | solution.py:411
  72.2 38.2 %collective-permute-start.32 = (bf16[768,1024]{1,0:T(8,128)(2,1)S(1)}, bf16[768,1024]{1,0:T(8,128)(2,1)S(1)}, u32[]{:S(2)}, u32[]{:S(2)}) collective-permute-start(bf16[768,1024]{1,0:T(8,128)(2,1)S(1)} %shard_map.118), channel_id=1, source_target_pairs={{0,16},{16,0},{1,17},{17,1},{2,18},{18,2},{3,19},{19,3},{4,20},{20... | collective-permute-start | bytes 4718600 | tf_op jit(solution)/shard_map/groups/ppermute | solution.py:593
  74.9 10.0 %collective-permute-start.24 = (bf16[144,1024]{1,0:T(8,128)(2,1)S(1)}, bf16[144,1024]{1,0:T(8,128)(2,1)S(1)}, u32[]{:S(2)}, u32[]{:S(2)}) collective-permute-start(bf16[144,1024]{1,0:T(8,128)(2,1)S(1)} %get-tuple-element.116), channel_id=1, source_target_pairs={{4,0},{8,4},{12,8},{14,12},{10,14},{6,10},{2,6},{0,2},{5,1},{9,5},... | collective-permute-start | bytes 884744 | tf_op jit(solution)/shard_map/back_grad/ppermute | solution.py:413
  76.5 9.9 %collective-permute-start.25 = (bf16[144,1024]{1,0:T(8,128)(2,1)S(1)}, bf16[144,1024]{1,0:T(8,128)(2,1)S(1)}, u32[]{:S(2)}, u32[]{:S(2)}) collective-permute-start(bf16[144,1024]{1,0:T(8,128)(2,1)S(1)} %get-tuple-element.117), channel_id=1, source_target_pairs={{0,4},{4,8},{8,12},{12,14},{14,10},{10,6},{6,2},{2,0},{1,5},{5,9},... | collective-permute-start | bytes 884744 | tf_op jit(solution)/shard_map/onward_grad/ppermute | solution.py:411
  80.8 9.7 %collective-permute-start.22 = (bf16[128,1024]{1,0:T(8,128)(2,1)S(1)}, bf16[128,1024]{1,0:T(8,128)(2,1)S(1)}, u32[]{:S(2)}, u32[]{:S(2)}) collective-permute-start(bf16[128,1024]{1,0:T(8,128)(2,1)S(1)} %get-tuple-element.120), channel_id=1, source_target_pairs={{4,0},{8,4},{12,8},{14,12},{10,14},{6,10},{2,6},{0,2},{5,1},{9,5},... | collective-permute-start | bytes 786440 | tf_op jit(solution)/shard_map/back_mixed/ppermute | solution.py:413
  82.4 9.6 %collective-permute-start.23 = (bf16[128,1024]{1,0:T(8,128)(2,1)S(1)}, bf16[128,1024]{1,0:T(8,128)(2,1)S(1)}, u32[]{:S(2)}, u32[]{:S(2)}) collective-permute-start(bf16[128,1024]{1,0:T(8,128)(2,1)S(1)} %get-tuple-element.121), channel_id=1, source_target_pairs={{0,4},{4,8},{8,12},{12,14},{14,10},{10,6},{6,2},{2,0},{1,5},{5,9},... | collective-permute-start | bytes 786440 | tf_op jit(solution)/shard_map/onward_mixed/ppermute | solution.py:411
  87.6 10.0 %collective-permute-start.28 = (bf16[144,1024]{1,0:T(8,128)(2,1)S(1)}, bf16[144,1024]{1,0:T(8,128)(2,1)S(1)}, u32[]{:S(2)}, u32[]{:S(2)}) collective-permute-start(bf16[144,1024]{1,0:T(8,128)(2,1)S(1)} %get-tuple-element.124), channel_id=1, source_target_pairs={{4,0},{8,4},{12,8},{14,12},{10,14},{6,10},{2,6},{0,2},{5,1},{9,5},... | collective-permute-start | bytes 884744 | tf_op jit(solution)/shard_map/back_grad/ppermute | solution.py:413
  89.2 9.9 %collective-permute-start.29 = (bf16[144,1024]{1,0:T(8,128)(2,1)S(1)}, bf16[144,1024]{1,0:T(8,128)(2,1)S(1)}, u32[]{:S(2)}, u32[]{:S(2)}) collective-permute-start(bf16[144,1024]{1,0:T(8,128)(2,1)S(1)} %get-tuple-element.125), channel_id=1, source_target_pairs={{0,4},{4,8},{8,12},{12,14},{14,10},{10,6},{6,2},{2,0},{1,5},{5,9},... | collective-permute-start | bytes 884744 | tf_op jit(solution)/shard_map/onward_grad/ppermute | solution.py:411
  93.2 10.0 %collective-permute-start.26 = (bf16[128,1024]{1,0:T(8,128)(2,1)S(1)}, bf16[128,1024]{1,0:T(8,128)(2,1)S(1)}, u32[]{:S(2)}, u32[]{:S(2)}) collective-permute-start(bf16[128,1024]{1,0:T(8,128)(2,1)S(1)} %get-tuple-element.128), channel_id=1, source_target_pairs={{4,0},{8,4},{12,8},{14,12},{10,14},{6,10},{2,6},{0,2},{5,1},{9,5},... | collective-permute-start | bytes 786440 | tf_op jit(solution)/shard_map/back_mixed/ppermute | solution.py:413
  94.9 9.5 %collective-permute-start.27 = (bf16[128,1024]{1,0:T(8,128)(2,1)S(1)}, bf16[128,1024]{1,0:T(8,128)(2,1)S(1)}, u32[]{:S(2)}, u32[]{:S(2)}) collective-permute-start(bf16[128,1024]{1,0:T(8,128)(2,1)S(1)} %get-tuple-element.129), channel_id=1, source_target_pairs={{0,4},{4,8},{8,12},{12,14},{14,10},{10,6},{6,2},{2,0},{1,5},{5,9},... | collective-permute-start | bytes 786440 | tf_op jit(solution)/shard_map/onward_mixed/ppermute | solution.py:411
  100.3 7.0 %collective-permute-start.30 = (bf16[144,1024]{1,0:T(8,128)(2,1)S(1)}, bf16[144,1024]{1,0:T(8,128)(2,1)S(1)}, u32[]{:S(2)}, u32[]{:S(2)}) collective-permute-start(bf16[144,1024]{1,0:T(8,128)(2,1)S(1)} %get-tuple-element.132), channel_id=1, source_target_pairs={{4,0},{8,4},{12,8},{14,12},{10,14},{6,10},{2,6},{0,2},{5,1},{9,5},... | collective-permute-start | bytes 884744 | tf_op jit(solution)/shard_map/back_grad/ppermute | solution.py:413
  101.2 7.5 %collective-permute-start.31 = (bf16[144,1024]{1,0:T(8,128)(2,1)S(1)}, bf16[144,1024]{1,0:T(8,128)(2,1)S(1)}, u32[]{:S(2)}, u32[]{:S(2)}) collective-permute-start(bf16[144,1024]{1,0:T(8,128)(2,1)S(1)} %get-tuple-element.133), channel_id=1, source_target_pairs={{0,4},{4,8},{8,12},{12,14},{14,10},{10,6},{6,2},{2,0},{1,5},{5,9},... | collective-permute-start | bytes 884744 | tf_op jit(solution)/shard_map/onward_grad/ppermute | solution.py:411
  (9 other events, 46.5 us)

commit v7 on v6

--- a/solution.py
+++ b/solution.py
@@ -476,7 +476,7 @@
             shapes = [jax.ShapeDtypeStruct((count + extra, width), BF16)] * 2
         kernel = functools.partial(return_kernel, kind, at, first_row, count, experts, rows)
         operands = [mine, arrived, weights, *sums, *more]
-        return call(kernel, shapes, operands, scalars, 22 * 10**8)
+        return call(kernel, shapes, operands, scalars, 30 * 10**8)
 
     apart_pairs = [(2 * i, 2 * j) for i, j in onward_pairs]
     apart_pairs += [(2 * i + 1, 2 * j + 1) for i, j in back_pairs]
@@ -661,15 +661,14 @@
         sent, back_in = back_step(step, back_in, sent)
     own = (0, ends, ends_arrived)
     mixed = returned("own", 0, *own, out_all[0], tied(mixed_in, sent))[0]
-    grad_tokens, grad_gates = returned(
-        "own", units, *own, in_all[0], tied(back_in, (mixed,)), (routes.T,)
-    )
     if n_dp == 2:
-        came = tied((came,), (grad_tokens,))[0]
-        grad_out, grad_in = summed(parts, parts_came, came)
+        grad_out, grad_in = summed(parts, parts_came, tied((came,), (mixed,))[0])
     else:
         both = parts.astype(F32) + parts_came.astype(F32)
         grad_out, grad_in = over_many_groups(both[:units], both[units:])
+    grad_tokens, grad_gates = returned(
+        "own", units, *own, in_all[0], tied(back_in, (mixed, grad_out)), (routes.T,)
+    )
     return (mixed, grad_tokens, grad_gates.T, grad_in[None], grad_out[None])
 
 

time: 112 us -> 111 us (level)
  waiting for transfers between devices: 49.2 us -> 47.7 us
    ppermute x10, waiting for transfers between devices: 13.3 us -> 11.9 us  [both_ways(): return (forth, lax.ppermute(back_value, 'expert', back_pairs))]
    ppermute x10, waiting for transfers between devices: 13.1 us -> 11.8 us  [both_ways(): forth = lax.ppermute(forth_value, 'expert', onward_pairs)]
    ppermute x1, waiting for transfers between devices: 0.01 us -> 1.2 us  [over_groups(): return ((sent,), lax.ppermute(sent, 'dp', [(0, 1), (1, 0)]))]
  transfers between devices with their start and end apart: 33 -> 33, of which waited for: 26 -> 25; matrix products, arithmetic and copies ran while one was open for 0% -> 0% of each run, Pallas kernels for 25% -> 25%
where the time goes in v7:
time: 111 us
  waiting for transfers between devices  47.7 us (43%)
  Pallas kernels  32.5 us (29%)
  starting transfers between devices  27 us (24%)
  local copies, waits for them, and re-layouts  2.34 us (2%)
    pallas_call x21, Pallas kernels, call(): pl.pallas_call(kernel, out_shape=out_shape, in_specs=[pl.BlockSpec(memory...  25.1 us
    ppermute x6, waiting for transfers between devices, apart(): return lax.ppermute(value, ('expert', 'tensor'), apart_pairs)  17.5 us
    ppermute x10, starting transfers between devices, both_ways(): return (forth, lax.ppermute(back_value, 'expert', back_pairs))  16.9 us
    ppermute x10, waiting for transfers between devices, both_ways(): return (forth, lax.ppermute(back_value, 'expert', back_pairs))  11.9 us
    ppermute x10, waiting for transfers between devices, both_ways(): forth = lax.ppermute(forth_value, 'expert', onward_pairs)  11.8 us
    ppermute x6, waiting for transfers between devices, swap_cores(): return lax.ppermute(value, 'tensor', [(0, 1), (1, 0)])  5.28 us
    ppermute x10, starting transfers between devices, both_ways(): forth = lax.ppermute(forth_value, 'expert', onward_pairs)  4.59 us
    pallas_call x1, Pallas kernels, weight_parts(): pl.pallas_call(functools.partial(weight_kernel, steps + 1, rows), out_sha...  4.05 us
  transfers between devices with their start and end apart: 33, of which 25 were waited for; matrix products, arithmetic and copies ran while one was open for 0% of the time, Pallas kernels for 25%

profile of v7, /device:TPU:0, one launch (start us, length us, event | category | flops | bytes accessed | tf_op | source)
XLA Modules:
  0.0 110.7 jit_solution(6973579848860889627)
XLA Ops:
  1.2 2.5 %collective-permute-start.4 = (bf16[128,1024]{1,0:T(8,128)(2,1)}, bf16[128,1024]{1,0:T(8,128)(2,1)S(1)}, u32[]{:S(2)}, u32[]{:S(2)}) collective-permute-start(bf16[128,1024]{1,0:T(8,128)(2,1)} %refs_11_.1), channel_id=1, source_target_pairs={{4,0},{8,4},{12,8},{14,12},{10,14},{6,10},{2,6},{0,2},{5,1},{9,5},... | collective-permute-start | bytes 786440 | tf_op jit(solution)/shard_map/back_tok1/ppermute | solution.py:413
  6.6 2.0 %collective-permute-start.1 = (bf16[144,1024]{1,0:T(8,128)(2,1)S(1)}, bf16[144,1024]{1,0:T(8,128)(2,1)S(1)}, u32[]{:S(2)}, u32[]{:S(2)}) collective-permute-start(bf16[144,1024]{1,0:T(8,128)(2,1)S(1)} %shard_map.101.refs_0_.refs_6_), channel_id=1, source_target_pairs={{4,0},{8,4},{12,8},{14,12},{10,14},{6,10},{2,6},{0,2},{5,1},{9,5},... | collective-permute-start | bytes 884744 | tf_op jit(solution)/shard_map/back_cot1/ppermute | solution.py:413
  8.7 2.5 %collective-permute-done.4.second = bf16[128,1024]{1,0:T(8,128)(2,1)S(1)} collective-permute-done((bf16[128,1024]{1,0:T(8,128)(2,1)}, bf16[128,1024]{1,0:T(8,128)(2,1)S(1)}, u32[]{:S(2)}, u32[]{:S(2)}) %collective-permute-start.4) | collective-permute-done | bytes 262176 | tf_op jit(solution)/shard_map/back_tok1/ppermute | solution.py:413
  11.2 1.9 %collective-permute-done.3.first = bf16[128,1024]{1,0:T(8,128)(2,1)S(1)} collective-permute-done((bf16[128,1024]{1,0:T(8,128)(2,1)}, bf16[128,1024]{1,0:T(8,128)(2,1)S(1)}, u32[]{:S(2)}, u32[]{:S(2)}) %collective-permute-start.3) | collective-permute-done | bytes 262176 | tf_op jit(solution)/shard_map/onward_tok1/ppermute | solution.py:411
  13.8 1.5 %collective-permute-done.5.other = bf16[128,1024]{1,0:T(8,128)(2,1)S(1)} collective-permute-done((bf16[128,1024]{1,0:T(8,128)(2,1)S(1)}, bf16[128,1024]{1,0:T(8,128)(2,1)S(1)}, u32[]{:S(2)}, u32[]{:S(2)}) %collective-permute-start.5) | collective-permute-done | bytes 262176 | tf_op jit(solution)/shard_map/swap_tok1/ppermute | solution.py:25
  15.9 1.4 %collective-permute-done.1.second = bf16[144,1024]{1,0:T(8,128)(2,1)S(1)} collective-permute-done((bf16[144,1024]{1,0:T(8,128)(2,1)S(1)}, bf16[144,1024]{1,0:T(8,128)(2,1)S(1)}, u32[]{:S(2)}, u32[]{:S(2)}) %collective-permute-start.1) | collective-permute-done | bytes 294944 | tf_op jit(solution)/shard_map/back_cot1/ppermute | solution.py:413
  17.3 1.4 %collective-permute-done.first = bf16[144,1024]{1,0:T(8,128)(2,1)S(1)} collective-permute-done((bf16[144,1024]{1,0:T(8,128)(2,1)S(1)}, bf16[144,1024]{1,0:T(8,128)(2,1)S(1)}, u32[]{:S(2)}, u32[]{:S(2)}) %collective-permute-start) | collective-permute-done | bytes 294944 | tf_op jit(solution)/shard_map/onward_cot1/ppermute | solution.py:411
  20.0 3.7 %collective-permute-done.6.other.refs_1_.refs_2_ = bf16[1040,1024]{1,0:T(8,128)(2,1)S(1)} collective-permute-done((bf16[1040,1024]{1,0:T(8,128)(2,1)S(1)}, bf16[1040,1024]{1,0:T(8,128)(2,1)S(1)}, u32[]{:S(2)}, u32[]{:S(2)}) %collective-permute-start.6) | collective-permute-done | bytes 2129952 | tf_op jit(solution)/shard_map/swap_cot1/ppermute | solution.py:25
  24.8 1.9 %shard_map.106 = (bf16[128,768]{1,0:T(8,128)(2,1)S(1)}, f32[128,768]{1,0:T(8,128)S(1)}, bf16[768,1024]{1,0:T(8,128)(2,1)S(1)}, bf16[1024,768]{1,0:T(8,128)(2,1)S(1)}, bf16[1024,768]{1,0:T(8,128)(2,1)S(1)}) custom-call(s32[3]{0:T(128)S(1)} %pad_add_fusion.scalars, bf16[384,2048]{1,0:T(8,128)(2,1)S(1)} %bitcast.13, ...), custom_call_target="tpu_custom_call" | custom-call | flops 1000000000 | tf_op jit(solution)/shard_map/pallas_call | solution.py:41
  26.8 2.1 %collective-permute-done.9.refs_0_.refs_9_ = bf16[128,2048]{1,0:T(8,128)(2,1)S(1)} collective-permute-done((bf16[128,2048]{1,0:T(8,128)(2,1)S(1)}, bf16[128,2048]{1,0:T(8,128)(2,1)S(1)}, u32[]{:S(2)}, u32[]{:S(2)}) %collective-permute-start.9) | collective-permute-done | bytes 524320 | tf_op jit(solution)/shard_map/onward_tok2/ppermute | solution.py:486
  29.2 2.0 %shard_map.107 = (bf16[128,1664]{1,0:T(8,128)(2,1)S(1)}, bf16[768,1024]{1,0:T(8,128)(2,1)S(1)}, bf16[1024,768]{1,0:T(8,128)(2,1)S(1)}, bf16[1024,768]{1,0:T(8,128)(2,1)S(1)}) custom-call(s32[3]{0:T(128)S(1)} %pad_add_fusion.scalars, bf16[384,2048]{1,0:T(8,128)(2,1)S(1)} %bitcast.11, bf16[1040,1024]{1,0:T(8,128)(2,1)S(1)} %collective-permute-done.6.other.refs_1_.refs_2_, ...), custom_call_target="tpu_custom_call" | custom-call | flops 1000000000 | tf_op jit(solution)/shard_map/pallas_call | solution.py:41
  31.3 3.9 %collective-permute-done.7.refs_0_.refs_4_ = bf16[144,2048]{1,0:T(8,128)(2,1)S(1)} collective-permute-done((bf16[144,2048]{1,0:T(8,128)(2,1)S(1)}, bf16[144,2048]{1,0:T(8,128)(2,1)S(1)}, u32[]{:S(2)}, u32[]{:S(2)}) %collective-permute-start.7) | collective-permute-done | bytes 589856 | tf_op jit(solution)/shard_map/onward_cot2/ppermute | solution.py:486
  36.8 4.0 %collective-permute-done.11.refs_0_.refs_10_ = bf16[128,2048]{1,0:T(8,128)(2,1)S(1)} collective-permute-done((bf16[128,2048]{1,0:T(8,128)(2,1)S(1)}, bf16[128,2048]{1,0:T(8,128)(2,1)S(1)}, u32[]{:S(2)}, u32[]{:S(2)}) %collective-permute-start.11) | collective-permute-done | bytes 524320 | tf_op jit(solution)/shard_map/onward_tok3/ppermute | solution.py:486
  42.5 4.6 %collective-permute-done.8.refs_2_.refs_5_ = bf16[144,2048]{1,0:T(8,128)(2,1)S(1)} collective-permute-done((bf16[144,2048]{1,0:T(8,128)(2,1)S(1)}, bf16[144,2048]{1,0:T(8,128)(2,1)S(1)}, u32[]{:S(2)}, u32[]{:S(2)}) %collective-permute-start.8) | collective-permute-done | bytes 589856 | tf_op jit(solution)/shard_map/onward_cot3/ppermute | solution.py:486
  52.4 1.8 %collective-permute-done.10.refs_2_.refs_7_ = bf16[80,2048]{1,0:T(8,128)(2,1)S(1)} collective-permute-done((bf16[80,2048]{1,0:T(8,128)(2,1)S(1)}, bf16[80,2048]{1,0:T(8,128)(2,1)S(1)}, u32[]{:S(2)}, u32[]{:S(2)}) %collective-permute-start.10) | collective-permute-done | bytes 327712 | tf_op jit(solution)/shard_map/onward_cot4/ppermute | solution.py:486
  56.1 4.0 %shard_map.114 = (bf16[1536,1024]{1,0:T(8,128)(2,1)S(1)}, bf16[1536,1024]{1,0:T(8,128)(2,1)S(1)}) custom-call(s32[3]{0:T(128)S(1)} %pad_add_fusion.scalars, bf16[384,1664]{1,0:T(8,128)(2,1)S(1)} %shard_map.111.refs_0_.mine_ref, bf16[128,1664]{1,0:T(8,128)(2,1)S(1)} %shard_map.113.refs_1_.mine_ref, ...), custom_call_target="tpu_custom_call" | custom-call | flops 4000000000 | tf_op jit(solution)/shard_map/pallas_call | solution.py:571
  61.3 1.6 %collective-permute-start.15 = (bf16[64,1024]{1,0:T(8,128)(2,1)S(1)}, bf16[64,1024]{1,0:T(8,128)(2,1)S(1)}, u32[]{:S(2)}, u32[]{:S(2)}) collective-permute-start(bf16[64,1024]{1,0:T(8,128)(2,1)S(1)} %get-tuple-element.101), channel_id=1, source_target_pairs={{4,0},{8,4},{12,8},{14,12},{10,14},{6,10},{2,6},{0,2},{5,1},{9,5},... | collective-permute-start | bytes 393224 | tf_op jit(solution)/shard_map/back_mixed/ppermute | solution.py:413
  64.3 1.8 %collective-permute-start.19 = (bf16[80,1024]{1,0:T(8,128)(2,1)S(1)}, bf16[80,1024]{1,0:T(8,128)(2,1)S(1)}, u32[]{:S(2)}, u32[]{:S(2)}) collective-permute-start(bf16[80,1024]{1,0:T(8,128)(2,1)S(1)} %get-tuple-element.105), channel_id=1, source_target_pairs={{4,0},{8,4},{12,8},{14,12},{10,14},{6,10},{2,6},{0,2},{5,1},{9,5},... | collective-permute-start | bytes 491528 | tf_op jit(solution)/shard_map/back_grad/ppermute | solution.py:413
  69.7 1.6 %collective-permute-start.17 = (bf16[128,1024]{1,0:T(8,128)(2,1)S(1)}, bf16[128,1024]{1,0:T(8,128)(2,1)S(1)}, u32[]{:S(2)}, u32[]{:S(2)}) collective-permute-start(bf16[128,1024]{1,0:T(8,128)(2,1)S(1)} %get-tuple-element.109), channel_id=1, source_target_pairs={{4,0},{8,4},{12,8},{14,12},{10,14},{6,10},{2,6},{0,2},{5,1},{9,5},... | collective-permute-start | bytes 786440 | tf_op jit(solution)/shard_map/back_mixed/ppermute | solution.py:413
  72.2 1.6 %collective-permute-start.32 = (bf16[768,1024]{1,0:T(8,128)(2,1)S(1)}, bf16[768,1024]{1,0:T(8,128)(2,1)S(1)}, u32[]{:S(2)}, u32[]{:S(2)}) collective-permute-start(bf16[768,1024]{1,0:T(8,128)(2,1)S(1)} %shard_map.118), channel_id=1, source_target_pairs={{0,16},{16,0},{1,17},{17,1},{2,18},{18,2},{3,19},{19,3},{4,20},{20... | collective-permute-start | bytes 4718600 | tf_op jit(solution)/shard_map/groups/ppermute | solution.py:593
  74.9 1.6 %collective-permute-start.24 = (bf16[144,1024]{1,0:T(8,128)(2,1)S(1)}, bf16[144,1024]{1,0:T(8,128)(2,1)S(1)}, u32[]{:S(2)}, u32[]{:S(2)}) collective-permute-start(bf16[144,1024]{1,0:T(8,128)(2,1)S(1)} %get-tuple-element.116), channel_id=1, source_target_pairs={{4,0},{8,4},{12,8},{14,12},{10,14},{6,10},{2,6},{0,2},{5,1},{9,5},... | collective-permute-start | bytes 884744 | tf_op jit(solution)/shard_map/back_grad/ppermute | solution.py:413
  80.8 1.6 %collective-permute-start.22 = (bf16[128,1024]{1,0:T(8,128)(2,1)S(1)}, bf16[128,1024]{1,0:T(8,128)(2,1)S(1)}, u32[]{:S(2)}, u32[]{:S(2)}) collective-permute-start(bf16[128,1024]{1,0:T(8,128)(2,1)S(1)} %get-tuple-element.120), channel_id=1, source_target_pairs={{4,0},{8,4},{12,8},{14,12},{10,14},{6,10},{2,6},{0,2},{5,1},{9,5},... | collective-permute-start | bytes 786440 | tf_op jit(solution)/shard_map/back_mixed/ppermute | solution.py:413
  82.9 2.0 %collective-permute-done.24.refs_0_ = bf16[144,1024]{1,0:T(8,128)(2,1)S(1)} collective-permute-done((bf16[144,1024]{1,0:T(8,128)(2,1)S(1)}, bf16[144,1024]{1,0:T(8,128)(2,1)S(1)}, u32[]{:S(2)}, u32[]{:S(2)}) %collective-permute-start.24) | collective-permute-done | bytes 294944 | tf_op jit(solution)/shard_map/back_grad/ppermute | solution.py:413
  84.9 1.6 %collective-permute-done.25.refs_1_ = bf16[144,1024]{1,0:T(8,128)(2,1)S(1)} collective-permute-done((bf16[144,1024]{1,0:T(8,128)(2,1)S(1)}, bf16[144,1024]{1,0:T(8,128)(2,1)S(1)}, u32[]{:S(2)}, u32[]{:S(2)}) %collective-permute-start.25) | collective-permute-done | bytes 294944 | tf_op jit(solution)/shard_map/onward_grad/ppermute | solution.py:411
  87.6 1.6 %collective-permute-start.28 = (bf16[144,1024]{1,0:T(8,128)(2,1)S(1)}, bf16[144,1024]{1,0:T(8,128)(2,1)S(1)}, u32[]{:S(2)}, u32[]{:S(2)}) collective-permute-start(bf16[144,1024]{1,0:T(8,128)(2,1)S(1)} %get-tuple-element.124), channel_id=1, source_target_pairs={{4,0},{8,4},{12,8},{14,12},{10,14},{6,10},{2,6},{0,2},{5,1},{9,5},... | collective-permute-start | bytes 884744 | tf_op jit(solution)/shard_map/back_grad/ppermute | solution.py:413
  90.5 1.6 %collective-permute-done.23.refs_1_ = bf16[128,1024]{1,0:T(8,128)(2,1)S(1)} collective-permute-done((bf16[128,1024]{1,0:T(8,128)(2,1)S(1)}, bf16[128,1024]{1,0:T(8,128)(2,1)S(1)}, u32[]{:S(2)}, u32[]{:S(2)}) %collective-permute-start.23) | collective-permute-done | bytes 262176 | tf_op jit(solution)/shard_map/onward_mixed/ppermute | solution.py:411
  93.2 1.6 %collective-permute-start.26 = (bf16[128,1024]{1,0:T(8,128)(2,1)S(1)}, bf16[128,1024]{1,0:T(8,128)(2,1)S(1)}, u32[]{:S(2)}, u32[]{:S(2)}) collective-permute-start(bf16[128,1024]{1,0:T(8,128)(2,1)S(1)} %get-tuple-element.128), channel_id=1, source_target_pairs={{4,0},{8,4},{12,8},{14,12},{10,14},{6,10},{2,6},{0,2},{5,1},{9,5},... | collective-permute-start | bytes 786440 | tf_op jit(solution)/shard_map/back_mixed/ppermute | solution.py:413
  95.3 2.3 %collective-permute-done.28.refs_0_ = bf16[144,1024]{1,0:T(8,128)(2,1)S(1)} collective-permute-done((bf16[144,1024]{1,0:T(8,128)(2,1)S(1)}, bf16[144,1024]{1,0:T(8,128)(2,1)S(1)}, u32[]{:S(2)}, u32[]{:S(2)}) %collective-permute-start.28) | collective-permute-done | bytes 294944 | tf_op jit(solution)/shard_map/back_grad/ppermute | solution.py:413
  97.6 1.6 %collective-permute-done.29.refs_1_ = bf16[144,1024]{1,0:T(8,128)(2,1)S(1)} collective-permute-done((bf16[144,1024]{1,0:T(8,128)(2,1)S(1)}, bf16[144,1024]{1,0:T(8,128)(2,1)S(1)}, u32[]{:S(2)}, u32[]{:S(2)}) %collective-permute-start.29) | collective-permute-done | bytes 294944 | tf_op jit(solution)/shard_map/onward_grad/ppermute | solution.py:411
  104.4 1.6 %shard_map.124 = bf16[128,1024]{1,0:T(8,128)(2,1)} custom-call(s32[3]{0:T(128)S(1)} %pad_add_fusion.scalars, bf16[128,1664]{1,0:T(8,128)(2,1)S(1)} %shard_map.113.refs_1_.mine_ref, bf16[128,1664]{1,0:T(8,128)(2,1)S(1)} %collective-permute-done.13.arrived_ref, bf16[768,1024]{1,0:T(8,128)(2,1)S(1)} %get-tuple-element.97.w_ref, ...), custom_call_target="tpu_custom_call" | custom-call | flops 3000000000 | tf_op jit(solution)/shard_map/pallas_call | solution.py:41
  107.2 1.8 %shard_map.125 = (f32[384,1024]{1,0:T(8,128)}, f32[384,1024]{1,0:T(8,128)}) custom-call(bf16[1536,1024]{1,0:T(8,128)(2,1)S(1)} %get-tuple-element.99.own_ref, bf16[1536,1024]{1,0:T(8,128)(2,1)S(1)} %collective-permute-done.21.came_ref.other_ref, bf16[768,1024]{1,0:T(8,128)(2,1)S(1)} %collective-permute-done.32.came_ref), custom_call_target="tpu_custom_call" | custom-call | flops 1000000000 | tf_op jit(solution)/shard_map/pallas_call | solution.py:612
  109.0 1.7 %shard_map.126 = (bf16[128,1024]{1,0:T(8,128)(2,1)}, f32[4,128]{1,0:T(4,128)}) custom-call(s32[3]{0:T(128)S(1)} %pad_add_fusion.scalars, bf16[128,1664]{1,0:T(8,128)(2,1)S(1)} %shard_map.113.refs_1_.mine_ref, bf16[128,1664]{1,0:T(8,128)(2,1)S(1)} %collective-permute-done.13.arrived_ref, bf16[768,1024]{1,0:T(8,128)(2,1)S(1)} %get-tuple-element.104.w_ref, ...), custom_call_target="tpu_custom_call" | custom-call | flops 3000000000 | tf_op jit(solution)/shard_map/pallas_call | solution.py:41
  (79 shorter events, 41.1 us)
Async XLA Ops:
  0.6 18.1 %collective-permute-start.2 = (bf16[384,2048]{1,0:T(8,128)(2,1)}, bf16[384,2048]{1,0:T(8,128)(2,1)S(1)}, u32[]{:S(2)}, u32[]{:S(2)}) collective-permute-start(bf16[384,2048]{1,0:T(8,128)(2,1)} %bitcast.12), channel_id=1, source_target_pairs={{0,1},{1,0},{2,3},{3,2},{4,5},{5,4},{6,7},{7,6},{8,9},{9,8},{10,11... | collective-permute-start | bytes 4718600 | tf_op jit(solution)/shard_map/swap_weights/ppermute | solution.py:25
  1.2 10.0 %collective-permute-start.4 = (bf16[128,1024]{1,0:T(8,128)(2,1)}, bf16[128,1024]{1,0:T(8,128)(2,1)S(1)}, u32[]{:S(2)}, u32[]{:S(2)}) collective-permute-start(bf16[128,1024]{1,0:T(8,128)(2,1)} %refs_11_.1), channel_id=1, source_target_pairs={{4,0},{8,4},{12,8},{14,12},{10,14},{6,10},{2,6},{0,2},{5,1},{9,5},... | collective-permute-start | bytes 786440 | tf_op jit(solution)/shard_map/back_tok1/ppermute | solution.py:413
  3.8 9.4 %collective-permute-start.3 = (bf16[128,1024]{1,0:T(8,128)(2,1)}, bf16[128,1024]{1,0:T(8,128)(2,1)S(1)}, u32[]{:S(2)}, u32[]{:S(2)}) collective-permute-start(bf16[128,1024]{1,0:T(8,128)(2,1)} %refs_11_.1), channel_id=1, source_target_pairs={{0,4},{4,8},{8,12},{12,14},{14,10},{10,6},{6,2},{2,0},{1,5},{5,9},... | collective-permute-start | bytes 786440 | tf_op jit(solution)/shard_map/onward_tok1/ppermute | solution.py:411
  6.6 10.7 %collective-permute-start.1 = (bf16[144,1024]{1,0:T(8,128)(2,1)S(1)}, bf16[144,1024]{1,0:T(8,128)(2,1)S(1)}, u32[]{:S(2)}, u32[]{:S(2)}) collective-permute-start(bf16[144,1024]{1,0:T(8,128)(2,1)S(1)} %shard_map.101.refs_0_.refs_6_), channel_id=1, source_target_pairs={{4,0},{8,4},{12,8},{14,12},{10,14},{6,10},{2,6},{0,2},{5,1},{9,5},... | collective-permute-start | bytes 884744 | tf_op jit(solution)/shard_map/back_cot1/ppermute | solution.py:413
  8.6 10.1 %collective-permute-start = (bf16[144,1024]{1,0:T(8,128)(2,1)S(1)}, bf16[144,1024]{1,0:T(8,128)(2,1)S(1)}, u32[]{:S(2)}, u32[]{:S(2)}) collective-permute-start(bf16[144,1024]{1,0:T(8,128)(2,1)S(1)} %shard_map.101.refs_0_.refs_6_), channel_id=1, source_target_pairs={{0,4},{4,8},{8,12},{12,14},{14,10},{10,6},{6,2},{2,0},{1,5},{5,9},... | collective-permute-start | bytes 884744 | tf_op jit(solution)/shard_map/onward_cot1/ppermute | solution.py:411
  19.5 4.3 %collective-permute-start.6 = (bf16[1040,1024]{1,0:T(8,128)(2,1)S(1)}, bf16[1040,1024]{1,0:T(8,128)(2,1)S(1)}, u32[]{:S(2)}, u32[]{:S(2)}) collective-permute-start(bf16[1040,1024]{1,0:T(8,128)(2,1)S(1)} %shard_map.104), channel_id=1, source_target_pairs={{0,1},{1,0},{2,3},{3,2},{4,5},{5,4},{6,7},{7,6},{8,9},{9,8},{10,11... | collective-permute-start | bytes 6389768 | tf_op jit(solution)/shard_map/swap_cot1/ppermute | solution.py:25
  19.6 9.2 %collective-permute-start.9 = (bf16[128,2048]{1,0:T(8,128)(2,1)S(1)}, bf16[128,2048]{1,0:T(8,128)(2,1)S(1)}, u32[]{:S(2)}, u32[]{:S(2)}) collective-permute-start(bf16[128,2048]{1,0:T(8,128)(2,1)S(1)} %shard_map.103.refs_2_.refs_8_), channel_id=1, source_target_pairs={{0,4},{4,8},{8,12},{12,14},{14,10},{10,6},{6,2},{2,0},{5,1},{9,5},... | collective-permute-start | bytes 1572872 | tf_op jit(solution)/shard_map/onward_tok2/ppermute | solution.py:486
  24.4 10.8 %collective-permute-start.7 = (bf16[144,2048]{1,0:T(8,128)(2,1)S(1)}, bf16[144,2048]{1,0:T(8,128)(2,1)S(1)}, u32[]{:S(2)}, u32[]{:S(2)}) collective-permute-start(bf16[144,2048]{1,0:T(8,128)(2,1)S(1)} %shard_map.105.refs_2_.refs_3_), channel_id=1, source_target_pairs={{0,4},{4,8},{8,12},{12,14},{14,10},{10,6},{6,2},{2,0},{5,1},{9,5},... | collective-permute-start | bytes 1769480 | tf_op jit(solution)/shard_map/onward_cot2/ppermute | solution.py:486
  28.8 11.9 %collective-permute-start.11 = (bf16[128,2048]{1,0:T(8,128)(2,1)S(1)}, bf16[128,2048]{1,0:T(8,128)(2,1)S(1)}, u32[]{:S(2)}, u32[]{:S(2)}) collective-permute-start(bf16[128,2048]{1,0:T(8,128)(2,1)S(1)} %collective-permute-done.9.refs_0_.refs_9_), channel_id=1, source_target_pairs={{0,4},{4,8},{8,12},{12,14},{14,10},{10,6},{6,2},{2,0},{5,1},{9,5},... | collective-permute-start | bytes 1572872 | tf_op jit(solution)/shard_map/onward_tok3/ppermute | solution.py:486
  35.2 11.9 %collective-permute-start.8 = (bf16[144,2048]{1,0:T(8,128)(2,1)S(1)}, bf16[144,2048]{1,0:T(8,128)(2,1)S(1)}, u32[]{:S(2)}, u32[]{:S(2)}) collective-permute-start(bf16[144,2048]{1,0:T(8,128)(2,1)S(1)} %collective-permute-done.7.refs_0_.refs_4_), channel_id=1, source_target_pairs={{0,4},{4,8},{8,12},{12,14},{14,10},{10,6},{6,2},{2,0},{5,1},{9,5},... | collective-permute-start | bytes 1769480 | tf_op jit(solution)/shard_map/onward_cot3/ppermute | solution.py:486
  40.8 9.1 %collective-permute-start.12 = (bf16[64,2048]{1,0:T(8,128)(2,1)S(1)}, bf16[64,2048]{1,0:T(8,128)(2,1)S(1)}, u32[]{:S(2)}, u32[]{:S(2)}) collective-permute-start(bf16[64,2048]{1,0:T(8,128)(2,1)S(1)} %slice_select_fusion.1), channel_id=1, source_target_pairs={{0,4},{4,8},{8,12},{12,14},{14,10},{10,6},{6,2},{2,0},{5,1},{9,5},... | collective-permute-start | bytes 786440 | tf_op jit(solution)/shard_map/onward_tok4/ppermute | solution.py:486
  47.1 7.1 %collective-permute-start.10 = (bf16[80,2048]{1,0:T(8,128)(2,1)S(1)}, bf16[80,2048]{1,0:T(8,128)(2,1)S(1)}, u32[]{:S(2)}, u32[]{:S(2)}) collective-permute-start(bf16[80,2048]{1,0:T(8,128)(2,1)S(1)} %slice_select_fusion), channel_id=1, source_target_pairs={{0,4},{4,8},{8,12},{12,14},{14,10},{10,6},{6,2},{2,0},{5,1},{9,5},... | collective-permute-start | bytes 983048 | tf_op jit(solution)/shard_map/onward_cot4/ppermute | solution.py:486
  55.6 4.6 %collective-permute-start.14 = (bf16[384,1664]{1,0:T(8,128)(2,1)S(1)}, bf16[384,1664]{1,0:T(8,128)(2,1)S(1)}, u32[]{:S(2)}, u32[]{:S(2)}) collective-permute-start(bf16[384,1664]{1,0:T(8,128)(2,1)S(1)} %shard_map.111.refs_0_.mine_ref), channel_id=1, source_target_pairs={{0,1},{1,0},{2,3},{3,2},{4,5},{5,4},{6,7},{7,6},{8,9},{9,8},{10,11... | collective-permute-start | bytes 3833864 | tf_op jit(solution)/shard_map/swap_lefts/ppermute | solution.py:25
  55.6 4.6 %collective-permute-start.13 = (bf16[128,1664]{1,0:T(8,128)(2,1)S(1)}, bf16[128,1664]{1,0:T(8,128)(2,1)S(1)}, u32[]{:S(2)}, u32[]{:S(2)}) collective-permute-start(bf16[128,1664]{1,0:T(8,128)(2,1)S(1)} %shard_map.113.refs_1_.mine_ref), channel_id=1, source_target_pairs={{0,1},{1,0},{2,3},{3,2},{4,5},{5,4},{6,7},{7,6},{8,9},{9,8},{10,11... | collective-permute-start | bytes 1277960 | tf_op jit(solution)/shard_map/swap_ends/ppermute | solution.py:25
  61.2 10.6 %collective-permute-start.21 = (bf16[1536,1024]{1,0:T(8,128)(2,1)S(1)}, bf16[1536,1024]{1,0:T(8,128)(2,1)S(1)}, u32[]{:S(2)}, u32[]{:S(2)}) collective-permute-start(bf16[1536,1024]{1,0:T(8,128)(2,1)S(1)} %get-tuple-element.112), channel_id=1, source_target_pairs={{0,1},{1,0},{2,3},{3,2},{4,5},{5,4},{6,7},{7,6},{8,9},{9,8},{10,11... | collective-permute-start | bytes 9437192 | tf_op jit(solution)/shard_map/swap_parts/ppermute | solution.py:25
  61.3 6.0 %collective-permute-start.15 = (bf16[64,1024]{1,0:T(8,128)(2,1)S(1)}, bf16[64,1024]{1,0:T(8,128)(2,1)S(1)}, u32[]{:S(2)}, u32[]{:S(2)}) collective-permute-start(bf16[64,1024]{1,0:T(8,128)(2,1)S(1)} %get-tuple-element.101), channel_id=1, source_target_pairs={{4,0},{8,4},{12,8},{14,12},{10,14},{6,10},{2,6},{0,2},{5,1},{9,5},... | collective-permute-start | bytes 393224 | tf_op jit(solution)/shard_map/back_mixed/ppermute | solution.py:413
  62.9 5.7 %collective-permute-start.16 = (bf16[64,1024]{1,0:T(8,128)(2,1)S(1)}, bf16[64,1024]{1,0:T(8,128)(2,1)S(1)}, u32[]{:S(2)}, u32[]{:S(2)}) collective-permute-start(bf16[64,1024]{1,0:T(8,128)(2,1)S(1)} %get-tuple-element.102), channel_id=1, source_target_pairs={{0,4},{4,8},{8,12},{12,14},{14,10},{10,6},{6,2},{2,0},{1,5},{5,9},... | collective-permute-start | bytes 393224 | tf_op jit(solution)/shard_map/onward_mixed/ppermute | solution.py:411
  64.3 9.5 %collective-permute-start.19 = (bf16[80,1024]{1,0:T(8,128)(2,1)S(1)}, bf16[80,1024]{1,0:T(8,128)(2,1)S(1)}, u32[]{:S(2)}, u32[]{:S(2)}) collective-permute-start(bf16[80,1024]{1,0:T(8,128)(2,1)S(1)} %get-tuple-element.105), channel_id=1, source_target_pairs={{4,0},{8,4},{12,8},{14,12},{10,14},{6,10},{2,6},{0,2},{5,1},{9,5},... | collective-permute-start | bytes 491528 | tf_op jit(solution)/shard_map/back_grad/ppermute | solution.py:413
  66.1 7.7 %collective-permute-start.20 = (bf16[80,1024]{1,0:T(8,128)(2,1)S(1)}, bf16[80,1024]{1,0:T(8,128)(2,1)S(1)}, u32[]{:S(2)}, u32[]{:S(2)}) collective-permute-start(bf16[80,1024]{1,0:T(8,128)(2,1)S(1)} %get-tuple-element.106), channel_id=1, source_target_pairs={{0,4},{4,8},{8,12},{12,14},{14,10},{10,6},{6,2},{2,0},{1,5},{5,9},... | collective-permute-start | bytes 491528 | tf_op jit(solution)/shard_map/onward_grad/ppermute | solution.py:411
  69.7 8.7 %collective-permute-start.17 = (bf16[128,1024]{1,0:T(8,128)(2,1)S(1)}, bf16[128,1024]{1,0:T(8,128)(2,1)S(1)}, u32[]{:S(2)}, u32[]{:S(2)}) collective-permute-start(bf16[128,1024]{1,0:T(8,128)(2,1)S(1)} %get-tuple-element.109), channel_id=1, source_target_pairs={{4,0},{8,4},{12,8},{14,12},{10,14},{6,10},{2,6},{0,2},{5,1},{9,5},... | collective-permute-start | bytes 786440 | tf_op jit(solution)/shard_map/back_mixed/ppermute | solution.py:413
  71.3 8.3 %collective-permute-start.18 = (bf16[128,1024]{1,0:T(8,128)(2,1)S(1)}, bf16[128,1024]{1,0:T(8,128)(2,1)S(1)}, u32[]{:S(2)}, u32[]{:S(2)}) collective-permute-start(bf16[128,1024]{1,0:T(8,128)(2,1)S(1)} %get-tuple-element.110), channel_id=1, source_target_pairs={{0,4},{4,8},{8,12},{12,14},{14,10},{10,6},{6,2},{2,0},{1,5},{5,9},... | collective-permute-start | bytes 786440 | tf_op jit(solution)/shard_map/onward_mixed/ppermute | solution.py:411
  72.2 35.0 %collective-permute-start.32 = (bf16[768,1024]{1,0:T(8,128)(2,1)S(1)}, bf16[768,1024]{1,0:T(8,128)(2,1)S(1)}, u32[]{:S(2)}, u32[]{:S(2)}) collective-permute-start(bf16[768,1024]{1,0:T(8,128)(2,1)S(1)} %shard_map.118), channel_id=1, source_target_pairs={{0,16},{16,0},{1,17},{17,1},{2,18},{18,2},{3,19},{19,3},{4,20},{20... | collective-permute-start | bytes 4718600 | tf_op jit(solution)/shard_map/groups/ppermute | solution.py:593
  74.9 10.0 %collective-permute-start.24 = (bf16[144,1024]{1,0:T(8,128)(2,1)S(1)}, bf16[144,1024]{1,0:T(8,128)(2,1)S(1)}, u32[]{:S(2)}, u32[]{:S(2)}) collective-permute-start(bf16[144,1024]{1,0:T(8,128)(2,1)S(1)} %get-tuple-element.116), channel_id=1, source_target_pairs={{4,0},{8,4},{12,8},{14,12},{10,14},{6,10},{2,6},{0,2},{5,1},{9,5},... | collective-permute-start | bytes 884744 | tf_op jit(solution)/shard_map/back_grad/ppermute | solution.py:413
  76.5 9.9 %collective-permute-start.25 = (bf16[144,1024]{1,0:T(8,128)(2,1)S(1)}, bf16[144,1024]{1,0:T(8,128)(2,1)S(1)}, u32[]{:S(2)}, u32[]{:S(2)}) collective-permute-start(bf16[144,1024]{1,0:T(8,128)(2,1)S(1)} %get-tuple-element.117), channel_id=1, source_target_pairs={{0,4},{4,8},{8,12},{12,14},{14,10},{10,6},{6,2},{2,0},{1,5},{5,9},... | collective-permute-start | bytes 884744 | tf_op jit(solution)/shard_map/onward_grad/ppermute | solution.py:411
  80.8 9.7 %collective-permute-start.22 = (bf16[128,1024]{1,0:T(8,128)(2,1)S(1)}, bf16[128,1024]{1,0:T(8,128)(2,1)S(1)}, u32[]{:S(2)}, u32[]{:S(2)}) collective-permute-start(bf16[128,1024]{1,0:T(8,128)(2,1)S(1)} %get-tuple-element.120), channel_id=1, source_target_pairs={{4,0},{8,4},{12,8},{14,12},{10,14},{6,10},{2,6},{0,2},{5,1},{9,5},... | collective-permute-start | bytes 786440 | tf_op jit(solution)/shard_map/back_mixed/ppermute | solution.py:413
  82.4 9.6 %collective-permute-start.23 = (bf16[128,1024]{1,0:T(8,128)(2,1)S(1)}, bf16[128,1024]{1,0:T(8,128)(2,1)S(1)}, u32[]{:S(2)}, u32[]{:S(2)}) collective-permute-start(bf16[128,1024]{1,0:T(8,128)(2,1)S(1)} %get-tuple-element.121), channel_id=1, source_target_pairs={{0,4},{4,8},{8,12},{12,14},{14,10},{10,6},{6,2},{2,0},{1,5},{5,9},... | collective-permute-start | bytes 786440 | tf_op jit(solution)/shard_map/onward_mixed/ppermute | solution.py:411
  87.6 10.0 %collective-permute-start.28 = (bf16[144,1024]{1,0:T(8,128)(2,1)S(1)}, bf16[144,1024]{1,0:T(8,128)(2,1)S(1)}, u32[]{:S(2)}, u32[]{:S(2)}) collective-permute-start(bf16[144,1024]{1,0:T(8,128)(2,1)S(1)} %get-tuple-element.124), channel_id=1, source_target_pairs={{4,0},{8,4},{12,8},{14,12},{10,14},{6,10},{2,6},{0,2},{5,1},{9,5},... | collective-permute-start | bytes 884744 | tf_op jit(solution)/shard_map/back_grad/ppermute | solution.py:413
  89.2 9.9 %collective-permute-start.29 = (bf16[144,1024]{1,0:T(8,128)(2,1)S(1)}, bf16[144,1024]{1,0:T(8,128)(2,1)S(1)}, u32[]{:S(2)}, u32[]{:S(2)}) collective-permute-start(bf16[144,1024]{1,0:T(8,128)(2,1)S(1)} %get-tuple-element.125), channel_id=1, source_target_pairs={{0,4},{4,8},{8,12},{12,14},{14,10},{10,6},{6,2},{2,0},{1,5},{5,9},... | collective-permute-start | bytes 884744 | tf_op jit(solution)/shard_map/onward_grad/ppermute | solution.py:411
  93.2 10.0 %collective-permute-start.26 = (bf16[128,1024]{1,0:T(8,128)(2,1)S(1)}, bf16[128,1024]{1,0:T(8,128)(2,1)S(1)}, u32[]{:S(2)}, u32[]{:S(2)}) collective-permute-start(bf16[128,1024]{1,0:T(8,128)(2,1)S(1)} %get-tuple-element.128), channel_id=1, source_target_pairs={{4,0},{8,4},{12,8},{14,12},{10,14},{6,10},{2,6},{0,2},{5,1},{9,5},... | collective-permute-start | bytes 786440 | tf_op jit(solution)/shard_map/back_mixed/ppermute | solution.py:413
  94.9 9.5 %collective-permute-start.27 = (bf16[128,1024]{1,0:T(8,128)(2,1)S(1)}, bf16[128,1024]{1,0:T(8,128)(2,1)S(1)}, u32[]{:S(2)}, u32[]{:S(2)}) collective-permute-start(bf16[128,1024]{1,0:T(8,128)(2,1)S(1)} %get-tuple-element.129), channel_id=1, source_target_pairs={{0,4},{4,8},{8,12},{12,14},{14,10},{10,6},{6,2},{2,0},{1,5},{5,9},... | collective-permute-start | bytes 786440 | tf_op jit(solution)/shard_map/onward_mixed/ppermute | solution.py:411
  100.3 8.7 %collective-permute-start.30 = (bf16[144,1024]{1,0:T(8,128)(2,1)S(1)}, bf16[144,1024]{1,0:T(8,128)(2,1)S(1)}, u32[]{:S(2)}, u32[]{:S(2)}) collective-permute-start(bf16[144,1024]{1,0:T(8,128)(2,1)S(1)} %get-tuple-element.132), channel_id=1, source_target_pairs={{4,0},{8,4},{12,8},{14,12},{10,14},{6,10},{2,6},{0,2},{5,1},{9,5},... | collective-permute-start | bytes 884744 | tf_op jit(solution)/shard_map/back_grad/ppermute | solution.py:413
  101.2 7.8 %collective-permute-start.31 = (bf16[144,1024]{1,0:T(8,128)(2,1)S(1)}, bf16[144,1024]{1,0:T(8,128)(2,1)S(1)}, u32[]{:S(2)}, u32[]{:S(2)}) collective-permute-start(bf16[144,1024]{1,0:T(8,128)(2,1)S(1)} %get-tuple-element.133), channel_id=1, source_target_pairs={{0,4},{4,8},{8,12},{12,14},{14,10},{10,6},{6,2},{2,0},{1,5},{5,9},... | collective-permute-start | bytes 884744 | tf_op jit(solution)/shard_map/onward_grad/ppermute | solution.py:411
  (9 other events, 42.0 us)
